TPU v7x, 32 devices: a whole 2x2x4 slice. The times are simulated.
32 devices in a mesh: dp: 4 (over y, x), expert: 8 (over z, core).
Axes of the slice: x: 2, y: 2, z: 4, core: 2. Of those that a mesh axis runs over, the one named last changes fastest.
Arguments:
- tokens: bfloat16 [4096, 7168], P('expert', 'dp'), may hold values from -6 to 6
- grad_out: bfloat16 [4096, 7168], P('expert', 'dp'), may hold values from -6 to 6
- route_ids: int32 [4096, 1], P('expert'), may hold values from 0 to 7; in each aligned block of 512 rows (0 to 511, 512 to 1023, ...) at most 80 rows name the same one
- gate_codes: int32 [4096, 1], P('expert'), may hold values from 1 to 255
- gate_weight: bfloat16 [8, 7168, 1024], P('expert', 'dp'), may hold values from -0.0625 to 0.0625
- up_weight: bfloat16 [8, 7168, 1024], P('expert', 'dp'), may hold values from -0.0625 to 0.0625
- down_weight: bfloat16 [8, 1024, 7168], P('expert', None, 'dp'), may hold values from -0.1875 to 0.1875
- momentum: bfloat16 [8, 1024, 7168], P('expert', None, 'dp'), may hold values from -6 to 6
Outputs:
- grad_tokens: bfloat16 [4096, 7168], P('expert', 'dp')
- new_down: bfloat16 [8, 1024, 7168], P('expert', None, 'dp')
- new_momentum: bfloat16 [8, 1024, 7168], P('expert', None, 'dp')
Inputs may be any that keep to these rules, and one draw needn't show every extreme that they name: `route_ids`: each token names one expert. Among the 512 tokens of one index of the expert axis no expert is named by more than 80 tokens, a bound that some block reaches.
All inputs are finite; a program needn't handle non-finite values.
Results may differ from a plain program's by a relative error of at most 0.022.
Values may be sent and summed in bfloat16 or wider, within the bound.
No kernel may reach another device: no remote copies, remote signals or barrier semaphores. Data moves between devices by JAX's collectives and lax.ppermute only.
A program may use at most 128 MiB of HBM per device.

v0:
```python
import jax
import jax.numpy as jnp
from jax import lax
from jax.sharding import PartitionSpec as P

first_beta = 0.9
second_beta = 0.9
learn_rate = 0.01
decay_rate = 3.0
soft_width = 1.0


def activate(terms):
    pre_gate = terms[:, 0, :]
    pre_up = terms[:, 1, :]
    grad_hidden = terms[:, 2, :]
    sigmoid = jax.nn.sigmoid(pre_gate)
    active = pre_gate * sigmoid
    hidden = (active * pre_up).astype(jnp.bfloat16)
    d_gate = (grad_hidden * pre_up * sigmoid * (1.0 + pre_gate * (1.0 - sigmoid))).astype(
        jnp.bfloat16
    )
    d_up = (grad_hidden * active).astype(jnp.bfloat16)
    return (hidden, d_gate, d_up)


def contract_last(left, right):
    return lax.dot_general(
        left, right, (((1,), (1,)), ((), ())), preferred_element_type=jnp.float32
    )


def contract_first(left, right):
    return lax.dot_general(
        left, right, (((0,), (0,)), ((), ())), preferred_element_type=jnp.float32
    )


def local(tokens, grad_out, route_ids, gate_codes, gate_weight, up_weight, down_weight, momentum):
    n_expert = lax.axis_size("expert")
    tok_rows, slab = tokens.shape
    top = route_ids.shape[1]
    capacity = max(2, tok_rows * top * 5 // (4 * n_expert))
    flat_ids = route_ids.reshape(-1)
    expert_iota = jnp.arange(n_expert, dtype=jnp.int32)
    onehot = (flat_ids[:, None] == expert_iota[None, :]).astype(jnp.int32)
    before = jnp.cumsum(onehot, axis=0) - onehot
    slot = jnp.sum(before * onehot, axis=1)
    target = flat_ids * capacity + slot
    slot_iota = jnp.arange(n_expert * capacity, dtype=jnp.int32)
    placed = (
        (target[None, :] == slot_iota[:, None])
        .astype(jnp.float32)
        .reshape(n_expert * capacity, tok_rows, top)
    )
    route_scale = gate_codes.astype(jnp.float32) / 256.0
    picker = jnp.sum(placed, axis=2).astype(jnp.bfloat16)
    scaler = jnp.sum(placed * route_scale[None, :, :], axis=2).astype(jnp.bfloat16)
    send_x = jnp.dot(picker, tokens, preferred_element_type=jnp.float32).astype(jnp.bfloat16)
    send_dy = jnp.dot(scaler, grad_out, preferred_element_type=jnp.float32).astype(jnp.bfloat16)
    send_x = send_x.reshape(n_expert, capacity, slab)
    send_dy = send_dy.reshape(n_expert, capacity, slab)
    recv_x, recv_dy = (
        lax.all_to_all(send_x, "expert", split_axis=0, concat_axis=0, tiled=True),
        lax.all_to_all(send_dy, "expert", split_axis=0, concat_axis=0, tiled=True),
    )
    x_rows = recv_x.reshape(-1, slab)
    dy_rows = recv_dy.reshape(-1, slab)
    w_gate = gate_weight[0]
    w_up = up_weight[0]
    w_down = down_weight[0]
    dy_part = dy_rows
    gate_part = jnp.dot(x_rows, w_gate, preferred_element_type=jnp.float32)
    up_part = jnp.dot(x_rows, w_up, preferred_element_type=jnp.float32)
    back_part = contract_last(dy_part, w_down)
    shares = lax.psum_scatter(
        jnp.stack([gate_part, up_part, back_part], axis=1).astype(jnp.bfloat16),
        "dp",
        scatter_dimension=0,
        tiled=True,
    ).astype(jnp.float32)
    hidden, d_gate, d_up = activate(shares)
    hidden_part = lax.all_gather(hidden, "dp", axis=0, tiled=True)
    gate_part = lax.all_gather(d_gate, "dp", axis=0, tiled=True)
    up_part = lax.all_gather(d_up, "dp", axis=0, tiled=True)
    dy_part = dy_rows
    grad_w = contract_first(hidden_part, dy_part)
    rows_x = contract_last(gate_part, w_gate) + contract_last(up_part, w_up)
    grad_x = rows_x
    grad_down, grad_x = (grad_w, grad_x)
    back = grad_x.astype(jnp.bfloat16).reshape(n_expert, capacity, slab)
    returned = lax.all_to_all(back, "expert", split_axis=0, concat_axis=0, tiled=True)
    returned = returned.reshape(n_expert * capacity, slab)
    grad_tokens = contract_first(picker, returned).astype(jnp.bfloat16)
    moment = momentum[0].astype(jnp.float32)
    weight = w_down.astype(jnp.float32)
    blend = first_beta * moment + (1.0 - first_beta) * grad_down
    step = blend / jnp.sqrt(blend * blend + soft_width * soft_width)
    agree = jnp.maximum(step * jnp.sign(weight), 0.0)
    new_down = (weight - learn_rate * (step + decay_rate * agree * weight)).astype(jnp.bfloat16)
    new_moment = (second_beta * moment + (1.0 - second_beta) * grad_down).astype(jnp.bfloat16)
    return (grad_tokens, new_down[None], new_moment[None])


def solution(mesh):
    placed = (
        P("expert", "dp"),
        P("expert", "dp"),
        P("expert", None),
        P("expert", None),
        P("expert", "dp", None),
        P("expert", "dp", None),
        P("expert", None, "dp"),
        P("expert", None, "dp"),
    )
    return jax.shard_map(
        local,
        mesh=mesh,
        in_specs=placed,
        out_specs=(P("expert", "dp"), P("expert", None, "dp"), P("expert", None, "dp")),
        check_vma=False,
    )
```

profile of v0, /device:TPU:9, one launch (start us, length us, event | category | flops | bytes accessed | tf_op | source)
XLA Modules:
  0.0 323.8 jit_solution(4868232194379886442)
XLA Ops:
  7.2 0.0 copy-start
  7.2 0.8 fusion.47
  8.0 1.1 reduce-window.6
  9.1 0.2 slice_reduce_fusion
  9.4 0.8 fusion.46
  10.2 0.7 multiply_add_fusion
  10.8 0.0 copy-done
  10.8 2.7 convolution_convert_fusion.1
  13.6 0.0 copy-start.2
  13.6 5.8 %all-to-all-start = ((bf16[8,80,1792]{2,1,0:T(8,128)(2,1)}), bf16[8,80,1792]{2,1,0:T(8,128)(2,1)}, u32[]{:S(2)}, u32[]{:S(2)}) async-start(bf16[8,80,1792]{2,1,0:T(8,128)(2,1)} %bitcast.98), calls=%async_computation | async-start | bytes 4587520 | tf_op jit(solution)/shard_map/all_to_all | solution.py:64
  19.4 0.0 copy-done.2
  19.4 4.2 %convolution_convert_fusion = bf16[640,1792]{1,0:T(8,128)(2,1)} fusion(bf16[512,1792]{1,0:T(8,128)(2,1)} %param.9, f32[512]{0:T(512)S(1)} %bitcast.102, s32[512]{0:T(512)S(1)} %multiply_add_fusion), kind=kOutput, calls=%fused_computation.24 | convolution fusion | flops 1176207360 | bytes 4132864 | tf_op jit(solution)/shard_map/dot_general | solution.py:60
  23.6 45.5 %all-to-all-done = bf16[8,80,1792]{2,1,0:T(8,128)(2,1)} async-done(((bf16[8,80,1792]{2,1,0:T(8,128)(2,1)}), bf16[8,80,1792]{2,1,0:T(8,128)(2,1)}, u32[]{:S(2)}, u32[]{:S(2)}) %all-to-all-start) | async-done | bytes 2293792 | tf_op jit(solution)/shard_map/all_to_all | solution.py:64
  69.1 7.9 %all-to-all-start.1 = ((bf16[8,80,1792]{2,1,0:T(8,128)(2,1)}), bf16[8,80,1792]{2,1,0:T(8,128)(2,1)}, u32[]{:S(2)}, u32[]{:S(2)}) async-start(bf16[8,80,1792]{2,1,0:T(8,128)(2,1)} %bitcast.97), calls=%async_computation.1 | async-start | bytes 4587520 | tf_op jit(solution)/shard_map/all_to_all | solution.py:65
  77.0 0.0 reduce-scatter.2.cloned.1.call-start
  77.0 0.0 copy-start.3
  77.0 5.4 %fusion.31 = bf16[640,1,1024]{2,0,1:T(8,128)(2,1)S(1)} fusion(bf16[640,1792]{1,0:T(8,128)(2,1)} %bitcast.6, bf16[1,1792,1024]{2,1,0:T(8,128)(2,1)} %param.13), kind=kOutput, calls=%fused_computation.31 | convolution fusion | flops 2349465600 | bytes 7274496 | tf_op jit(solution)/shard_map/dot_general | solution.py:74
  82.4 0.0 copy-done.3
  82.4 5.3 %fusion.34 = bf16[640,1,1024]{2,0,1:T(8,128)(2,1)} fusion(bf16[640,1792]{1,0:T(8,128)(2,1)} %bitcast.6, bf16[1,1792,1024]{2,1,0:T(8,128)(2,1)S(1)} %copy-done.3), kind=kOutput, calls=%fused_computation.32 | convolution fusion | flops 2349465600 | bytes 7274496 | tf_op jit(solution)/shard_map/dot_general | solution.py:73
  87.7 39.0 %all-to-all-done.1 = bf16[8,80,1792]{2,1,0:T(8,128)(2,1)} async-done(((bf16[8,80,1792]{2,1,0:T(8,128)(2,1)}), bf16[8,80,1792]{2,1,0:T(8,128)(2,1)}, u32[]{:S(2)}, u32[]{:S(2)}) %all-to-all-start.1) | async-done | bytes 2293792 | tf_op jit(solution)/shard_map/all_to_all | solution.py:65
  126.7 0.0 copy-start.1
  126.7 5.4 %fusion.28 = bf16[640,1,1024]{2,0,1:T(8,128)(2,1)S(1)} fusion(bf16[640,1792]{1,0:T(8,128)(2,1)} %bitcast.13, bf16[1,1024,1792]{2,1,0:T(8,128)(2,1)} %param.14), kind=kOutput, calls=%fused_computation.30 | convolution fusion | flops 2349465600 | bytes 7274496 | tf_op jit(solution)/shard_map/dot_general | solution.py:28
  132.1 0.0 copy-done.1
  132.1 2.1 pad_maximum_fusion
  134.2 0.0 reduce-scatter.2.cloned.1.call-update
  134.3 0.0 all-gather.6.cloned.1.call-start
  134.3 52.4 %reduce-scatter.2.cloned.1.call-done = bf16[160,3,1024]{2,0,1:T(8,128)(2,1)} async-done(((bf16[640,3,1024]{2,0,1:T(8,128)(2,1)}), bf16[160,3,1024]{2,0,1:T(8,128)(2,1)}) %reduce-scatter.2.cloned.1.call-update) | async-done | bytes 983056 | tf_op jit(solution)/shard_map/reduce_scatter | solution.py:76
  186.7 1.4 convert_element_type.104
  188.1 1.4 multiply_convert_fusion
  189.5 0.0 all-gather.6.cloned.1.call-update
  189.5 0.2 all-gather.4.cloned.1.call-start
  189.7 0.5 all-gather.4.cloned.1.call-update
  190.2 28.2 %all-gather.6.cloned.1.call-done = bf16[640,1024]{1,0:T(8,128)(2,1)} async-done(((bf16[160,1024]{1,0:T(8,128)(2,1)}), bf16[640,1024]{1,0:T(8,128)(2,1)}) %all-gather.6.cloned.1.call-update) | async-done | bytes 1310736 | tf_op jit(solution)/shard_map/all_gather | solution.py:85
  218.5 7.1 %fusion.8 = f32[640,1792]{1,0:T(8,128)} fusion(bf16[640,1024]{1,0:T(8,128)(2,1)} %all-gather.6.cloned.1.call-done, bf16[1,1792,1024]{2,1,0:T(8,128)(2,1)} %param.13), kind=kOutput, calls=%fused_computation.14 | convolution fusion | flops 2348810240 | bytes 9568256 | tf_op jit(solution)/shard_map/dot_general | solution.py:28
  225.5 24.2 %all-gather.4.cloned.1.call-done = bf16[640,1024]{1,0:T(8,128)(2,1)} async-done(((bf16[160,1024]{1,0:T(8,128)(2,1)}), bf16[640,1024]{1,0:T(8,128)(2,1)}) %all-gather.4.cloned.1.call-update) | async-done | bytes 1310736 | tf_op jit(solution)/shard_map/all_gather | solution.py:84
  249.7 7.8 %add_convert_fusion = bf16[640,1792]{1,0:T(8,128)(2,1)} fusion(f32[640,1792]{1,0:T(8,128)} %fusion.8, bf16[640,1024]{1,0:T(8,128)(2,1)} %all-gather.4.cloned.1.call-done, bf16[1,1792,1024]{2,1,0:T(8,128)(2,1)} %param.12), kind=kOutput, calls=%fused_computation.10 | convolution fusion | flops 2351104000 | bytes 11862016 | tf_op jit(solution)/shard_map/dot_general | solution.py:28
  257.5 5.5 %all-to-all-start.2 = ((bf16[8,80,1792]{2,1,0:T(8,128)(2,1)}), bf16[8,80,1792]{2,1,0:T(8,128)(2,1)}, u32[]{:S(2)}, u32[]{:S(2)}) async-start(bf16[8,80,1792]{2,1,0:T(8,128)(2,1)} %bitcast.96), calls=%async_computation.3 | async-start | bytes 4587520 | tf_op jit(solution)/shard_map/all_to_all | solution.py:92
  263.0 0.0 all-gather.8.cloned.1.call-start
  263.0 0.6 all-gather.8.cloned.1.call-update
  263.6 30.8 %all-gather.8.cloned.1.call-done = bf16[640,1024]{1,0:T(8,128)(2,1)} async-done(((bf16[160,1024]{1,0:T(8,128)(2,1)}), bf16[640,1024]{1,0:T(8,128)(2,1)}) %all-gather.8.cloned.1.call-update) | async-done | bytes 1310736 | tf_op jit(solution)/shard_map/all_gather | solution.py:83
  294.4 13.5 %convert_bitcast_fusion = (bf16[1,1024,1792]{2,1,0:T(8,128)(2,1)}, bf16[1,1024,1792]{2,1,0:T(8,128)(2,1)}) fusion(bf16[1,1024,1792]{2,1,0:T(8,128)(2,1)} %param.14, bf16[640,1024]{1,0:T(8,128)(2,1)} %all-gather.8.cloned.1.call-done, bf16[640,1792]{1,0:T(8,128)(2,1)} %bitcast.13, bf16[1,1024,1792]{2,1,0:T(8,128)(2,1)} %param.15), kind=kOutput, calls=%fused_computation.22 | convolution fusion | flops 2381840384 | bytes 18284544 | tf_op jit(solution)/shard_map/dot_general | solution.py:34
  307.9 4.8 %all-to-all-done.2 = bf16[8,80,1792]{2,1,0:T(8,128)(2,1)} async-done(((bf16[8,80,1792]{2,1,0:T(8,128)(2,1)}), bf16[8,80,1792]{2,1,0:T(8,128)(2,1)}, u32[]{:S(2)}, u32[]{:S(2)}) %all-to-all-start.2) | async-done | bytes 2293792 | tf_op jit(solution)/shard_map/all_to_all | solution.py:92
  312.7 4.5 %convolution_convert_fusion.2 = bf16[512,1792]{1,0:T(8,128)(2,1)} fusion(bf16[640,1792]{1,0:T(8,128)(2,1)} %bitcast.20, s32[512]{0:T(512)S(1)} %multiply_add_fusion), kind=kOutput, calls=%fused_computation.26 | convolution fusion | flops 1176305664 | bytes 4130816 | tf_op jit(solution)/shard_map/dot_general | solution.py:34
  (3 shorter events, 0.0 us)
Async XLA Ops:
  7.2 3.7 %copy-start = (bf16[512,1792]{1,0:T(8,128)(2,1)S(1)}, bf16[512,1792]{1,0:T(8,128)(2,1)}, u32[]{:S(2)}) copy-start(bf16[512,1792]{1,0:T(8,128)(2,1)} %param.8) | copy-start | bytes 5505028
  13.6 5.8 %copy-start.2 = (s32[512,1]{0,1:T(1,128)S(1)}, s32[512,1]{0,1:T(1,128)}, u32[]{:S(2)}) copy-start(s32[512,1]{0,1:T(1,128)} %param.11) | copy-start | bytes 6148
  13.6 55.5 %all-to-all-start = ((bf16[8,80,1792]{2,1,0:T(8,128)(2,1)}), bf16[8,80,1792]{2,1,0:T(8,128)(2,1)}, u32[]{:S(2)}, u32[]{:S(2)}) async-start(bf16[8,80,1792]{2,1,0:T(8,128)(2,1)} %bitcast.98), calls=%async_computation | async-start | bytes 4587520 | tf_op jit(solution)/shard_map/all_to_all | solution.py:64
  69.1 57.6 %all-to-all-start.1 = ((bf16[8,80,1792]{2,1,0:T(8,128)(2,1)}), bf16[8,80,1792]{2,1,0:T(8,128)(2,1)}, u32[]{:S(2)}, u32[]{:S(2)}) async-start(bf16[8,80,1792]{2,1,0:T(8,128)(2,1)} %bitcast.97), calls=%async_computation.1 | async-start | bytes 4587520 | tf_op jit(solution)/shard_map/all_to_all | solution.py:65
  77.0 109.7 %reduce-scatter.2.cloned.1.call-start = ((), (), s32[]{:S(2)}) async-start(), calls=%async_computation.4 | async-start | bytes 4915200 | tf_op jit(solution)/shard_map/reduce_scatter | solution.py:76
  77.0 5.4 %copy-start.3 = (bf16[1,1792,1024]{2,1,0:T(8,128)(2,1)S(1)}, bf16[1,1792,1024]{2,1,0:T(8,128)(2,1)}, u32[]{:S(2)}) copy-start(bf16[1,1792,1024]{2,1,0:T(8,128)(2,1)} %param.12) | copy-start | bytes 11010052
  126.7 5.4 %copy-start.1 = (bf16[640,1,1024]{2,0,1:T(8,128)(2,1)S(1)}, bf16[640,1,1024]{2,0,1:T(8,128)(2,1)}, u32[]{:S(2)}) copy-start(bf16[640,1,1024]{2,0,1:T(8,128)(2,1)} %fusion.34) | copy-start | bytes 3932164
  134.3 84.2 %all-gather.6.cloned.1.call-start = ((), (), s32[]{:S(2)}) async-start(), calls=%async_computation.6 | async-start | bytes 1638400 | tf_op jit(solution)/shard_map/all_gather | solution.py:85
  189.5 60.2 %all-gather.4.cloned.1.call-start = ((), (), s32[]{:S(2)}) async-start(), calls=%async_computation.5 | async-start | bytes 1638400 | tf_op jit(solution)/shard_map/all_gather | solution.py:84
  257.5 55.2 %all-to-all-start.2 = ((bf16[8,80,1792]{2,1,0:T(8,128)(2,1)}), bf16[8,80,1792]{2,1,0:T(8,128)(2,1)}, u32[]{:S(2)}, u32[]{:S(2)}) async-start(bf16[8,80,1792]{2,1,0:T(8,128)(2,1)} %bitcast.96), calls=%async_computation.3 | async-start | bytes 4587520 | tf_op jit(solution)/shard_map/all_to_all | solution.py:92
  263.0 31.4 %all-gather.8.cloned.1.call-start = ((), (), s32[]{:S(2)}) async-start(), calls=%async_computation.7 | async-start | bytes 1638400 | tf_op jit(solution)/shard_map/all_gather | solution.py:83
Sparse Core Ops, SparseCore 0:
  134.4 52.2 reduce-scatter.1
  189.6 28.7 all-gather.5
  220.9 28.7 all-gather.3
  265.9 28.4 all-gather.7
where the time goes:
time: 329 us; the launch traced here: 324 us
  waiting for transfers between devices  226 us (69%)
  matrix products  56 us (17%)
  starting transfers between devices  19.4 us (6%)
  between operations  13.8 us (4%)
  other arithmetic  8.33 us (3%)
    reduce_scatter x1, waiting for transfers between devices, local(): lax.psum_scatter(jnp.stack([gate_part, up_part, back_part], axis=1).astyp...  52.4 us
    all_to_all x1, waiting for transfers between devices, local(): lax.all_to_all(send_x, 'expert', split_axis=0, concat_axis=0, tiled=True)  45.5 us
    all_to_all x1, waiting for transfers between devices, local(): lax.all_to_all(send_dy, 'expert', split_axis=0, concat_axis=0, tiled=True)  39 us
    all_gather x1, waiting for transfers between devices, local(): hidden_part = lax.all_gather(hidden, 'dp', axis=0, tiled=True)  30.8 us
    all_gather x1, waiting for transfers between devices, local(): up_part = lax.all_gather(d_up, 'dp', axis=0, tiled=True)  28.2 us
    all_gather x1, waiting for transfers between devices, local(): gate_part = lax.all_gather(d_gate, 'dp', axis=0, tiled=True)  24.2 us
    dot_general x3, matrix products, contract_last(): lax.dot_general(left, right, (((1,), (1,)), ((), ())), preferred_element_...  20.3 us
    dot_general x2, matrix products, contract_first(): lax.dot_general(left, right, (((0,), (0,)), ((), ())), preferred_element_...  18 us
  transfers between devices with their start and end apart: 7, of which 7 were waited for; matrix products, arithmetic and copies ran while one was open for 11% of the time, Pallas kernels for 0%

commit v1 on v0

v1 whole, which is shorter than its diff:
```python
import functools

import jax
import jax.numpy as jnp
from jax import lax
from jax.experimental import pallas as pl
from jax.experimental.pallas import tpu as pltpu
from jax.sharding import PartitionSpec as P

first_beta = 0.9
learn_rate = 0.01
decay_rate = 3.0
soft_width = 1.0

TILE = 256
VMEM_BYTES = 24 * 1024 * 1024

bf16 = jnp.bfloat16
f32 = jnp.float32


def grouping(n):
    half = n // 2
    step = max(1, half // 4)
    far = [list(range(i, i + step)) for i in range(half, n, step)]
    cut = half - step
    return far, [list(range(cut)), list(range(cut, half))]


def skipping(body, n_in, n_deps):
    def run(*refs):
        body(*refs[:n_in], *refs[n_in + n_deps :])

    return run


def call(body, operands, deps, out_shape, in_specs, out_specs, grid=(), scalars=0, scratch=(), aliases=None):
    any_spec = pl.BlockSpec(memory_space=pl.ANY)
    return pl.pallas_call(
        skipping(body, len(operands), len(deps)),
        out_shape=out_shape,
        grid_spec=pltpu.PrefetchScalarGridSpec(
            num_scalar_prefetch=scalars,
            grid=grid,
            in_specs=list(in_specs) + [any_spec] * len(deps),
            out_specs=out_specs,
            scratch_shapes=list(scratch),
        ),
        input_output_aliases=aliases or {},
        compiler_params=pltpu.CompilerParams(vmem_limit_bytes=VMEM_BYTES),
        cost_estimate=pl.CostEstimate(flops=0, bytes_accessed=0, transcendentals=0),
    )(*operands, *deps)


def dot(a, b, ca=1, cb=0):
    return lax.dot_general(a, b, (((ca,), (cb,)), ((), ())), preferred_element_type=f32)


def whole(shape):
    return pl.BlockSpec(shape, lambda *_: (0,) * len(shape))


def after_body(*refs):
    pass


def after(value, deps):
    any_spec = pl.BlockSpec(memory_space=pl.ANY)
    return call(
        after_body, [value], deps, jax.ShapeDtypeStruct(value.shape, value.dtype), [any_spec], any_spec, aliases={0: 0}
    )


def dispatch_body(n, cap, offs, first, *refs):
    if first:
        me_ref, ids_ref, codes_ref, x_ref, g_ref, target_ref, *outs = refs
        ids = ids_ref[...]
        t = ids.shape[1]
        hot = (lax.broadcasted_iota(jnp.int32, (n, t), 0) == ids).astype(f32)
        before = (
            lax.broadcasted_iota(jnp.int32, (t, t), 0) < lax.broadcasted_iota(jnp.int32, (t, t), 1)
        ).astype(f32)
        counts = dot(hot.astype(bf16), before.astype(bf16))
        rank = jnp.sum(hot * counts, axis=0, keepdims=True).astype(jnp.int32)
        target = ids * cap + rank
        target_ref[...] = target
    else:
        me_ref, tgt_ref, codes_ref, x_ref, g_ref, *outs = refs
        target = tgt_ref[...]
    t, s = x_ref.shape
    scale = codes_ref[...].astype(f32) / 256.0
    slots = lax.broadcasted_iota(jnp.int32, (cap, t), 0)
    hits = [slots + (me_ref[0] ^ k) * cap == target for k in offs]
    pick = jnp.concatenate([jnp.where(h, 1.0, 0.0).astype(bf16) for h in hits], axis=0)
    scaled = jnp.concatenate([jnp.where(h, scale, 0.0).astype(bf16) for h in hits], axis=0)
    for c in range(0, s, TILE):
        for left, ref, base in ((pick, x_ref, 0), (scaled, g_ref, s)):
            rows = dot(left, ref[:, c : c + TILE]).astype(bf16)
            for i, out in enumerate(outs):
                out[:, base + c : base + c + TILE] = rows[i * cap : (i + 1) * cap]


def dispatch(n, cap, offs, me, marks, codes, x, g, first, deps):
    t, s = x.shape
    out_shape = [jax.ShapeDtypeStruct((cap, 2 * s), bf16) for _ in offs]
    if first:
        out_shape = [jax.ShapeDtypeStruct((1, t), jnp.int32)] + out_shape
    vmem = pl.BlockSpec(memory_space=pltpu.VMEM)
    return call(
        functools.partial(dispatch_body, n, cap, offs, first),
        [me, marks, codes, x, g],
        deps,
        out_shape,
        [pl.BlockSpec(memory_space=pltpu.SMEM)] + [vmem] * 4,
        [vmem] * len(out_shape),
    )


def forward_body(cap, nb, ndp, dp_ref, *refs):
    blocks, (wg, wu, wd), outs, rows = refs[:nb], refs[nb : nb + 3], refs[nb + 3 : -1], refs[-1]
    d = pl.program_id(0)
    s = wg.shape[0]
    hq = wg.shape[1]

    @pl.when(d == 0)
    def _():
        for i, blk in enumerate(blocks):
            rows[i * cap : (i + 1) * cap, :] = blk[...]

    x = rows[:, :s]
    r = rows[:, s:]
    a = dot(x, wg[...]).astype(bf16)
    b = dot(x, wu[...]).astype(bf16)
    q = dot(r, wd[...], 1, 1).astype(bf16)
    for k in range(ndp):

        @pl.when(d == k)
        def _():
            outs[k][:, :hq] = a
            outs[k][:, hq : 2 * hq] = b
            outs[k][:, 2 * hq :] = q


def forward(cap, ndp, dp_idx, blocks, wg, wu, wd, deps):
    s, h = wg.shape
    hq = h // ndp
    nb = len(blocks)
    rows = nb * cap
    return call(
        functools.partial(forward_body, cap, nb, ndp),
        [dp_idx, *blocks, wg, wu, wd],
        deps,
        [jax.ShapeDtypeStruct((rows, 3 * hq), bf16)] * ndp,
        [whole((cap, 2 * s))] * nb
        + [pl.BlockSpec((s, hq), lambda d, i: (0, i[0] ^ d))] * 2
        + [pl.BlockSpec((hq, s), lambda d, i: (i[0] ^ d, 0))],
        [whole((rows, 3 * hq))] * ndp,
        grid=(ndp,),
        scalars=1,
        scratch=[pltpu.VMEM((rows, 2 * s), bf16)],
    )


def activate_body(*refs):
    *parts, out = refs
    hq = out.shape[1] // 3

    def total(j):
        t = parts[0][:, j * hq : (j + 1) * hq].astype(f32)
        for p in parts[1:]:
            t = t + p[:, j * hq : (j + 1) * hq].astype(f32)
        return t

    a, b, q = total(0), total(1), total(2)
    sigma = jax.nn.sigmoid(a)
    act = a * sigma
    out[:, :hq] = (act * b).astype(bf16)
    out[:, hq : 2 * hq] = (q * b * sigma * (1.0 + a * (1.0 - sigma))).astype(bf16)
    out[:, 2 * hq :] = (q * act).astype(bf16)


def activate(parts, deps):
    vmem = pl.BlockSpec(memory_space=pltpu.VMEM)
    return call(
        activate_body, parts, deps, jax.ShapeDtypeStruct(parts[0].shape, bf16), [vmem] * len(parts), vmem
    )


def backward_body(cap, nb, ndp, dp_ref, *refs):
    pieces, (wg, wu), outs, (dg, du) = refs[:ndp], refs[ndp : ndp + 2], refs[ndp + 2 : -2], refs[-2:]
    hq = pieces[0].shape[1] // 3

    @pl.when(pl.program_id(0) == 0)
    def _():
        for d, piece in enumerate(pieces):
            at = pl.ds(pl.multiple_of((dp_ref[0] ^ d) * hq, hq), hq)
            dg[:, at] = piece[:, hq : 2 * hq]
            du[:, at] = piece[:, 2 * hq :]

    rows = (dot(dg[...], wg[...], 1, 1) + dot(du[...], wu[...], 1, 1)).astype(bf16)
    for i, out in enumerate(outs):
        out[...] = rows[i * cap : (i + 1) * cap]


def backward(cap, nb, ndp, dp_idx, pieces, wg, wu, deps):
    s, h = wg.shape
    return call(
        functools.partial(backward_body, cap, nb, ndp),
        [dp_idx, *pieces, wg, wu],
        deps,
        [jax.ShapeDtypeStruct((cap, s), bf16)] * nb,
        [whole(pieces[0].shape)] * ndp + [pl.BlockSpec((TILE, h), lambda c, i: (c, 0))] * 2,
        [pl.BlockSpec((cap, TILE), lambda c, i: (0, c))] * nb,
        grid=(s // TILE,),
        scalars=1,
        scratch=[pltpu.VMEM((nb * cap, h), bf16)] * 2,
    )


def down_body(cap, sizes, ndp, dp_ref, *refs):
    n_pieces = len(sizes) * ndp
    n_blocks = sum(sizes)
    pieces = refs[:n_pieces]
    blocks = refs[n_pieces : n_pieces + n_blocks]
    wd, mom, new_w, new_m, hid_t, dy = refs[n_pieces + n_blocks :]
    hq = pieces[0].shape[1]

    @pl.when(pl.program_id(0) == 0)
    def _():
        base = 0
        for g, size in enumerate(sizes):
            for d in range(ndp):
                at = pl.ds(pl.multiple_of((dp_ref[0] ^ d) * hq, hq), hq)
                piece = pieces[g * ndp + d][...].astype(f32)
                hid_t[at, base : base + size * cap] = piece.T.astype(bf16)
            base += size * cap

    for i, blk in enumerate(blocks):
        dy[i * cap : (i + 1) * cap, :] = blk[...]
    step_rows = 128
    for c in range(0, hid_t.shape[0], step_rows):
        at = slice(c, c + step_rows)
        grad = dot(hid_t[at, :], dy[...])
        w = wd[at, :].astype(f32)
        blend = first_beta * mom[at, :].astype(f32) + (1.0 - first_beta) * grad
        step = blend * lax.rsqrt(blend * blend + soft_width * soft_width)
        agree = jnp.where((step > 0.0) == (w > 0.0), jnp.abs(step), 0.0)
        new_w[at, :] = (w - learn_rate * (step + decay_rate * agree * w)).astype(bf16)
        new_m[at, :] = blend.astype(bf16)


def down(cap, sizes, ndp, dp_idx, pieces, blocks, wd, mom, deps):
    h, s = wd.shape
    hq = h // ndp
    rows = cap * sum(sizes)
    col = pl.BlockSpec((h, TILE), lambda c, i: (0, c))
    return call(
        functools.partial(down_body, cap, sizes, ndp),
        [dp_idx, *pieces, *blocks, wd, mom],
        deps,
        [jax.ShapeDtypeStruct((h, s), bf16)] * 2,
        [whole((p.shape[0], hq)) for p in pieces]
        + [pl.BlockSpec((cap, TILE), lambda c, i: (0, s // TILE + c))] * len(blocks)
        + [col, col],
        [col, col],
        grid=(s // TILE,),
        scalars=1,
        scratch=[pltpu.VMEM((h, rows), bf16), pltpu.VMEM((rows, TILE), bf16)],
    )


def combine_body(cap, offs, chained, me_ref, tgt_ref, *refs):
    nb = len(offs)
    backs = refs[:nb]
    prev = refs[nb] if chained else None
    out, pick_t, rows = refs[-3:]

    @pl.when(pl.program_id(0) == 0)
    def _():
        target = tgt_ref[...]
        slots = lax.broadcasted_iota(jnp.int32, (cap, target.shape[1]), 0)
        for i, k in enumerate(offs):
            hit = jnp.where(slots + (me_ref[0] ^ k) * cap == target, 1.0, 0.0)
            pick_t[i * cap : (i + 1) * cap, :] = hit.astype(bf16)

    for i, blk in enumerate(backs):
        rows[i * cap : (i + 1) * cap, :] = blk[...]
    total = dot(pick_t[...], rows[...], 0, 0)
    if chained:
        total = total + prev[...].astype(f32)
    out[...] = total.astype(bf16)


def combine(cap, offs, me, target, backs, prev, deps):
    t = target.shape[1]
    s = backs[0].shape[1]
    nb = len(offs)
    col = pl.BlockSpec((t, TILE), lambda c, i: (0, c))
    extra = [] if prev is None else [prev]
    return call(
        functools.partial(combine_body, cap, offs, prev is not None),
        [me, target, *backs, *extra],
        deps,
        jax.ShapeDtypeStruct((t, s), bf16),
        [whole((1, t))] + [pl.BlockSpec((cap, TILE), lambda c, i: (0, c))] * nb + [col] * len(extra),
        col,
        grid=(s // TILE,),
        scalars=1,
        scratch=[pltpu.VMEM((nb * cap, t), bf16), pltpu.VMEM((nb * cap, TILE), bf16)],
    )


def local(tokens, grad_out, route_ids, gate_codes, gate_weight, up_weight, down_weight, momentum):
    n = lax.axis_size("expert")
    ndp = lax.axis_size("dp")
    t = tokens.shape[0]
    most = max(2, t * 5 // (4 * n))
    cap = -(-most // 16) * 16
    me = lax.axis_index("expert").astype(jnp.int32).reshape(1)
    dp_idx = lax.axis_index("dp").astype(jnp.int32).reshape(1)
    ids = route_ids.reshape(1, t)
    codes = gate_codes.reshape(1, t)
    wg, wu, wd, mom = gate_weight[0], up_weight[0], down_weight[0], momentum[0]

    def swap_expert(v, k):
        return lax.ppermute(v, "expert", [(i, i ^ k) for i in range(n)])

    def swap_dp(v, k):
        return lax.ppermute(v, "dp", [(i, i ^ k) for i in range(ndp)])

    far, near = grouping(n)
    chunks = [near[0] + far[0], near[1] + far[1]] + far[2:]
    send, got, ready, back, pieces, parts = {}, {}, {}, {}, {}, {}
    mark = []

    def push(offs, deps):
        for k in offs:
            if deps:
                send[k] = after(send[k], mark + deps)
                mark[:] = [send[k]]
            got[k] = swap_expert(send[k], k)

    def give_back(offs, deps):
        for k in offs:
            rows = ready[k]
            if deps:
                rows = after(rows, mark + deps)
                mark[:] = [rows]
            back[k] = swap_expert(rows, k) if k else rows

    def fwd(c):
        own, *others = forward(cap, ndp, dp_idx, [got[k] for k in chunks[c]], wg, wu, wd, mark)
        mark[:] = [own]
        parts[c] = [own] + [swap_dp(v, d + 1) for d, v in enumerate(others)]

    def act(c):
        own = activate(parts[c], mark)
        mark[:] = [own]
        pieces[c] = [own] + [swap_dp(own, d) for d in range(1, ndp)]

    def bwd(c):
        rows = backward(cap, len(chunks[c]), ndp, dp_idx, pieces[c], wg, wu, mark)
        mark[:] = [rows[0]]
        ready.update(zip(chunks[c], rows))

    def gotten(offs):
        return [got[k] for k in offs]

    target, *sends = dispatch(n, cap, far[0], me, ids, codes, tokens, grad_out, True, [])
    send.update(zip(far[0], sends))
    mark[:] = [sends[0]]
    push(far[0], [])
    for offs in (near[0], far[1] + near[1], far[2] + far[3]):
        sends = dispatch(n, cap, offs, me, target, codes, tokens, grad_out, False, mark)
        send.update(zip(offs, sends))
        mark[:] = [sends[0]]
        if offs is near[0]:
            push(offs, [])
            got[0] = send[0]
    inner = [k for k in near[0] if k > 1]

    push(far[1], gotten(far[0]))
    push(near[1], gotten(inner))
    fwd(0)
    push(far[2], gotten(far[1]))
    act(0)
    fwd(1)
    push(far[3], gotten(far[2]))
    bwd(0)
    give_back([0, 1], [])
    fwd(2)
    act(1)
    give_back(far[0], gotten(far[3]))
    give_back(inner, gotten(far[3]))
    fwd(3)
    bwd(1)
    give_back(far[1], [back[k] for k in far[0]])
    give_back(near[1], [back[k] for k in inner])
    act(2)
    act(3)
    bwd(2)
    give_back(far[2], [back[k] for k in far[1]])
    bwd(3)
    order = range(len(chunks))
    flat = [k for c in order for k in chunks[c]]
    new_down, new_moment = down(
        cap,
        [len(chunks[c]) for c in order],
        ndp,
        dp_idx,
        [p for c in order for p in pieces[c]],
        gotten(flat),
        wd,
        mom,
        mark,
    )
    mark[:] = [new_down]
    give_back(far[3], [back[k] for k in far[2]])
    early = [k for k in flat if k not in far[3]]
    part = combine(cap, early, me, target, [back[k] for k in early], None, mark)
    grad_tokens = combine(cap, far[3], me, target, [back[k] for k in far[3]], part, [])
    return (grad_tokens, new_down[None], new_moment[None])


def solution(mesh):
    placed = (
        P("expert", "dp"),
        P("expert", "dp"),
        P("expert", None),
        P("expert", None),
        P("expert", "dp", None),
        P("expert", "dp", None),
        P("expert", None, "dp"),
        P("expert", None, "dp"),
    )
    return jax.shard_map(
        local,
        mesh=mesh,
        in_specs=placed,
        out_specs=(P("expert", "dp"), P("expert", None, "dp"), P("expert", None, "dp")),
        check_vma=False,
    )
```

time: 329 us -> 205 us (0.62); the launches traced: 324 us -> 204 us
  waiting for transfers between devices: 226 us -> 82 us
  Pallas kernels: 0 us -> 56.6 us
  matrix products: 56 us -> 0 us
  starting transfers between devices: 19.4 us -> 50.5 us
  local copies, waits for them, and re-layouts: 0.24 us -> 14.4 us
  between operations: 13.8 us -> 0.93 us
  other arithmetic: 8.33 us -> 0 us
    all_to_all x3 -> x0, waiting for transfers between devices: 89.2 us -> none  [the longest x1 45.5 us: local(): lax.all_to_all(send_x, 'expert', split_axis=0, concat_axis=0, tiled=True)]
    all_gather x3 -> x0, waiting for transfers between devices: 83.2 us -> none  [the longest x1 30.8 us: local(): hidden_part = lax.all_gather(hidden, 'dp', axis=0, tiled=True)]
    ppermute x0 -> x38, waiting for transfers between devices: none -> 82 us  [the longest x14 42.4 us: swap_expert(): return lax.ppermute(v, 'expert', [(i, i ^ k) for i in range(n)])]
    pallas_call x0 -> x29, Pallas kernels: none -> 56.6 us  [call(): pl.pallas_call(skipping(body, len(operands), len(deps)), out_shape=out_sh...]
    dot_general x9 -> x0, matrix products: 56 us -> none  [the longest x3 20.3 us: contract_last(): lax.dot_general(left, right, (((1,), (1,)), ((), ())), preferred_element_...]
    reduce_scatter x1 -> x0, waiting for transfers between devices: 52.4 us -> none  [local(): lax.psum_scatter(jnp.stack([gate_part, up_part, back_part], axis=1).astyp...]
    ppermute x0 -> x38, starting transfers between devices: none -> 50.5 us  [the longest x14 27.1 us: swap_expert(): return lax.ppermute(v, 'expert', [(i, i ^ k) for i in range(n)])]
    all_to_all x3 -> x0, starting transfers between devices: 19.1 us -> none  [the longest x1 7.92 us: local(): lax.all_to_all(send_dy, 'expert', split_axis=0, concat_axis=0, tiled=True)]
  transfers between devices with their start and end apart: 7 -> 38, of which waited for: 7 -> 20; matrix products, arithmetic and copies ran while one was open for 11% -> 0% of each run, Pallas kernels for 0% -> 25%
where the time goes in v1:
time: 205 us; the launch traced here: 204 us
  waiting for transfers between devices  82 us (40%)
  Pallas kernels  56.6 us (28%)
  starting transfers between devices  50.5 us (25%)
  local copies, waits for them, and re-layouts  14.4 us (7%)
    pallas_call x29, Pallas kernels, call(): pl.pallas_call(skipping(body, len(operands), len(deps)), out_shape=out_sh...  56.6 us
    ppermute x14, waiting for transfers between devices, swap_expert(): return lax.ppermute(v, 'expert', [(i, i ^ k) for i in range(n)])  42.4 us
    ppermute x24, waiting for transfers between devices, swap_dp(): return lax.ppermute(v, 'dp', [(i, i ^ k) for i in range(ndp)])  39.6 us
    ppermute x14, starting transfers between devices, swap_expert(): return lax.ppermute(v, 'expert', [(i, i ^ k) for i in range(n)])  27.1 us
    ppermute x24, starting transfers between devices, swap_dp(): return lax.ppermute(v, 'dp', [(i, i ^ k) for i in range(ndp)])  23.3 us
    unnamed x37, local copies, waits for them, and re-layouts  14.4 us
  transfers between devices with their start and end apart: 38, of which 20 were waited for; matrix products, arithmetic and copies ran while one was open for 0% of the time, Pallas kernels for 25%

profile of v1, /device:TPU:9, one launch (start us, length us, event | category | flops | bytes accessed | tf_op | source)
XLA Modules:
  0.0 204.5 jit_solution(9723994498481424449)
XLA Ops:
  0.6 1.5 copy-done.6
  2.1 1.5 copy-done.8
  5.9 2.4 %collective-permute-start = (bf16[80,3584]{1,0:T(8,128)(2,1)S(1)}, bf16[80,3584]{1,0:T(8,128)(2,1)S(1)}, u32[]{:S(2)}, u32[]{:S(2)}) collective-permute-start(bf16[80,3584]{1,0:T(8,128)(2,1)S(1)} %get-tuple-element.37.refs_5_), channel_id=1, source_target_pairs={{0,4},{1,5},{2,6},{3,7},{4,0},{5,1},{6,2},{7,3},{8,12},{9,13},{10,... | collective-permute-start | bytes 1720328 | tf_op jit(solution)/shard_map/ppermute | solution.py:326
  8.3 2.0 %shard_map.104 = (bf16[80,3584]{1,0:T(8,128)(2,1)S(1)}, bf16[80,3584]{1,0:T(8,128)(2,1)}, bf16[80,3584]{1,0:T(8,128)(2,1)}) custom-call(s32[1]{0:T(128)} %bitcast.refs_0_, s32[1,512]{1,0:T(1,128)S(1)} %get-tuple-element.36.refs_1_, s32[1,512]{1,0:T(1,128)S(1)} %bitcast.34, bf16[512,1792]{1,0:T(8,128)(2,1)S(1)} %copy-done.7, bf16[512,1792]{1,0:T(8,128)(2,1)S(1)} %copy-done.9, ...), custom_call_target="tpu_custom_call" | custom-call | tf_op jit(solution)/shard_map/pallas_call | solution.py:39
  10.5 1.2 collective-permute-start.4
  14.1 19.1 %collective-permute-done.refs_2_.refs_4_.refs_20_ = bf16[80,3584]{1,0:T(8,128)(2,1)S(1)} collective-permute-done((bf16[80,3584]{1,0:T(8,128)(2,1)S(1)}, bf16[80,3584]{1,0:T(8,128)(2,1)S(1)}, u32[]{:S(2)}, u32[]{:S(2)}) %collective-permute-start) | collective-permute-done | bytes 573472 | tf_op jit(solution)/shard_map/ppermute | solution.py:326
  33.2 3.5 %collective-permute-start.3 = (bf16[80,3584]{1,0:T(8,128)(2,1)S(1)}, bf16[80,3584]{1,0:T(8,128)(2,1)S(1)}, u32[]{:S(2)}, u32[]{:S(2)}) collective-permute-start(bf16[80,3584]{1,0:T(8,128)(2,1)S(1)} %shard_map.107.refs_1_), channel_id=1, source_target_pairs={{0,5},{1,4},{2,7},{3,6},{4,1},{5,0},{6,3},{7,2},{8,13},{9,12},{10,... | collective-permute-start | bytes 1720328 | tf_op jit(solution)/shard_map/ppermute | solution.py:326
  37.9 2.0 copy-done
  39.9 2.0 copy-done.2
  41.9 2.0 copy-done.4
  44.0 6.7 %shard_map.109 = (bf16[320,768]{1,0:T(8,128)(2,1)S(1)}, bf16[320,768]{1,0:T(8,128)(2,1)S(1)}, bf16[320,768]{1,0:T(8,128)(2,1)S(1)}, bf16[320,768]{1,0:T(8,128)(2,1)S(1)}) custom-call(s32[1]{0:T(128)} %bitcast.3.refs_0_, bf16[80,3584]{1,0:T(8,128)(2,1)S(1)} %get-tuple-element.38.refs_5_.refs_1_.refs_17_, ...), custom_call_target="tpu_custom_call" | custom-call | tf_op jit(solution)/shard_map/pallas_call | solution.py:39
  50.7 1.3 collective-permute-start.5
  52.0 1.2 collective-permute-start.6
  54.6 4.1 %collective-permute-done.3.refs_2_.refs_22_ = bf16[80,3584]{1,0:T(8,128)(2,1)S(1)} collective-permute-done((bf16[80,3584]{1,0:T(8,128)(2,1)S(1)}, bf16[80,3584]{1,0:T(8,128)(2,1)S(1)}, u32[]{:S(2)}, u32[]{:S(2)}) %collective-permute-start.3) | collective-permute-done | bytes 573472 | tf_op jit(solution)/shard_map/ppermute | solution.py:326
  58.7 1.7 collective-permute-start.8
  60.4 3.2 %collective-permute-done.5.refs_1_ = bf16[320,768]{1,0:T(8,128)(2,1)S(1)} collective-permute-done((bf16[320,768]{1,0:T(8,128)(2,1)S(1)}, bf16[320,768]{1,0:T(8,128)(2,1)S(1)}, u32[]{:S(2)}, u32[]{:S(2)}) %collective-permute-start.5) | collective-permute-done | bytes 491552 | tf_op jit(solution)/shard_map/ppermute | solution.py:329
  63.7 10.3 %collective-permute-done.6.refs_2_ = bf16[320,768]{1,0:T(8,128)(2,1)S(1)} collective-permute-done((bf16[320,768]{1,0:T(8,128)(2,1)S(1)}, bf16[320,768]{1,0:T(8,128)(2,1)S(1)}, u32[]{:S(2)}, u32[]{:S(2)}) %collective-permute-start.6) | collective-permute-done | bytes 491552 | tf_op jit(solution)/shard_map/ppermute | solution.py:329
  74.0 1.2 collective-permute-done.7.refs_3_
  78.0 6.6 %collective-permute-done.2.refs_1_.refs_21_ = bf16[80,3584]{1,0:T(8,128)(2,1)S(1)} collective-permute-done((bf16[80,3584]{1,0:T(8,128)(2,1)S(1)}, bf16[80,3584]{1,0:T(8,128)(2,1)S(1)}, u32[]{:S(2)}, u32[]{:S(2)}) %collective-permute-start.2) | collective-permute-done | bytes 573472 | tf_op jit(solution)/shard_map/ppermute | solution.py:326
  84.7 4.2 %shard_map.112 = (bf16[160,768]{1,0:T(8,128)(2,1)S(1)}, bf16[160,768]{1,0:T(8,128)(2,1)S(1)}, bf16[160,768]{1,0:T(8,128)(2,1)S(1)}, bf16[160,768]{1,0:T(8,128)(2,1)S(1)}) custom-call(s32[1]{0:T(128)} %bitcast.3.refs_0_, bf16[80,3584]{1,0:T(8,128)(2,1)S(1)} %collective-permute-done.2.refs_1_.refs_21_, ...), custom_call_target="tpu_custom_call" | custom-call | tf_op jit(solution)/shard_map/pallas_call | solution.py:39
  89.0 1.2 collective-permute-start.10
  91.7 8.5 %collective-permute-done.11.refs_3_ = bf16[320,768]{1,0:T(8,128)(2,1)S(1)} collective-permute-done((bf16[320,768]{1,0:T(8,128)(2,1)S(1)}, bf16[320,768]{1,0:T(8,128)(2,1)S(1)}, u32[]{:S(2)}, u32[]{:S(2)}) %collective-permute-start.11) | collective-permute-done | bytes 491552 | tf_op jit(solution)/shard_map/ppermute | solution.py:329
  101.5 4.1 %shard_map.114 = (bf16[80,1792]{1,0:T(8,128)(2,1)S(1)}, bf16[80,1792]{1,0:T(8,128)(2,1)S(1)}, bf16[80,1792]{1,0:T(8,128)(2,1)S(1)}, bf16[80,1792]{1,0:T(8,128)(2,1)S(1)}) custom-call(s32[1]{0:T(128)} %bitcast.3.refs_0_, bf16[320,768]{1,0:T(8,128)(2,1)S(1)} %shard_map.111.refs_6_.refs_1_, bf16[320,768]{1,0:T(8,128)(2,1)S(1)} %collective-permute-done.10.refs_2_, ...), custom_call_target="tpu_custom_call" | custom-call | tf_op jit(solution)/shard_map/pallas_call | solution.py:39
  105.7 4.0 %shard_map.115 = (bf16[80,768]{1,0:T(8,128)(2,1)S(1)}, bf16[80,768]{1,0:T(8,128)(2,1)S(1)}, bf16[80,768]{1,0:T(8,128)(2,1)S(1)}, bf16[80,768]{1,0:T(8,128)(2,1)S(1)}) custom-call(s32[1]{0:T(128)} %bitcast.3.refs_0_, bf16[80,3584]{1,0:T(8,128)(2,1)S(1)} %collective-permute-done.8.refs_2_.refs_1_.refs_23_, bf16[1792,1024]{1,0:T(8,128)(2,1)S(1)} %bitcast.13, ...), custom_call_target="tpu_custom_call" | custom-call | tf_op jit(solution)/shard_map/pallas_call | solution.py:39
  109.7 3.3 %collective-permute-done.15.refs_3_ = bf16[160,768]{1,0:T(8,128)(2,1)S(1)} collective-permute-done((bf16[160,768]{1,0:T(8,128)(2,1)S(1)}, bf16[160,768]{1,0:T(8,128)(2,1)S(1)}, u32[]{:S(2)}, u32[]{:S(2)}) %collective-permute-start.15) | collective-permute-done | bytes 245792 | tf_op jit(solution)/shard_map/ppermute | solution.py:329
  113.2 1.2 collective-permute-start.24
  114.4 1.8 collective-permute-done.9.refs_2_.refs_1_.refs_24_
  116.2 2.8 %collective-permute-start.25 = (bf16[80,1792]{1,0:T(8,128)(2,1)S(1)}, bf16[80,1792]{1,0:T(8,128)(2,1)S(1)}, u32[]{:S(2)}, u32[]{:S(2)}) collective-permute-start(bf16[80,1792]{1,0:T(8,128)(2,1)S(1)} %shard_map.117.refs_1_), channel_id=1, source_target_pairs={{0,4},{1,5},{2,6},{3,7},{4,0},{5,1},{6,2},{7,3},{8,12},{9,13},{10,... | collective-permute-start | bytes 860168 | tf_op jit(solution)/shard_map/ppermute | solution.py:326
  119.0 1.2 collective-permute-start.23
  121.7 4.0 %shard_map.119 = (bf16[80,768]{1,0:T(8,128)(2,1)S(1)}, bf16[80,768]{1,0:T(8,128)(2,1)S(1)}, bf16[80,768]{1,0:T(8,128)(2,1)S(1)}, bf16[80,768]{1,0:T(8,128)(2,1)S(1)}) custom-call(s32[1]{0:T(128)} %bitcast.3.refs_0_, bf16[80,3584]{1,0:T(8,128)(2,1)S(1)} %collective-permute-done.9.refs_2_.refs_1_.refs_24_, bf16[1792,1024]{1,0:T(8,128)(2,1)S(1)} %bitcast.14, ...), custom_call_target="tpu_custom_call" | custom-call | tf_op jit(solution)/shard_map/pallas_call | solution.py:39
  126.0 3.7 %shard_map.120 = (bf16[80,1792]{1,0:T(8,128)(2,1)S(1)}, bf16[80,1792]{1,0:T(8,128)(2,1)S(1)}) custom-call(s32[1]{0:T(128)} %bitcast.3.refs_0_, bf16[160,768]{1,0:T(8,128)(2,1)S(1)} %shard_map.116.refs_1_.refs_5_, bf16[160,768]{1,0:T(8,128)(2,1)S(1)} %collective-permute-done.22.refs_2_.refs_6_, bf16[160,768]{1,0:T(8,128)(2,1)S(1)} %collective-permute-done.23.refs_3_.refs_7_, ...), custom_call_target="tpu_custom_call" | custom-call | tf_op jit(solution)/shard_map/pallas_call | solution.py:39
  130.5 7.3 %collective-permute-start.33 = (bf16[80,1792]{1,0:T(8,128)(2,1)S(1)}, bf16[80,1792]{1,0:T(8,128)(2,1)S(1)}, u32[]{:S(2)}, u32[]{:S(2)}) collective-permute-start(bf16[80,1792]{1,0:T(8,128)(2,1)S(1)} %shard_map.121.refs_1_), channel_id=1, source_target_pairs={{0,5},{1,4},{2,7},{3,6},{4,1},{5,0},{6,3},{7,2},{8,13},{9,12},{10,... | collective-permute-start | bytes 860168 | tf_op jit(solution)/shard_map/ppermute | solution.py:326
  140.7 4.7 %collective-permute-done.20.refs_2_ = bf16[80,768]{1,0:T(8,128)(2,1)S(1)} collective-permute-done((bf16[80,768]{1,0:T(8,128)(2,1)S(1)}, bf16[80,768]{1,0:T(8,128)(2,1)S(1)}, u32[]{:S(2)}, u32[]{:S(2)}) %collective-permute-start.20) | collective-permute-done | bytes 122912 | tf_op jit(solution)/shard_map/ppermute | solution.py:329
  145.4 1.3 collective-permute-start.18
  147.9 2.9 %collective-permute-done.17.refs_2_ = bf16[80,768]{1,0:T(8,128)(2,1)S(1)} collective-permute-done((bf16[80,768]{1,0:T(8,128)(2,1)S(1)}, bf16[80,768]{1,0:T(8,128)(2,1)S(1)}, u32[]{:S(2)}, u32[]{:S(2)}) %collective-permute-start.17) | collective-permute-done | bytes 122912 | tf_op jit(solution)/shard_map/ppermute | solution.py:329
  150.8 2.1 %collective-permute-start.30 = (bf16[80,768]{1,0:T(8,128)(2,1)S(1)}, bf16[80,768]{1,0:T(8,128)(2,1)S(1)}, u32[]{:S(2)}, u32[]{:S(2)}) collective-permute-start(bf16[80,768]{1,0:T(8,128)(2,1)S(1)} %shard_map.123.refs_4_.refs_1_.refs_9_), channel_id=1, source_target_pairs={{0,8},{8,0},{16,24},{24,16},{1,9},{9,1},{17,25},{25,17},{2,10},{10... | collective-permute-start | bytes 368648 | tf_op jit(solution)/shard_map/ppermute | solution.py:329
  153.0 2.3 %collective-permute-done.31.refs_3_.refs_11_ = bf16[80,768]{1,0:T(8,128)(2,1)S(1)} collective-permute-done((bf16[80,768]{1,0:T(8,128)(2,1)S(1)}, bf16[80,768]{1,0:T(8,128)(2,1)S(1)}, u32[]{:S(2)}, u32[]{:S(2)}) %collective-permute-start.31) | collective-permute-done | bytes 122912 | tf_op jit(solution)/shard_map/ppermute | solution.py:329
  156.5 3.3 %shard_map.125.refs_1_ = bf16[80,1792]{1,0:T(8,128)(2,1)S(1)} custom-call(s32[1]{0:T(128)} %bitcast.3.refs_0_, bf16[80,768]{1,0:T(8,128)(2,1)S(1)} %shard_map.123.refs_4_.refs_1_.refs_9_, bf16[80,768]{1,0:T(8,128)(2,1)S(1)} %collective-permute-done.30.refs_2_.refs_10_, bf16[80,768]{1,0:T(8,128)(2,1)S(1)} %collective-permute-done.31.refs_3_.refs_11_, ...), custom_call_target="tpu_custom_call" | custom-call | tf_op jit(solution)/shard_map/pallas_call | solution.py:39
  159.9 1.8 collective-permute-start.29
  162.9 1.2 collective-permute-start.36
  165.1 3.1 %collective-permute-start.37 = (bf16[80,1792]{1,0:T(8,128)(2,1)S(1)}, bf16[80,1792]{1,0:T(8,128)(2,1)S(1)}, u32[]{:S(2)}, u32[]{:S(2)}) collective-permute-start(bf16[80,1792]{1,0:T(8,128)(2,1)S(1)} %shard_map.122.refs_4_), channel_id=1, source_target_pairs={{0,3},{1,2},{2,1},{3,0},{4,7},{5,6},{6,5},{7,4},{8,11},{9,10},{10,... | collective-permute-start | bytes 860168 | tf_op jit(solution)/shard_map/ppermute | solution.py:326
  168.8 3.3 %shard_map.127.refs_27_.refs_0_ = bf16[80,1792]{1,0:T(8,128)(2,1)S(1)} custom-call(s32[1]{0:T(128)} %bitcast.3.refs_0_, bf16[80,768]{1,0:T(8,128)(2,1)S(1)} %shard_map.124.refs_7_.refs_1_.refs_13_, bf16[80,768]{1,0:T(8,128)(2,1)S(1)} %collective-permute-done.27.refs_2_.refs_14_, bf16[80,768]{1,0:T(8,128)(2,1)S(1)} %collective-permute-done.28.refs_3_.refs_15_, ...), custom_call_target="tpu_custom_call" | custom-call | tf_op jit(solution)/shard_map/pallas_call | solution.py:39
  172.1 10.5 %shard_map.128 = (bf16[1024,1792]{1,0:T(8,128)(2,1)}, bf16[1024,1792]{1,0:T(8,128)(2,1)}) custom-call(s32[1]{0:T(128)} %bitcast.3.refs_0_, bf16[320,768]{1,0:T(8,128)(2,1)S(1)} %shard_map.111.refs_6_.refs_1_, bf16[320,768]{1,0:T(8,128)(2,1)S(1)} %collective-permute-done.10.refs_2_, bf16[320,768]{1,0:T(8,128)(2,1)S(1)} %collective-permute-done.11.refs_3_, ...), custom_call_target="tpu_custom_call" | custom-call | tf_op jit(solution)/shard_map/pallas_call | solution.py:39
  182.6 2.0 copy-done.11
  184.7 2.4 %collective-permute-start.35 = (bf16[80,1792]{1,0:T(8,128)(2,1)S(1)}, bf16[80,1792]{1,0:T(8,128)(2,1)S(1)}, u32[]{:S(2)}, u32[]{:S(2)}) collective-permute-start(bf16[80,1792]{1,0:T(8,128)(2,1)S(1)} %shard_map.129.refs_9_), channel_id=1, source_target_pairs={{0,7},{1,6},{2,5},{3,4},{4,3},{5,2},{6,1},{7,0},{8,15},{9,14},{10,... | collective-permute-start | bytes 860168 | tf_op jit(solution)/shard_map/ppermute | solution.py:326
  187.1 3.4 %shard_map.130.refs_3_ = bf16[512,1792]{1,0:T(8,128)(2,1)S(1)} custom-call(s32[1]{0:T(128)} %bitcast.refs_0_, s32[1,512]{1,0:T(1,128)S(1)} %get-tuple-element.36.refs_1_, bf16[80,1792]{1,0:T(8,128)(2,1)S(1)} %get-tuple-element.55.refs_5_.refs_2_, bf16[80,1792]{1,0:T(8,128)(2,1)S(1)} %collective-permute-done.36.refs_3_, ...), custom_call_target="tpu_custom_call" | custom-call | tf_op jit(solution)/shard_map/pallas_call | solution.py:39
  190.5 10.0 %collective-permute-done.35.refs_2_ = bf16[80,1792]{1,0:T(8,128)(2,1)S(1)} collective-permute-done((bf16[80,1792]{1,0:T(8,128)(2,1)S(1)}, bf16[80,1792]{1,0:T(8,128)(2,1)S(1)}, u32[]{:S(2)}, u32[]{:S(2)}) %collective-permute-start.35) | collective-permute-done | bytes 286752 | tf_op jit(solution)/shard_map/ppermute | solution.py:326
  200.5 4.0 %shard_map.131 = bf16[512,1792]{1,0:T(8,128)(2,1)} custom-call(s32[1]{0:T(128)} %bitcast.refs_0_, s32[1,512]{1,0:T(1,128)S(1)} %get-tuple-element.36.refs_1_, bf16[80,1792]{1,0:T(8,128)(2,1)S(1)} %collective-permute-done.35.refs_2_, bf16[512,1792]{1,0:T(8,128)(2,1)S(1)} %shard_map.130.refs_3_), custom_call_target="tpu_custom_call" | custom-call | tf_op jit(solution)/shard_map/pallas_call | solution.py:39
  (94 shorter events, 23.9 us)
Async XLA Ops:
  5.0 3.3 %copy-start.7 = (bf16[512,1792]{1,0:T(8,128)(2,1)S(1)}, bf16[512,1792]{1,0:T(8,128)(2,1)}, u32[]{:S(2)}) copy-start(bf16[512,1792]{1,0:T(8,128)(2,1)} %refs_3_.7) | copy-start | bytes 5505028
  5.0 3.3 %copy-start.9 = (bf16[512,1792]{1,0:T(8,128)(2,1)S(1)}, bf16[512,1792]{1,0:T(8,128)(2,1)}, u32[]{:S(2)}) copy-start(bf16[512,1792]{1,0:T(8,128)(2,1)} %refs_4_.7) | copy-start | bytes 5505028
  5.9 27.3 %collective-permute-start = (bf16[80,3584]{1,0:T(8,128)(2,1)S(1)}, bf16[80,3584]{1,0:T(8,128)(2,1)S(1)}, u32[]{:S(2)}, u32[]{:S(2)}) collective-permute-start(bf16[80,3584]{1,0:T(8,128)(2,1)S(1)} %get-tuple-element.37.refs_5_), channel_id=1, source_target_pairs={{0,4},{1,5},{2,6},{3,7},{4,0},{5,1},{6,2},{7,3},{8,12},{9,13},{10,... | collective-permute-start | bytes 1720328 | tf_op jit(solution)/shard_map/ppermute | solution.py:326
  10.4 26.4 %collective-permute-start.1 = (bf16[80,3584]{1,0:T(8,128)(2,1)}, bf16[80,3584]{1,0:T(8,128)(2,1)S(1)}, u32[]{:S(2)}, u32[]{:S(2)}) collective-permute-start(bf16[80,3584]{1,0:T(8,128)(2,1)} %get-tuple-element.43), channel_id=1, source_target_pairs={{0,2},{1,3},{2,0},{3,1},{4,6},{5,7},{6,4},{7,5},{8,10},{9,11},{10,... | collective-permute-start | bytes 1720328 | tf_op jit(solution)/shard_map/ppermute | solution.py:326
  10.5 27.3 %collective-permute-start.4 = (bf16[80,3584]{1,0:T(8,128)(2,1)}, bf16[80,3584]{1,0:T(8,128)(2,1)}, u32[]{:S(2)}, u32[]{:S(2)}) collective-permute-start(bf16[80,3584]{1,0:T(8,128)(2,1)} %get-tuple-element.44), channel_id=1, source_target_pairs={{0,1},{1,0},{2,3},{3,2},{4,5},{5,4},{6,7},{7,6},{8,9},{9,8},{10,11... | collective-permute-start | bytes 1720328 | tf_op jit(solution)/shard_map/ppermute | solution.py:326
  14.1 19.1 %copy-start.12 = (bf16[80,3584]{1,0:T(8,128)(2,1)}, bf16[80,3584]{1,0:T(8,128)(2,1)S(1)}, u32[]{:S(2)}) copy-start(bf16[80,3584]{1,0:T(8,128)(2,1)S(1)} %get-tuple-element.40.refs_0_) | copy-start | bytes 1720324
  33.2 25.5 %collective-permute-start.3 = (bf16[80,3584]{1,0:T(8,128)(2,1)S(1)}, bf16[80,3584]{1,0:T(8,128)(2,1)S(1)}, u32[]{:S(2)}, u32[]{:S(2)}) collective-permute-start(bf16[80,3584]{1,0:T(8,128)(2,1)S(1)} %shard_map.107.refs_1_), channel_id=1, source_target_pairs={{0,5},{1,4},{2,7},{3,6},{4,1},{5,0},{6,3},{7,2},{8,13},{9,12},{10,... | collective-permute-start | bytes 1720328 | tf_op jit(solution)/shard_map/ppermute | solution.py:326
  37.8 2.0 copy-start
  44.0 40.7 %copy-start.3 = (bf16[1,1792,1024]{2,1,0:T(8,128)(2,1)S(1)}, bf16[1,1792,1024]{2,1,0:T(8,128)(2,1)}, u32[]{:S(2)}) copy-start(bf16[1,1792,1024]{2,1,0:T(8,128)(2,1)} %param.13) | copy-start | bytes 11010052
  44.0 40.7 %copy-start.5 = (bf16[1,1024,1792]{2,1,0:T(8,128)(2,1)S(1)}, bf16[1,1024,1792]{2,1,0:T(8,128)(2,1)}, u32[]{:S(2)}) copy-start(bf16[1,1024,1792]{2,1,0:T(8,128)(2,1)} %param.14) | copy-start | bytes 11010052
  50.7 34.0 %copy-start.1 = (bf16[1,1792,1024]{2,1,0:T(8,128)(2,1)S(1)}, bf16[1,1792,1024]{2,1,0:T(8,128)(2,1)}, u32[]{:S(2)}) copy-start(bf16[1,1792,1024]{2,1,0:T(8,128)(2,1)} %param.12) | copy-start | bytes 11010052
  50.7 13.0 %collective-permute-start.5 = (bf16[320,768]{1,0:T(8,128)(2,1)S(1)}, bf16[320,768]{1,0:T(8,128)(2,1)S(1)}, u32[]{:S(2)}, u32[]{:S(2)}) collective-permute-start(bf16[320,768]{1,0:T(8,128)(2,1)S(1)} %get-tuple-element.46), channel_id=1, source_target_pairs={{0,8},{8,0},{16,24},{24,16},{1,9},{9,1},{17,25},{25,17},{2,10},{10... | collective-permute-start | bytes 1474568 | tf_op jit(solution)/shard_map/ppermute | solution.py:329
  52.0 22.0 %collective-permute-start.6 = (bf16[320,768]{1,0:T(8,128)(2,1)S(1)}, bf16[320,768]{1,0:T(8,128)(2,1)S(1)}, u32[]{:S(2)}, u32[]{:S(2)}) collective-permute-start(bf16[320,768]{1,0:T(8,128)(2,1)S(1)} %get-tuple-element.47), channel_id=1, source_target_pairs={{0,16},{8,24},{16,0},{24,8},{1,17},{9,25},{17,1},{25,9},{2,18},{10... | collective-permute-start | bytes 1474568 | tf_op jit(solution)/shard_map/ppermute | solution.py:329
  53.2 22.0 %collective-permute-start.7 = (bf16[320,768]{1,0:T(8,128)(2,1)S(1)}, bf16[320,768]{1,0:T(8,128)(2,1)S(1)}, u32[]{:S(2)}, u32[]{:S(2)}) collective-permute-start(bf16[320,768]{1,0:T(8,128)(2,1)S(1)} %get-tuple-element.48), channel_id=1, source_target_pairs={{0,24},{8,16},{16,8},{24,0},{1,25},{9,17},{17,9},{25,1},{2,26},{10... | collective-permute-start | bytes 1474568 | tf_op jit(solution)/shard_map/ppermute | solution.py:329
  53.4 31.3 %collective-permute-start.2 = (bf16[80,3584]{1,0:T(8,128)(2,1)S(1)}, bf16[80,3584]{1,0:T(8,128)(2,1)S(1)}, u32[]{:S(2)}, u32[]{:S(2)}) collective-permute-start(bf16[80,3584]{1,0:T(8,128)(2,1)S(1)} %shard_map.108.refs_8_), channel_id=1, source_target_pairs={{0,3},{1,2},{2,1},{3,0},{4,7},{5,6},{6,5},{7,4},{8,11},{9,10},{10,... | collective-permute-start | bytes 1720328 | tf_op jit(solution)/shard_map/ppermute | solution.py:326
  58.7 30.2 %collective-permute-start.8 = (bf16[80,3584]{1,0:T(8,128)(2,1)S(1)}, bf16[80,3584]{1,0:T(8,128)(2,1)S(1)}, u32[]{:S(2)}, u32[]{:S(2)}) collective-permute-start(bf16[80,3584]{1,0:T(8,128)(2,1)S(1)} %shard_map.110.refs_4_), channel_id=1, source_target_pairs={{0,6},{1,7},{2,4},{3,5},{4,2},{5,3},{6,0},{7,1},{8,14},{9,15},{10,... | collective-permute-start | bytes 1720328 | tf_op jit(solution)/shard_map/ppermute | solution.py:326
  75.6 13.3 %copy-start.13 = (bf16[80,3584]{1,0:T(8,128)(2,1)S(1)}, bf16[80,3584]{1,0:T(8,128)(2,1)}, u32[]{:S(2)}) copy-start(bf16[80,3584]{1,0:T(8,128)(2,1)} %copy-done.12) | copy-start | bytes 1720324
  75.6 14.9 %collective-permute-start.12 = (bf16[320,768]{1,0:T(8,128)(2,1)S(1)}, bf16[320,768]{1,0:T(8,128)(2,1)S(1)}, u32[]{:S(2)}, u32[]{:S(2)}) collective-permute-start(bf16[320,768]{1,0:T(8,128)(2,1)S(1)} %shard_map.111.refs_6_.refs_1_), channel_id=1, source_target_pairs={{0,24},{8,16},{16,8},{24,0},{1,25},{9,17},{17,9},{25,1},{2,26},{10... | collective-permute-start | bytes 1474568 | tf_op jit(solution)/shard_map/ppermute | solution.py:329
  76.8 23.4 %collective-permute-start.11 = (bf16[320,768]{1,0:T(8,128)(2,1)S(1)}, bf16[320,768]{1,0:T(8,128)(2,1)S(1)}, u32[]{:S(2)}, u32[]{:S(2)}) collective-permute-start(bf16[320,768]{1,0:T(8,128)(2,1)S(1)} %shard_map.111.refs_6_.refs_1_), channel_id=1, source_target_pairs={{0,16},{8,24},{16,0},{24,8},{1,17},{9,25},{17,1},{25,9},{2,18},{10... | collective-permute-start | bytes 1474568 | tf_op jit(solution)/shard_map/ppermute | solution.py:329
  88.9 27.3 %collective-permute-start.9 = (bf16[80,3584]{1,0:T(8,128)(2,1)S(1)}, bf16[80,3584]{1,0:T(8,128)(2,1)S(1)}, u32[]{:S(2)}, u32[]{:S(2)}) collective-permute-start(bf16[80,3584]{1,0:T(8,128)(2,1)S(1)} %shard_map.113.refs_7_), channel_id=1, source_target_pairs={{0,7},{1,6},{2,5},{3,4},{4,3},{5,2},{6,1},{7,0},{8,15},{9,14},{10,... | collective-permute-start | bytes 1720328 | tf_op jit(solution)/shard_map/ppermute | solution.py:326
  89.0 12.5 %collective-permute-start.10 = (bf16[320,768]{1,0:T(8,128)(2,1)S(1)}, bf16[320,768]{1,0:T(8,128)(2,1)S(1)}, u32[]{:S(2)}, u32[]{:S(2)}) collective-permute-start(bf16[320,768]{1,0:T(8,128)(2,1)S(1)} %shard_map.111.refs_6_.refs_1_), channel_id=1, source_target_pairs={{0,8},{8,0},{16,24},{24,16},{1,9},{9,1},{17,25},{25,17},{2,10},{10... | collective-permute-start | bytes 1474568 | tf_op jit(solution)/shard_map/ppermute | solution.py:329
  90.2 19.5 %collective-permute-start.13 = (bf16[160,768]{1,0:T(8,128)(2,1)S(1)}, bf16[160,768]{1,0:T(8,128)(2,1)S(1)}, u32[]{:S(2)}, u32[]{:S(2)}) collective-permute-start(bf16[160,768]{1,0:T(8,128)(2,1)S(1)} %get-tuple-element.52), channel_id=1, source_target_pairs={{0,8},{8,0},{16,24},{24,16},{1,9},{9,1},{17,25},{25,17},{2,10},{10... | collective-permute-start | bytes 737288 | tf_op jit(solution)/shard_map/ppermute | solution.py:329
  90.5 19.2 %collective-permute-start.14 = (bf16[160,768]{1,0:T(8,128)(2,1)S(1)}, bf16[160,768]{1,0:T(8,128)(2,1)S(1)}, u32[]{:S(2)}, u32[]{:S(2)}) collective-permute-start(bf16[160,768]{1,0:T(8,128)(2,1)S(1)} %get-tuple-element.53), channel_id=1, source_target_pairs={{0,16},{8,24},{16,0},{24,8},{1,17},{9,25},{17,1},{25,9},{2,18},{10... | collective-permute-start | bytes 737288 | tf_op jit(solution)/shard_map/ppermute | solution.py:329
  100.3 12.7 %collective-permute-start.15 = (bf16[160,768]{1,0:T(8,128)(2,1)S(1)}, bf16[160,768]{1,0:T(8,128)(2,1)S(1)}, u32[]{:S(2)}, u32[]{:S(2)}) collective-permute-start(bf16[160,768]{1,0:T(8,128)(2,1)S(1)} %get-tuple-element.54), channel_id=1, source_target_pairs={{0,24},{8,16},{16,8},{24,0},{1,25},{9,17},{17,9},{25,1},{2,26},{10... | collective-permute-start | bytes 737288 | tf_op jit(solution)/shard_map/ppermute | solution.py:329
  113.2 7.3 %collective-permute-start.24 = (bf16[160,768]{1,0:T(8,128)(2,1)S(1)}, bf16[160,768]{1,0:T(8,128)(2,1)S(1)}, u32[]{:S(2)}, u32[]{:S(2)}) collective-permute-start(bf16[160,768]{1,0:T(8,128)(2,1)S(1)} %shard_map.116.refs_1_.refs_5_), channel_id=1, source_target_pairs={{0,24},{8,16},{16,8},{24,0},{1,25},{9,17},{17,9},{25,1},{2,26},{10... | collective-permute-start | bytes 737288 | tf_op jit(solution)/shard_map/ppermute | solution.py:329
  116.2 14.2 %collective-permute-start.25 = (bf16[80,1792]{1,0:T(8,128)(2,1)S(1)}, bf16[80,1792]{1,0:T(8,128)(2,1)S(1)}, u32[]{:S(2)}, u32[]{:S(2)}) collective-permute-start(bf16[80,1792]{1,0:T(8,128)(2,1)S(1)} %shard_map.117.refs_1_), channel_id=1, source_target_pairs={{0,4},{1,5},{2,6},{3,7},{4,0},{5,1},{6,2},{7,3},{8,12},{9,13},{10,... | collective-permute-start | bytes 860168 | tf_op jit(solution)/shard_map/ppermute | solution.py:326
  119.0 6.8 %collective-permute-start.23 = (bf16[160,768]{1,0:T(8,128)(2,1)S(1)}, bf16[160,768]{1,0:T(8,128)(2,1)S(1)}, u32[]{:S(2)}, u32[]{:S(2)}) collective-permute-start(bf16[160,768]{1,0:T(8,128)(2,1)S(1)} %shard_map.116.refs_1_.refs_5_), channel_id=1, source_target_pairs={{0,16},{8,24},{16,0},{24,8},{1,17},{9,25},{17,1},{25,9},{2,18},{10... | collective-permute-start | bytes 737288 | tf_op jit(solution)/shard_map/ppermute | solution.py:329
  120.3 5.7 %collective-permute-start.22 = (bf16[160,768]{1,0:T(8,128)(2,1)S(1)}, bf16[160,768]{1,0:T(8,128)(2,1)S(1)}, u32[]{:S(2)}, u32[]{:S(2)}) collective-permute-start(bf16[160,768]{1,0:T(8,128)(2,1)S(1)} %shard_map.116.refs_1_.refs_5_), channel_id=1, source_target_pairs={{0,8},{8,0},{16,24},{24,16},{1,9},{9,1},{17,25},{25,17},{2,10},{10... | collective-permute-start | bytes 737288 | tf_op jit(solution)/shard_map/ppermute | solution.py:329
  120.5 19.9 %collective-permute-start.26 = (bf16[80,1792]{1,0:T(8,128)(2,1)S(1)}, bf16[80,1792]{1,0:T(8,128)(2,1)S(1)}, u32[]{:S(2)}, u32[]{:S(2)}) collective-permute-start(bf16[80,1792]{1,0:T(8,128)(2,1)S(1)} %shard_map.118.refs_5_), channel_id=1, source_target_pairs={{0,2},{1,3},{2,0},{3,1},{4,6},{5,7},{6,4},{7,5},{8,10},{9,11},{10,... | collective-permute-start | bytes 860168 | tf_op jit(solution)/shard_map/ppermute | solution.py:326
  120.5 18.7 %collective-permute-start.19 = (bf16[80,768]{1,0:T(8,128)(2,1)S(1)}, bf16[80,768]{1,0:T(8,128)(2,1)S(1)}, u32[]{:S(2)}, u32[]{:S(2)}) collective-permute-start(bf16[80,768]{1,0:T(8,128)(2,1)S(1)} %get-tuple-element.61), channel_id=1, source_target_pairs={{0,8},{8,0},{16,24},{24,16},{1,9},{9,1},{17,25},{25,17},{2,10},{10... | collective-permute-start | bytes 368648 | tf_op jit(solution)/shard_map/ppermute | solution.py:329
  130.5 29.4 %collective-permute-start.33 = (bf16[80,1792]{1,0:T(8,128)(2,1)S(1)}, bf16[80,1792]{1,0:T(8,128)(2,1)S(1)}, u32[]{:S(2)}, u32[]{:S(2)}) collective-permute-start(bf16[80,1792]{1,0:T(8,128)(2,1)S(1)} %shard_map.121.refs_1_), channel_id=1, source_target_pairs={{0,5},{1,4},{2,7},{3,6},{4,1},{5,0},{6,3},{7,2},{8,13},{9,12},{10,... | collective-permute-start | bytes 860168 | tf_op jit(solution)/shard_map/ppermute | solution.py:326
  137.8 7.6 %collective-permute-start.20 = (bf16[80,768]{1,0:T(8,128)(2,1)S(1)}, bf16[80,768]{1,0:T(8,128)(2,1)S(1)}, u32[]{:S(2)}, u32[]{:S(2)}) collective-permute-start(bf16[80,768]{1,0:T(8,128)(2,1)S(1)} %get-tuple-element.62), channel_id=1, source_target_pairs={{0,16},{8,24},{16,0},{24,8},{1,17},{9,25},{17,1},{25,9},{2,18},{10... | collective-permute-start | bytes 368648 | tf_op jit(solution)/shard_map/ppermute | solution.py:329
  138.0 8.6 %collective-permute-start.21 = (bf16[80,768]{1,0:T(8,128)(2,1)S(1)}, bf16[80,768]{1,0:T(8,128)(2,1)S(1)}, u32[]{:S(2)}, u32[]{:S(2)}) collective-permute-start(bf16[80,768]{1,0:T(8,128)(2,1)S(1)} %get-tuple-element.63), channel_id=1, source_target_pairs={{0,24},{8,16},{16,8},{24,0},{1,25},{9,17},{17,9},{25,1},{2,26},{10... | collective-permute-start | bytes 368648 | tf_op jit(solution)/shard_map/ppermute | solution.py:329
  139.2 8.7 %collective-permute-start.16 = (bf16[80,768]{1,0:T(8,128)(2,1)S(1)}, bf16[80,768]{1,0:T(8,128)(2,1)S(1)}, u32[]{:S(2)}, u32[]{:S(2)}) collective-permute-start(bf16[80,768]{1,0:T(8,128)(2,1)S(1)} %get-tuple-element.58), channel_id=1, source_target_pairs={{0,8},{8,0},{16,24},{24,16},{1,9},{9,1},{17,25},{25,17},{2,10},{10... | collective-permute-start | bytes 368648 | tf_op jit(solution)/shard_map/ppermute | solution.py:329
  140.4 10.4 %collective-permute-start.17 = (bf16[80,768]{1,0:T(8,128)(2,1)S(1)}, bf16[80,768]{1,0:T(8,128)(2,1)S(1)}, u32[]{:S(2)}, u32[]{:S(2)}) collective-permute-start(bf16[80,768]{1,0:T(8,128)(2,1)S(1)} %get-tuple-element.59), channel_id=1, source_target_pairs={{0,16},{8,24},{16,0},{24,8},{1,17},{9,25},{17,1},{25,9},{2,18},{10... | collective-permute-start | bytes 368648 | tf_op jit(solution)/shard_map/ppermute | solution.py:329
  145.4 7.5 %collective-permute-start.18 = (bf16[80,768]{1,0:T(8,128)(2,1)S(1)}, bf16[80,768]{1,0:T(8,128)(2,1)S(1)}, u32[]{:S(2)}, u32[]{:S(2)}) collective-permute-start(bf16[80,768]{1,0:T(8,128)(2,1)S(1)} %get-tuple-element.60), channel_id=1, source_target_pairs={{0,24},{8,16},{16,8},{24,0},{1,25},{9,17},{17,9},{25,1},{2,26},{10... | collective-permute-start | bytes 368648 | tf_op jit(solution)/shard_map/ppermute | solution.py:329
  146.7 6.3 %collective-permute-start.32 = (bf16[80,768]{1,0:T(8,128)(2,1)S(1)}, bf16[80,768]{1,0:T(8,128)(2,1)S(1)}, u32[]{:S(2)}, u32[]{:S(2)}) collective-permute-start(bf16[80,768]{1,0:T(8,128)(2,1)S(1)} %shard_map.123.refs_4_.refs_1_.refs_9_), channel_id=1, source_target_pairs={{0,24},{8,16},{16,8},{24,0},{1,25},{9,17},{17,9},{25,1},{2,26},{10... | collective-permute-start | bytes 368648 | tf_op jit(solution)/shard_map/ppermute | solution.py:329
  147.9 7.4 %collective-permute-start.31 = (bf16[80,768]{1,0:T(8,128)(2,1)S(1)}, bf16[80,768]{1,0:T(8,128)(2,1)S(1)}, u32[]{:S(2)}, u32[]{:S(2)}) collective-permute-start(bf16[80,768]{1,0:T(8,128)(2,1)S(1)} %shard_map.123.refs_4_.refs_1_.refs_9_), channel_id=1, source_target_pairs={{0,16},{8,24},{16,0},{24,8},{1,17},{9,25},{17,1},{25,9},{2,18},{10... | collective-permute-start | bytes 368648 | tf_op jit(solution)/shard_map/ppermute | solution.py:329
  150.8 5.7 %collective-permute-start.30 = (bf16[80,768]{1,0:T(8,128)(2,1)S(1)}, bf16[80,768]{1,0:T(8,128)(2,1)S(1)}, u32[]{:S(2)}, u32[]{:S(2)}) collective-permute-start(bf16[80,768]{1,0:T(8,128)(2,1)S(1)} %shard_map.123.refs_4_.refs_1_.refs_9_), channel_id=1, source_target_pairs={{0,8},{8,0},{16,24},{24,16},{1,9},{9,1},{17,25},{25,17},{2,10},{10... | collective-permute-start | bytes 368648 | tf_op jit(solution)/shard_map/ppermute | solution.py:329
  159.9 22.8 %collective-permute-start.34 = (bf16[80,1792]{1,0:T(8,128)(2,1)S(1)}, bf16[80,1792]{1,0:T(8,128)(2,1)S(1)}, u32[]{:S(2)}, u32[]{:S(2)}) collective-permute-start(bf16[80,1792]{1,0:T(8,128)(2,1)S(1)} %shard_map.126.refs_7_), channel_id=1, source_target_pairs={{0,6},{1,7},{2,4},{3,5},{4,2},{5,3},{6,0},{7,1},{8,14},{9,15},{10,... | collective-permute-start | bytes 860168 | tf_op jit(solution)/shard_map/ppermute | solution.py:326
  159.9 5.2 %collective-permute-start.29 = (bf16[80,768]{1,0:T(8,128)(2,1)S(1)}, bf16[80,768]{1,0:T(8,128)(2,1)S(1)}, u32[]{:S(2)}, u32[]{:S(2)}) collective-permute-start(bf16[80,768]{1,0:T(8,128)(2,1)S(1)} %shard_map.124.refs_7_.refs_1_.refs_13_), channel_id=1, source_target_pairs={{0,24},{8,16},{16,8},{24,0},{1,25},{9,17},{17,9},{25,1},{2,26},{10... | collective-permute-start | bytes 368648 | tf_op jit(solution)/shard_map/ppermute | solution.py:329
  161.8 7.0 %collective-permute-start.28 = (bf16[80,768]{1,0:T(8,128)(2,1)S(1)}, bf16[80,768]{1,0:T(8,128)(2,1)S(1)}, u32[]{:S(2)}, u32[]{:S(2)}) collective-permute-start(bf16[80,768]{1,0:T(8,128)(2,1)S(1)} %shard_map.124.refs_7_.refs_1_.refs_13_), channel_id=1, source_target_pairs={{0,16},{8,24},{16,0},{24,8},{1,17},{9,25},{17,1},{25,9},{2,18},{10... | collective-permute-start | bytes 368648 | tf_op jit(solution)/shard_map/ppermute | solution.py:329
  162.5 6.3 %collective-permute-start.27 = (bf16[80,768]{1,0:T(8,128)(2,1)S(1)}, bf16[80,768]{1,0:T(8,128)(2,1)S(1)}, u32[]{:S(2)}, u32[]{:S(2)}) collective-permute-start(bf16[80,768]{1,0:T(8,128)(2,1)S(1)} %shard_map.124.refs_7_.refs_1_.refs_13_), channel_id=1, source_target_pairs={{0,8},{8,0},{16,24},{24,16},{1,9},{9,1},{17,25},{25,17},{2,10},{10... | collective-permute-start | bytes 368648 | tf_op jit(solution)/shard_map/ppermute | solution.py:329
  162.9 9.2 %copy-start.10 = (bf16[1,1024,1792]{2,1,0:T(8,128)(2,1)S(1)}, bf16[1,1024,1792]{2,1,0:T(8,128)(2,1)}, u32[]{:S(2)}) copy-start(bf16[1,1024,1792]{2,1,0:T(8,128)(2,1)} %param.15) | copy-start | bytes 11010052
  162.9 24.1 %collective-permute-start.36 = (bf16[80,1792]{1,0:T(8,128)(2,1)S(1)}, bf16[80,1792]{1,0:T(8,128)(2,1)S(1)}, u32[]{:S(2)}, u32[]{:S(2)}) collective-permute-start(bf16[80,1792]{1,0:T(8,128)(2,1)S(1)} %get-tuple-element.67), channel_id=1, source_target_pairs={{0,1},{1,0},{2,3},{3,2},{4,5},{5,4},{6,7},{7,6},{8,9},{9,8},{10,11... | collective-permute-start | bytes 860168 | tf_op jit(solution)/shard_map/ppermute | solution.py:326
  165.1 22.0 %collective-permute-start.37 = (bf16[80,1792]{1,0:T(8,128)(2,1)S(1)}, bf16[80,1792]{1,0:T(8,128)(2,1)S(1)}, u32[]{:S(2)}, u32[]{:S(2)}) collective-permute-start(bf16[80,1792]{1,0:T(8,128)(2,1)S(1)} %shard_map.122.refs_4_), channel_id=1, source_target_pairs={{0,3},{1,2},{2,1},{3,0},{4,7},{5,6},{6,5},{7,4},{8,11},{9,10},{10,... | collective-permute-start | bytes 860168 | tf_op jit(solution)/shard_map/ppermute | solution.py:326
  182.6 2.0 copy-start.11
  184.7 15.9 %collective-permute-start.35 = (bf16[80,1792]{1,0:T(8,128)(2,1)S(1)}, bf16[80,1792]{1,0:T(8,128)(2,1)S(1)}, u32[]{:S(2)}, u32[]{:S(2)}) collective-permute-start(bf16[80,1792]{1,0:T(8,128)(2,1)S(1)} %shard_map.129.refs_9_), channel_id=1, source_target_pairs={{0,7},{1,6},{2,5},{3,4},{4,3},{5,2},{6,1},{7,0},{8,15},{9,14},{10,... | collective-permute-start | bytes 860168 | tf_op jit(solution)/shard_map/ppermute | solution.py:326
  (8 other events, 10.3 us)

commit v2 on v1

--- a/solution.py
+++ b/solution.py
@@ -23,8 +23,8 @@
     half = n // 2
     step = max(1, half // 4)
     far = [list(range(i, i + step)) for i in range(half, n, step)]
-    cut = half - step
-    return far, [list(range(cut)), list(range(cut, half))]
+    cuts = [0, half - 2 * step, half - step, half]
+    return far, [list(range(i, j)) for i, j in zip(cuts, cuts[1:])]
 
 
 def skipping(body, n_in, n_deps):
@@ -329,7 +329,7 @@
         return lax.ppermute(v, "dp", [(i, i ^ k) for i in range(ndp)])
 
     far, near = grouping(n)
-    chunks = [near[0] + far[0], near[1] + far[1]] + far[2:]
+    chunks = [near[0], near[1] + far[0], near[2] + far[1], far[2], far[3]]
     send, got, ready, back, pieces, parts = {}, {}, {}, {}, {}, {}
     mark = []
 
@@ -338,7 +338,7 @@
             if deps:
                 send[k] = after(send[k], mark + deps)
                 mark[:] = [send[k]]
-            got[k] = swap_expert(send[k], k)
+            got[k] = swap_expert(send[k], k) if k else send[k]
 
     def give_back(offs, deps):
         for k in offs:
@@ -370,37 +370,37 @@
     send.update(zip(far[0], sends))
     mark[:] = [sends[0]]
     push(far[0], [])
-    for offs in (near[0], far[1] + near[1], far[2] + far[3]):
+    for offs in (near[0], near[1], far[1] + near[2], far[2] + far[3]):
         sends = dispatch(n, cap, offs, me, target, codes, tokens, grad_out, False, mark)
         send.update(zip(offs, sends))
         mark[:] = [sends[0]]
-        if offs is near[0]:
+        if offs in near:
             push(offs, [])
-            got[0] = send[0]
-    inner = [k for k in near[0] if k > 1]
-
+
+    fwd(0)
+    act(0)
     push(far[1], gotten(far[0]))
-    push(near[1], gotten(inner))
-    fwd(0)
+    push(near[2], gotten(near[1]))
+    fwd(1)
+    bwd(0)
+    give_back(near[0], [])
+    act(1)
     push(far[2], gotten(far[1]))
-    act(0)
-    fwd(1)
+    fwd(2)
+    bwd(1)
+    act(2)
     push(far[3], gotten(far[2]))
-    bwd(0)
-    give_back([0, 1], [])
-    fwd(2)
-    act(1)
-    give_back(far[0], gotten(far[3]))
-    give_back(inner, gotten(far[3]))
     fwd(3)
-    bwd(1)
-    give_back(far[1], [back[k] for k in far[0]])
-    give_back(near[1], [back[k] for k in inner])
-    act(2)
+    bwd(2)
     act(3)
-    bwd(2)
+    give_back(far[0] + near[1], gotten(far[3]))
+    fwd(4)
+    bwd(3)
+    act(4)
+    give_back(far[1] + near[2], [back[k] for k in far[0] + near[1]])
+    bwd(4)
     give_back(far[2], [back[k] for k in far[1]])
-    bwd(3)
+    give_back(far[3], [])
     order = range(len(chunks))
     flat = [k for c in order for k in chunks[c]]
     new_down, new_moment = down(
@@ -415,10 +415,10 @@
         mark,
     )
     mark[:] = [new_down]
-    give_back(far[3], [back[k] for k in far[2]])
-    early = [k for k in flat if k not in far[3]]
+    tail = far[2] + far[3]
+    early = [k for k in flat if k not in tail]
     part = combine(cap, early, me, target, [back[k] for k in early], None, mark)
-    grad_tokens = combine(cap, far[3], me, target, [back[k] for k in far[3]], part, [])
+    grad_tokens = combine(cap, tail, me, target, [back[k] for k in tail], part, [])
     return (grad_tokens, new_down[None], new_moment[None])
 
 

time: 205 us -> 191 us (0.932)
  waiting for transfers between devices: 82 us -> 61.5 us
  Pallas kernels: 56.6 us -> 64.5 us
  starting transfers between devices: 50.5 us -> 46.6 us
  local copies, waits for them, and re-layouts: 14.4 us -> 16.7 us
    ppermute x14, waiting for transfers between devices: 42.4 us -> 17.1 us  [swap_expert(): return lax.ppermute(v, 'expert', [(i, i ^ k) for i in range(n)])]
    pallas_call x29 -> x32, Pallas kernels: 56.6 us -> 64.5 us  [call(): pl.pallas_call(skipping(body, len(operands), len(deps)), out_shape=out_sh...]
    ppermute x14, starting transfers between devices: 27.1 us -> 19.4 us  [swap_expert(): return lax.ppermute(v, 'expert', [(i, i ^ k) for i in range(n)])]
    ppermute x24 -> x30, waiting for transfers between devices: 39.6 us -> 44.4 us  [swap_dp(): return lax.ppermute(v, 'dp', [(i, i ^ k) for i in range(ndp)])]
    ppermute x24 -> x30, starting transfers between devices: 23.3 us -> 27.2 us  [swap_dp(): return lax.ppermute(v, 'dp', [(i, i ^ k) for i in range(ndp)])]
    unnamed x37 -> x44, local copies, waits for them, and re-layouts: 14.4 us -> 16.7 us
  transfers between devices with their start and end apart: 38 -> 44, of which waited for: 20 -> 19; matrix products, arithmetic and copies ran while one was open for 0% -> 0% of each run, Pallas kernels for 25% -> 30%
where the time goes in v2:
time: 191 us; the launch traced here: 190 us
  Pallas kernels  64.5 us (34%)
  waiting for transfers between devices  61.5 us (32%)
  starting transfers between devices  46.6 us (24%)
  local copies, waits for them, and re-layouts  16.7 us (9%)
    pallas_call x32, Pallas kernels, call(): pl.pallas_call(skipping(body, len(operands), len(deps)), out_shape=out_sh...  64.5 us
    ppermute x30, waiting for transfers between devices, swap_dp(): return lax.ppermute(v, 'dp', [(i, i ^ k) for i in range(ndp)])  44.4 us
    ppermute x30, starting transfers between devices, swap_dp(): return lax.ppermute(v, 'dp', [(i, i ^ k) for i in range(ndp)])  27.2 us
    ppermute x14, starting transfers between devices, swap_expert(): return lax.ppermute(v, 'expert', [(i, i ^ k) for i in range(n)])  19.4 us
    ppermute x14, waiting for transfers between devices, swap_expert(): return lax.ppermute(v, 'expert', [(i, i ^ k) for i in range(n)])  17.1 us
    unnamed x44, local copies, waits for them, and re-layouts  16.7 us
  transfers between devices with their start and end apart: 44, of which 19 were waited for; matrix products, arithmetic and copies ran while one was open for 0% of the time, Pallas kernels for 30%

profile of v2, /device:TPU:9, one launch (start us, length us, event | category | flops | bytes accessed | tf_op | source)
XLA Modules:
  0.0 190.3 jit_solution(2030339428378111615)
XLA Ops:
  0.6 1.5 copy-done.4
  2.1 1.5 copy-done.6
  5.0 1.8 shard_map.103
  7.3 1.6 shard_map.104
  9.5 2.3 %collective-permute-start.1 = (bf16[80,3584]{1,0:T(8,128)(2,1)}, bf16[80,3584]{1,0:T(8,128)(2,1)S(1)}, u32[]{:S(2)}, u32[]{:S(2)}) collective-permute-start(bf16[80,3584]{1,0:T(8,128)(2,1)} %get-tuple-element.40.refs_5_), channel_id=1, source_target_pairs={{0,4},{1,5},{2,6},{3,7},{4,0},{5,1},{6,2},{7,3},{8,12},{9,13},{10,... | collective-permute-start | bytes 1720328 | tf_op jit(solution)/shard_map/ppermute | solution.py:326
  11.8 1.6 shard_map.105.refs_5_
  16.0 1.6 copy-done.8
  20.9 2.0 %copy-done.1 = bf16[1,1792,1024]{2,1,0:T(8,128)(2,1)S(1)} copy-done((bf16[1,1792,1024]{2,1,0:T(8,128)(2,1)S(1)}, bf16[1,1792,1024]{2,1,0:T(8,128)(2,1)}, u32[]{:S(2)}) %copy-start.1) | copy-done | bytes 3670040
  22.9 2.0 %copy-done.2 = bf16[1,1024,1792]{2,1,0:T(8,128)(2,1)S(1)} copy-done((bf16[1,1024,1792]{2,1,0:T(8,128)(2,1)S(1)}, bf16[1,1024,1792]{2,1,0:T(8,128)(2,1)}, u32[]{:S(2)}) %copy-start.2) | copy-done | bytes 3670040
  25.0 5.1 %shard_map.108 = (bf16[160,768]{1,0:T(8,128)(2,1)S(1)}, bf16[160,768]{1,0:T(8,128)(2,1)S(1)}, bf16[160,768]{1,0:T(8,128)(2,1)S(1)}, bf16[160,768]{1,0:T(8,128)(2,1)S(1)}) custom-call(s32[1]{0:T(128)} %bitcast.3.refs_0_, bf16[80,3584]{1,0:T(8,128)(2,1)S(1)} %get-tuple-element.41.refs_5_.refs_1_.refs_21_, ...), custom_call_target="tpu_custom_call" | custom-call | tf_op jit(solution)/shard_map/pallas_call | solution.py:39
  32.7 4.3 %collective-permute-done.3.refs_1_ = bf16[160,768]{1,0:T(8,128)(2,1)S(1)} collective-permute-done((bf16[160,768]{1,0:T(8,128)(2,1)S(1)}, bf16[160,768]{1,0:T(8,128)(2,1)S(1)}, u32[]{:S(2)}, u32[]{:S(2)}) %collective-permute-start.3) | collective-permute-done | bytes 245792 | tf_op jit(solution)/shard_map/ppermute | solution.py:329
  37.9 5.4 %collective-permute-done.5.refs_3_ = bf16[160,768]{1,0:T(8,128)(2,1)S(1)} collective-permute-done((bf16[160,768]{1,0:T(8,128)(2,1)S(1)}, bf16[160,768]{1,0:T(8,128)(2,1)S(1)}, u32[]{:S(2)}, u32[]{:S(2)}) %collective-permute-start.5) | collective-permute-done | bytes 245792 | tf_op jit(solution)/shard_map/ppermute | solution.py:329
  43.5 1.6 collective-permute-start.12
  47.8 2.2 %collective-permute-start.14 = (bf16[80,3584]{1,0:T(8,128)(2,1)S(1)}, bf16[80,3584]{1,0:T(8,128)(2,1)S(1)}, u32[]{:S(2)}, u32[]{:S(2)}) collective-permute-start(bf16[80,3584]{1,0:T(8,128)(2,1)S(1)} %shard_map.111.refs_6_), channel_id=1, source_target_pairs={{0,3},{1,2},{2,1},{3,0},{4,7},{5,6},{6,5},{7,4},{8,11},{9,10},{10,... | collective-permute-start | bytes 1720328 | tf_op jit(solution)/shard_map/ppermute | solution.py:326
  50.0 4.2 %shard_map.112 = (bf16[160,768]{1,0:T(8,128)(2,1)S(1)}, bf16[160,768]{1,0:T(8,128)(2,1)S(1)}, bf16[160,768]{1,0:T(8,128)(2,1)S(1)}, bf16[160,768]{1,0:T(8,128)(2,1)S(1)}) custom-call(s32[1]{0:T(128)} %bitcast.3.refs_0_, bf16[80,3584]{1,0:T(8,128)(2,1)S(1)} %collective-permute-done.refs_2_.refs_1_.refs_23_, ...), custom_call_target="tpu_custom_call" | custom-call | tf_op jit(solution)/shard_map/pallas_call | solution.py:39
  55.3 4.0 %collective-permute-done.10.refs_3_ = bf16[160,768]{1,0:T(8,128)(2,1)S(1)} collective-permute-done((bf16[160,768]{1,0:T(8,128)(2,1)S(1)}, bf16[160,768]{1,0:T(8,128)(2,1)S(1)}, u32[]{:S(2)}, u32[]{:S(2)}) %collective-permute-start.10) | collective-permute-done | bytes 245792 | tf_op jit(solution)/shard_map/ppermute | solution.py:329
  61.4 3.7 %shard_map.113 = (bf16[80,1792]{1,0:T(8,128)(2,1)S(1)}, bf16[80,1792]{1,0:T(8,128)(2,1)S(1)}) custom-call(s32[1]{0:T(128)} %bitcast.3.refs_0_, bf16[160,768]{1,0:T(8,128)(2,1)S(1)} %shard_map.109.refs_1_, bf16[160,768]{1,0:T(8,128)(2,1)S(1)} %collective-permute-done.9.refs_2_, bf16[160,768]{1,0:T(8,128)(2,1)S(1)} %collective-permute-done.10.refs_3_, ...), custom_call_target="tpu_custom_call" | custom-call | tf_op jit(solution)/shard_map/pallas_call | solution.py:39
  65.1 6.5 %collective-permute-done.7.refs_2_ = bf16[160,768]{1,0:T(8,128)(2,1)S(1)} collective-permute-done((bf16[160,768]{1,0:T(8,128)(2,1)S(1)}, bf16[160,768]{1,0:T(8,128)(2,1)S(1)}, u32[]{:S(2)}, u32[]{:S(2)}) %collective-permute-start.7) | collective-permute-done | bytes 245792 | tf_op jit(solution)/shard_map/ppermute | solution.py:329
  71.8 2.1 %collective-permute-start.13 = (bf16[80,3584]{1,0:T(8,128)(2,1)S(1)}, bf16[80,3584]{1,0:T(8,128)(2,1)S(1)}, u32[]{:S(2)}, u32[]{:S(2)}) collective-permute-start(bf16[80,3584]{1,0:T(8,128)(2,1)S(1)} %shard_map.115.refs_6_), channel_id=1, source_target_pairs={{0,6},{1,7},{2,4},{3,5},{4,2},{5,3},{6,0},{7,1},{8,14},{9,15},{10,... | collective-permute-start | bytes 1720328 | tf_op jit(solution)/shard_map/ppermute | solution.py:326
  75.0 1.4 collective-permute-start.19
  76.5 4.2 %shard_map.116 = (bf16[160,768]{1,0:T(8,128)(2,1)S(1)}, bf16[160,768]{1,0:T(8,128)(2,1)S(1)}, bf16[160,768]{1,0:T(8,128)(2,1)S(1)}, bf16[160,768]{1,0:T(8,128)(2,1)S(1)}) custom-call(s32[1]{0:T(128)} %bitcast.3.refs_0_, bf16[80,3584]{1,0:T(8,128)(2,1)S(1)} %collective-permute-done.14.refs_1_.refs_25_, ...), custom_call_target="tpu_custom_call" | custom-call | tf_op jit(solution)/shard_map/pallas_call | solution.py:39
  80.7 1.4 collective-permute-start.15
  82.2 5.7 %collective-permute-done.19.refs_3_.refs_7_ = bf16[160,768]{1,0:T(8,128)(2,1)S(1)} collective-permute-done((bf16[160,768]{1,0:T(8,128)(2,1)S(1)}, bf16[160,768]{1,0:T(8,128)(2,1)S(1)}, u32[]{:S(2)}, u32[]{:S(2)}) %collective-permute-start.19) | collective-permute-done | bytes 245792 | tf_op jit(solution)/shard_map/ppermute | solution.py:329
  89.0 3.7 %shard_map.117 = (bf16[80,1792]{1,0:T(8,128)(2,1)S(1)}, bf16[80,1792]{1,0:T(8,128)(2,1)S(1)}) custom-call(s32[1]{0:T(128)} %bitcast.3.refs_0_, bf16[160,768]{1,0:T(8,128)(2,1)S(1)} %shard_map.114.refs_1_.refs_5_, bf16[160,768]{1,0:T(8,128)(2,1)S(1)} %collective-permute-done.18.refs_2_.refs_6_, bf16[160,768]{1,0:T(8,128)(2,1)S(1)} %collective-permute-done.19.refs_3_.refs_7_, ...), custom_call_target="tpu_custom_call" | custom-call | tf_op jit(solution)/shard_map/pallas_call | solution.py:39
  92.7 1.5 collective-permute-done.16.refs_2_
  94.2 2.6 %collective-permute-done.17.refs_3_ = bf16[160,768]{1,0:T(8,128)(2,1)S(1)} collective-permute-done((bf16[160,768]{1,0:T(8,128)(2,1)S(1)}, bf16[160,768]{1,0:T(8,128)(2,1)S(1)}, u32[]{:S(2)}, u32[]{:S(2)}) %collective-permute-start.17) | collective-permute-done | bytes 245792 | tf_op jit(solution)/shard_map/ppermute | solution.py:329
  98.2 3.1 %collective-permute-start.30 = (bf16[80,3584]{1,0:T(8,128)(2,1)S(1)}, bf16[80,3584]{1,0:T(8,128)(2,1)S(1)}, u32[]{:S(2)}, u32[]{:S(2)}) collective-permute-start(bf16[80,3584]{1,0:T(8,128)(2,1)S(1)} %shard_map.119.refs_5_), channel_id=1, source_target_pairs={{0,7},{1,6},{2,5},{3,4},{4,3},{5,2},{6,1},{7,0},{8,15},{9,14},{10,... | collective-permute-start | bytes 1720328 | tf_op jit(solution)/shard_map/ppermute | solution.py:326
  104.0 4.0 %shard_map.120 = (bf16[80,768]{1,0:T(8,128)(2,1)S(1)}, bf16[80,768]{1,0:T(8,128)(2,1)S(1)}, bf16[80,768]{1,0:T(8,128)(2,1)S(1)}, bf16[80,768]{1,0:T(8,128)(2,1)S(1)}) custom-call(s32[1]{0:T(128)} %bitcast.3.refs_0_, bf16[80,3584]{1,0:T(8,128)(2,1)S(1)} %collective-permute-done.13.refs_2_.refs_1_.refs_27_, bf16[1792,1024]{1,0:T(8,128)(2,1)S(1)} %bitcast.15, ...), custom_call_target="tpu_custom_call" | custom-call | tf_op jit(solution)/shard_map/pallas_call | solution.py:39
  108.1 1.4 collective-permute-start.21
  110.2 5.0 %collective-permute-done.25.refs_3_.refs_11_ = bf16[160,768]{1,0:T(8,128)(2,1)S(1)} collective-permute-done((bf16[160,768]{1,0:T(8,128)(2,1)S(1)}, bf16[160,768]{1,0:T(8,128)(2,1)S(1)}, u32[]{:S(2)}, u32[]{:S(2)}) %collective-permute-start.25) | collective-permute-done | bytes 245792 | tf_op jit(solution)/shard_map/ppermute | solution.py:329
  116.3 3.7 %shard_map.121 = (bf16[80,1792]{1,0:T(8,128)(2,1)S(1)}, bf16[80,1792]{1,0:T(8,128)(2,1)S(1)}) custom-call(s32[1]{0:T(128)} %bitcast.3.refs_0_, bf16[160,768]{1,0:T(8,128)(2,1)S(1)} %shard_map.118.refs_1_.refs_9_, bf16[160,768]{1,0:T(8,128)(2,1)S(1)} %collective-permute-done.24.refs_2_.refs_10_, ...), custom_call_target="tpu_custom_call" | custom-call | tf_op jit(solution)/shard_map/pallas_call | solution.py:39
  120.7 6.3 %collective-permute-done.30.refs_2_.refs_1_.refs_28_ = bf16[80,3584]{1,0:T(8,128)(2,1)S(1)} collective-permute-done((bf16[80,3584]{1,0:T(8,128)(2,1)S(1)}, bf16[80,3584]{1,0:T(8,128)(2,1)S(1)}, u32[]{:S(2)}, u32[]{:S(2)}) %collective-permute-start.30) | collective-permute-done | bytes 573472 | tf_op jit(solution)/shard_map/ppermute | solution.py:326
  127.0 1.7 collective-permute-start.37
  129.9 1.5 collective-permute-start.28
  131.4 4.0 %shard_map.125 = (bf16[80,768]{1,0:T(8,128)(2,1)S(1)}, bf16[80,768]{1,0:T(8,128)(2,1)S(1)}, bf16[80,768]{1,0:T(8,128)(2,1)S(1)}, bf16[80,768]{1,0:T(8,128)(2,1)S(1)}) custom-call(s32[1]{0:T(128)} %bitcast.3.refs_0_, bf16[80,3584]{1,0:T(8,128)(2,1)S(1)} %collective-permute-done.30.refs_2_.refs_1_.refs_28_, bf16[1792,1024]{1,0:T(8,128)(2,1)S(1)} %bitcast.17, ...), custom_call_target="tpu_custom_call" | custom-call | tf_op jit(solution)/shard_map/pallas_call | solution.py:39
  135.4 1.5 collective-permute-start.31
  138.2 3.3 %shard_map.126.refs_4_.refs_0_ = bf16[80,1792]{1,0:T(8,128)(2,1)S(1)} custom-call(s32[1]{0:T(128)} %bitcast.3.refs_0_, bf16[80,768]{1,0:T(8,128)(2,1)S(1)} %shard_map.122.refs_1_.refs_13_, bf16[80,768]{1,0:T(8,128)(2,1)S(1)} %collective-permute-done.27.refs_2_.refs_14_, bf16[80,768]{1,0:T(8,128)(2,1)S(1)} %collective-permute-done.28.refs_3_.refs_15_, ...), custom_call_target="tpu_custom_call" | custom-call | tf_op jit(solution)/shard_map/pallas_call | solution.py:39
  141.6 1.7 collective-permute-done.33.refs_3_
  143.4 3.4 %collective-permute-start.39 = (bf16[80,1792]{1,0:T(8,128)(2,1)S(1)}, bf16[80,1792]{1,0:T(8,128)(2,1)S(1)}, u32[]{:S(2)}, u32[]{:S(2)}) collective-permute-start(bf16[80,1792]{1,0:T(8,128)(2,1)S(1)} %shard_map.128.refs_1_), channel_id=1, source_target_pairs={{0,5},{1,4},{2,7},{3,6},{4,1},{5,0},{6,3},{7,2},{8,13},{9,12},{10,... | collective-permute-start | bytes 860168 | tf_op jit(solution)/shard_map/ppermute | solution.py:326
  149.7 3.3 %collective-permute-done.36.refs_4_.refs_20_ = bf16[80,768]{1,0:T(8,128)(2,1)S(1)} collective-permute-done((bf16[80,768]{1,0:T(8,128)(2,1)S(1)}, bf16[80,768]{1,0:T(8,128)(2,1)S(1)}, u32[]{:S(2)}, u32[]{:S(2)}) %collective-permute-start.36) | collective-permute-done | bytes 122912 | tf_op jit(solution)/shard_map/ppermute | solution.py:329
  153.1 2.5 %collective-permute-done.35.refs_3_.refs_19_ = bf16[80,768]{1,0:T(8,128)(2,1)S(1)} collective-permute-done((bf16[80,768]{1,0:T(8,128)(2,1)S(1)}, bf16[80,768]{1,0:T(8,128)(2,1)S(1)}, u32[]{:S(2)}, u32[]{:S(2)}) %collective-permute-start.35) | collective-permute-done | bytes 122912 | tf_op jit(solution)/shard_map/ppermute | solution.py:329
  155.5 3.3 %shard_map.130.refs_1_ = bf16[80,1792]{1,0:T(8,128)(2,1)S(1)} custom-call(s32[1]{0:T(128)} %bitcast.3.refs_0_, bf16[80,768]{1,0:T(8,128)(2,1)S(1)} %shard_map.127.refs_1_.refs_17_, bf16[80,768]{1,0:T(8,128)(2,1)S(1)} %collective-permute-done.34.refs_2_.refs_18_, bf16[80,768]{1,0:T(8,128)(2,1)S(1)} %collective-permute-done.35.refs_3_.refs_19_, ...), custom_call_target="tpu_custom_call" | custom-call | tf_op jit(solution)/shard_map/pallas_call | solution.py:39
  160.7 11.0 %shard_map.132 = (bf16[1024,1792]{1,0:T(8,128)(2,1)}, bf16[1024,1792]{1,0:T(8,128)(2,1)}) custom-call(s32[1]{0:T(128)} %bitcast.3.refs_0_, bf16[160,768]{1,0:T(8,128)(2,1)S(1)} %shard_map.109.refs_1_, bf16[160,768]{1,0:T(8,128)(2,1)S(1)} %collective-permute-done.9.refs_2_, bf16[160,768]{1,0:T(8,128)(2,1)S(1)} %collective-permute-done.10.refs_3_, ...), custom_call_target="tpu_custom_call" | custom-call | tf_op jit(solution)/shard_map/pallas_call | solution.py:39
  171.7 6.3 %collective-permute-done.43.refs_6_ = bf16[80,1792]{1,0:T(8,128)(2,1)S(1)} collective-permute-done((bf16[80,1792]{1,0:T(8,128)(2,1)S(1)}, bf16[80,1792]{1,0:T(8,128)(2,1)S(1)}, u32[]{:S(2)}, u32[]{:S(2)}) %collective-permute-start.43) | collective-permute-done | bytes 286752 | tf_op jit(solution)/shard_map/ppermute | solution.py:326
  178.0 2.0 %copy-done.13 = bf16[1024,1792]{1,0:T(8,128)(2,1)S(1)} copy-done((bf16[1024,1792]{1,0:T(8,128)(2,1)S(1)}, bf16[1024,1792]{1,0:T(8,128)(2,1)}, u32[]{:S(2)}) %copy-start.13) | copy-done | bytes 3670040
  180.0 2.9 %shard_map.133.refs_4_ = bf16[512,1792]{1,0:T(8,128)(2,1)S(1)} custom-call(s32[1]{0:T(128)} %bitcast.refs_0_, s32[1,512]{1,0:T(1,128)S(1)} %copy-done.18, bf16[80,1792]{1,0:T(8,128)(2,1)S(1)} %get-tuple-element.54.refs_4_.refs_2_, bf16[80,1792]{1,0:T(8,128)(2,1)S(1)} %collective-permute-done.42.refs_3_, ...), custom_call_target="tpu_custom_call" | custom-call | tf_op jit(solution)/shard_map/pallas_call | solution.py:39
  182.9 3.3 %collective-permute-done.40.refs_2_ = bf16[80,1792]{1,0:T(8,128)(2,1)S(1)} collective-permute-done((bf16[80,1792]{1,0:T(8,128)(2,1)S(1)}, bf16[80,1792]{1,0:T(8,128)(2,1)S(1)}, u32[]{:S(2)}, u32[]{:S(2)}) %collective-permute-start.40) | collective-permute-done | bytes 286752 | tf_op jit(solution)/shard_map/ppermute | solution.py:326
  186.2 4.1 %shard_map.134 = bf16[512,1792]{1,0:T(8,128)(2,1)} custom-call(s32[1]{0:T(128)} %bitcast.refs_0_, s32[1,512]{1,0:T(1,128)S(1)} %copy-done.18, bf16[80,1792]{1,0:T(8,128)(2,1)S(1)} %collective-permute-done.40.refs_2_, bf16[80,1792]{1,0:T(8,128)(2,1)S(1)} %collective-permute-done.41.refs_3_, bf16[512,1792]{1,0:T(8,128)(2,1)S(1)} %shard_map.133.refs_4_), custom_call_target="tpu_custom_call" | custom-call | tf_op jit(solution)/shard_map/pallas_call | solution.py:39
  (116 shorter events, 34.6 us)
Async XLA Ops:
  8.8 12.0 %collective-permute-start.2 = (bf16[80,3584]{1,0:T(8,128)(2,1)}, bf16[80,3584]{1,0:T(8,128)(2,1)}, u32[]{:S(2)}, u32[]{:S(2)}) collective-permute-start(bf16[80,3584]{1,0:T(8,128)(2,1)} %get-tuple-element.45), channel_id=1, source_target_pairs={{0,1},{1,0},{2,3},{3,2},{4,5},{5,4},{6,7},{7,6},{8,9},{9,8},{10,11... | collective-permute-start | bytes 1720328 | tf_op jit(solution)/shard_map/ppermute | solution.py:326
  9.5 34.0 %collective-permute-start.1 = (bf16[80,3584]{1,0:T(8,128)(2,1)}, bf16[80,3584]{1,0:T(8,128)(2,1)S(1)}, u32[]{:S(2)}, u32[]{:S(2)}) collective-permute-start(bf16[80,3584]{1,0:T(8,128)(2,1)} %get-tuple-element.40.refs_5_), channel_id=1, source_target_pairs={{0,4},{1,5},{2,6},{3,7},{4,0},{5,1},{6,2},{7,3},{8,12},{9,13},{10,... | collective-permute-start | bytes 1720328 | tf_op jit(solution)/shard_map/ppermute | solution.py:326
  13.4 34.4 %collective-permute-start = (bf16[80,3584]{1,0:T(8,128)(2,1)}, bf16[80,3584]{1,0:T(8,128)(2,1)S(1)}, u32[]{:S(2)}, u32[]{:S(2)}) collective-permute-start(bf16[80,3584]{1,0:T(8,128)(2,1)} %shard_map.105.refs_5_), channel_id=1, source_target_pairs={{0,2},{1,3},{2,0},{3,1},{4,6},{5,7},{6,4},{7,5},{8,10},{9,11},{10,... | collective-permute-start | bytes 1720328 | tf_op jit(solution)/shard_map/ppermute | solution.py:326
  24.9 18.6 %copy-start.11 = (bf16[80,3584]{1,0:T(8,128)(2,1)S(1)}, bf16[80,3584]{1,0:T(8,128)(2,1)}, u32[]{:S(2)}) copy-start(bf16[80,3584]{1,0:T(8,128)(2,1)} %copy-done.9) | copy-start | bytes 1720324
  30.0 17.8 %copy-start.15 = (bf16[80,3584]{1,0:T(8,128)(2,1)S(1)}, bf16[80,3584]{1,0:T(8,128)(2,1)}, u32[]{:S(2)}) copy-start(bf16[80,3584]{1,0:T(8,128)(2,1)} %copy-done.14) | copy-start | bytes 1720324
  30.0 7.0 %collective-permute-start.3 = (bf16[160,768]{1,0:T(8,128)(2,1)S(1)}, bf16[160,768]{1,0:T(8,128)(2,1)S(1)}, u32[]{:S(2)}, u32[]{:S(2)}) collective-permute-start(bf16[160,768]{1,0:T(8,128)(2,1)S(1)} %get-tuple-element.47), channel_id=1, source_target_pairs={{0,8},{8,0},{16,24},{24,16},{1,9},{9,1},{17,25},{25,17},{2,10},{10... | collective-permute-start | bytes 737288 | tf_op jit(solution)/shard_map/ppermute | solution.py:329
  31.3 6.6 %collective-permute-start.4 = (bf16[160,768]{1,0:T(8,128)(2,1)S(1)}, bf16[160,768]{1,0:T(8,128)(2,1)S(1)}, u32[]{:S(2)}, u32[]{:S(2)}) collective-permute-start(bf16[160,768]{1,0:T(8,128)(2,1)S(1)} %get-tuple-element.48), channel_id=1, source_target_pairs={{0,16},{8,24},{16,0},{24,8},{1,17},{9,25},{17,1},{25,9},{2,18},{10... | collective-permute-start | bytes 737288 | tf_op jit(solution)/shard_map/ppermute | solution.py:329
  32.5 10.8 %collective-permute-start.5 = (bf16[160,768]{1,0:T(8,128)(2,1)S(1)}, bf16[160,768]{1,0:T(8,128)(2,1)S(1)}, u32[]{:S(2)}, u32[]{:S(2)}) collective-permute-start(bf16[160,768]{1,0:T(8,128)(2,1)S(1)} %get-tuple-element.49), channel_id=1, source_target_pairs={{0,24},{8,16},{16,8},{24,0},{1,25},{9,17},{17,9},{25,1},{2,26},{10... | collective-permute-start | bytes 737288 | tf_op jit(solution)/shard_map/ppermute | solution.py:329
  43.5 28.2 %collective-permute-start.12 = (bf16[80,3584]{1,0:T(8,128)(2,1)S(1)}, bf16[80,3584]{1,0:T(8,128)(2,1)S(1)}, u32[]{:S(2)}, u32[]{:S(2)}) collective-permute-start(bf16[80,3584]{1,0:T(8,128)(2,1)S(1)} %shard_map.110.refs_1_), channel_id=1, source_target_pairs={{0,5},{1,4},{2,7},{3,6},{4,1},{5,0},{6,3},{7,2},{8,13},{9,12},{10,... | collective-permute-start | bytes 1720328 | tf_op jit(solution)/shard_map/ppermute | solution.py:326
  45.2 9.0 %collective-permute-start.11 = (bf16[160,768]{1,0:T(8,128)(2,1)S(1)}, bf16[160,768]{1,0:T(8,128)(2,1)S(1)}, u32[]{:S(2)}, u32[]{:S(2)}) collective-permute-start(bf16[160,768]{1,0:T(8,128)(2,1)S(1)} %shard_map.109.refs_1_), channel_id=1, source_target_pairs={{0,24},{8,16},{16,8},{24,0},{1,25},{9,17},{17,9},{25,1},{2,26},{10... | collective-permute-start | bytes 737288 | tf_op jit(solution)/shard_map/ppermute | solution.py:329
  46.4 12.8 %collective-permute-start.10 = (bf16[160,768]{1,0:T(8,128)(2,1)S(1)}, bf16[160,768]{1,0:T(8,128)(2,1)S(1)}, u32[]{:S(2)}, u32[]{:S(2)}) collective-permute-start(bf16[160,768]{1,0:T(8,128)(2,1)S(1)} %shard_map.109.refs_1_), channel_id=1, source_target_pairs={{0,16},{8,24},{16,0},{24,8},{1,17},{9,25},{17,1},{25,9},{2,18},{10... | collective-permute-start | bytes 737288 | tf_op jit(solution)/shard_map/ppermute | solution.py:329
  47.3 13.1 %collective-permute-start.9 = (bf16[160,768]{1,0:T(8,128)(2,1)S(1)}, bf16[160,768]{1,0:T(8,128)(2,1)S(1)}, u32[]{:S(2)}, u32[]{:S(2)}) collective-permute-start(bf16[160,768]{1,0:T(8,128)(2,1)S(1)} %shard_map.109.refs_1_), channel_id=1, source_target_pairs={{0,8},{8,0},{16,24},{24,16},{1,9},{9,1},{17,25},{25,17},{2,10},{10... | collective-permute-start | bytes 737288 | tf_op jit(solution)/shard_map/ppermute | solution.py:329
  47.8 28.6 %collective-permute-start.14 = (bf16[80,3584]{1,0:T(8,128)(2,1)S(1)}, bf16[80,3584]{1,0:T(8,128)(2,1)S(1)}, u32[]{:S(2)}, u32[]{:S(2)}) collective-permute-start(bf16[80,3584]{1,0:T(8,128)(2,1)S(1)} %shard_map.111.refs_6_), channel_id=1, source_target_pairs={{0,3},{1,2},{2,1},{3,0},{4,7},{5,6},{6,5},{7,4},{8,11},{9,10},{10,... | collective-permute-start | bytes 1720328 | tf_op jit(solution)/shard_map/ppermute | solution.py:326
  54.2 10.8 %collective-permute-start.6 = (bf16[160,768]{1,0:T(8,128)(2,1)S(1)}, bf16[160,768]{1,0:T(8,128)(2,1)S(1)}, u32[]{:S(2)}, u32[]{:S(2)}) collective-permute-start(bf16[160,768]{1,0:T(8,128)(2,1)S(1)} %get-tuple-element.51), channel_id=1, source_target_pairs={{0,8},{8,0},{16,24},{24,16},{1,9},{9,1},{17,25},{25,17},{2,10},{10... | collective-permute-start | bytes 737288 | tf_op jit(solution)/shard_map/ppermute | solution.py:329
  59.2 12.3 %collective-permute-start.7 = (bf16[160,768]{1,0:T(8,128)(2,1)S(1)}, bf16[160,768]{1,0:T(8,128)(2,1)S(1)}, u32[]{:S(2)}, u32[]{:S(2)}) collective-permute-start(bf16[160,768]{1,0:T(8,128)(2,1)S(1)} %get-tuple-element.52), channel_id=1, source_target_pairs={{0,16},{8,24},{16,0},{24,8},{1,17},{9,25},{17,1},{25,9},{2,18},{10... | collective-permute-start | bytes 737288 | tf_op jit(solution)/shard_map/ppermute | solution.py:329
  60.5 11.1 %collective-permute-start.8 = (bf16[160,768]{1,0:T(8,128)(2,1)S(1)}, bf16[160,768]{1,0:T(8,128)(2,1)S(1)}, u32[]{:S(2)}, u32[]{:S(2)}) collective-permute-start(bf16[160,768]{1,0:T(8,128)(2,1)S(1)} %get-tuple-element.53), channel_id=1, source_target_pairs={{0,24},{8,16},{16,8},{24,0},{1,25},{9,17},{17,9},{25,1},{2,26},{10... | collective-permute-start | bytes 737288 | tf_op jit(solution)/shard_map/ppermute | solution.py:329
  61.4 15.1 %copy-start.3 = (bf16[1,1024,1792]{2,1,0:T(8,128)(2,1)S(1)}, bf16[1,1024,1792]{2,1,0:T(8,128)(2,1)}, u32[]{:S(2)}) copy-start(bf16[1,1024,1792]{2,1,0:T(8,128)(2,1)} %param.14) | copy-start | bytes 11010052
  71.8 26.5 %collective-permute-start.13 = (bf16[80,3584]{1,0:T(8,128)(2,1)S(1)}, bf16[80,3584]{1,0:T(8,128)(2,1)S(1)}, u32[]{:S(2)}, u32[]{:S(2)}) collective-permute-start(bf16[80,3584]{1,0:T(8,128)(2,1)S(1)} %shard_map.115.refs_6_), channel_id=1, source_target_pairs={{0,6},{1,7},{2,4},{3,5},{4,2},{5,3},{6,0},{7,1},{8,14},{9,15},{10,... | collective-permute-start | bytes 1720328 | tf_op jit(solution)/shard_map/ppermute | solution.py:326
  73.8 8.3 %collective-permute-start.20 = (bf16[160,768]{1,0:T(8,128)(2,1)S(1)}, bf16[160,768]{1,0:T(8,128)(2,1)S(1)}, u32[]{:S(2)}, u32[]{:S(2)}) collective-permute-start(bf16[160,768]{1,0:T(8,128)(2,1)S(1)} %shard_map.114.refs_1_.refs_5_), channel_id=1, source_target_pairs={{0,24},{8,16},{16,8},{24,0},{1,25},{9,17},{17,9},{25,1},{2,26},{10... | collective-permute-start | bytes 737288 | tf_op jit(solution)/shard_map/ppermute | solution.py:329
  75.0 12.9 %collective-permute-start.19 = (bf16[160,768]{1,0:T(8,128)(2,1)S(1)}, bf16[160,768]{1,0:T(8,128)(2,1)S(1)}, u32[]{:S(2)}, u32[]{:S(2)}) collective-permute-start(bf16[160,768]{1,0:T(8,128)(2,1)S(1)} %shard_map.114.refs_1_.refs_5_), channel_id=1, source_target_pairs={{0,16},{8,24},{16,0},{24,8},{1,17},{9,25},{17,1},{25,9},{2,18},{10... | collective-permute-start | bytes 737288 | tf_op jit(solution)/shard_map/ppermute | solution.py:329
  76.3 12.7 %collective-permute-start.18 = (bf16[160,768]{1,0:T(8,128)(2,1)S(1)}, bf16[160,768]{1,0:T(8,128)(2,1)S(1)}, u32[]{:S(2)}, u32[]{:S(2)}) collective-permute-start(bf16[160,768]{1,0:T(8,128)(2,1)S(1)} %shard_map.114.refs_1_.refs_5_), channel_id=1, source_target_pairs={{0,8},{8,0},{16,24},{24,16},{1,9},{9,1},{17,25},{25,17},{2,10},{10... | collective-permute-start | bytes 737288 | tf_op jit(solution)/shard_map/ppermute | solution.py:329
  80.7 12.0 %collective-permute-start.15 = (bf16[160,768]{1,0:T(8,128)(2,1)S(1)}, bf16[160,768]{1,0:T(8,128)(2,1)S(1)}, u32[]{:S(2)}, u32[]{:S(2)}) collective-permute-start(bf16[160,768]{1,0:T(8,128)(2,1)S(1)} %get-tuple-element.57), channel_id=1, source_target_pairs={{0,8},{8,0},{16,24},{24,16},{1,9},{9,1},{17,25},{25,17},{2,10},{10... | collective-permute-start | bytes 737288 | tf_op jit(solution)/shard_map/ppermute | solution.py:329
  82.1 12.1 %collective-permute-start.16 = (bf16[160,768]{1,0:T(8,128)(2,1)S(1)}, bf16[160,768]{1,0:T(8,128)(2,1)S(1)}, u32[]{:S(2)}, u32[]{:S(2)}) collective-permute-start(bf16[160,768]{1,0:T(8,128)(2,1)S(1)} %get-tuple-element.58), channel_id=1, source_target_pairs={{0,16},{8,24},{16,0},{24,8},{1,17},{9,25},{17,1},{25,9},{2,18},{10... | collective-permute-start | bytes 737288 | tf_op jit(solution)/shard_map/ppermute | solution.py:329
  87.9 8.9 %collective-permute-start.17 = (bf16[160,768]{1,0:T(8,128)(2,1)S(1)}, bf16[160,768]{1,0:T(8,128)(2,1)S(1)}, u32[]{:S(2)}, u32[]{:S(2)}) collective-permute-start(bf16[160,768]{1,0:T(8,128)(2,1)S(1)} %get-tuple-element.59), channel_id=1, source_target_pairs={{0,24},{8,16},{16,8},{24,0},{1,25},{9,17},{17,9},{25,1},{2,26},{10... | collective-permute-start | bytes 737288 | tf_op jit(solution)/shard_map/ppermute | solution.py:329
  98.2 28.7 %collective-permute-start.30 = (bf16[80,3584]{1,0:T(8,128)(2,1)S(1)}, bf16[80,3584]{1,0:T(8,128)(2,1)S(1)}, u32[]{:S(2)}, u32[]{:S(2)}) collective-permute-start(bf16[80,3584]{1,0:T(8,128)(2,1)S(1)} %shard_map.119.refs_5_), channel_id=1, source_target_pairs={{0,7},{1,6},{2,5},{3,4},{4,3},{5,2},{6,1},{7,0},{8,15},{9,14},{10,... | collective-permute-start | bytes 1720328 | tf_op jit(solution)/shard_map/ppermute | solution.py:326
  101.4 8.5 %collective-permute-start.26 = (bf16[160,768]{1,0:T(8,128)(2,1)S(1)}, bf16[160,768]{1,0:T(8,128)(2,1)S(1)}, u32[]{:S(2)}, u32[]{:S(2)}) collective-permute-start(bf16[160,768]{1,0:T(8,128)(2,1)S(1)} %shard_map.118.refs_1_.refs_9_), channel_id=1, source_target_pairs={{0,24},{8,16},{16,8},{24,0},{1,25},{9,17},{17,9},{25,1},{2,26},{10... | collective-permute-start | bytes 737288 | tf_op jit(solution)/shard_map/ppermute | solution.py:329
  102.5 12.6 %collective-permute-start.25 = (bf16[160,768]{1,0:T(8,128)(2,1)S(1)}, bf16[160,768]{1,0:T(8,128)(2,1)S(1)}, u32[]{:S(2)}, u32[]{:S(2)}) collective-permute-start(bf16[160,768]{1,0:T(8,128)(2,1)S(1)} %shard_map.118.refs_1_.refs_9_), channel_id=1, source_target_pairs={{0,16},{8,24},{16,0},{24,8},{1,17},{9,25},{17,1},{25,9},{2,18},{10... | collective-permute-start | bytes 737288 | tf_op jit(solution)/shard_map/ppermute | solution.py:329
  103.9 12.4 %collective-permute-start.24 = (bf16[160,768]{1,0:T(8,128)(2,1)S(1)}, bf16[160,768]{1,0:T(8,128)(2,1)S(1)}, u32[]{:S(2)}, u32[]{:S(2)}) collective-permute-start(bf16[160,768]{1,0:T(8,128)(2,1)S(1)} %shard_map.118.refs_1_.refs_9_), channel_id=1, source_target_pairs={{0,8},{8,0},{16,24},{24,16},{1,9},{9,1},{17,25},{25,17},{2,10},{10... | collective-permute-start | bytes 737288 | tf_op jit(solution)/shard_map/ppermute | solution.py:329
  108.1 11.9 %collective-permute-start.21 = (bf16[80,768]{1,0:T(8,128)(2,1)S(1)}, bf16[80,768]{1,0:T(8,128)(2,1)S(1)}, u32[]{:S(2)}, u32[]{:S(2)}) collective-permute-start(bf16[80,768]{1,0:T(8,128)(2,1)S(1)} %get-tuple-element.62), channel_id=1, source_target_pairs={{0,8},{8,0},{16,24},{24,16},{1,9},{9,1},{17,25},{25,17},{2,10},{10... | collective-permute-start | bytes 368648 | tf_op jit(solution)/shard_map/ppermute | solution.py:329
  109.9 10.1 %collective-permute-start.22 = (bf16[80,768]{1,0:T(8,128)(2,1)S(1)}, bf16[80,768]{1,0:T(8,128)(2,1)S(1)}, u32[]{:S(2)}, u32[]{:S(2)}) collective-permute-start(bf16[80,768]{1,0:T(8,128)(2,1)S(1)} %get-tuple-element.63), channel_id=1, source_target_pairs={{0,16},{8,24},{16,0},{24,8},{1,17},{9,25},{17,1},{25,9},{2,18},{10... | collective-permute-start | bytes 368648 | tf_op jit(solution)/shard_map/ppermute | solution.py:329
  115.2 5.4 %collective-permute-start.23 = (bf16[80,768]{1,0:T(8,128)(2,1)S(1)}, bf16[80,768]{1,0:T(8,128)(2,1)S(1)}, u32[]{:S(2)}, u32[]{:S(2)}) collective-permute-start(bf16[80,768]{1,0:T(8,128)(2,1)S(1)} %get-tuple-element.64), channel_id=1, source_target_pairs={{0,24},{8,16},{16,8},{24,0},{1,25},{9,17},{17,9},{25,1},{2,26},{10... | collective-permute-start | bytes 368648 | tf_op jit(solution)/shard_map/ppermute | solution.py:329
  127.0 16.4 %collective-permute-start.38 = (bf16[80,1792]{1,0:T(8,128)(2,1)S(1)}, bf16[80,1792]{1,0:T(8,128)(2,1)S(1)}, u32[]{:S(2)}, u32[]{:S(2)}) collective-permute-start(bf16[80,1792]{1,0:T(8,128)(2,1)S(1)} %shard_map.124.refs_5_), channel_id=1, source_target_pairs={{0,2},{1,3},{2,0},{3,1},{4,6},{5,7},{6,4},{7,5},{8,10},{9,11},{10,... | collective-permute-start | bytes 860168 | tf_op jit(solution)/shard_map/ppermute | solution.py:326
  127.0 16.4 %collective-permute-start.37 = (bf16[80,1792]{1,0:T(8,128)(2,1)S(1)}, bf16[80,1792]{1,0:T(8,128)(2,1)S(1)}, u32[]{:S(2)}, u32[]{:S(2)}) collective-permute-start(bf16[80,1792]{1,0:T(8,128)(2,1)S(1)} %shard_map.123.refs_1_), channel_id=1, source_target_pairs={{0,4},{1,5},{2,6},{3,7},{4,0},{5,1},{6,2},{7,3},{8,12},{9,13},{10,... | collective-permute-start | bytes 860168 | tf_op jit(solution)/shard_map/ppermute | solution.py:326
  128.7 6.7 %collective-permute-start.29 = (bf16[80,768]{1,0:T(8,128)(2,1)S(1)}, bf16[80,768]{1,0:T(8,128)(2,1)S(1)}, u32[]{:S(2)}, u32[]{:S(2)}) collective-permute-start(bf16[80,768]{1,0:T(8,128)(2,1)S(1)} %shard_map.122.refs_1_.refs_13_), channel_id=1, source_target_pairs={{0,24},{8,16},{16,8},{24,0},{1,25},{9,17},{17,9},{25,1},{2,26},{10... | collective-permute-start | bytes 368648 | tf_op jit(solution)/shard_map/ppermute | solution.py:329
  129.9 7.2 %collective-permute-start.28 = (bf16[80,768]{1,0:T(8,128)(2,1)S(1)}, bf16[80,768]{1,0:T(8,128)(2,1)S(1)}, u32[]{:S(2)}, u32[]{:S(2)}) collective-permute-start(bf16[80,768]{1,0:T(8,128)(2,1)S(1)} %shard_map.122.refs_1_.refs_13_), channel_id=1, source_target_pairs={{0,16},{8,24},{16,0},{24,8},{1,17},{9,25},{17,1},{25,9},{2,18},{10... | collective-permute-start | bytes 368648 | tf_op jit(solution)/shard_map/ppermute | solution.py:329
  131.4 6.0 %collective-permute-start.27 = (bf16[80,768]{1,0:T(8,128)(2,1)S(1)}, bf16[80,768]{1,0:T(8,128)(2,1)S(1)}, u32[]{:S(2)}, u32[]{:S(2)}) collective-permute-start(bf16[80,768]{1,0:T(8,128)(2,1)S(1)} %shard_map.122.refs_1_.refs_13_), channel_id=1, source_target_pairs={{0,8},{8,0},{16,24},{24,16},{1,9},{9,1},{17,25},{25,17},{2,10},{10... | collective-permute-start | bytes 368648 | tf_op jit(solution)/shard_map/ppermute | solution.py:329
  135.4 6.2 %collective-permute-start.31 = (bf16[80,768]{1,0:T(8,128)(2,1)S(1)}, bf16[80,768]{1,0:T(8,128)(2,1)S(1)}, u32[]{:S(2)}, u32[]{:S(2)}) collective-permute-start(bf16[80,768]{1,0:T(8,128)(2,1)S(1)} %get-tuple-element.68), channel_id=1, source_target_pairs={{0,8},{8,0},{16,24},{24,16},{1,9},{9,1},{17,25},{25,17},{2,10},{10... | collective-permute-start | bytes 368648 | tf_op jit(solution)/shard_map/ppermute | solution.py:329
  137.1 4.5 %collective-permute-start.32 = (bf16[80,768]{1,0:T(8,128)(2,1)S(1)}, bf16[80,768]{1,0:T(8,128)(2,1)S(1)}, u32[]{:S(2)}, u32[]{:S(2)}) collective-permute-start(bf16[80,768]{1,0:T(8,128)(2,1)S(1)} %get-tuple-element.69), channel_id=1, source_target_pairs={{0,16},{8,24},{16,0},{24,8},{1,17},{9,25},{17,1},{25,9},{2,18},{10... | collective-permute-start | bytes 368648 | tf_op jit(solution)/shard_map/ppermute | solution.py:329
  137.3 5.9 %collective-permute-start.33 = (bf16[80,768]{1,0:T(8,128)(2,1)S(1)}, bf16[80,768]{1,0:T(8,128)(2,1)S(1)}, u32[]{:S(2)}, u32[]{:S(2)}) collective-permute-start(bf16[80,768]{1,0:T(8,128)(2,1)S(1)} %get-tuple-element.70), channel_id=1, source_target_pairs={{0,24},{8,16},{16,8},{24,0},{1,25},{9,17},{17,9},{25,1},{2,26},{10... | collective-permute-start | bytes 368648 | tf_op jit(solution)/shard_map/ppermute | solution.py:329
  143.4 16.5 %collective-permute-start.39 = (bf16[80,1792]{1,0:T(8,128)(2,1)S(1)}, bf16[80,1792]{1,0:T(8,128)(2,1)S(1)}, u32[]{:S(2)}, u32[]{:S(2)}) collective-permute-start(bf16[80,1792]{1,0:T(8,128)(2,1)S(1)} %shard_map.128.refs_1_), channel_id=1, source_target_pairs={{0,5},{1,4},{2,7},{3,6},{4,1},{5,0},{6,3},{7,2},{8,13},{9,12},{10,... | collective-permute-start | bytes 860168 | tf_op jit(solution)/shard_map/ppermute | solution.py:326
  146.8 6.3 %collective-permute-start.36 = (bf16[80,768]{1,0:T(8,128)(2,1)S(1)}, bf16[80,768]{1,0:T(8,128)(2,1)S(1)}, u32[]{:S(2)}, u32[]{:S(2)}) collective-permute-start(bf16[80,768]{1,0:T(8,128)(2,1)S(1)} %shard_map.127.refs_1_.refs_17_), channel_id=1, source_target_pairs={{0,24},{8,16},{16,8},{24,0},{1,25},{9,17},{17,9},{25,1},{2,26},{10... | collective-permute-start | bytes 368648 | tf_op jit(solution)/shard_map/ppermute | solution.py:329
  147.7 7.9 %collective-permute-start.35 = (bf16[80,768]{1,0:T(8,128)(2,1)S(1)}, bf16[80,768]{1,0:T(8,128)(2,1)S(1)}, u32[]{:S(2)}, u32[]{:S(2)}) collective-permute-start(bf16[80,768]{1,0:T(8,128)(2,1)S(1)} %shard_map.127.refs_1_.refs_17_), channel_id=1, source_target_pairs={{0,16},{8,24},{16,0},{24,8},{1,17},{9,25},{17,1},{25,9},{2,18},{10... | collective-permute-start | bytes 368648 | tf_op jit(solution)/shard_map/ppermute | solution.py:329
  148.3 7.3 %collective-permute-start.34 = (bf16[80,768]{1,0:T(8,128)(2,1)S(1)}, bf16[80,768]{1,0:T(8,128)(2,1)S(1)}, u32[]{:S(2)}, u32[]{:S(2)}) collective-permute-start(bf16[80,768]{1,0:T(8,128)(2,1)S(1)} %shard_map.127.refs_1_.refs_17_), channel_id=1, source_target_pairs={{0,8},{8,0},{16,24},{24,16},{1,9},{9,1},{17,25},{25,17},{2,10},{10... | collective-permute-start | bytes 368648 | tf_op jit(solution)/shard_map/ppermute | solution.py:329
  149.4 22.2 %collective-permute-start.42 = (bf16[80,1792]{1,0:T(8,128)(2,1)S(1)}, bf16[80,1792]{1,0:T(8,128)(2,1)S(1)}, u32[]{:S(2)}, u32[]{:S(2)}) collective-permute-start(bf16[80,1792]{1,0:T(8,128)(2,1)S(1)} %get-tuple-element.72), channel_id=1, source_target_pairs={{0,1},{1,0},{2,3},{3,2},{4,5},{5,4},{6,7},{7,6},{8,9},{9,8},{10,11... | collective-permute-start | bytes 860168 | tf_op jit(solution)/shard_map/ppermute | solution.py:326
  153.1 24.9 %collective-permute-start.43 = (bf16[80,1792]{1,0:T(8,128)(2,1)S(1)}, bf16[80,1792]{1,0:T(8,128)(2,1)S(1)}, u32[]{:S(2)}, u32[]{:S(2)}) collective-permute-start(bf16[80,1792]{1,0:T(8,128)(2,1)S(1)} %shard_map.129.refs_7_), channel_id=1, source_target_pairs={{0,3},{1,2},{2,1},{3,0},{4,7},{5,6},{6,5},{7,4},{8,11},{9,10},{10,... | collective-permute-start | bytes 860168 | tf_op jit(solution)/shard_map/ppermute | solution.py:326
  158.9 24.0 %collective-permute-start.41 = (bf16[80,1792]{1,0:T(8,128)(2,1)S(1)}, bf16[80,1792]{1,0:T(8,128)(2,1)S(1)}, u32[]{:S(2)}, u32[]{:S(2)}) collective-permute-start(bf16[80,1792]{1,0:T(8,128)(2,1)S(1)} %shard_map.130.refs_1_), channel_id=1, source_target_pairs={{0,7},{1,6},{2,5},{3,4},{4,3},{5,2},{6,1},{7,0},{8,15},{9,14},{10,... | collective-permute-start | bytes 860168 | tf_op jit(solution)/shard_map/ppermute | solution.py:326
  159.8 26.4 %collective-permute-start.40 = (bf16[80,1792]{1,0:T(8,128)(2,1)S(1)}, bf16[80,1792]{1,0:T(8,128)(2,1)S(1)}, u32[]{:S(2)}, u32[]{:S(2)}) collective-permute-start(bf16[80,1792]{1,0:T(8,128)(2,1)S(1)} %shard_map.131.refs_31_), channel_id=1, source_target_pairs={{0,6},{1,7},{2,4},{3,5},{4,2},{5,3},{6,0},{7,1},{8,14},{9,15},{10,... | collective-permute-start | bytes 860168 | tf_op jit(solution)/shard_map/ppermute | solution.py:326
  160.7 17.3 %copy-start.18 = (s32[1,512]{1,0:T(1,128)S(1)}, s32[1,512]{1,0:T(1,128)}, u32[]{:S(2)}) copy-start(s32[1,512]{1,0:T(1,128)} %copy-done.16) | copy-start | bytes 6148
  (18 other events, 42.9 us)

commit v3 on v2

--- a/solution.py
+++ b/solution.py
@@ -222,11 +222,12 @@
     n_blocks = sum(sizes)
     pieces = refs[:n_pieces]
     blocks = refs[n_pieces : n_pieces + n_blocks]
-    wd, mom, new_w, new_m, hid_t, dy = refs[n_pieces + n_blocks :]
+    wd, mom, new_w, new_m, token, hid_t, dy = refs[n_pieces + n_blocks :]
     hq = pieces[0].shape[1]
 
     @pl.when(pl.program_id(0) == 0)
     def _():
+        token[...] = jnp.zeros_like(token)
         base = 0
         for g, size in enumerate(sizes):
             for d in range(ndp):
@@ -258,11 +259,11 @@
         functools.partial(down_body, cap, sizes, ndp),
         [dp_idx, *pieces, *blocks, wd, mom],
         deps,
-        [jax.ShapeDtypeStruct((h, s), bf16)] * 2,
+        [jax.ShapeDtypeStruct((h, s), bf16)] * 2 + [jax.ShapeDtypeStruct((8, 128), f32)],
         [whole((p.shape[0], hq)) for p in pieces]
         + [pl.BlockSpec((cap, TILE), lambda c, i: (0, s // TILE + c))] * len(blocks)
         + [col, col],
-        [col, col],
+        [col, col, whole((8, 128))],
         grid=(s // TILE,),
         scalars=1,
         scratch=[pltpu.VMEM((h, rows), bf16), pltpu.VMEM((rows, TILE), bf16)],
@@ -329,7 +330,7 @@
         return lax.ppermute(v, "dp", [(i, i ^ k) for i in range(ndp)])
 
     far, near = grouping(n)
-    chunks = [near[0], near[1] + far[0], near[2] + far[1], far[2], far[3]]
+    chunks = [near[0], far[0], far[1] + near[1], far[2] + near[2], far[3]]
     send, got, ready, back, pieces, parts = {}, {}, {}, {}, {}, {}
     mark = []
 
@@ -366,44 +367,44 @@
     def gotten(offs):
         return [got[k] for k in offs]
 
-    target, *sends = dispatch(n, cap, far[0], me, ids, codes, tokens, grad_out, True, [])
-    send.update(zip(far[0], sends))
+    offs = far[0] + near[0]
+    target, *sends = dispatch(n, cap, offs, me, ids, codes, tokens, grad_out, True, [])
+    send.update(zip(offs, sends))
     mark[:] = [sends[0]]
-    push(far[0], [])
-    for offs in (near[0], near[1], far[1] + near[2], far[2] + far[3]):
-        sends = dispatch(n, cap, offs, me, target, codes, tokens, grad_out, False, mark)
-        send.update(zip(offs, sends))
-        mark[:] = [sends[0]]
-        if offs in near:
-            push(offs, [])
+    push(offs, [])
+    offs = far[1] + near[1] + far[2] + near[2] + far[3]
+    sends = dispatch(n, cap, offs, me, target, codes, tokens, grad_out, False, mark)
+    send.update(zip(offs, sends))
+    mark[:] = [sends[0]]
 
     fwd(0)
+    push(far[1] + near[1], gotten(far[0]))
     act(0)
-    push(far[1], gotten(far[0]))
-    push(near[2], gotten(near[1]))
     fwd(1)
     bwd(0)
+    act(1)
+    push(far[2] + near[2], gotten(far[1] + near[1]))
     give_back(near[0], [])
-    act(1)
-    push(far[2], gotten(far[1]))
     fwd(2)
     bwd(1)
     act(2)
-    push(far[3], gotten(far[2]))
+    push(far[3], gotten(far[2] + near[2]))
     fwd(3)
     bwd(2)
+    give_back(near[1], [])
     act(3)
-    give_back(far[0] + near[1], gotten(far[3]))
+    give_back(far[0], gotten(far[3]) + [back[k] for k in near[1] + near[0][1:]])
+    give_back(far[1], [])
     fwd(4)
     bwd(3)
     act(4)
-    give_back(far[1] + near[2], [back[k] for k in far[0] + near[1]])
+    give_back(far[2], [back[k] for k in far[0]])
+    give_back(near[2], [])
     bwd(4)
-    give_back(far[2], [back[k] for k in far[1]])
     give_back(far[3], [])
     order = range(len(chunks))
     flat = [k for c in order for k in chunks[c]]
-    new_down, new_moment = down(
+    new_down, new_moment, token = down(
         cap,
         [len(chunks[c]) for c in order],
         ndp,
@@ -414,7 +415,7 @@
         mom,
         mark,
     )
-    mark[:] = [new_down]
+    mark[:] = [token]
     tail = far[2] + far[3]
     early = [k for k in flat if k not in tail]
     part = combine(cap, early, me, target, [back[k] for k in early], None, mark)

time: 191 us -> 182 us (0.953)
  starting transfers between devices: 46.6 us -> 52.1 us
  waiting for transfers between devices: 61.5 us -> 56.4 us
  local copies, waits for them, and re-layouts: 16.7 us -> 12 us
  Pallas kernels: 64.5 us -> 60.5 us
    ppermute x30, waiting for transfers between devices: 44.4 us -> 19.2 us  [swap_dp(): return lax.ppermute(v, 'dp', [(i, i ^ k) for i in range(ndp)])]
    ppermute x14, waiting for transfers between devices: 17.1 us -> 37.2 us  [swap_expert(): return lax.ppermute(v, 'expert', [(i, i ^ k) for i in range(n)])]
    unnamed x44 -> x32, local copies, waits for them, and re-layouts: 16.7 us -> 12 us
    pallas_call x32 -> x27, Pallas kernels: 64.5 us -> 60.5 us  [call(): pl.pallas_call(skipping(body, len(operands), len(deps)), out_shape=out_sh...]
    ppermute x30, starting transfers between devices: 27.2 us -> 30.7 us  [swap_dp(): return lax.ppermute(v, 'dp', [(i, i ^ k) for i in range(ndp)])]
    ppermute x14, starting transfers between devices: 19.4 us -> 21.4 us  [swap_expert(): return lax.ppermute(v, 'expert', [(i, i ^ k) for i in range(n)])]
  transfers between devices with their start and end apart: 44 -> 44, of which waited for: 19 -> 18; matrix products, arithmetic and copies ran while one was open for 0% -> 0% of each run, Pallas kernels for 30% -> 30%
where the time goes in v3:
time: 182 us
  Pallas kernels  60.5 us (33%)
  waiting for transfers between devices  56.4 us (31%)
  starting transfers between devices  52.1 us (29%)
  local copies, waits for them, and re-layouts  12 us (7%)
    pallas_call x27, Pallas kernels, call(): pl.pallas_call(skipping(body, len(operands), len(deps)), out_shape=out_sh...  60.5 us
    ppermute x14, waiting for transfers between devices, swap_expert(): return lax.ppermute(v, 'expert', [(i, i ^ k) for i in range(n)])  37.2 us
    ppermute x30, starting transfers between devices, swap_dp(): return lax.ppermute(v, 'dp', [(i, i ^ k) for i in range(ndp)])  30.7 us
    ppermute x14, starting transfers between devices, swap_expert(): return lax.ppermute(v, 'expert', [(i, i ^ k) for i in range(n)])  21.4 us
    ppermute x30, waiting for transfers between devices, swap_dp(): return lax.ppermute(v, 'dp', [(i, i ^ k) for i in range(ndp)])  19.2 us
    unnamed x32, local copies, waits for them, and re-layouts  12 us
  transfers between devices with their start and end apart: 44, of which 18 were waited for; matrix products, arithmetic and copies ran while one was open for 0% of the time, Pallas kernels for 30%

profile of v3, /device:TPU:9, one launch (start us, length us, event | category | flops | bytes accessed | tf_op | source)
XLA Modules:
  0.0 181.9 jit_solution(4030735743407841148)
XLA Ops:
  0.6 1.5 copy-done.5
  2.1 1.5 copy-done.7
  5.0 2.2 %shard_map.103 = (s32[1,512]{1,0:T(1,128)S(1)}, bf16[80,3584]{1,0:T(8,128)(2,1)}, bf16[80,3584]{1,0:T(8,128)(2,1)S(1)}, bf16[80,3584]{1,0:T(8,128)(2,1)}) custom-call(s32[1]{0:T(128)} %bitcast.refs_0_, s32[1,512]{1,0:T(1,128)S(1)} %bitcast.39, s32[1,512]{1,0:T(1,128)S(1)} %bitcast.37, bf16[512,1792]{1,0:T(8,128)(2,1)S(1)} %copy-done.5, ...), custom_call_target="tpu_custom_call" | custom-call | tf_op jit(solution)/shard_map/pallas_call | solution.py:39
  8.5 2.3 %collective-permute-start = (bf16[80,3584]{1,0:T(8,128)(2,1)}, bf16[80,3584]{1,0:T(8,128)(2,1)S(1)}, u32[]{:S(2)}, u32[]{:S(2)}) collective-permute-start(bf16[80,3584]{1,0:T(8,128)(2,1)} %get-tuple-element.42.refs_5_), channel_id=1, source_target_pairs={{0,4},{1,5},{2,6},{3,7},{4,0},{5,1},{6,2},{7,3},{8,12},{9,13},{10,... | collective-permute-start | bytes 1720328 | tf_op jit(solution)/shard_map/ppermute | solution.py:327
  10.8 1.6 copy-done.8
  13.8 1.7 shard_map.104
  15.5 2.0 %copy-done.1 = bf16[1,1792,1024]{2,1,0:T(8,128)(2,1)S(1)} copy-done((bf16[1,1792,1024]{2,1,0:T(8,128)(2,1)S(1)}, bf16[1,1792,1024]{2,1,0:T(8,128)(2,1)}, u32[]{:S(2)}) %copy-start.1) | copy-done | bytes 3670040
  17.5 2.0 %copy-done.3 = bf16[1,1024,1792]{2,1,0:T(8,128)(2,1)S(1)} copy-done((bf16[1,1024,1792]{2,1,0:T(8,128)(2,1)S(1)}, bf16[1,1024,1792]{2,1,0:T(8,128)(2,1)}, u32[]{:S(2)}) %copy-start.3) | copy-done | bytes 3670040
  19.6 4.2 %shard_map.105 = (bf16[160,768]{1,0:T(8,128)(2,1)S(1)}, bf16[160,768]{1,0:T(8,128)(2,1)S(1)}, bf16[160,768]{1,0:T(8,128)(2,1)S(1)}, bf16[160,768]{1,0:T(8,128)(2,1)S(1)}) custom-call(s32[1]{0:T(128)} %bitcast.3.refs_0_, bf16[80,3584]{1,0:T(8,128)(2,1)S(1)} %get-tuple-element.44.refs_1_.refs_21_, ...), custom_call_target="tpu_custom_call" | custom-call | tf_op jit(solution)/shard_map/pallas_call | solution.py:39
  23.8 1.3 collective-permute-start.2
  25.1 1.2 collective-permute-start.3
  26.5 9.5 %collective-permute-done.refs_2_.refs_1_.refs_23_ = bf16[80,3584]{1,0:T(8,128)(2,1)S(1)} collective-permute-done((bf16[80,3584]{1,0:T(8,128)(2,1)}, bf16[80,3584]{1,0:T(8,128)(2,1)S(1)}, u32[]{:S(2)}, u32[]{:S(2)}) %collective-permute-start) | collective-permute-done | bytes 573472 | tf_op jit(solution)/shard_map/ppermute | solution.py:327
  36.8 2.5 %collective-permute-start.11 = (bf16[80,3584]{1,0:T(8,128)(2,1)S(1)}, bf16[80,3584]{1,0:T(8,128)(2,1)S(1)}, u32[]{:S(2)}, u32[]{:S(2)}) collective-permute-start(bf16[80,3584]{1,0:T(8,128)(2,1)S(1)} %shard_map.106.refs_1_), channel_id=1, source_target_pairs={{0,5},{1,4},{2,7},{3,6},{4,1},{5,0},{6,3},{7,2},{8,13},{9,12},{10,... | collective-permute-start | bytes 1720328 | tf_op jit(solution)/shard_map/ppermute | solution.py:327
  39.6 2.2 %collective-permute-start.10 = (bf16[160,768]{1,0:T(8,128)(2,1)S(1)}, bf16[160,768]{1,0:T(8,128)(2,1)S(1)}, u32[]{:S(2)}, u32[]{:S(2)}) collective-permute-start(bf16[160,768]{1,0:T(8,128)(2,1)S(1)} %shard_map.108.refs_5_.refs_1_), channel_id=1, source_target_pairs={{0,24},{8,16},{16,8},{24,0},{1,25},{9,17},{17,9},{25,1},{2,26},{10... | collective-permute-start | bytes 737288 | tf_op jit(solution)/shard_map/ppermute | solution.py:330
  42.3 4.0 %shard_map.109 = (bf16[80,768]{1,0:T(8,128)(2,1)S(1)}, bf16[80,768]{1,0:T(8,128)(2,1)S(1)}, bf16[80,768]{1,0:T(8,128)(2,1)S(1)}, bf16[80,768]{1,0:T(8,128)(2,1)S(1)}) custom-call(s32[1]{0:T(128)} %bitcast.3.refs_0_, bf16[80,3584]{1,0:T(8,128)(2,1)S(1)} %collective-permute-done.refs_2_.refs_1_.refs_23_, bf16[1792,1024]{1,0:T(8,128)(2,1)S(1)} %bitcast.11, ...), custom_call_target="tpu_custom_call" | custom-call | tf_op jit(solution)/shard_map/pallas_call | solution.py:39
  46.3 1.8 collective-permute-done.10.refs_4_
  49.3 4.4 %collective-permute-done.9.refs_3_ = bf16[160,768]{1,0:T(8,128)(2,1)S(1)} collective-permute-done((bf16[160,768]{1,0:T(8,128)(2,1)S(1)}, bf16[160,768]{1,0:T(8,128)(2,1)S(1)}, u32[]{:S(2)}, u32[]{:S(2)}) %collective-permute-start.9) | collective-permute-done | bytes 245792 | tf_op jit(solution)/shard_map/ppermute | solution.py:330
  53.7 1.2 collective-permute-start.6
  56.1 3.7 %shard_map.110 = (bf16[80,1792]{1,0:T(8,128)(2,1)S(1)}, bf16[80,1792]{1,0:T(8,128)(2,1)S(1)}) custom-call(s32[1]{0:T(128)} %bitcast.3.refs_0_, bf16[160,768]{1,0:T(8,128)(2,1)S(1)} %shard_map.108.refs_5_.refs_1_, bf16[160,768]{1,0:T(8,128)(2,1)S(1)} %collective-permute-done.8.refs_2_, bf16[160,768]{1,0:T(8,128)(2,1)S(1)} %collective-permute-done.9.refs_3_, ...), custom_call_target="tpu_custom_call" | custom-call | tf_op jit(solution)/shard_map/pallas_call | solution.py:39
  60.6 4.0 %collective-permute-done.11.refs_2_.refs_1_.refs_24_ = bf16[80,3584]{1,0:T(8,128)(2,1)S(1)} collective-permute-done((bf16[80,3584]{1,0:T(8,128)(2,1)S(1)}, bf16[80,3584]{1,0:T(8,128)(2,1)S(1)}, u32[]{:S(2)}, u32[]{:S(2)}) %collective-permute-start.11) | collective-permute-done | bytes 573472 | tf_op jit(solution)/shard_map/ppermute | solution.py:327
  64.7 3.3 %collective-permute-start.13 = (bf16[80,3584]{1,0:T(8,128)(2,1)S(1)}, bf16[80,3584]{1,0:T(8,128)(2,1)S(1)}, u32[]{:S(2)}, u32[]{:S(2)}) collective-permute-start(bf16[80,3584]{1,0:T(8,128)(2,1)S(1)} %shard_map.112.refs_1_), channel_id=1, source_target_pairs={{0,6},{1,7},{2,4},{3,5},{4,2},{5,3},{6,0},{7,1},{8,14},{9,15},{10,... | collective-permute-start | bytes 1720328 | tf_op jit(solution)/shard_map/ppermute | solution.py:327
  67.9 2.2 %collective-permute-start.20 = (bf16[80,768]{1,0:T(8,128)(2,1)S(1)}, bf16[80,768]{1,0:T(8,128)(2,1)S(1)}, u32[]{:S(2)}, u32[]{:S(2)}) collective-permute-start(bf16[80,768]{1,0:T(8,128)(2,1)S(1)} %shard_map.111.refs_1_.refs_5_), channel_id=1, source_target_pairs={{0,24},{8,16},{16,8},{24,0},{1,25},{9,17},{17,9},{25,1},{2,26},{10... | collective-permute-start | bytes 368648 | tf_op jit(solution)/shard_map/ppermute | solution.py:330
  70.6 4.2 %shard_map.114 = (bf16[160,768]{1,0:T(8,128)(2,1)S(1)}, bf16[160,768]{1,0:T(8,128)(2,1)S(1)}, bf16[160,768]{1,0:T(8,128)(2,1)S(1)}, bf16[160,768]{1,0:T(8,128)(2,1)S(1)}) custom-call(s32[1]{0:T(128)} %bitcast.3.refs_0_, bf16[80,3584]{1,0:T(8,128)(2,1)S(1)} %collective-permute-done.11.refs_2_.refs_1_.refs_24_, ...), custom_call_target="tpu_custom_call" | custom-call | tf_op jit(solution)/shard_map/pallas_call | solution.py:39
  74.8 1.3 collective-permute-start.15
  76.7 1.2 collective-permute-start.16
  79.1 3.3 %shard_map.115.refs_4_.refs_0_ = bf16[80,1792]{1,0:T(8,128)(2,1)S(1)} custom-call(s32[1]{0:T(128)} %bitcast.3.refs_0_, bf16[80,768]{1,0:T(8,128)(2,1)S(1)} %shard_map.111.refs_1_.refs_5_, bf16[80,768]{1,0:T(8,128)(2,1)S(1)} %collective-permute-done.18.refs_2_.refs_6_, bf16[80,768]{1,0:T(8,128)(2,1)S(1)} %collective-permute-done.19.refs_3_.refs_7_, ...), custom_call_target="tpu_custom_call" | custom-call | tf_op jit(solution)/shard_map/pallas_call | solution.py:39
  82.4 5.0 %collective-permute-done.16.refs_2_ = bf16[160,768]{1,0:T(8,128)(2,1)S(1)} collective-permute-done((bf16[160,768]{1,0:T(8,128)(2,1)S(1)}, bf16[160,768]{1,0:T(8,128)(2,1)S(1)}, u32[]{:S(2)}, u32[]{:S(2)}) %collective-permute-start.16) | collective-permute-done | bytes 245792 | tf_op jit(solution)/shard_map/ppermute | solution.py:330
  88.8 1.3 collective-permute-start.25
  91.3 2.0 %collective-permute-done.13.refs_2_.refs_1_.refs_26_ = bf16[80,3584]{1,0:T(8,128)(2,1)S(1)} collective-permute-done((bf16[80,3584]{1,0:T(8,128)(2,1)S(1)}, bf16[80,3584]{1,0:T(8,128)(2,1)S(1)}, u32[]{:S(2)}, u32[]{:S(2)}) %collective-permute-start.13) | collective-permute-done | bytes 573472 | tf_op jit(solution)/shard_map/ppermute | solution.py:327
  93.3 2.2 %collective-permute-start.30 = (bf16[80,3584]{1,0:T(8,128)(2,1)S(1)}, bf16[80,3584]{1,0:T(8,128)(2,1)S(1)}, u32[]{:S(2)}, u32[]{:S(2)}) collective-permute-start(bf16[80,3584]{1,0:T(8,128)(2,1)S(1)} %shard_map.117.refs_6_), channel_id=1, source_target_pairs={{0,7},{1,6},{2,5},{3,4},{4,3},{5,2},{6,1},{7,0},{8,15},{9,14},{10,... | collective-permute-start | bytes 1720328 | tf_op jit(solution)/shard_map/ppermute | solution.py:327
  95.5 4.2 %shard_map.118 = (bf16[160,768]{1,0:T(8,128)(2,1)S(1)}, bf16[160,768]{1,0:T(8,128)(2,1)S(1)}, bf16[160,768]{1,0:T(8,128)(2,1)S(1)}, bf16[160,768]{1,0:T(8,128)(2,1)S(1)}) custom-call(s32[1]{0:T(128)} %bitcast.3.refs_0_, bf16[80,3584]{1,0:T(8,128)(2,1)S(1)} %collective-permute-done.13.refs_2_.refs_1_.refs_26_, ...), custom_call_target="tpu_custom_call" | custom-call | tf_op jit(solution)/shard_map/pallas_call | solution.py:39
  99.7 1.3 collective-permute-start.21
  101.0 1.2 collective-permute-start.22
  102.5 1.5 collective-permute-start.32
  104.0 3.7 %shard_map.119 = (bf16[80,1792]{1,0:T(8,128)(2,1)S(1)}, bf16[80,1792]{1,0:T(8,128)(2,1)S(1)}) custom-call(s32[1]{0:T(128)} %bitcast.3.refs_0_, bf16[160,768]{1,0:T(8,128)(2,1)S(1)} %shard_map.116.refs_1_.refs_9_, bf16[160,768]{1,0:T(8,128)(2,1)S(1)} %collective-permute-done.24.refs_2_.refs_10_, ...), custom_call_target="tpu_custom_call" | custom-call | tf_op jit(solution)/shard_map/pallas_call | solution.py:39
  108.8 5.2 %collective-permute-done.23.refs_3_ = bf16[160,768]{1,0:T(8,128)(2,1)S(1)} collective-permute-done((bf16[160,768]{1,0:T(8,128)(2,1)S(1)}, bf16[160,768]{1,0:T(8,128)(2,1)S(1)}, u32[]{:S(2)}, u32[]{:S(2)}) %collective-permute-start.23) | collective-permute-done | bytes 245792 | tf_op jit(solution)/shard_map/ppermute | solution.py:330
  116.9 4.4 %collective-permute-done.30.refs_2_.refs_1_.refs_28_ = bf16[80,3584]{1,0:T(8,128)(2,1)S(1)} collective-permute-done((bf16[80,3584]{1,0:T(8,128)(2,1)S(1)}, bf16[80,3584]{1,0:T(8,128)(2,1)S(1)}, u32[]{:S(2)}, u32[]{:S(2)}) %collective-permute-start.30) | collective-permute-done | bytes 573472 | tf_op jit(solution)/shard_map/ppermute | solution.py:327
  121.3 4.0 %shard_map.122 = (bf16[80,768]{1,0:T(8,128)(2,1)S(1)}, bf16[80,768]{1,0:T(8,128)(2,1)S(1)}, bf16[80,768]{1,0:T(8,128)(2,1)S(1)}, bf16[80,768]{1,0:T(8,128)(2,1)S(1)}) custom-call(s32[1]{0:T(128)} %bitcast.3.refs_0_, bf16[80,3584]{1,0:T(8,128)(2,1)S(1)} %collective-permute-done.30.refs_2_.refs_1_.refs_28_, bf16[1792,1024]{1,0:T(8,128)(2,1)S(1)} %bitcast.17, ...), custom_call_target="tpu_custom_call" | custom-call | tf_op jit(solution)/shard_map/pallas_call | solution.py:39
  125.3 1.3 collective-permute-start.33
  129.4 3.7 %shard_map.123 = (bf16[80,1792]{1,0:T(8,128)(2,1)S(1)}, bf16[80,1792]{1,0:T(8,128)(2,1)S(1)}) custom-call(s32[1]{0:T(128)} %bitcast.3.refs_0_, bf16[160,768]{1,0:T(8,128)(2,1)S(1)} %shard_map.120.refs_1_.refs_13_, bf16[160,768]{1,0:T(8,128)(2,1)S(1)} %collective-permute-done.27.refs_2_.refs_14_, ...), custom_call_target="tpu_custom_call" | custom-call | tf_op jit(solution)/shard_map/pallas_call | solution.py:39
  136.4 4.5 %collective-permute-start.42 = (bf16[80,1792]{1,0:T(8,128)(2,1)S(1)}, bf16[80,1792]{1,0:T(8,128)(2,1)S(1)}, u32[]{:S(2)}, u32[]{:S(2)}) collective-permute-start(bf16[80,1792]{1,0:T(8,128)(2,1)S(1)} %get-tuple-element.67.refs_4_), channel_id=1, source_target_pairs={{0,5},{1,4},{2,7},{3,6},{4,1},{5,0},{6,3},{7,2},{8,13},{9,12},{10,... | collective-permute-start | bytes 860168 | tf_op jit(solution)/shard_map/ppermute | solution.py:327
  141.8 3.3 %shard_map.126.refs_31_ = bf16[80,1792]{1,0:T(8,128)(2,1)S(1)} custom-call(s32[1]{0:T(128)} %bitcast.3.refs_0_, bf16[80,768]{1,0:T(8,128)(2,1)S(1)} %shard_map.124.refs_1_.refs_17_, bf16[80,768]{1,0:T(8,128)(2,1)S(1)} %collective-permute-done.38.refs_2_.refs_18_, bf16[80,768]{1,0:T(8,128)(2,1)S(1)} %collective-permute-done.39.refs_3_.refs_19_, ...), custom_call_target="tpu_custom_call" | custom-call | tf_op jit(solution)/shard_map/pallas_call | solution.py:39
  145.1 2.2 %collective-permute-start.41 = (bf16[80,1792]{1,0:T(8,128)(2,1)S(1)}, bf16[80,1792]{1,0:T(8,128)(2,1)S(1)}, u32[]{:S(2)}, u32[]{:S(2)}) collective-permute-start(bf16[80,1792]{1,0:T(8,128)(2,1)S(1)} %shard_map.126.refs_31_), channel_id=1, source_target_pairs={{0,7},{1,6},{2,5},{3,4},{4,3},{5,2},{6,1},{7,0},{8,15},{9,14},{10,... | collective-permute-start | bytes 860168 | tf_op jit(solution)/shard_map/ppermute | solution.py:327
  147.8 10.4 %shard_map.127 = (bf16[1024,1792]{1,0:T(8,128)(2,1)}, bf16[1024,1792]{1,0:T(8,128)(2,1)}, f32[8,128]{1,0:T(8,128)S(1)}) custom-call(s32[1]{0:T(128)} %bitcast.3.refs_0_, bf16[160,768]{1,0:T(8,128)(2,1)S(1)} %shard_map.108.refs_5_.refs_1_, bf16[160,768]{1,0:T(8,128)(2,1)S(1)} %collective-permute-done.8.refs_2_, ...), custom_call_target="tpu_custom_call" | custom-call | tf_op jit(solution)/shard_map/pallas_call | solution.py:39
  158.2 2.9 %shard_map.128.refs_4_ = bf16[512,1792]{1,0:T(8,128)(2,1)S(1)} custom-call(s32[1]{0:T(128)} %bitcast.refs_0_, s32[1,512]{1,0:T(1,128)S(1)} %copy-done.12, bf16[80,1792]{1,0:T(8,128)(2,1)S(1)} %get-tuple-element.56.refs_4_.refs_2_, bf16[80,1792]{1,0:T(8,128)(2,1)S(1)} %collective-permute-done.32.refs_4_.refs_3_, ...), custom_call_target="tpu_custom_call" | custom-call | tf_op jit(solution)/shard_map/pallas_call | solution.py:39
  161.2 10.8 %collective-permute-done.41.refs_3_ = bf16[80,1792]{1,0:T(8,128)(2,1)S(1)} collective-permute-done((bf16[80,1792]{1,0:T(8,128)(2,1)S(1)}, bf16[80,1792]{1,0:T(8,128)(2,1)S(1)}, u32[]{:S(2)}, u32[]{:S(2)}) %collective-permute-start.41) | collective-permute-done | bytes 286752 | tf_op jit(solution)/shard_map/ppermute | solution.py:327
  172.0 5.9 %collective-permute-done.37.refs_2_ = bf16[80,1792]{1,0:T(8,128)(2,1)S(1)} collective-permute-done((bf16[80,1792]{1,0:T(8,128)(2,1)S(1)}, bf16[80,1792]{1,0:T(8,128)(2,1)S(1)}, u32[]{:S(2)}, u32[]{:S(2)}) %collective-permute-start.37) | collective-permute-done | bytes 286752 | tf_op jit(solution)/shard_map/ppermute | solution.py:327
  177.8 4.1 %shard_map.129 = bf16[512,1792]{1,0:T(8,128)(2,1)} custom-call(s32[1]{0:T(128)} %bitcast.refs_0_, s32[1,512]{1,0:T(1,128)S(1)} %copy-done.12, bf16[80,1792]{1,0:T(8,128)(2,1)S(1)} %collective-permute-done.37.refs_2_, bf16[80,1792]{1,0:T(8,128)(2,1)S(1)} %collective-permute-done.41.refs_3_, bf16[512,1792]{1,0:T(8,128)(2,1)S(1)} %shard_map.128.refs_4_), custom_call_target="tpu_custom_call" | custom-call | tf_op jit(solution)/shard_map/pallas_call | solution.py:39
  (99 shorter events, 25.2 us)
Async XLA Ops:
  7.8 7.7 %collective-permute-start.1 = (bf16[80,3584]{1,0:T(8,128)(2,1)}, bf16[80,3584]{1,0:T(8,128)(2,1)S(1)}, u32[]{:S(2)}, u32[]{:S(2)}) collective-permute-start(bf16[80,3584]{1,0:T(8,128)(2,1)} %get-tuple-element.45), channel_id=1, source_target_pairs={{0,1},{1,0},{2,3},{3,2},{4,5},{5,4},{6,7},{7,6},{8,9},{9,8},{10,11... | collective-permute-start | bytes 1720328 | tf_op jit(solution)/shard_map/ppermute | solution.py:327
  8.5 27.6 %collective-permute-start = (bf16[80,3584]{1,0:T(8,128)(2,1)}, bf16[80,3584]{1,0:T(8,128)(2,1)S(1)}, u32[]{:S(2)}, u32[]{:S(2)}) collective-permute-start(bf16[80,3584]{1,0:T(8,128)(2,1)} %get-tuple-element.42.refs_5_), channel_id=1, source_target_pairs={{0,4},{1,5},{2,6},{3,7},{4,0},{5,1},{6,2},{7,3},{8,12},{9,13},{10,... | collective-permute-start | bytes 1720328 | tf_op jit(solution)/shard_map/ppermute | solution.py:327
  23.8 18.5 %copy-start.2 = (bf16[1,1792,1024]{2,1,0:T(8,128)(2,1)S(1)}, bf16[1,1792,1024]{2,1,0:T(8,128)(2,1)}, u32[]{:S(2)}) copy-start(bf16[1,1792,1024]{2,1,0:T(8,128)(2,1)} %param.13) | copy-start | bytes 11010052
  23.8 15.6 %collective-permute-start.2 = (bf16[160,768]{1,0:T(8,128)(2,1)S(1)}, bf16[160,768]{1,0:T(8,128)(2,1)S(1)}, u32[]{:S(2)}, u32[]{:S(2)}) collective-permute-start(bf16[160,768]{1,0:T(8,128)(2,1)S(1)} %get-tuple-element.48), channel_id=1, source_target_pairs={{0,8},{8,0},{16,24},{24,16},{1,9},{9,1},{17,25},{25,17},{2,10},{10... | collective-permute-start | bytes 737288 | tf_op jit(solution)/shard_map/ppermute | solution.py:330
  25.1 14.3 %collective-permute-start.3 = (bf16[160,768]{1,0:T(8,128)(2,1)S(1)}, bf16[160,768]{1,0:T(8,128)(2,1)S(1)}, u32[]{:S(2)}, u32[]{:S(2)}) collective-permute-start(bf16[160,768]{1,0:T(8,128)(2,1)S(1)} %get-tuple-element.49), channel_id=1, source_target_pairs={{0,16},{8,24},{16,0},{24,8},{1,17},{9,25},{17,1},{25,9},{2,18},{10... | collective-permute-start | bytes 737288 | tf_op jit(solution)/shard_map/ppermute | solution.py:330
  26.3 13.0 %collective-permute-start.4 = (bf16[160,768]{1,0:T(8,128)(2,1)S(1)}, bf16[160,768]{1,0:T(8,128)(2,1)S(1)}, u32[]{:S(2)}, u32[]{:S(2)}) collective-permute-start(bf16[160,768]{1,0:T(8,128)(2,1)S(1)} %get-tuple-element.50), channel_id=1, source_target_pairs={{0,24},{8,16},{16,8},{24,0},{1,25},{9,17},{17,9},{25,1},{2,26},{10... | collective-permute-start | bytes 737288 | tf_op jit(solution)/shard_map/ppermute | solution.py:330
  36.0 24.6 %collective-permute-start.12 = (bf16[80,3584]{1,0:T(8,128)(2,1)S(1)}, bf16[80,3584]{1,0:T(8,128)(2,1)S(1)}, u32[]{:S(2)}, u32[]{:S(2)}) collective-permute-start(bf16[80,3584]{1,0:T(8,128)(2,1)S(1)} %shard_map.107.refs_4_), channel_id=1, source_target_pairs={{0,2},{1,3},{2,0},{3,1},{4,6},{5,7},{6,4},{7,5},{8,10},{9,11},{10,... | collective-permute-start | bytes 1720328 | tf_op jit(solution)/shard_map/ppermute | solution.py:327
  36.8 27.8 %collective-permute-start.11 = (bf16[80,3584]{1,0:T(8,128)(2,1)S(1)}, bf16[80,3584]{1,0:T(8,128)(2,1)S(1)}, u32[]{:S(2)}, u32[]{:S(2)}) collective-permute-start(bf16[80,3584]{1,0:T(8,128)(2,1)S(1)} %shard_map.106.refs_1_), channel_id=1, source_target_pairs={{0,5},{1,4},{2,7},{3,6},{4,1},{5,0},{6,3},{7,2},{8,13},{9,12},{10,... | collective-permute-start | bytes 1720328 | tf_op jit(solution)/shard_map/ppermute | solution.py:327
  39.6 8.5 %collective-permute-start.10 = (bf16[160,768]{1,0:T(8,128)(2,1)S(1)}, bf16[160,768]{1,0:T(8,128)(2,1)S(1)}, u32[]{:S(2)}, u32[]{:S(2)}) collective-permute-start(bf16[160,768]{1,0:T(8,128)(2,1)S(1)} %shard_map.108.refs_5_.refs_1_), channel_id=1, source_target_pairs={{0,24},{8,16},{16,8},{24,0},{1,25},{9,17},{17,9},{25,1},{2,26},{10... | collective-permute-start | bytes 737288 | tf_op jit(solution)/shard_map/ppermute | solution.py:330
  41.8 11.9 %collective-permute-start.9 = (bf16[160,768]{1,0:T(8,128)(2,1)S(1)}, bf16[160,768]{1,0:T(8,128)(2,1)S(1)}, u32[]{:S(2)}, u32[]{:S(2)}) collective-permute-start(bf16[160,768]{1,0:T(8,128)(2,1)S(1)} %shard_map.108.refs_5_.refs_1_), channel_id=1, source_target_pairs={{0,16},{8,24},{16,0},{24,8},{1,17},{9,25},{17,1},{25,9},{2,18},{10... | collective-permute-start | bytes 737288 | tf_op jit(solution)/shard_map/ppermute | solution.py:330
  42.0 12.9 %collective-permute-start.8 = (bf16[160,768]{1,0:T(8,128)(2,1)S(1)}, bf16[160,768]{1,0:T(8,128)(2,1)S(1)}, u32[]{:S(2)}, u32[]{:S(2)}) collective-permute-start(bf16[160,768]{1,0:T(8,128)(2,1)S(1)} %shard_map.108.refs_5_.refs_1_), channel_id=1, source_target_pairs={{0,8},{8,0},{16,24},{24,16},{1,9},{9,1},{17,25},{25,17},{2,10},{10... | collective-permute-start | bytes 737288 | tf_op jit(solution)/shard_map/ppermute | solution.py:330
  48.1 11.7 %collective-permute-start.5 = (bf16[80,768]{1,0:T(8,128)(2,1)S(1)}, bf16[80,768]{1,0:T(8,128)(2,1)S(1)}, u32[]{:S(2)}, u32[]{:S(2)}) collective-permute-start(bf16[80,768]{1,0:T(8,128)(2,1)S(1)} %get-tuple-element.53), channel_id=1, source_target_pairs={{0,8},{8,0},{16,24},{24,16},{1,9},{9,1},{17,25},{25,17},{2,10},{10... | collective-permute-start | bytes 368648 | tf_op jit(solution)/shard_map/ppermute | solution.py:330
  53.7 6.1 %collective-permute-start.6 = (bf16[80,768]{1,0:T(8,128)(2,1)S(1)}, bf16[80,768]{1,0:T(8,128)(2,1)S(1)}, u32[]{:S(2)}, u32[]{:S(2)}) collective-permute-start(bf16[80,768]{1,0:T(8,128)(2,1)S(1)} %get-tuple-element.54), channel_id=1, source_target_pairs={{0,16},{8,24},{16,0},{24,8},{1,17},{9,25},{17,1},{25,9},{2,18},{10... | collective-permute-start | bytes 368648 | tf_op jit(solution)/shard_map/ppermute | solution.py:330
  54.9 5.1 %collective-permute-start.7 = (bf16[80,768]{1,0:T(8,128)(2,1)S(1)}, bf16[80,768]{1,0:T(8,128)(2,1)S(1)}, u32[]{:S(2)}, u32[]{:S(2)}) collective-permute-start(bf16[80,768]{1,0:T(8,128)(2,1)S(1)} %get-tuple-element.55), channel_id=1, source_target_pairs={{0,24},{8,16},{16,8},{24,0},{1,25},{9,17},{17,9},{25,1},{2,26},{10... | collective-permute-start | bytes 368648 | tf_op jit(solution)/shard_map/ppermute | solution.py:330
  59.8 10.8 %copy-start.4 = (bf16[1,1024,1792]{2,1,0:T(8,128)(2,1)S(1)}, bf16[1,1024,1792]{2,1,0:T(8,128)(2,1)}, u32[]{:S(2)}) copy-start(bf16[1,1024,1792]{2,1,0:T(8,128)(2,1)} %param.14) | copy-start | bytes 11010052
  64.7 26.6 %collective-permute-start.14 = (bf16[80,3584]{1,0:T(8,128)(2,1)S(1)}, bf16[80,3584]{1,0:T(8,128)(2,1)S(1)}, u32[]{:S(2)}, u32[]{:S(2)}) collective-permute-start(bf16[80,3584]{1,0:T(8,128)(2,1)S(1)} %shard_map.113.refs_6_), channel_id=1, source_target_pairs={{0,3},{1,2},{2,1},{3,0},{4,7},{5,6},{6,5},{7,4},{8,11},{9,10},{10,... | collective-permute-start | bytes 1720328 | tf_op jit(solution)/shard_map/ppermute | solution.py:327
  64.7 28.6 %collective-permute-start.13 = (bf16[80,3584]{1,0:T(8,128)(2,1)S(1)}, bf16[80,3584]{1,0:T(8,128)(2,1)S(1)}, u32[]{:S(2)}, u32[]{:S(2)}) collective-permute-start(bf16[80,3584]{1,0:T(8,128)(2,1)S(1)} %shard_map.112.refs_1_), channel_id=1, source_target_pairs={{0,6},{1,7},{2,4},{3,5},{4,2},{5,3},{6,0},{7,1},{8,14},{9,15},{10,... | collective-permute-start | bytes 1720328 | tf_op jit(solution)/shard_map/ppermute | solution.py:327
  67.9 6.9 %collective-permute-start.20 = (bf16[80,768]{1,0:T(8,128)(2,1)S(1)}, bf16[80,768]{1,0:T(8,128)(2,1)S(1)}, u32[]{:S(2)}, u32[]{:S(2)}) collective-permute-start(bf16[80,768]{1,0:T(8,128)(2,1)S(1)} %shard_map.111.refs_1_.refs_5_), channel_id=1, source_target_pairs={{0,24},{8,16},{16,8},{24,0},{1,25},{9,17},{17,9},{25,1},{2,26},{10... | collective-permute-start | bytes 368648 | tf_op jit(solution)/shard_map/ppermute | solution.py:330
  70.1 6.6 %collective-permute-start.19 = (bf16[80,768]{1,0:T(8,128)(2,1)S(1)}, bf16[80,768]{1,0:T(8,128)(2,1)S(1)}, u32[]{:S(2)}, u32[]{:S(2)}) collective-permute-start(bf16[80,768]{1,0:T(8,128)(2,1)S(1)} %shard_map.111.refs_1_.refs_5_), channel_id=1, source_target_pairs={{0,16},{8,24},{16,0},{24,8},{1,17},{9,25},{17,1},{25,9},{2,18},{10... | collective-permute-start | bytes 368648 | tf_op jit(solution)/shard_map/ppermute | solution.py:330
  70.3 7.6 %collective-permute-start.18 = (bf16[80,768]{1,0:T(8,128)(2,1)S(1)}, bf16[80,768]{1,0:T(8,128)(2,1)S(1)}, u32[]{:S(2)}, u32[]{:S(2)}) collective-permute-start(bf16[80,768]{1,0:T(8,128)(2,1)S(1)} %shard_map.111.refs_1_.refs_5_), channel_id=1, source_target_pairs={{0,8},{8,0},{16,24},{24,16},{1,9},{9,1},{17,25},{25,17},{2,10},{10... | collective-permute-start | bytes 368648 | tf_op jit(solution)/shard_map/ppermute | solution.py:330
  74.8 7.6 %collective-permute-start.15 = (bf16[160,768]{1,0:T(8,128)(2,1)S(1)}, bf16[160,768]{1,0:T(8,128)(2,1)S(1)}, u32[]{:S(2)}, u32[]{:S(2)}) collective-permute-start(bf16[160,768]{1,0:T(8,128)(2,1)S(1)} %get-tuple-element.60), channel_id=1, source_target_pairs={{0,8},{8,0},{16,24},{24,16},{1,9},{9,1},{17,25},{25,17},{2,10},{10... | collective-permute-start | bytes 737288 | tf_op jit(solution)/shard_map/ppermute | solution.py:330
  76.7 10.8 %collective-permute-start.16 = (bf16[160,768]{1,0:T(8,128)(2,1)S(1)}, bf16[160,768]{1,0:T(8,128)(2,1)S(1)}, u32[]{:S(2)}, u32[]{:S(2)}) collective-permute-start(bf16[160,768]{1,0:T(8,128)(2,1)S(1)} %get-tuple-element.61), channel_id=1, source_target_pairs={{0,16},{8,24},{16,0},{24,8},{1,17},{9,25},{17,1},{25,9},{2,18},{10... | collective-permute-start | bytes 737288 | tf_op jit(solution)/shard_map/ppermute | solution.py:330
  78.0 9.5 %collective-permute-start.17 = (bf16[160,768]{1,0:T(8,128)(2,1)S(1)}, bf16[160,768]{1,0:T(8,128)(2,1)S(1)}, u32[]{:S(2)}, u32[]{:S(2)}) collective-permute-start(bf16[160,768]{1,0:T(8,128)(2,1)S(1)} %get-tuple-element.62), channel_id=1, source_target_pairs={{0,24},{8,16},{16,8},{24,0},{1,25},{9,17},{17,9},{25,1},{2,26},{10... | collective-permute-start | bytes 737288 | tf_op jit(solution)/shard_map/ppermute | solution.py:330
  87.7 13.3 %collective-permute-start.26 = (bf16[160,768]{1,0:T(8,128)(2,1)S(1)}, bf16[160,768]{1,0:T(8,128)(2,1)S(1)}, u32[]{:S(2)}, u32[]{:S(2)}) collective-permute-start(bf16[160,768]{1,0:T(8,128)(2,1)S(1)} %shard_map.116.refs_1_.refs_9_), channel_id=1, source_target_pairs={{0,24},{8,16},{16,8},{24,0},{1,25},{9,17},{17,9},{25,1},{2,26},{10... | collective-permute-start | bytes 737288 | tf_op jit(solution)/shard_map/ppermute | solution.py:330
  88.8 13.4 %collective-permute-start.25 = (bf16[160,768]{1,0:T(8,128)(2,1)S(1)}, bf16[160,768]{1,0:T(8,128)(2,1)S(1)}, u32[]{:S(2)}, u32[]{:S(2)}) collective-permute-start(bf16[160,768]{1,0:T(8,128)(2,1)S(1)} %shard_map.116.refs_1_.refs_9_), channel_id=1, source_target_pairs={{0,16},{8,24},{16,0},{24,8},{1,17},{9,25},{17,1},{25,9},{2,18},{10... | collective-permute-start | bytes 737288 | tf_op jit(solution)/shard_map/ppermute | solution.py:330
  90.2 12.3 %collective-permute-start.24 = (bf16[160,768]{1,0:T(8,128)(2,1)S(1)}, bf16[160,768]{1,0:T(8,128)(2,1)S(1)}, u32[]{:S(2)}, u32[]{:S(2)}) collective-permute-start(bf16[160,768]{1,0:T(8,128)(2,1)S(1)} %shard_map.116.refs_1_.refs_9_), channel_id=1, source_target_pairs={{0,8},{8,0},{16,24},{24,16},{1,9},{9,1},{17,25},{25,17},{2,10},{10... | collective-permute-start | bytes 737288 | tf_op jit(solution)/shard_map/ppermute | solution.py:330
  93.3 28.0 %collective-permute-start.30 = (bf16[80,3584]{1,0:T(8,128)(2,1)S(1)}, bf16[80,3584]{1,0:T(8,128)(2,1)S(1)}, u32[]{:S(2)}, u32[]{:S(2)}) collective-permute-start(bf16[80,3584]{1,0:T(8,128)(2,1)S(1)} %shard_map.117.refs_6_), channel_id=1, source_target_pairs={{0,7},{1,6},{2,5},{3,4},{4,3},{5,2},{6,1},{7,0},{8,15},{9,14},{10,... | collective-permute-start | bytes 1720328 | tf_op jit(solution)/shard_map/ppermute | solution.py:327
  99.7 8.1 %collective-permute-start.21 = (bf16[160,768]{1,0:T(8,128)(2,1)S(1)}, bf16[160,768]{1,0:T(8,128)(2,1)S(1)}, u32[]{:S(2)}, u32[]{:S(2)}) collective-permute-start(bf16[160,768]{1,0:T(8,128)(2,1)S(1)} %get-tuple-element.64), channel_id=1, source_target_pairs={{0,8},{8,0},{16,24},{24,16},{1,9},{9,1},{17,25},{25,17},{2,10},{10... | collective-permute-start | bytes 737288 | tf_op jit(solution)/shard_map/ppermute | solution.py:330
  101.0 7.7 %collective-permute-start.22 = (bf16[160,768]{1,0:T(8,128)(2,1)S(1)}, bf16[160,768]{1,0:T(8,128)(2,1)S(1)}, u32[]{:S(2)}, u32[]{:S(2)}) collective-permute-start(bf16[160,768]{1,0:T(8,128)(2,1)S(1)} %get-tuple-element.65), channel_id=1, source_target_pairs={{0,16},{8,24},{16,0},{24,8},{1,17},{9,25},{17,1},{25,9},{2,18},{10... | collective-permute-start | bytes 737288 | tf_op jit(solution)/shard_map/ppermute | solution.py:330
  102.2 11.7 %collective-permute-start.23 = (bf16[160,768]{1,0:T(8,128)(2,1)S(1)}, bf16[160,768]{1,0:T(8,128)(2,1)S(1)}, u32[]{:S(2)}, u32[]{:S(2)}) collective-permute-start(bf16[160,768]{1,0:T(8,128)(2,1)S(1)} %get-tuple-element.66), channel_id=1, source_target_pairs={{0,24},{8,16},{16,8},{24,0},{1,25},{9,17},{17,9},{25,1},{2,26},{10... | collective-permute-start | bytes 737288 | tf_op jit(solution)/shard_map/ppermute | solution.py:330
  102.5 14.1 %collective-permute-start.32 = (bf16[80,1792]{1,0:T(8,128)(2,1)S(1)}, bf16[80,1792]{1,0:T(8,128)(2,1)S(1)}, u32[]{:S(2)}, u32[]{:S(2)}) collective-permute-start(bf16[80,1792]{1,0:T(8,128)(2,1)S(1)} %get-tuple-element.69), channel_id=1, source_target_pairs={{0,1},{1,0},{2,3},{3,2},{4,5},{5,4},{6,7},{7,6},{8,9},{9,8},{10,11... | collective-permute-start | bytes 860168 | tf_op jit(solution)/shard_map/ppermute | solution.py:327
  107.8 9.0 %collective-permute-start.31 = (bf16[80,1792]{1,0:T(8,128)(2,1)S(1)}, bf16[80,1792]{1,0:T(8,128)(2,1)S(1)}, u32[]{:S(2)}, u32[]{:S(2)}) collective-permute-start(bf16[80,1792]{1,0:T(8,128)(2,1)S(1)} %get-tuple-element.68), channel_id=1, source_target_pairs={{0,2},{1,3},{2,0},{3,1},{4,6},{5,7},{6,4},{7,5},{8,10},{9,11},{10,... | collective-permute-start | bytes 860168 | tf_op jit(solution)/shard_map/ppermute | solution.py:327
  114.1 12.5 %collective-permute-start.29 = (bf16[160,768]{1,0:T(8,128)(2,1)S(1)}, bf16[160,768]{1,0:T(8,128)(2,1)S(1)}, u32[]{:S(2)}, u32[]{:S(2)}) collective-permute-start(bf16[160,768]{1,0:T(8,128)(2,1)S(1)} %shard_map.120.refs_1_.refs_13_), channel_id=1, source_target_pairs={{0,24},{8,16},{16,8},{24,0},{1,25},{9,17},{17,9},{25,1},{2,26},{10... | collective-permute-start | bytes 737288 | tf_op jit(solution)/shard_map/ppermute | solution.py:330
  115.4 12.9 %collective-permute-start.28 = (bf16[160,768]{1,0:T(8,128)(2,1)S(1)}, bf16[160,768]{1,0:T(8,128)(2,1)S(1)}, u32[]{:S(2)}, u32[]{:S(2)}) collective-permute-start(bf16[160,768]{1,0:T(8,128)(2,1)S(1)} %shard_map.120.refs_1_.refs_13_), channel_id=1, source_target_pairs={{0,16},{8,24},{16,0},{24,8},{1,17},{9,25},{17,1},{25,9},{2,18},{10... | collective-permute-start | bytes 737288 | tf_op jit(solution)/shard_map/ppermute | solution.py:330
  116.5 12.9 %collective-permute-start.27 = (bf16[160,768]{1,0:T(8,128)(2,1)S(1)}, bf16[160,768]{1,0:T(8,128)(2,1)S(1)}, u32[]{:S(2)}, u32[]{:S(2)}) collective-permute-start(bf16[160,768]{1,0:T(8,128)(2,1)S(1)} %shard_map.120.refs_1_.refs_13_), channel_id=1, source_target_pairs={{0,8},{8,0},{16,24},{24,16},{1,9},{9,1},{17,25},{25,17},{2,10},{10... | collective-permute-start | bytes 737288 | tf_op jit(solution)/shard_map/ppermute | solution.py:330
  121.3 19.6 %collective-permute-start.36 = (bf16[80,1792]{1,0:T(8,128)(2,1)S(1)}, bf16[80,1792]{1,0:T(8,128)(2,1)S(1)}, u32[]{:S(2)}, u32[]{:S(2)}) collective-permute-start(bf16[80,1792]{1,0:T(8,128)(2,1)S(1)} %shard_map.121.refs_5_), channel_id=1, source_target_pairs={{0,4},{1,5},{2,6},{3,7},{4,0},{5,1},{6,2},{7,3},{8,12},{9,13},{10,... | collective-permute-start | bytes 860168 | tf_op jit(solution)/shard_map/ppermute | solution.py:327
  125.3 7.8 %collective-permute-start.33 = (bf16[80,768]{1,0:T(8,128)(2,1)S(1)}, bf16[80,768]{1,0:T(8,128)(2,1)S(1)}, u32[]{:S(2)}, u32[]{:S(2)}) collective-permute-start(bf16[80,768]{1,0:T(8,128)(2,1)S(1)} %get-tuple-element.72), channel_id=1, source_target_pairs={{0,8},{8,0},{16,24},{24,16},{1,9},{9,1},{17,25},{25,17},{2,10},{10... | collective-permute-start | bytes 368648 | tf_op jit(solution)/shard_map/ppermute | solution.py:330
  126.6 6.5 %collective-permute-start.34 = (bf16[80,768]{1,0:T(8,128)(2,1)S(1)}, bf16[80,768]{1,0:T(8,128)(2,1)S(1)}, u32[]{:S(2)}, u32[]{:S(2)}) collective-permute-start(bf16[80,768]{1,0:T(8,128)(2,1)S(1)} %get-tuple-element.73), channel_id=1, source_target_pairs={{0,16},{8,24},{16,0},{24,8},{1,17},{9,25},{17,1},{25,9},{2,18},{10... | collective-permute-start | bytes 368648 | tf_op jit(solution)/shard_map/ppermute | solution.py:330
  128.2 5.3 %collective-permute-start.35 = (bf16[80,768]{1,0:T(8,128)(2,1)S(1)}, bf16[80,768]{1,0:T(8,128)(2,1)S(1)}, u32[]{:S(2)}, u32[]{:S(2)}) collective-permute-start(bf16[80,768]{1,0:T(8,128)(2,1)S(1)} %get-tuple-element.74), channel_id=1, source_target_pairs={{0,24},{8,16},{16,8},{24,0},{1,25},{9,17},{17,9},{25,1},{2,26},{10... | collective-permute-start | bytes 368648 | tf_op jit(solution)/shard_map/ppermute | solution.py:330
  133.7 7.4 %collective-permute-start.40 = (bf16[80,768]{1,0:T(8,128)(2,1)S(1)}, bf16[80,768]{1,0:T(8,128)(2,1)S(1)}, u32[]{:S(2)}, u32[]{:S(2)}) collective-permute-start(bf16[80,768]{1,0:T(8,128)(2,1)S(1)} %shard_map.124.refs_1_.refs_17_), channel_id=1, source_target_pairs={{0,24},{8,16},{16,8},{24,0},{1,25},{9,17},{17,9},{25,1},{2,26},{10... | collective-permute-start | bytes 368648 | tf_op jit(solution)/shard_map/ppermute | solution.py:330
  134.9 6.9 %collective-permute-start.39 = (bf16[80,768]{1,0:T(8,128)(2,1)S(1)}, bf16[80,768]{1,0:T(8,128)(2,1)S(1)}, u32[]{:S(2)}, u32[]{:S(2)}) collective-permute-start(bf16[80,768]{1,0:T(8,128)(2,1)S(1)} %shard_map.124.refs_1_.refs_17_), channel_id=1, source_target_pairs={{0,16},{8,24},{16,0},{24,8},{1,17},{9,25},{17,1},{25,9},{2,18},{10... | collective-permute-start | bytes 368648 | tf_op jit(solution)/shard_map/ppermute | solution.py:330
  136.0 5.7 %collective-permute-start.38 = (bf16[80,768]{1,0:T(8,128)(2,1)S(1)}, bf16[80,768]{1,0:T(8,128)(2,1)S(1)}, u32[]{:S(2)}, u32[]{:S(2)}) collective-permute-start(bf16[80,768]{1,0:T(8,128)(2,1)S(1)} %shard_map.124.refs_1_.refs_17_), channel_id=1, source_target_pairs={{0,8},{8,0},{16,24},{24,16},{1,9},{9,1},{17,25},{25,17},{2,10},{10... | collective-permute-start | bytes 368648 | tf_op jit(solution)/shard_map/ppermute | solution.py:330
  136.4 21.8 %collective-permute-start.42 = (bf16[80,1792]{1,0:T(8,128)(2,1)S(1)}, bf16[80,1792]{1,0:T(8,128)(2,1)S(1)}, u32[]{:S(2)}, u32[]{:S(2)}) collective-permute-start(bf16[80,1792]{1,0:T(8,128)(2,1)S(1)} %get-tuple-element.67.refs_4_), channel_id=1, source_target_pairs={{0,5},{1,4},{2,7},{3,6},{4,1},{5,0},{6,3},{7,2},{8,13},{9,12},{10,... | collective-permute-start | bytes 860168 | tf_op jit(solution)/shard_map/ppermute | solution.py:327
  140.9 17.3 %collective-permute-start.43 = (bf16[80,1792]{1,0:T(8,128)(2,1)S(1)}, bf16[80,1792]{1,0:T(8,128)(2,1)S(1)}, u32[]{:S(2)}, u32[]{:S(2)}) collective-permute-start(bf16[80,1792]{1,0:T(8,128)(2,1)S(1)} %get-tuple-element.75), channel_id=1, source_target_pairs={{0,3},{1,2},{2,1},{3,0},{4,7},{5,6},{6,5},{7,4},{8,11},{9,10},{10,... | collective-permute-start | bytes 860168 | tf_op jit(solution)/shard_map/ppermute | solution.py:327
  141.1 6.7 %copy-start.9 = (bf16[1,1024,1792]{2,1,0:T(8,128)(2,1)S(1)}, bf16[1,1024,1792]{2,1,0:T(8,128)(2,1)}, u32[]{:S(2)}) copy-start(bf16[1,1024,1792]{2,1,0:T(8,128)(2,1)} %param.15) | copy-start | bytes 11010052
  145.1 26.9 %collective-permute-start.41 = (bf16[80,1792]{1,0:T(8,128)(2,1)S(1)}, bf16[80,1792]{1,0:T(8,128)(2,1)S(1)}, u32[]{:S(2)}, u32[]{:S(2)}) collective-permute-start(bf16[80,1792]{1,0:T(8,128)(2,1)S(1)} %shard_map.126.refs_31_), channel_id=1, source_target_pairs={{0,7},{1,6},{2,5},{3,4},{4,3},{5,2},{6,1},{7,0},{8,15},{9,14},{10,... | collective-permute-start | bytes 860168 | tf_op jit(solution)/shard_map/ppermute | solution.py:327
  147.3 30.5 %collective-permute-start.37 = (bf16[80,1792]{1,0:T(8,128)(2,1)S(1)}, bf16[80,1792]{1,0:T(8,128)(2,1)S(1)}, u32[]{:S(2)}, u32[]{:S(2)}) collective-permute-start(bf16[80,1792]{1,0:T(8,128)(2,1)S(1)} %shard_map.125.refs_7_), channel_id=1, source_target_pairs={{0,6},{1,7},{2,4},{3,5},{4,2},{5,3},{6,0},{7,1},{8,14},{9,15},{10,... | collective-permute-start | bytes 860168 | tf_op jit(solution)/shard_map/ppermute | solution.py:327
  147.8 10.4 %copy-start.12 = (s32[1,512]{1,0:T(1,128)S(1)}, s32[1,512]{1,0:T(1,128)}, u32[]{:S(2)}) copy-start(s32[1,512]{1,0:T(1,128)} %copy-done.10) | copy-start | bytes 6148
  (12 other events, 22.5 us)

commit v4 on v3

--- a/solution.py
+++ b/solution.py
@@ -14,6 +14,7 @@
 
 TILE = 256
 VMEM_BYTES = 24 * 1024 * 1024
+LEAD_BYTES = 60 * 1024 * 1024
 
 bf16 = jnp.bfloat16
 f32 = jnp.float32
@@ -34,7 +35,7 @@
     return run
 
 
-def call(body, operands, deps, out_shape, in_specs, out_specs, grid=(), scalars=0, scratch=(), aliases=None):
+def call(body, operands, deps, out_shape, in_specs, out_specs, grid=(), scalars=0, scratch=(), aliases=None, limit=VMEM_BYTES):
     any_spec = pl.BlockSpec(memory_space=pl.ANY)
     return pl.pallas_call(
         skipping(body, len(operands), len(deps)),
@@ -47,7 +48,7 @@
             scratch_shapes=list(scratch),
         ),
         input_output_aliases=aliases or {},
-        compiler_params=pltpu.CompilerParams(vmem_limit_bytes=VMEM_BYTES),
+        compiler_params=pltpu.CompilerParams(vmem_limit_bytes=limit),
         cost_estimate=pl.CostEstimate(flops=0, bytes_accessed=0, transcendentals=0),
     )(*operands, *deps)
 
@@ -71,48 +72,69 @@
     )
 
 
-def dispatch_body(n, cap, offs, first, *refs):
-    if first:
-        me_ref, ids_ref, codes_ref, x_ref, g_ref, target_ref, *outs = refs
-        ids = ids_ref[...]
-        t = ids.shape[1]
-        hot = (lax.broadcasted_iota(jnp.int32, (n, t), 0) == ids).astype(f32)
-        before = (
-            lax.broadcasted_iota(jnp.int32, (t, t), 0) < lax.broadcasted_iota(jnp.int32, (t, t), 1)
-        ).astype(f32)
-        counts = dot(hot.astype(bf16), before.astype(bf16))
-        rank = jnp.sum(hot * counts, axis=0, keepdims=True).astype(jnp.int32)
-        target = ids * cap + rank
-        target_ref[...] = target
-    else:
-        me_ref, tgt_ref, codes_ref, x_ref, g_ref, *outs = refs
-        target = tgt_ref[...]
-    t, s = x_ref.shape
-    scale = codes_ref[...].astype(f32) / 256.0
-    slots = lax.broadcasted_iota(jnp.int32, (cap, t), 0)
-    hits = [slots + (me_ref[0] ^ k) * cap == target for k in offs]
+def picks(cap, offs, me, target, scale):
+    slots = lax.broadcasted_iota(jnp.int32, (cap, target.shape[1]), 0)
+    hits = [slots + (me ^ k) * cap == target for k in offs]
     pick = jnp.concatenate([jnp.where(h, 1.0, 0.0).astype(bf16) for h in hits], axis=0)
     scaled = jnp.concatenate([jnp.where(h, scale, 0.0).astype(bf16) for h in hits], axis=0)
-    for c in range(0, s, TILE):
-        for left, ref, base in ((pick, x_ref, 0), (scaled, g_ref, s)):
-            rows = dot(left, ref[:, c : c + TILE]).astype(bf16)
-            for i, out in enumerate(outs):
-                out[:, base + c : base + c + TILE] = rows[i * cap : (i + 1) * cap]
-
-
-def dispatch(n, cap, offs, me, marks, codes, x, g, first, deps):
+    return pick, scaled
+
+
+def dispatch_body(n, cap, offs, cuts, me_ref, ids_ref, codes_ref, x_ref, g_ref, target_ref, *refs):
+    *outs, ids_v, codes_v, x_v, g_v, sems = refs
+    small = [
+        pltpu.make_async_copy(ids_ref, ids_v, sems.at[0]),
+        pltpu.make_async_copy(codes_ref, codes_v, sems.at[1]),
+    ]
+    large = []
+    for c0, c1 in cuts:
+        for ref, buf in ((x_ref, x_v), (g_ref, g_v)):
+            large.append(pltpu.make_async_copy(ref.at[:, c0:c1], buf.at[:, c0:c1], sems.at[2 + len(large)]))
+    for copy in small + large:
+        copy.start()
+    small[0].wait()
+    ids = ids_v[...]
+    t, s = x_v.shape
+    hot = (lax.broadcasted_iota(jnp.int32, (n, t), 0) == ids).astype(f32)
+    before = (
+        lax.broadcasted_iota(jnp.int32, (t, t), 0) < lax.broadcasted_iota(jnp.int32, (t, t), 1)
+    ).astype(f32)
+    counts = dot(hot.astype(bf16), before.astype(bf16))
+    rank = jnp.sum(hot * counts, axis=0, keepdims=True).astype(jnp.int32)
+    target = ids * cap + rank
+    target_ref[...] = target
+    small[1].wait()
+    pick, scaled = picks(cap, offs, me_ref[0], target, codes_v[...].astype(f32) / 256.0)
+    for j, (c0, c1) in enumerate(cuts):
+        for which, (left, buf, base) in enumerate(((pick, x_v, 0), (scaled, g_v, s))):
+            large[2 * j + which].wait()
+            for c in range(c0, c1, TILE):
+                rows = dot(left, buf[:, c : c + TILE]).astype(bf16)
+                for i, out in enumerate(outs):
+                    out[:, base + c : base + c + TILE] = rows[i * cap : (i + 1) * cap]
+
+
+def dispatch(n, cap, offs, me, ids, codes, x, g, deps):
     t, s = x.shape
-    out_shape = [jax.ShapeDtypeStruct((cap, 2 * s), bf16) for _ in offs]
-    if first:
-        out_shape = [jax.ShapeDtypeStruct((1, t), jnp.int32)] + out_shape
-    vmem = pl.BlockSpec(memory_space=pltpu.VMEM)
-    return call(
-        functools.partial(dispatch_body, n, cap, offs, first),
-        [me, marks, codes, x, g],
+    half = s // (2 * TILE) * TILE
+    cuts = [(0, half), (half, s)]
+    out_shape = [jax.ShapeDtypeStruct((1, t), jnp.int32)] + [jax.ShapeDtypeStruct((cap, 2 * s), bf16) for _ in offs]
+    far_memory = pl.BlockSpec(memory_space=pltpu.HBM)
+    return call(
+        functools.partial(dispatch_body, n, cap, offs, cuts),
+        [me, ids, codes, x, g],
         deps,
         out_shape,
-        [pl.BlockSpec(memory_space=pltpu.SMEM)] + [vmem] * 4,
-        [vmem] * len(out_shape),
+        [pl.BlockSpec(memory_space=pltpu.SMEM)] + [far_memory] * 4,
+        [pl.BlockSpec(memory_space=pltpu.VMEM)] * len(out_shape),
+        scratch=[
+            pltpu.VMEM((1, t), jnp.int32),
+            pltpu.VMEM((1, t), jnp.int32),
+            pltpu.VMEM((t, s), bf16),
+            pltpu.VMEM((t, s), bf16),
+            pltpu.SemaphoreType.DMA((2 + 2 * len(cuts),)),
+        ],
+        limit=LEAD_BYTES,
     )
 
 
@@ -280,13 +302,12 @@
     def _():
         target = tgt_ref[...]
         slots = lax.broadcasted_iota(jnp.int32, (cap, target.shape[1]), 0)
-        for i, k in enumerate(offs):
-            hit = jnp.where(slots + (me_ref[0] ^ k) * cap == target, 1.0, 0.0)
-            pick_t[i * cap : (i + 1) * cap, :] = hit.astype(bf16)
+        hits = [jnp.where(slots + (me_ref[0] ^ k) * cap == target, 1.0, 0.0) for k in offs]
+        pick_t[...] = jnp.concatenate(hits, axis=0).T.astype(bf16)
 
     for i, blk in enumerate(backs):
         rows[i * cap : (i + 1) * cap, :] = blk[...]
-    total = dot(pick_t[...], rows[...], 0, 0)
+    total = dot(pick_t[...], rows[...])
     if chained:
         total = total + prev[...].astype(f32)
     out[...] = total.astype(bf16)
@@ -296,18 +317,19 @@
     t = target.shape[1]
     s = backs[0].shape[1]
     nb = len(offs)
-    col = pl.BlockSpec((t, TILE), lambda c, i: (0, c))
+    wide = s // 2
+    col = pl.BlockSpec((t, wide), lambda c, i: (0, c))
     extra = [] if prev is None else [prev]
     return call(
         functools.partial(combine_body, cap, offs, prev is not None),
         [me, target, *backs, *extra],
         deps,
         jax.ShapeDtypeStruct((t, s), bf16),
-        [whole((1, t))] + [pl.BlockSpec((cap, TILE), lambda c, i: (0, c))] * nb + [col] * len(extra),
+        [whole((1, t))] + [pl.BlockSpec((cap, wide), lambda c, i: (0, c))] * nb + [col] * len(extra),
         col,
-        grid=(s // TILE,),
+        grid=(s // wide,),
         scalars=1,
-        scratch=[pltpu.VMEM((nb * cap, t), bf16), pltpu.VMEM((nb * cap, TILE), bf16)],
+        scratch=[pltpu.VMEM((t, nb * cap), bf16), pltpu.VMEM((nb * cap, wide), bf16)],
     )
 
 
@@ -336,7 +358,7 @@
 
     def push(offs, deps):
         for k in offs:
-            if deps:
+            if deps is not None:
                 send[k] = after(send[k], mark + deps)
                 mark[:] = [send[k]]
             got[k] = swap_expert(send[k], k) if k else send[k]
@@ -344,7 +366,7 @@
     def give_back(offs, deps):
         for k in offs:
             rows = ready[k]
-            if deps:
+            if deps is not None:
                 rows = after(rows, mark + deps)
                 mark[:] = [rows]
             back[k] = swap_expert(rows, k) if k else rows
@@ -368,40 +390,41 @@
         return [got[k] for k in offs]
 
     offs = far[0] + near[0]
-    target, *sends = dispatch(n, cap, offs, me, ids, codes, tokens, grad_out, True, [])
+    target, *sends = dispatch(n, cap, offs, me, ids, codes, tokens, grad_out, [])
     send.update(zip(offs, sends))
     mark[:] = [sends[0]]
-    push(offs, [])
+    push(offs, None)
     offs = far[1] + near[1] + far[2] + near[2] + far[3]
-    sends = dispatch(n, cap, offs, me, target, codes, tokens, grad_out, False, mark)
+    _, *sends = dispatch(n, cap, offs, me, ids, codes, tokens, grad_out, mark)
     send.update(zip(offs, sends))
     mark[:] = [sends[0]]
 
     fwd(0)
-    push(far[1] + near[1], gotten(far[0]))
+    push(far[1], [])
+    push(near[1], gotten(far[0]))
     act(0)
     fwd(1)
     bwd(0)
     act(1)
-    push(far[2] + near[2], gotten(far[1] + near[1]))
-    give_back(near[0], [])
+    push(far[2], gotten(near[1]))
+    push(near[2], gotten(far[1]))
+    give_back(near[0], None)
     fwd(2)
     bwd(1)
     act(2)
     push(far[3], gotten(far[2] + near[2]))
     fwd(3)
     bwd(2)
-    give_back(near[1], [])
+    give_back(near[1], None)
     act(3)
     give_back(far[0], gotten(far[3]) + [back[k] for k in near[1] + near[0][1:]])
-    give_back(far[1], [])
     fwd(4)
     bwd(3)
+    give_back(far[1] + far[2], [back[k] for k in far[0]])
     act(4)
-    give_back(far[2], [back[k] for k in far[0]])
+    bwd(4)
+    give_back(far[3], None)
     give_back(near[2], [])
-    bwd(4)
-    give_back(far[3], [])
     order = range(len(chunks))
     flat = [k for c in order for k in chunks[c]]
     new_down, new_moment, token = down(
@@ -416,7 +439,7 @@
         mark,
     )
     mark[:] = [token]
-    tail = far[2] + far[3]
+    tail = near[2] + far[3]
     early = [k for k in flat if k not in tail]
     part = combine(cap, early, me, target, [back[k] for k in early], None, mark)
     grad_tokens = combine(cap, tail, me, target, [back[k] for k in tail], part, [])

time: 182 us -> 174 us (0.956)
  waiting for transfers between devices: 56.4 us -> 51.6 us
  local copies, waits for them, and re-layouts: 12 us -> 7.22 us
  Pallas kernels: 60.5 us -> 63.2 us
  starting transfers between devices: 52.1 us -> 49.8 us
    ppermute x14, waiting for transfers between devices: 37.2 us -> 30.2 us  [swap_expert(): return lax.ppermute(v, 'expert', [(i, i ^ k) for i in range(n)])]
    unnamed x32 -> x30, local copies, waits for them, and re-layouts: 12 us -> 7.22 us
    pallas_call x27 -> x29, Pallas kernels: 60.5 us -> 63.2 us  [call(): pl.pallas_call(skipping(body, len(operands), len(deps)), out_shape=out_sh...]
    ppermute x30, starting transfers between devices: 30.7 us -> 28.5 us  [swap_dp(): return lax.ppermute(v, 'dp', [(i, i ^ k) for i in range(ndp)])]
    ppermute x30, waiting for transfers between devices: 19.2 us -> 21.4 us  [swap_dp(): return lax.ppermute(v, 'dp', [(i, i ^ k) for i in range(ndp)])]
  transfers between devices with their start and end apart: 44 -> 44, of which waited for: 18 -> 22; matrix products, arithmetic and copies ran while one was open for 0% -> 0% of each run, Pallas kernels for 30% -> 33%
where the time goes in v4:
time: 174 us; the launch traced here: 173 us
  Pallas kernels  63.2 us (36%)
  waiting for transfers between devices  51.6 us (30%)
  starting transfers between devices  49.8 us (29%)
  local copies, waits for them, and re-layouts  7.22 us (4%)
    pallas_call x29, Pallas kernels, call(): pl.pallas_call(skipping(body, len(operands), len(deps)), out_shape=out_sh...  63.2 us
    ppermute x14, waiting for transfers between devices, swap_expert(): return lax.ppermute(v, 'expert', [(i, i ^ k) for i in range(n)])  30.2 us
    ppermute x30, starting transfers between devices, swap_dp(): return lax.ppermute(v, 'dp', [(i, i ^ k) for i in range(ndp)])  28.5 us
    ppermute x30, waiting for transfers between devices, swap_dp(): return lax.ppermute(v, 'dp', [(i, i ^ k) for i in range(ndp)])  21.4 us
    ppermute x14, starting transfers between devices, swap_expert(): return lax.ppermute(v, 'expert', [(i, i ^ k) for i in range(n)])  21.2 us
    unnamed x30, local copies, waits for them, and re-layouts  7.22 us
  transfers between devices with their start and end apart: 44, of which 22 were waited for; matrix products, arithmetic and copies ran while one was open for 0% of the time, Pallas kernels for 33%

profile of v4, /device:TPU:9, one launch (start us, length us, event | category | flops | bytes accessed | tf_op | source)
XLA Modules:
  0.0 172.7 jit_solution(17059995026321750693)
XLA Ops:
  0.6 4.1 %shard_map.103 = (s32[1,512]{1,0:T(1,128)}, bf16[80,3584]{1,0:T(8,128)(2,1)}, bf16[80,3584]{1,0:T(8,128)(2,1)}, bf16[80,3584]{1,0:T(8,128)(2,1)}) custom-call(s32[1]{0:T(128)} %bitcast.refs_0_, s32[1,512]{1,0:T(1,128)} %bitcast.37, s32[1,512]{1,0:T(1,128)} %bitcast.39, bf16[512,1792]{1,0:T(8,128)(2,1)} %refs_3_.3, bf16[512,1792]{1,0:T(8,128)(2,1)} %refs_4_.3), custom_call_target="tpu_custom_call" | custom-call | tf_op jit(solution)/shard_map/pallas_call | solution.py:40
  5.5 2.3 %collective-permute-start = (bf16[80,3584]{1,0:T(8,128)(2,1)}, bf16[80,3584]{1,0:T(8,128)(2,1)S(1)}, u32[]{:S(2)}, u32[]{:S(2)}) collective-permute-start(bf16[80,3584]{1,0:T(8,128)(2,1)} %get-tuple-element.42.refs_5_), channel_id=1, source_target_pairs={{0,4},{1,5},{2,6},{3,7},{4,0},{5,1},{6,2},{7,3},{8,12},{9,13},{10,... | collective-permute-start | bytes 1720328 | tf_op jit(solution)/shard_map/ppermute | solution.py:349
  7.8 5.1 %shard_map.104 = (s32[1,512]{1,0:T(1,128)}, bf16[80,3584]{1,0:T(8,128)(2,1)}, bf16[80,3584]{1,0:T(8,128)(2,1)}, bf16[80,3584]{1,0:T(8,128)(2,1)}, bf16[80,3584]{1,0:T(8,128)(2,1)}, /*index=5*/bf16[80,3584]{1,0:T(8,128)(2,1)}) custom-call(s32[1]{0:T(128)} %bitcast.refs_0_, s32[1,512]{1,0:T(1,128)} %bitcast.38, s32[1,512]{1,0:T(1,128)} %bitcast.40, ...), custom_call_target="tpu_custom_call" | custom-call | tf_op jit(solution)/shard_map/pallas_call | solution.py:40
  13.0 2.0 %copy-done = bf16[1,1792,1024]{2,1,0:T(8,128)(2,1)S(1)} copy-done((bf16[1,1792,1024]{2,1,0:T(8,128)(2,1)S(1)}, bf16[1,1792,1024]{2,1,0:T(8,128)(2,1)}, u32[]{:S(2)}) %copy-start) | copy-done | bytes 3670040
  15.0 2.0 %copy-done.2 = bf16[1,1792,1024]{2,1,0:T(8,128)(2,1)S(1)} copy-done((bf16[1,1792,1024]{2,1,0:T(8,128)(2,1)S(1)}, bf16[1,1792,1024]{2,1,0:T(8,128)(2,1)}, u32[]{:S(2)}) %copy-start.2) | copy-done | bytes 3670040
  17.0 2.0 %copy-done.4 = bf16[1,1024,1792]{2,1,0:T(8,128)(2,1)S(1)} copy-done((bf16[1,1024,1792]{2,1,0:T(8,128)(2,1)S(1)}, bf16[1,1024,1792]{2,1,0:T(8,128)(2,1)}, u32[]{:S(2)}) %copy-start.4) | copy-done | bytes 3670040
  20.1 4.4 %shard_map.105 = (bf16[160,768]{1,0:T(8,128)(2,1)S(1)}, bf16[160,768]{1,0:T(8,128)(2,1)S(1)}, bf16[160,768]{1,0:T(8,128)(2,1)S(1)}, bf16[160,768]{1,0:T(8,128)(2,1)S(1)}) custom-call(s32[1]{0:T(128)} %bitcast.3.refs_0_, bf16[80,3584]{1,0:T(8,128)(2,1)S(1)} %copy-done.9, bf16[80,3584]{1,0:T(8,128)(2,1)S(1)} %collective-permute-done.1.refs_2_.refs_22_, ...), custom_call_target="tpu_custom_call" | custom-call | tf_op jit(solution)/shard_map/pallas_call | solution.py:40
  24.6 1.3 collective-permute-start.2
  27.3 5.7 %collective-permute-done.refs_2_.refs_1_.refs_23_ = bf16[80,3584]{1,0:T(8,128)(2,1)S(1)} collective-permute-done((bf16[80,3584]{1,0:T(8,128)(2,1)}, bf16[80,3584]{1,0:T(8,128)(2,1)S(1)}, u32[]{:S(2)}, u32[]{:S(2)}) %collective-permute-start) | collective-permute-done | bytes 573472 | tf_op jit(solution)/shard_map/ppermute | solution.py:349
  33.7 2.6 %collective-permute-start.13 = (bf16[80,3584]{1,0:T(8,128)(2,1)S(1)}, bf16[80,3584]{1,0:T(8,128)(2,1)S(1)}, u32[]{:S(2)}, u32[]{:S(2)}) collective-permute-start(bf16[80,3584]{1,0:T(8,128)(2,1)S(1)} %shard_map.106.refs_1_), channel_id=1, source_target_pairs={{0,5},{1,4},{2,7},{3,6},{4,1},{5,0},{6,3},{7,2},{8,13},{9,12},{10,... | collective-permute-start | bytes 1720328 | tf_op jit(solution)/shard_map/ppermute | solution.py:349
  36.4 1.7 %collective-permute-done.4.refs_3_ = bf16[160,768]{1,0:T(8,128)(2,1)S(1)} collective-permute-done((bf16[160,768]{1,0:T(8,128)(2,1)S(1)}, bf16[160,768]{1,0:T(8,128)(2,1)S(1)}, u32[]{:S(2)}, u32[]{:S(2)}) %collective-permute-start.4) | collective-permute-done | bytes 245792 | tf_op jit(solution)/shard_map/ppermute | solution.py:352
  41.1 4.0 %shard_map.109 = (bf16[80,768]{1,0:T(8,128)(2,1)S(1)}, bf16[80,768]{1,0:T(8,128)(2,1)S(1)}, bf16[80,768]{1,0:T(8,128)(2,1)S(1)}, bf16[80,768]{1,0:T(8,128)(2,1)S(1)}) custom-call(s32[1]{0:T(128)} %bitcast.3.refs_0_, bf16[80,3584]{1,0:T(8,128)(2,1)S(1)} %collective-permute-done.refs_2_.refs_1_.refs_23_, bf16[1792,1024]{1,0:T(8,128)(2,1)S(1)} %bitcast.11, ...), custom_call_target="tpu_custom_call" | custom-call | tf_op jit(solution)/shard_map/pallas_call | solution.py:40
  45.4 1.4 collective-permute-start.5
  46.8 5.7 %collective-permute-done.9.refs_3_ = bf16[160,768]{1,0:T(8,128)(2,1)S(1)} collective-permute-done((bf16[160,768]{1,0:T(8,128)(2,1)S(1)}, bf16[160,768]{1,0:T(8,128)(2,1)S(1)}, u32[]{:S(2)}, u32[]{:S(2)}) %collective-permute-start.9) | collective-permute-done | bytes 245792 | tf_op jit(solution)/shard_map/ppermute | solution.py:352
  54.8 3.7 %shard_map.110 = (bf16[80,1792]{1,0:T(8,128)(2,1)S(1)}, bf16[80,1792]{1,0:T(8,128)(2,1)S(1)}) custom-call(s32[1]{0:T(128)} %bitcast.3.refs_0_, bf16[160,768]{1,0:T(8,128)(2,1)S(1)} %shard_map.108.refs_5_.refs_1_, bf16[160,768]{1,0:T(8,128)(2,1)S(1)} %collective-permute-done.8.refs_2_, bf16[160,768]{1,0:T(8,128)(2,1)S(1)} %collective-permute-done.9.refs_3_, ...), custom_call_target="tpu_custom_call" | custom-call | tf_op jit(solution)/shard_map/pallas_call | solution.py:40
  58.8 2.8 %collective-permute-done.13.refs_2_.refs_1_.refs_24_ = bf16[80,3584]{1,0:T(8,128)(2,1)S(1)} collective-permute-done((bf16[80,3584]{1,0:T(8,128)(2,1)S(1)}, bf16[80,3584]{1,0:T(8,128)(2,1)S(1)}, u32[]{:S(2)}, u32[]{:S(2)}) %collective-permute-start.13) | collective-permute-done | bytes 573472 | tf_op jit(solution)/shard_map/ppermute | solution.py:349
  61.7 1.3 collective-permute-start.14
  63.0 2.2 %collective-permute-start.20 = (bf16[80,768]{1,0:T(8,128)(2,1)S(1)}, bf16[80,768]{1,0:T(8,128)(2,1)S(1)}, u32[]{:S(2)}, u32[]{:S(2)}) collective-permute-start(bf16[80,768]{1,0:T(8,128)(2,1)S(1)} %shard_map.111.refs_1_.refs_5_), channel_id=1, source_target_pairs={{0,24},{8,16},{16,8},{24,0},{1,25},{9,17},{17,9},{25,1},{2,26},{10... | collective-permute-start | bytes 368648 | tf_op jit(solution)/shard_map/ppermute | solution.py:352
  65.7 4.2 %shard_map.114 = (bf16[160,768]{1,0:T(8,128)(2,1)S(1)}, bf16[160,768]{1,0:T(8,128)(2,1)S(1)}, bf16[160,768]{1,0:T(8,128)(2,1)S(1)}, bf16[160,768]{1,0:T(8,128)(2,1)S(1)}) custom-call(s32[1]{0:T(128)} %bitcast.3.refs_0_, bf16[80,3584]{1,0:T(8,128)(2,1)S(1)} %collective-permute-done.13.refs_2_.refs_1_.refs_24_, ...), custom_call_target="tpu_custom_call" | custom-call | tf_op jit(solution)/shard_map/pallas_call | solution.py:40
  69.9 1.3 collective-permute-start.15
  71.8 1.2 collective-permute-start.16
  74.2 3.3 %shard_map.115.refs_4_.refs_0_ = bf16[80,1792]{1,0:T(8,128)(2,1)S(1)} custom-call(s32[1]{0:T(128)} %bitcast.3.refs_0_, bf16[80,768]{1,0:T(8,128)(2,1)S(1)} %shard_map.111.refs_1_.refs_5_, bf16[80,768]{1,0:T(8,128)(2,1)S(1)} %collective-permute-done.18.refs_2_.refs_6_, bf16[80,768]{1,0:T(8,128)(2,1)S(1)} %collective-permute-done.19.refs_3_.refs_7_, ...), custom_call_target="tpu_custom_call" | custom-call | tf_op jit(solution)/shard_map/pallas_call | solution.py:40
  77.5 1.9 %collective-permute-done.16.refs_2_ = bf16[160,768]{1,0:T(8,128)(2,1)S(1)} collective-permute-done((bf16[160,768]{1,0:T(8,128)(2,1)S(1)}, bf16[160,768]{1,0:T(8,128)(2,1)S(1)}, u32[]{:S(2)}, u32[]{:S(2)}) %collective-permute-start.16) | collective-permute-done | bytes 245792 | tf_op jit(solution)/shard_map/ppermute | solution.py:352
  79.4 2.9 %collective-permute-done.17.refs_3_ = bf16[160,768]{1,0:T(8,128)(2,1)S(1)} collective-permute-done((bf16[160,768]{1,0:T(8,128)(2,1)S(1)}, bf16[160,768]{1,0:T(8,128)(2,1)S(1)}, u32[]{:S(2)}, u32[]{:S(2)}) %collective-permute-start.17) | collective-permute-done | bytes 245792 | tf_op jit(solution)/shard_map/ppermute | solution.py:352
  83.8 1.3 collective-permute-start.25
  85.8 1.3 collective-permute-done.14.refs_3_.refs_2_.refs_27_
  87.2 3.4 %collective-permute-start.30 = (bf16[80,3584]{1,0:T(8,128)(2,1)S(1)}, bf16[80,3584]{1,0:T(8,128)(2,1)S(1)}, u32[]{:S(2)}, u32[]{:S(2)}) collective-permute-start(bf16[80,3584]{1,0:T(8,128)(2,1)S(1)} %shard_map.117.refs_6_), channel_id=1, source_target_pairs={{0,7},{1,6},{2,5},{3,4},{4,3},{5,2},{6,1},{7,0},{8,15},{9,14},{10,... | collective-permute-start | bytes 1720328 | tf_op jit(solution)/shard_map/ppermute | solution.py:349
  90.8 4.2 %shard_map.118 = (bf16[160,768]{1,0:T(8,128)(2,1)S(1)}, bf16[160,768]{1,0:T(8,128)(2,1)S(1)}, bf16[160,768]{1,0:T(8,128)(2,1)S(1)}, bf16[160,768]{1,0:T(8,128)(2,1)S(1)}) custom-call(s32[1]{0:T(128)} %bitcast.3.refs_0_, bf16[80,3584]{1,0:T(8,128)(2,1)S(1)} %collective-permute-done.12.refs_2_.refs_1_.refs_26_, ...), custom_call_target="tpu_custom_call" | custom-call | tf_op jit(solution)/shard_map/pallas_call | solution.py:40
  95.0 1.3 collective-permute-start.21
  96.4 1.3 collective-permute-start.23
  98.6 3.7 %shard_map.119 = (bf16[80,1792]{1,0:T(8,128)(2,1)S(1)}, bf16[80,1792]{1,0:T(8,128)(2,1)S(1)}) custom-call(s32[1]{0:T(128)} %bitcast.3.refs_0_, bf16[160,768]{1,0:T(8,128)(2,1)S(1)} %shard_map.116.refs_1_.refs_9_, bf16[160,768]{1,0:T(8,128)(2,1)S(1)} %collective-permute-done.24.refs_2_.refs_10_, ...), custom_call_target="tpu_custom_call" | custom-call | tf_op jit(solution)/shard_map/pallas_call | solution.py:40
  102.3 1.5 collective-permute-done.21.refs_1_
  104.1 4.4 %collective-permute-done.23.refs_3_ = bf16[160,768]{1,0:T(8,128)(2,1)S(1)} collective-permute-done((bf16[160,768]{1,0:T(8,128)(2,1)S(1)}, bf16[160,768]{1,0:T(8,128)(2,1)S(1)}, u32[]{:S(2)}, u32[]{:S(2)}) %collective-permute-start.23) | collective-permute-done | bytes 245792 | tf_op jit(solution)/shard_map/ppermute | solution.py:352
  108.8 2.1 %collective-permute-start.29 = (bf16[160,768]{1,0:T(8,128)(2,1)S(1)}, bf16[160,768]{1,0:T(8,128)(2,1)S(1)}, u32[]{:S(2)}, u32[]{:S(2)}) collective-permute-start(bf16[160,768]{1,0:T(8,128)(2,1)S(1)} %shard_map.120.refs_1_.refs_13_), channel_id=1, source_target_pairs={{0,24},{8,16},{16,8},{24,0},{1,25},{9,17},{17,9},{25,1},{2,26},{10... | collective-permute-start | bytes 737288 | tf_op jit(solution)/shard_map/ppermute | solution.py:352
  112.0 4.0 %collective-permute-done.30.refs_2_.refs_1_.refs_28_ = bf16[80,3584]{1,0:T(8,128)(2,1)S(1)} collective-permute-done((bf16[80,3584]{1,0:T(8,128)(2,1)S(1)}, bf16[80,3584]{1,0:T(8,128)(2,1)S(1)}, u32[]{:S(2)}, u32[]{:S(2)}) %collective-permute-start.30) | collective-permute-done | bytes 573472 | tf_op jit(solution)/shard_map/ppermute | solution.py:349
  116.2 4.0 %shard_map.122 = (bf16[80,768]{1,0:T(8,128)(2,1)S(1)}, bf16[80,768]{1,0:T(8,128)(2,1)S(1)}, bf16[80,768]{1,0:T(8,128)(2,1)S(1)}, bf16[80,768]{1,0:T(8,128)(2,1)S(1)}) custom-call(s32[1]{0:T(128)} %bitcast.3.refs_0_, bf16[80,3584]{1,0:T(8,128)(2,1)S(1)} %collective-permute-done.30.refs_2_.refs_1_.refs_28_, bf16[1792,1024]{1,0:T(8,128)(2,1)S(1)} %bitcast.17, ...), custom_call_target="tpu_custom_call" | custom-call | tf_op jit(solution)/shard_map/pallas_call | solution.py:40
  120.2 1.4 collective-permute-start.33
  121.6 1.3 collective-permute-done.28.refs_3_.refs_15_
  123.8 3.7 %shard_map.123 = (bf16[80,1792]{1,0:T(8,128)(2,1)S(1)}, bf16[80,1792]{1,0:T(8,128)(2,1)S(1)}) custom-call(s32[1]{0:T(128)} %bitcast.3.refs_0_, bf16[160,768]{1,0:T(8,128)(2,1)S(1)} %shard_map.120.refs_1_.refs_13_, bf16[160,768]{1,0:T(8,128)(2,1)S(1)} %collective-permute-done.27.refs_2_.refs_14_, ...), custom_call_target="tpu_custom_call" | custom-call | tf_op jit(solution)/shard_map/pallas_call | solution.py:40
  128.4 1.5 collective-permute-start.39
  132.1 5.7 %collective-permute-start.42 = (bf16[80,1792]{1,0:T(8,128)(2,1)S(1)}, bf16[80,1792]{1,0:T(8,128)(2,1)S(1)}, u32[]{:S(2)}, u32[]{:S(2)}) collective-permute-start(bf16[80,1792]{1,0:T(8,128)(2,1)S(1)} %shard_map.124.refs_1_), channel_id=1, source_target_pairs={{0,5},{1,4},{2,7},{3,6},{4,1},{5,0},{6,3},{7,2},{8,13},{9,12},{10,... | collective-permute-start | bytes 860168 | tf_op jit(solution)/shard_map/ppermute | solution.py:349
  137.8 3.3 %shard_map.127.refs_1_ = bf16[80,1792]{1,0:T(8,128)(2,1)S(1)} custom-call(s32[1]{0:T(128)} %bitcast.3.refs_0_, bf16[80,768]{1,0:T(8,128)(2,1)S(1)} %shard_map.126.refs_1_.refs_7_.refs_17_, bf16[80,768]{1,0:T(8,128)(2,1)S(1)} %collective-permute-done.37.refs_2_.refs_18_, bf16[80,768]{1,0:T(8,128)(2,1)S(1)} %collective-permute-done.38.refs_3_.refs_19_, ...), custom_call_target="tpu_custom_call" | custom-call | tf_op jit(solution)/shard_map/pallas_call | solution.py:40
  141.1 1.9 %collective-permute-start.40 = (bf16[80,1792]{1,0:T(8,128)(2,1)S(1)}, bf16[80,1792]{1,0:T(8,128)(2,1)S(1)}, u32[]{:S(2)}, u32[]{:S(2)}) collective-permute-start(bf16[80,1792]{1,0:T(8,128)(2,1)S(1)} %shard_map.128.refs_31_), channel_id=1, source_target_pairs={{0,3},{1,2},{2,1},{3,0},{4,7},{5,6},{6,5},{7,4},{8,11},{9,10},{10,... | collective-permute-start | bytes 860168 | tf_op jit(solution)/shard_map/ppermute | solution.py:349
  144.1 10.4 %shard_map.129 = (bf16[1024,1792]{1,0:T(8,128)(2,1)}, bf16[1024,1792]{1,0:T(8,128)(2,1)}, f32[8,128]{1,0:T(8,128)S(1)}) custom-call(s32[1]{0:T(128)} %bitcast.3.refs_0_, bf16[160,768]{1,0:T(8,128)(2,1)S(1)} %shard_map.108.refs_5_.refs_1_, bf16[160,768]{1,0:T(8,128)(2,1)S(1)} %collective-permute-done.8.refs_2_, ...), custom_call_target="tpu_custom_call" | custom-call | tf_op jit(solution)/shard_map/pallas_call | solution.py:40
  154.5 6.2 %collective-permute-done.42.refs_5_ = bf16[80,1792]{1,0:T(8,128)(2,1)S(1)} collective-permute-done((bf16[80,1792]{1,0:T(8,128)(2,1)S(1)}, bf16[80,1792]{1,0:T(8,128)(2,1)S(1)}, u32[]{:S(2)}, u32[]{:S(2)}) %collective-permute-start.42) | collective-permute-done | bytes 286752 | tf_op jit(solution)/shard_map/ppermute | solution.py:349
  160.7 2.0 %shard_map.130.refs_4_ = bf16[512,1792]{1,0:T(8,128)(2,1)S(1)} custom-call(s32[1]{0:T(128)} %bitcast.refs_0_, s32[1,512]{1,0:T(1,128)S(1)} %copy-done.14, bf16[80,1792]{1,0:T(8,128)(2,1)S(1)} %get-tuple-element.56.refs_4_.refs_2_, bf16[80,1792]{1,0:T(8,128)(2,1)S(1)} %collective-permute-done.32.refs_4_.refs_3_, ...), custom_call_target="tpu_custom_call" | custom-call | tf_op jit(solution)/shard_map/pallas_call | solution.py:40
  162.7 7.8 %collective-permute-done.41.refs_3_ = bf16[80,1792]{1,0:T(8,128)(2,1)S(1)} collective-permute-done((bf16[80,1792]{1,0:T(8,128)(2,1)S(1)}, bf16[80,1792]{1,0:T(8,128)(2,1)S(1)}, u32[]{:S(2)}, u32[]{:S(2)}) %collective-permute-start.41) | collective-permute-done | bytes 286752 | tf_op jit(solution)/shard_map/ppermute | solution.py:349
  170.5 2.2 %shard_map.131 = bf16[512,1792]{1,0:T(8,128)(2,1)} custom-call(s32[1]{0:T(128)} %bitcast.refs_0_, s32[1,512]{1,0:T(1,128)S(1)} %copy-done.14, bf16[80,1792]{1,0:T(8,128)(2,1)S(1)} %collective-permute-done.40.refs_2_, bf16[80,1792]{1,0:T(8,128)(2,1)S(1)} %collective-permute-done.41.refs_3_, bf16[512,1792]{1,0:T(8,128)(2,1)S(1)} %shard_map.130.refs_4_), custom_call_target="tpu_custom_call" | custom-call | tf_op jit(solution)/shard_map/pallas_call | solution.py:40
  (99 shorter events, 22.5 us)
Async XLA Ops:
  4.8 8.2 %collective-permute-start.1 = (bf16[80,3584]{1,0:T(8,128)(2,1)}, bf16[80,3584]{1,0:T(8,128)(2,1)S(1)}, u32[]{:S(2)}, u32[]{:S(2)}) collective-permute-start(bf16[80,3584]{1,0:T(8,128)(2,1)} %get-tuple-element.45), channel_id=1, source_target_pairs={{0,1},{1,0},{2,3},{3,2},{4,5},{5,4},{6,7},{7,6},{8,9},{9,8},{10,11... | collective-permute-start | bytes 1720328 | tf_op jit(solution)/shard_map/ppermute | solution.py:349
  5.5 27.6 %collective-permute-start = (bf16[80,3584]{1,0:T(8,128)(2,1)}, bf16[80,3584]{1,0:T(8,128)(2,1)S(1)}, u32[]{:S(2)}, u32[]{:S(2)}) collective-permute-start(bf16[80,3584]{1,0:T(8,128)(2,1)} %get-tuple-element.42.refs_5_), channel_id=1, source_target_pairs={{0,4},{1,5},{2,6},{3,7},{4,0},{5,1},{6,2},{7,3},{8,12},{9,13},{10,... | collective-permute-start | bytes 1720328 | tf_op jit(solution)/shard_map/ppermute | solution.py:349
  20.1 20.9 %copy-start.3 = (bf16[1,1792,1024]{2,1,0:T(8,128)(2,1)S(1)}, bf16[1,1792,1024]{2,1,0:T(8,128)(2,1)}, u32[]{:S(2)}) copy-start(bf16[1,1792,1024]{2,1,0:T(8,128)(2,1)} %param.13) | copy-start | bytes 11010052
  20.1 20.9 %copy-start.5 = (bf16[1,1024,1792]{2,1,0:T(8,128)(2,1)S(1)}, bf16[1,1024,1792]{2,1,0:T(8,128)(2,1)}, u32[]{:S(2)}) copy-start(bf16[1,1024,1792]{2,1,0:T(8,128)(2,1)} %param.14) | copy-start | bytes 11010052
  24.6 16.5 %copy-start.1 = (bf16[1,1792,1024]{2,1,0:T(8,128)(2,1)S(1)}, bf16[1,1792,1024]{2,1,0:T(8,128)(2,1)}, u32[]{:S(2)}) copy-start(bf16[1,1792,1024]{2,1,0:T(8,128)(2,1)} %param.12) | copy-start | bytes 11010052
  24.6 11.8 %collective-permute-start.2 = (bf16[160,768]{1,0:T(8,128)(2,1)S(1)}, bf16[160,768]{1,0:T(8,128)(2,1)S(1)}, u32[]{:S(2)}, u32[]{:S(2)}) collective-permute-start(bf16[160,768]{1,0:T(8,128)(2,1)S(1)} %get-tuple-element.48), channel_id=1, source_target_pairs={{0,8},{8,0},{16,24},{24,16},{1,9},{9,1},{17,25},{25,17},{2,10},{10... | collective-permute-start | bytes 737288 | tf_op jit(solution)/shard_map/ppermute | solution.py:352
  25.9 10.5 %collective-permute-start.3 = (bf16[160,768]{1,0:T(8,128)(2,1)S(1)}, bf16[160,768]{1,0:T(8,128)(2,1)S(1)}, u32[]{:S(2)}, u32[]{:S(2)}) collective-permute-start(bf16[160,768]{1,0:T(8,128)(2,1)S(1)} %get-tuple-element.49), channel_id=1, source_target_pairs={{0,16},{8,24},{16,0},{24,8},{1,17},{9,25},{17,1},{25,9},{2,18},{10... | collective-permute-start | bytes 737288 | tf_op jit(solution)/shard_map/ppermute | solution.py:352
  27.1 11.0 %collective-permute-start.4 = (bf16[160,768]{1,0:T(8,128)(2,1)S(1)}, bf16[160,768]{1,0:T(8,128)(2,1)S(1)}, u32[]{:S(2)}, u32[]{:S(2)}) collective-permute-start(bf16[160,768]{1,0:T(8,128)(2,1)S(1)} %get-tuple-element.50), channel_id=1, source_target_pairs={{0,24},{8,16},{16,8},{24,0},{1,25},{9,17},{17,9},{25,1},{2,26},{10... | collective-permute-start | bytes 737288 | tf_op jit(solution)/shard_map/ppermute | solution.py:352
  33.1 25.7 %collective-permute-start.11 = (bf16[80,3584]{1,0:T(8,128)(2,1)S(1)}, bf16[80,3584]{1,0:T(8,128)(2,1)S(1)}, u32[]{:S(2)}, u32[]{:S(2)}) collective-permute-start(bf16[80,3584]{1,0:T(8,128)(2,1)S(1)} %shard_map.107.refs_4_), channel_id=1, source_target_pairs={{0,2},{1,3},{2,0},{3,1},{4,6},{5,7},{6,4},{7,5},{8,10},{9,11},{10,... | collective-permute-start | bytes 1720328 | tf_op jit(solution)/shard_map/ppermute | solution.py:349
  33.7 27.9 %collective-permute-start.13 = (bf16[80,3584]{1,0:T(8,128)(2,1)S(1)}, bf16[80,3584]{1,0:T(8,128)(2,1)S(1)}, u32[]{:S(2)}, u32[]{:S(2)}) collective-permute-start(bf16[80,3584]{1,0:T(8,128)(2,1)S(1)} %shard_map.106.refs_1_), channel_id=1, source_target_pairs={{0,5},{1,4},{2,7},{3,6},{4,1},{5,0},{6,3},{7,2},{8,13},{9,12},{10,... | collective-permute-start | bytes 1720328 | tf_op jit(solution)/shard_map/ppermute | solution.py:349
  38.3 7.1 %collective-permute-start.10 = (bf16[160,768]{1,0:T(8,128)(2,1)S(1)}, bf16[160,768]{1,0:T(8,128)(2,1)S(1)}, u32[]{:S(2)}, u32[]{:S(2)}) collective-permute-start(bf16[160,768]{1,0:T(8,128)(2,1)S(1)} %shard_map.108.refs_5_.refs_1_), channel_id=1, source_target_pairs={{0,24},{8,16},{16,8},{24,0},{1,25},{9,17},{17,9},{25,1},{2,26},{10... | collective-permute-start | bytes 737288 | tf_op jit(solution)/shard_map/ppermute | solution.py:352
  39.5 12.9 %collective-permute-start.9 = (bf16[160,768]{1,0:T(8,128)(2,1)S(1)}, bf16[160,768]{1,0:T(8,128)(2,1)S(1)}, u32[]{:S(2)}, u32[]{:S(2)}) collective-permute-start(bf16[160,768]{1,0:T(8,128)(2,1)S(1)} %shard_map.108.refs_5_.refs_1_), channel_id=1, source_target_pairs={{0,16},{8,24},{16,0},{24,8},{1,17},{9,25},{17,1},{25,9},{2,18},{10... | collective-permute-start | bytes 737288 | tf_op jit(solution)/shard_map/ppermute | solution.py:352
  40.7 12.8 %collective-permute-start.8 = (bf16[160,768]{1,0:T(8,128)(2,1)S(1)}, bf16[160,768]{1,0:T(8,128)(2,1)S(1)}, u32[]{:S(2)}, u32[]{:S(2)}) collective-permute-start(bf16[160,768]{1,0:T(8,128)(2,1)S(1)} %shard_map.108.refs_5_.refs_1_), channel_id=1, source_target_pairs={{0,8},{8,0},{16,24},{24,16},{1,9},{9,1},{17,25},{25,17},{2,10},{10... | collective-permute-start | bytes 737288 | tf_op jit(solution)/shard_map/ppermute | solution.py:352
  45.4 13.1 %collective-permute-start.5 = (bf16[80,768]{1,0:T(8,128)(2,1)S(1)}, bf16[80,768]{1,0:T(8,128)(2,1)S(1)}, u32[]{:S(2)}, u32[]{:S(2)}) collective-permute-start(bf16[80,768]{1,0:T(8,128)(2,1)S(1)} %get-tuple-element.53), channel_id=1, source_target_pairs={{0,8},{8,0},{16,24},{24,16},{1,9},{9,1},{17,25},{25,17},{2,10},{10... | collective-permute-start | bytes 368648 | tf_op jit(solution)/shard_map/ppermute | solution.py:352
  52.4 6.1 %collective-permute-start.6 = (bf16[80,768]{1,0:T(8,128)(2,1)S(1)}, bf16[80,768]{1,0:T(8,128)(2,1)S(1)}, u32[]{:S(2)}, u32[]{:S(2)}) collective-permute-start(bf16[80,768]{1,0:T(8,128)(2,1)S(1)} %get-tuple-element.54), channel_id=1, source_target_pairs={{0,16},{8,24},{16,0},{24,8},{1,17},{9,25},{17,1},{25,9},{2,18},{10... | collective-permute-start | bytes 368648 | tf_op jit(solution)/shard_map/ppermute | solution.py:352
  53.6 5.1 %collective-permute-start.7 = (bf16[80,768]{1,0:T(8,128)(2,1)S(1)}, bf16[80,768]{1,0:T(8,128)(2,1)S(1)}, u32[]{:S(2)}, u32[]{:S(2)}) collective-permute-start(bf16[80,768]{1,0:T(8,128)(2,1)S(1)} %get-tuple-element.55), channel_id=1, source_target_pairs={{0,24},{8,16},{16,8},{24,0},{1,25},{9,17},{17,9},{25,1},{2,26},{10... | collective-permute-start | bytes 368648 | tf_op jit(solution)/shard_map/ppermute | solution.py:352
  58.8 27.1 %collective-permute-start.12 = (bf16[80,3584]{1,0:T(8,128)(2,1)S(1)}, bf16[80,3584]{1,0:T(8,128)(2,1)S(1)}, u32[]{:S(2)}, u32[]{:S(2)}) collective-permute-start(bf16[80,3584]{1,0:T(8,128)(2,1)S(1)} %shard_map.112.refs_1_), channel_id=1, source_target_pairs={{0,6},{1,7},{2,4},{3,5},{4,2},{5,3},{6,0},{7,1},{8,14},{9,15},{10,... | collective-permute-start | bytes 1720328 | tf_op jit(solution)/shard_map/ppermute | solution.py:349
  61.7 25.5 %collective-permute-start.14 = (bf16[80,3584]{1,0:T(8,128)(2,1)S(1)}, bf16[80,3584]{1,0:T(8,128)(2,1)S(1)}, u32[]{:S(2)}, u32[]{:S(2)}) collective-permute-start(bf16[80,3584]{1,0:T(8,128)(2,1)S(1)} %shard_map.113.refs_6_), channel_id=1, source_target_pairs={{0,3},{1,2},{2,1},{3,0},{4,7},{5,6},{6,5},{7,4},{8,11},{9,10},{10,... | collective-permute-start | bytes 1720328 | tf_op jit(solution)/shard_map/ppermute | solution.py:349
  63.0 6.9 %collective-permute-start.20 = (bf16[80,768]{1,0:T(8,128)(2,1)S(1)}, bf16[80,768]{1,0:T(8,128)(2,1)S(1)}, u32[]{:S(2)}, u32[]{:S(2)}) collective-permute-start(bf16[80,768]{1,0:T(8,128)(2,1)S(1)} %shard_map.111.refs_1_.refs_5_), channel_id=1, source_target_pairs={{0,24},{8,16},{16,8},{24,0},{1,25},{9,17},{17,9},{25,1},{2,26},{10... | collective-permute-start | bytes 368648 | tf_op jit(solution)/shard_map/ppermute | solution.py:352
  65.2 6.6 %collective-permute-start.19 = (bf16[80,768]{1,0:T(8,128)(2,1)S(1)}, bf16[80,768]{1,0:T(8,128)(2,1)S(1)}, u32[]{:S(2)}, u32[]{:S(2)}) collective-permute-start(bf16[80,768]{1,0:T(8,128)(2,1)S(1)} %shard_map.111.refs_1_.refs_5_), channel_id=1, source_target_pairs={{0,16},{8,24},{16,0},{24,8},{1,17},{9,25},{17,1},{25,9},{2,18},{10... | collective-permute-start | bytes 368648 | tf_op jit(solution)/shard_map/ppermute | solution.py:352
  65.4 7.6 %collective-permute-start.18 = (bf16[80,768]{1,0:T(8,128)(2,1)S(1)}, bf16[80,768]{1,0:T(8,128)(2,1)S(1)}, u32[]{:S(2)}, u32[]{:S(2)}) collective-permute-start(bf16[80,768]{1,0:T(8,128)(2,1)S(1)} %shard_map.111.refs_1_.refs_5_), channel_id=1, source_target_pairs={{0,8},{8,0},{16,24},{24,16},{1,9},{9,1},{17,25},{25,17},{2,10},{10... | collective-permute-start | bytes 368648 | tf_op jit(solution)/shard_map/ppermute | solution.py:352
  69.9 7.6 %collective-permute-start.15 = (bf16[160,768]{1,0:T(8,128)(2,1)S(1)}, bf16[160,768]{1,0:T(8,128)(2,1)S(1)}, u32[]{:S(2)}, u32[]{:S(2)}) collective-permute-start(bf16[160,768]{1,0:T(8,128)(2,1)S(1)} %get-tuple-element.60), channel_id=1, source_target_pairs={{0,8},{8,0},{16,24},{24,16},{1,9},{9,1},{17,25},{25,17},{2,10},{10... | collective-permute-start | bytes 737288 | tf_op jit(solution)/shard_map/ppermute | solution.py:352
  71.8 7.6 %collective-permute-start.16 = (bf16[160,768]{1,0:T(8,128)(2,1)S(1)}, bf16[160,768]{1,0:T(8,128)(2,1)S(1)}, u32[]{:S(2)}, u32[]{:S(2)}) collective-permute-start(bf16[160,768]{1,0:T(8,128)(2,1)S(1)} %get-tuple-element.61), channel_id=1, source_target_pairs={{0,16},{8,24},{16,0},{24,8},{1,17},{9,25},{17,1},{25,9},{2,18},{10... | collective-permute-start | bytes 737288 | tf_op jit(solution)/shard_map/ppermute | solution.py:352
  73.0 9.3 %collective-permute-start.17 = (bf16[160,768]{1,0:T(8,128)(2,1)S(1)}, bf16[160,768]{1,0:T(8,128)(2,1)S(1)}, u32[]{:S(2)}, u32[]{:S(2)}) collective-permute-start(bf16[160,768]{1,0:T(8,128)(2,1)S(1)} %get-tuple-element.62), channel_id=1, source_target_pairs={{0,24},{8,16},{16,8},{24,0},{1,25},{9,17},{17,9},{25,1},{2,26},{10... | collective-permute-start | bytes 737288 | tf_op jit(solution)/shard_map/ppermute | solution.py:352
  82.5 13.8 %collective-permute-start.26 = (bf16[160,768]{1,0:T(8,128)(2,1)S(1)}, bf16[160,768]{1,0:T(8,128)(2,1)S(1)}, u32[]{:S(2)}, u32[]{:S(2)}) collective-permute-start(bf16[160,768]{1,0:T(8,128)(2,1)S(1)} %shard_map.116.refs_1_.refs_9_), channel_id=1, source_target_pairs={{0,24},{8,16},{16,8},{24,0},{1,25},{9,17},{17,9},{25,1},{2,26},{10... | collective-permute-start | bytes 737288 | tf_op jit(solution)/shard_map/ppermute | solution.py:352
  83.8 12.7 %collective-permute-start.25 = (bf16[160,768]{1,0:T(8,128)(2,1)S(1)}, bf16[160,768]{1,0:T(8,128)(2,1)S(1)}, u32[]{:S(2)}, u32[]{:S(2)}) collective-permute-start(bf16[160,768]{1,0:T(8,128)(2,1)S(1)} %shard_map.116.refs_1_.refs_9_), channel_id=1, source_target_pairs={{0,16},{8,24},{16,0},{24,8},{1,17},{9,25},{17,1},{25,9},{2,18},{10... | collective-permute-start | bytes 737288 | tf_op jit(solution)/shard_map/ppermute | solution.py:352
  87.2 28.8 %collective-permute-start.30 = (bf16[80,3584]{1,0:T(8,128)(2,1)S(1)}, bf16[80,3584]{1,0:T(8,128)(2,1)S(1)}, u32[]{:S(2)}, u32[]{:S(2)}) collective-permute-start(bf16[80,3584]{1,0:T(8,128)(2,1)S(1)} %shard_map.117.refs_6_), channel_id=1, source_target_pairs={{0,7},{1,6},{2,5},{3,4},{4,3},{5,2},{6,1},{7,0},{8,15},{9,14},{10,... | collective-permute-start | bytes 1720328 | tf_op jit(solution)/shard_map/ppermute | solution.py:349
  90.5 7.9 %collective-permute-start.24 = (bf16[160,768]{1,0:T(8,128)(2,1)S(1)}, bf16[160,768]{1,0:T(8,128)(2,1)S(1)}, u32[]{:S(2)}, u32[]{:S(2)}) collective-permute-start(bf16[160,768]{1,0:T(8,128)(2,1)S(1)} %shard_map.116.refs_1_.refs_9_), channel_id=1, source_target_pairs={{0,8},{8,0},{16,24},{24,16},{1,9},{9,1},{17,25},{25,17},{2,10},{10... | collective-permute-start | bytes 737288 | tf_op jit(solution)/shard_map/ppermute | solution.py:352
  95.0 8.7 %collective-permute-start.21 = (bf16[160,768]{1,0:T(8,128)(2,1)S(1)}, bf16[160,768]{1,0:T(8,128)(2,1)S(1)}, u32[]{:S(2)}, u32[]{:S(2)}) collective-permute-start(bf16[160,768]{1,0:T(8,128)(2,1)S(1)} %get-tuple-element.64), channel_id=1, source_target_pairs={{0,8},{8,0},{16,24},{24,16},{1,9},{9,1},{17,25},{25,17},{2,10},{10... | collective-permute-start | bytes 737288 | tf_op jit(solution)/shard_map/ppermute | solution.py:352
  96.3 7.8 %collective-permute-start.22 = (bf16[160,768]{1,0:T(8,128)(2,1)S(1)}, bf16[160,768]{1,0:T(8,128)(2,1)S(1)}, u32[]{:S(2)}, u32[]{:S(2)}) collective-permute-start(bf16[160,768]{1,0:T(8,128)(2,1)S(1)} %get-tuple-element.65), channel_id=1, source_target_pairs={{0,16},{8,24},{16,0},{24,8},{1,17},{9,25},{17,1},{25,9},{2,18},{10... | collective-permute-start | bytes 737288 | tf_op jit(solution)/shard_map/ppermute | solution.py:352
  96.4 12.2 %collective-permute-start.23 = (bf16[160,768]{1,0:T(8,128)(2,1)S(1)}, bf16[160,768]{1,0:T(8,128)(2,1)S(1)}, u32[]{:S(2)}, u32[]{:S(2)}) collective-permute-start(bf16[160,768]{1,0:T(8,128)(2,1)S(1)} %get-tuple-element.66), channel_id=1, source_target_pairs={{0,24},{8,16},{16,8},{24,0},{1,25},{9,17},{17,9},{25,1},{2,26},{10... | collective-permute-start | bytes 737288 | tf_op jit(solution)/shard_map/ppermute | solution.py:352
  98.5 12.7 %collective-permute-start.32 = (bf16[80,1792]{1,0:T(8,128)(2,1)S(1)}, bf16[80,1792]{1,0:T(8,128)(2,1)S(1)}, u32[]{:S(2)}, u32[]{:S(2)}) collective-permute-start(bf16[80,1792]{1,0:T(8,128)(2,1)S(1)} %get-tuple-element.69), channel_id=1, source_target_pairs={{0,1},{1,0},{2,3},{3,2},{4,5},{5,4},{6,7},{7,6},{8,9},{9,8},{10,11... | collective-permute-start | bytes 860168 | tf_op jit(solution)/shard_map/ppermute | solution.py:349
  103.7 8.2 %collective-permute-start.31 = (bf16[80,1792]{1,0:T(8,128)(2,1)S(1)}, bf16[80,1792]{1,0:T(8,128)(2,1)S(1)}, u32[]{:S(2)}, u32[]{:S(2)}) collective-permute-start(bf16[80,1792]{1,0:T(8,128)(2,1)S(1)} %get-tuple-element.68), channel_id=1, source_target_pairs={{0,2},{1,3},{2,0},{3,1},{4,6},{5,7},{6,4},{7,5},{8,10},{9,11},{10,... | collective-permute-start | bytes 860168 | tf_op jit(solution)/shard_map/ppermute | solution.py:349
  108.8 12.8 %collective-permute-start.29 = (bf16[160,768]{1,0:T(8,128)(2,1)S(1)}, bf16[160,768]{1,0:T(8,128)(2,1)S(1)}, u32[]{:S(2)}, u32[]{:S(2)}) collective-permute-start(bf16[160,768]{1,0:T(8,128)(2,1)S(1)} %shard_map.120.refs_1_.refs_13_), channel_id=1, source_target_pairs={{0,24},{8,16},{16,8},{24,0},{1,25},{9,17},{17,9},{25,1},{2,26},{10... | collective-permute-start | bytes 737288 | tf_op jit(solution)/shard_map/ppermute | solution.py:352
  110.9 12.0 %collective-permute-start.28 = (bf16[160,768]{1,0:T(8,128)(2,1)S(1)}, bf16[160,768]{1,0:T(8,128)(2,1)S(1)}, u32[]{:S(2)}, u32[]{:S(2)}) collective-permute-start(bf16[160,768]{1,0:T(8,128)(2,1)S(1)} %shard_map.120.refs_1_.refs_13_), channel_id=1, source_target_pairs={{0,16},{8,24},{16,0},{24,8},{1,17},{9,25},{17,1},{25,9},{2,18},{10... | collective-permute-start | bytes 737288 | tf_op jit(solution)/shard_map/ppermute | solution.py:352
  116.0 12.2 %collective-permute-start.36 = (bf16[80,1792]{1,0:T(8,128)(2,1)S(1)}, bf16[80,1792]{1,0:T(8,128)(2,1)S(1)}, u32[]{:S(2)}, u32[]{:S(2)}) collective-permute-start(bf16[80,1792]{1,0:T(8,128)(2,1)S(1)} %shard_map.121.refs_5_), channel_id=1, source_target_pairs={{0,4},{1,5},{2,6},{3,7},{4,0},{5,1},{6,2},{7,3},{8,12},{9,13},{10,... | collective-permute-start | bytes 860168 | tf_op jit(solution)/shard_map/ppermute | solution.py:349
  116.0 7.8 %collective-permute-start.27 = (bf16[160,768]{1,0:T(8,128)(2,1)S(1)}, bf16[160,768]{1,0:T(8,128)(2,1)S(1)}, u32[]{:S(2)}, u32[]{:S(2)}) collective-permute-start(bf16[160,768]{1,0:T(8,128)(2,1)S(1)} %shard_map.120.refs_1_.refs_13_), channel_id=1, source_target_pairs={{0,8},{8,0},{16,24},{24,16},{1,9},{9,1},{17,25},{25,17},{2,10},{10... | collective-permute-start | bytes 737288 | tf_op jit(solution)/shard_map/ppermute | solution.py:352
  120.2 8.0 %collective-permute-start.33 = (bf16[80,768]{1,0:T(8,128)(2,1)S(1)}, bf16[80,768]{1,0:T(8,128)(2,1)S(1)}, u32[]{:S(2)}, u32[]{:S(2)}) collective-permute-start(bf16[80,768]{1,0:T(8,128)(2,1)S(1)} %get-tuple-element.72), channel_id=1, source_target_pairs={{0,8},{8,0},{16,24},{24,16},{1,9},{9,1},{17,25},{25,17},{2,10},{10... | collective-permute-start | bytes 368648 | tf_op jit(solution)/shard_map/ppermute | solution.py:352
  121.5 6.7 %collective-permute-start.34 = (bf16[80,768]{1,0:T(8,128)(2,1)S(1)}, bf16[80,768]{1,0:T(8,128)(2,1)S(1)}, u32[]{:S(2)}, u32[]{:S(2)}) collective-permute-start(bf16[80,768]{1,0:T(8,128)(2,1)S(1)} %get-tuple-element.73), channel_id=1, source_target_pairs={{0,16},{8,24},{16,0},{24,8},{1,17},{9,25},{17,1},{25,9},{2,18},{10... | collective-permute-start | bytes 368648 | tf_op jit(solution)/shard_map/ppermute | solution.py:352
  122.9 5.4 %collective-permute-start.35 = (bf16[80,768]{1,0:T(8,128)(2,1)S(1)}, bf16[80,768]{1,0:T(8,128)(2,1)S(1)}, u32[]{:S(2)}, u32[]{:S(2)}) collective-permute-start(bf16[80,768]{1,0:T(8,128)(2,1)S(1)} %get-tuple-element.74), channel_id=1, source_target_pairs={{0,24},{8,16},{16,8},{24,0},{1,25},{9,17},{17,9},{25,1},{2,26},{10... | collective-permute-start | bytes 368648 | tf_op jit(solution)/shard_map/ppermute | solution.py:352
  128.4 9.3 %collective-permute-start.39 = (bf16[80,768]{1,0:T(8,128)(2,1)S(1)}, bf16[80,768]{1,0:T(8,128)(2,1)S(1)}, u32[]{:S(2)}, u32[]{:S(2)}) collective-permute-start(bf16[80,768]{1,0:T(8,128)(2,1)S(1)} %shard_map.126.refs_1_.refs_7_.refs_17_), channel_id=1, source_target_pairs={{0,24},{8,16},{16,8},{24,0},{1,25},{9,17},{17,9},{25,1},{2,26},{10... | collective-permute-start | bytes 368648 | tf_op jit(solution)/shard_map/ppermute | solution.py:352
  129.9 7.8 %collective-permute-start.38 = (bf16[80,768]{1,0:T(8,128)(2,1)S(1)}, bf16[80,768]{1,0:T(8,128)(2,1)S(1)}, u32[]{:S(2)}, u32[]{:S(2)}) collective-permute-start(bf16[80,768]{1,0:T(8,128)(2,1)S(1)} %shard_map.126.refs_1_.refs_7_.refs_17_), channel_id=1, source_target_pairs={{0,16},{8,24},{16,0},{24,8},{1,17},{9,25},{17,1},{25,9},{2,18},{10... | collective-permute-start | bytes 368648 | tf_op jit(solution)/shard_map/ppermute | solution.py:352
  130.8 6.9 %collective-permute-start.37 = (bf16[80,768]{1,0:T(8,128)(2,1)S(1)}, bf16[80,768]{1,0:T(8,128)(2,1)S(1)}, u32[]{:S(2)}, u32[]{:S(2)}) collective-permute-start(bf16[80,768]{1,0:T(8,128)(2,1)S(1)} %shard_map.126.refs_1_.refs_7_.refs_17_), channel_id=1, source_target_pairs={{0,8},{8,0},{16,24},{24,16},{1,9},{9,1},{17,25},{25,17},{2,10},{10... | collective-permute-start | bytes 368648 | tf_op jit(solution)/shard_map/ppermute | solution.py:352
  131.2 23.3 %collective-permute-start.43 = (bf16[80,1792]{1,0:T(8,128)(2,1)S(1)}, bf16[80,1792]{1,0:T(8,128)(2,1)S(1)}, u32[]{:S(2)}, u32[]{:S(2)}) collective-permute-start(bf16[80,1792]{1,0:T(8,128)(2,1)S(1)} %shard_map.125.refs_4_), channel_id=1, source_target_pairs={{0,6},{1,7},{2,4},{3,5},{4,2},{5,3},{6,0},{7,1},{8,14},{9,15},{10,... | collective-permute-start | bytes 860168 | tf_op jit(solution)/shard_map/ppermute | solution.py:349
  132.1 28.6 %collective-permute-start.42 = (bf16[80,1792]{1,0:T(8,128)(2,1)S(1)}, bf16[80,1792]{1,0:T(8,128)(2,1)S(1)}, u32[]{:S(2)}, u32[]{:S(2)}) collective-permute-start(bf16[80,1792]{1,0:T(8,128)(2,1)S(1)} %shard_map.124.refs_1_), channel_id=1, source_target_pairs={{0,5},{1,4},{2,7},{3,6},{4,1},{5,0},{6,3},{7,2},{8,13},{9,12},{10,... | collective-permute-start | bytes 860168 | tf_op jit(solution)/shard_map/ppermute | solution.py:349
  141.1 21.6 %collective-permute-start.40 = (bf16[80,1792]{1,0:T(8,128)(2,1)S(1)}, bf16[80,1792]{1,0:T(8,128)(2,1)S(1)}, u32[]{:S(2)}, u32[]{:S(2)}) collective-permute-start(bf16[80,1792]{1,0:T(8,128)(2,1)S(1)} %shard_map.128.refs_31_), channel_id=1, source_target_pairs={{0,3},{1,2},{2,1},{3,0},{4,7},{5,6},{6,5},{7,4},{8,11},{9,10},{10,... | collective-permute-start | bytes 860168 | tf_op jit(solution)/shard_map/ppermute | solution.py:349
  143.0 27.5 %collective-permute-start.41 = (bf16[80,1792]{1,0:T(8,128)(2,1)S(1)}, bf16[80,1792]{1,0:T(8,128)(2,1)S(1)}, u32[]{:S(2)}, u32[]{:S(2)}) collective-permute-start(bf16[80,1792]{1,0:T(8,128)(2,1)S(1)} %shard_map.127.refs_1_), channel_id=1, source_target_pairs={{0,7},{1,6},{2,5},{3,4},{4,3},{5,2},{6,1},{7,0},{8,15},{9,14},{10,... | collective-permute-start | bytes 860168 | tf_op jit(solution)/shard_map/ppermute | solution.py:349
  144.1 16.6 %copy-start.14 = (s32[1,512]{1,0:T(1,128)S(1)}, s32[1,512]{1,0:T(1,128)}, u32[]{:S(2)}) copy-start(s32[1,512]{1,0:T(1,128)} %get-tuple-element.41.refs_1_) | copy-start | bytes 6148
  (11 other events, 75.0 us)

commit v5 on v4

--- a/solution.py
+++ b/solution.py
@@ -138,6 +138,18 @@
     )
 
 
+def join_body(first, second, out):
+    cap = first.shape[0]
+    out[:cap, :] = first[...]
+    out[cap:, :] = second[...]
+
+
+def join(first, second, deps):
+    cap, s = first.shape
+    vmem = pl.BlockSpec(memory_space=pltpu.VMEM)
+    return call(join_body, [first, second], deps, jax.ShapeDtypeStruct((2 * cap, s), bf16), [vmem] * 2, vmem)
+
+
 def forward_body(cap, nb, ndp, dp_ref, *refs):
     blocks, (wg, wu, wd), outs, rows = refs[:nb], refs[nb : nb + 3], refs[nb + 3 : -1], refs[-1]
     d = pl.program_id(0)
@@ -315,17 +327,19 @@
 
 def combine(cap, offs, me, target, backs, prev, deps):
     t = target.shape[1]
-    s = backs[0].shape[1]
+    s = backs[0][0].shape[1]
     nb = len(offs)
     wide = s // 2
     col = pl.BlockSpec((t, wide), lambda c, i: (0, c))
     extra = [] if prev is None else [prev]
     return call(
         functools.partial(combine_body, cap, offs, prev is not None),
-        [me, target, *backs, *extra],
+        [me, target, *[v for v, _ in backs], *extra],
         deps,
         jax.ShapeDtypeStruct((t, s), bf16),
-        [whole((1, t))] + [pl.BlockSpec((cap, wide), lambda c, i: (0, c))] * nb + [col] * len(extra),
+        [whole((1, t))]
+        + [pl.BlockSpec((cap, wide), lambda c, i, part=part: (part, c)) for _, part in backs]
+        + [col] * len(extra),
         col,
         grid=(s // wide,),
         scalars=1,
@@ -353,7 +367,7 @@
 
     far, near = grouping(n)
     chunks = [near[0], far[0], far[1] + near[1], far[2] + near[2], far[3]]
-    send, got, ready, back, pieces, parts = {}, {}, {}, {}, {}, {}
+    send, got, ready, back, pieces, parts, passed = {}, {}, {}, {}, {}, {}, {}
     mark = []
 
     def push(offs, deps):
@@ -369,7 +383,18 @@
             if deps is not None:
                 rows = after(rows, mark + deps)
                 mark[:] = [rows]
-            back[k] = swap_expert(rows, k) if k else rows
+            back[k] = (swap_expert(rows, k) if k else rows, 0)
+
+    def relay(offs, others):
+        for k, j in zip(offs, others):
+            passed[j] = swap_expert(ready[j], k ^ j)
+
+    def give_both(offs, others, deps):
+        for k, j in zip(offs, others):
+            rows = join(ready[k], passed[j], mark + deps)
+            mark[:] = [rows]
+            both = swap_expert(rows, k)
+            back[k], back[j] = (both, 0), (both, 1)
 
     def fwd(c):
         own, *others = forward(cap, ndp, dp_idx, [got[k] for k in chunks[c]], wg, wu, wd, mark)
@@ -415,16 +440,17 @@
     push(far[3], gotten(far[2] + near[2]))
     fwd(3)
     bwd(2)
-    give_back(near[1], None)
+    relay(far[0], far[1])
     act(3)
-    give_back(far[0], gotten(far[3]) + [back[k] for k in near[1] + near[0][1:]])
+    give_both(far[0], far[1], gotten(far[3]))
     fwd(4)
     bwd(3)
-    give_back(far[1] + far[2], [back[k] for k in far[0]])
+    give_back(far[2], None)
     act(4)
     bwd(4)
     give_back(far[3], None)
-    give_back(near[2], [])
+    give_back(near[1], None)
+    give_back(near[2], None)
     order = range(len(chunks))
     flat = [k for c in order for k in chunks[c]]
     new_down, new_moment, token = down(
@@ -439,7 +465,7 @@
         mark,
     )
     mark[:] = [token]
-    tail = near[2] + far[3]
+    tail = near[1] + near[2] + far[2] + far[3]
     early = [k for k in flat if k not in tail]
     part = combine(cap, early, me, target, [back[k] for k in early], None, mark)
     grad_tokens = combine(cap, tail, me, target, [back[k] for k in tail], part, [])

time: 174 us -> 170 us (0.977)
  waiting for transfers between devices: 51.6 us -> 47.9 us
  starting transfers between devices: 49.8 us -> 48 us
    ppermute x14, waiting for transfers between devices: 30.2 us -> 22.6 us  [swap_expert(): return lax.ppermute(v, 'expert', [(i, i ^ k) for i in range(n)])]
    ppermute x30, waiting for transfers between devices: 21.4 us -> 25.3 us  [swap_dp(): return lax.ppermute(v, 'dp', [(i, i ^ k) for i in range(ndp)])]
    ppermute x14, starting transfers between devices: 21.2 us -> 18.5 us  [swap_expert(): return lax.ppermute(v, 'expert', [(i, i ^ k) for i in range(n)])]
    pallas_call x29 -> x26, Pallas kernels: 63.2 us -> 63.8 us  [call(): pl.pallas_call(skipping(body, len(operands), len(deps)), out_shape=out_sh...]
  transfers between devices with their start and end apart: 44 -> 44, of which waited for: 22 -> 21; matrix products, arithmetic and copies ran while one was open for 0% -> 0% of each run, Pallas kernels for 33% -> 34%
where the time goes in v5:
time: 170 us; the launch traced here: 168 us
  Pallas kernels  63.8 us (38%)
  starting transfers between devices  48 us (28%)
  waiting for transfers between devices  47.9 us (28%)
  local copies, waits for them, and re-layouts  7.21 us (4%)
    pallas_call x26, Pallas kernels, call(): pl.pallas_call(skipping(body, len(operands), len(deps)), out_shape=out_sh...  63.8 us
    ppermute x30, starting transfers between devices, swap_dp(): return lax.ppermute(v, 'dp', [(i, i ^ k) for i in range(ndp)])  29.5 us
    ppermute x30, waiting for transfers between devices, swap_dp(): return lax.ppermute(v, 'dp', [(i, i ^ k) for i in range(ndp)])  25.3 us
    ppermute x14, waiting for transfers between devices, swap_expert(): return lax.ppermute(v, 'expert', [(i, i ^ k) for i in range(n)])  22.6 us
    ppermute x14, starting transfers between devices, swap_expert(): return lax.ppermute(v, 'expert', [(i, i ^ k) for i in range(n)])  18.5 us
    unnamed x30, local copies, waits for them, and re-layouts  7.21 us
  transfers between devices with their start and end apart: 44, of which 21 were waited for; matrix products, arithmetic and copies ran while one was open for 0% of the time, Pallas kernels for 34%

profile of v5, /device:TPU:9, one launch (start us, length us, event | category | flops | bytes accessed | tf_op | source)
XLA Modules:
  0.0 167.9 jit_solution(4193674893217752569)
XLA Ops:
  0.6 4.1 %shard_map.103 = (s32[1,512]{1,0:T(1,128)}, bf16[80,3584]{1,0:T(8,128)(2,1)}, bf16[80,3584]{1,0:T(8,128)(2,1)}, bf16[80,3584]{1,0:T(8,128)(2,1)}) custom-call(s32[1]{0:T(128)} %bitcast.refs_0_, s32[1,512]{1,0:T(1,128)} %bitcast.37, s32[1,512]{1,0:T(1,128)} %bitcast.39, bf16[512,1792]{1,0:T(8,128)(2,1)} %refs_3_.3, bf16[512,1792]{1,0:T(8,128)(2,1)} %refs_4_.3), custom_call_target="tpu_custom_call" | custom-call | tf_op jit(solution)/shard_map/pallas_call | solution.py:40
  5.5 2.3 %collective-permute-start.2 = (bf16[80,3584]{1,0:T(8,128)(2,1)}, bf16[80,3584]{1,0:T(8,128)(2,1)S(1)}, u32[]{:S(2)}, u32[]{:S(2)}) collective-permute-start(bf16[80,3584]{1,0:T(8,128)(2,1)} %get-tuple-element.42.refs_5_), channel_id=1, source_target_pairs={{0,4},{1,5},{2,6},{3,7},{4,0},{5,1},{6,2},{7,3},{8,12},{9,13},{10,... | collective-permute-start | bytes 1720328 | tf_op jit(solution)/shard_map/ppermute | solution.py:363
  7.8 5.1 %shard_map.104 = (s32[1,512]{1,0:T(1,128)}, bf16[80,3584]{1,0:T(8,128)(2,1)}, bf16[80,3584]{1,0:T(8,128)(2,1)}, bf16[80,3584]{1,0:T(8,128)(2,1)}, bf16[80,3584]{1,0:T(8,128)(2,1)}, /*index=5*/bf16[80,3584]{1,0:T(8,128)(2,1)}) custom-call(s32[1]{0:T(128)} %bitcast.refs_0_, s32[1,512]{1,0:T(1,128)} %bitcast.38, s32[1,512]{1,0:T(1,128)} %bitcast.40, ...), custom_call_target="tpu_custom_call" | custom-call | tf_op jit(solution)/shard_map/pallas_call | solution.py:40
  13.0 2.0 %copy-done = bf16[1,1792,1024]{2,1,0:T(8,128)(2,1)S(1)} copy-done((bf16[1,1792,1024]{2,1,0:T(8,128)(2,1)S(1)}, bf16[1,1792,1024]{2,1,0:T(8,128)(2,1)}, u32[]{:S(2)}) %copy-start) | copy-done | bytes 3670040
  15.0 2.0 %copy-done.2 = bf16[1,1792,1024]{2,1,0:T(8,128)(2,1)S(1)} copy-done((bf16[1,1792,1024]{2,1,0:T(8,128)(2,1)S(1)}, bf16[1,1792,1024]{2,1,0:T(8,128)(2,1)}, u32[]{:S(2)}) %copy-start.2) | copy-done | bytes 3670040
  17.0 2.0 %copy-done.4 = bf16[1,1024,1792]{2,1,0:T(8,128)(2,1)S(1)} copy-done((bf16[1,1024,1792]{2,1,0:T(8,128)(2,1)S(1)}, bf16[1,1024,1792]{2,1,0:T(8,128)(2,1)}, u32[]{:S(2)}) %copy-start.4) | copy-done | bytes 3670040
  20.1 4.4 %shard_map.105 = (bf16[160,768]{1,0:T(8,128)(2,1)S(1)}, bf16[160,768]{1,0:T(8,128)(2,1)S(1)}, bf16[160,768]{1,0:T(8,128)(2,1)S(1)}, bf16[160,768]{1,0:T(8,128)(2,1)S(1)}) custom-call(s32[1]{0:T(128)} %bitcast.3.refs_0_, bf16[80,3584]{1,0:T(8,128)(2,1)S(1)} %copy-done.9, bf16[80,3584]{1,0:T(8,128)(2,1)S(1)} %collective-permute-done.refs_2_.refs_22_, ...), custom_call_target="tpu_custom_call" | custom-call | tf_op jit(solution)/shard_map/pallas_call | solution.py:40
  24.6 1.3 collective-permute-start.4
  27.3 5.7 %collective-permute-done.2.refs_2_.refs_1_.refs_23_ = bf16[80,3584]{1,0:T(8,128)(2,1)S(1)} collective-permute-done((bf16[80,3584]{1,0:T(8,128)(2,1)}, bf16[80,3584]{1,0:T(8,128)(2,1)S(1)}, u32[]{:S(2)}, u32[]{:S(2)}) %collective-permute-start.2) | collective-permute-done | bytes 573472 | tf_op jit(solution)/shard_map/ppermute | solution.py:363
  33.7 2.6 %collective-permute-start.1 = (bf16[80,3584]{1,0:T(8,128)(2,1)S(1)}, bf16[80,3584]{1,0:T(8,128)(2,1)S(1)}, u32[]{:S(2)}, u32[]{:S(2)}) collective-permute-start(bf16[80,3584]{1,0:T(8,128)(2,1)S(1)} %shard_map.106.refs_1_), channel_id=1, source_target_pairs={{0,5},{1,4},{2,7},{3,6},{4,1},{5,0},{6,3},{7,2},{8,13},{9,12},{10,... | collective-permute-start | bytes 1720328 | tf_op jit(solution)/shard_map/ppermute | solution.py:363
  36.4 1.7 %collective-permute-done.6.refs_3_ = bf16[160,768]{1,0:T(8,128)(2,1)S(1)} collective-permute-done((bf16[160,768]{1,0:T(8,128)(2,1)S(1)}, bf16[160,768]{1,0:T(8,128)(2,1)S(1)}, u32[]{:S(2)}, u32[]{:S(2)}) %collective-permute-start.6) | collective-permute-done | bytes 245792 | tf_op jit(solution)/shard_map/ppermute | solution.py:366
  41.1 4.0 %shard_map.109 = (bf16[80,768]{1,0:T(8,128)(2,1)S(1)}, bf16[80,768]{1,0:T(8,128)(2,1)S(1)}, bf16[80,768]{1,0:T(8,128)(2,1)S(1)}, bf16[80,768]{1,0:T(8,128)(2,1)S(1)}) custom-call(s32[1]{0:T(128)} %bitcast.3.refs_0_, bf16[80,3584]{1,0:T(8,128)(2,1)S(1)} %collective-permute-done.2.refs_2_.refs_1_.refs_23_, bf16[1792,1024]{1,0:T(8,128)(2,1)S(1)} %bitcast.11, ...), custom_call_target="tpu_custom_call" | custom-call | tf_op jit(solution)/shard_map/pallas_call | solution.py:40
  45.4 1.4 collective-permute-start.7
  46.8 5.7 %collective-permute-done.11.refs_3_ = bf16[160,768]{1,0:T(8,128)(2,1)S(1)} collective-permute-done((bf16[160,768]{1,0:T(8,128)(2,1)S(1)}, bf16[160,768]{1,0:T(8,128)(2,1)S(1)}, u32[]{:S(2)}, u32[]{:S(2)}) %collective-permute-start.11) | collective-permute-done | bytes 245792 | tf_op jit(solution)/shard_map/ppermute | solution.py:366
  54.8 3.7 %shard_map.110 = (bf16[80,1792]{1,0:T(8,128)(2,1)S(1)}, bf16[80,1792]{1,0:T(8,128)(2,1)S(1)}) custom-call(s32[1]{0:T(128)} %bitcast.3.refs_0_, bf16[160,768]{1,0:T(8,128)(2,1)S(1)} %shard_map.108.refs_5_.refs_1_, bf16[160,768]{1,0:T(8,128)(2,1)S(1)} %collective-permute-done.10.refs_2_, bf16[160,768]{1,0:T(8,128)(2,1)S(1)} %collective-permute-done.11.refs_3_, ...), custom_call_target="tpu_custom_call" | custom-call | tf_op jit(solution)/shard_map/pallas_call | solution.py:40
  58.9 2.8 %collective-permute-done.1.refs_2_.refs_1_.refs_24_ = bf16[80,3584]{1,0:T(8,128)(2,1)S(1)} collective-permute-done((bf16[80,3584]{1,0:T(8,128)(2,1)S(1)}, bf16[80,3584]{1,0:T(8,128)(2,1)S(1)}, u32[]{:S(2)}, u32[]{:S(2)}) %collective-permute-start.1) | collective-permute-done | bytes 573472 | tf_op jit(solution)/shard_map/ppermute | solution.py:363
  61.7 1.3 collective-permute-start.23
  63.0 2.2 %collective-permute-start.18 = (bf16[80,768]{1,0:T(8,128)(2,1)S(1)}, bf16[80,768]{1,0:T(8,128)(2,1)S(1)}, u32[]{:S(2)}, u32[]{:S(2)}) collective-permute-start(bf16[80,768]{1,0:T(8,128)(2,1)S(1)} %shard_map.111.refs_1_.refs_5_), channel_id=1, source_target_pairs={{0,24},{8,16},{16,8},{24,0},{1,25},{9,17},{17,9},{25,1},{2,26},{10... | collective-permute-start | bytes 368648 | tf_op jit(solution)/shard_map/ppermute | solution.py:366
  65.7 4.2 %shard_map.114 = (bf16[160,768]{1,0:T(8,128)(2,1)S(1)}, bf16[160,768]{1,0:T(8,128)(2,1)S(1)}, bf16[160,768]{1,0:T(8,128)(2,1)S(1)}, bf16[160,768]{1,0:T(8,128)(2,1)S(1)}) custom-call(s32[1]{0:T(128)} %bitcast.3.refs_0_, bf16[80,3584]{1,0:T(8,128)(2,1)S(1)} %collective-permute-done.1.refs_2_.refs_1_.refs_24_, ...), custom_call_target="tpu_custom_call" | custom-call | tf_op jit(solution)/shard_map/pallas_call | solution.py:40
  69.9 1.3 collective-permute-start.13
  74.2 3.3 %shard_map.115.refs_4_.refs_0_ = bf16[80,1792]{1,0:T(8,128)(2,1)S(1)} custom-call(s32[1]{0:T(128)} %bitcast.3.refs_0_, bf16[80,768]{1,0:T(8,128)(2,1)S(1)} %shard_map.111.refs_1_.refs_5_, bf16[80,768]{1,0:T(8,128)(2,1)S(1)} %collective-permute-done.16.refs_2_.refs_6_, bf16[80,768]{1,0:T(8,128)(2,1)S(1)} %collective-permute-done.17.refs_3_.refs_7_, ...), custom_call_target="tpu_custom_call" | custom-call | tf_op jit(solution)/shard_map/pallas_call | solution.py:40
  77.5 1.9 %collective-permute-done.14.refs_2_ = bf16[160,768]{1,0:T(8,128)(2,1)S(1)} collective-permute-done((bf16[160,768]{1,0:T(8,128)(2,1)S(1)}, bf16[160,768]{1,0:T(8,128)(2,1)S(1)}, u32[]{:S(2)}, u32[]{:S(2)}) %collective-permute-start.14) | collective-permute-done | bytes 245792 | tf_op jit(solution)/shard_map/ppermute | solution.py:366
  79.4 2.9 %collective-permute-done.15.refs_3_ = bf16[160,768]{1,0:T(8,128)(2,1)S(1)} collective-permute-done((bf16[160,768]{1,0:T(8,128)(2,1)S(1)}, bf16[160,768]{1,0:T(8,128)(2,1)S(1)}, u32[]{:S(2)}, u32[]{:S(2)}) %collective-permute-start.15) | collective-permute-done | bytes 245792 | tf_op jit(solution)/shard_map/ppermute | solution.py:366
  83.8 1.3 collective-permute-start.20
  85.8 1.3 collective-permute-done.23.refs_3_.refs_2_.refs_27_
  87.2 3.4 %collective-permute-start.31 = (bf16[80,3584]{1,0:T(8,128)(2,1)S(1)}, bf16[80,3584]{1,0:T(8,128)(2,1)S(1)}, u32[]{:S(2)}, u32[]{:S(2)}) collective-permute-start(bf16[80,3584]{1,0:T(8,128)(2,1)S(1)} %shard_map.117.refs_6_), channel_id=1, source_target_pairs={{0,7},{1,6},{2,5},{3,4},{4,3},{5,2},{6,1},{7,0},{8,15},{9,14},{10,... | collective-permute-start | bytes 1720328 | tf_op jit(solution)/shard_map/ppermute | solution.py:363
  90.8 4.2 %shard_map.118 = (bf16[160,768]{1,0:T(8,128)(2,1)S(1)}, bf16[160,768]{1,0:T(8,128)(2,1)S(1)}, bf16[160,768]{1,0:T(8,128)(2,1)S(1)}, bf16[160,768]{1,0:T(8,128)(2,1)S(1)}) custom-call(s32[1]{0:T(128)} %bitcast.3.refs_0_, bf16[80,3584]{1,0:T(8,128)(2,1)S(1)} %collective-permute-done.22.refs_2_.refs_1_.refs_26_, ...), custom_call_target="tpu_custom_call" | custom-call | tf_op jit(solution)/shard_map/pallas_call | solution.py:40
  96.4 1.3 collective-permute-start.27
  98.5 3.7 %shard_map.119 = (bf16[80,1792]{1,0:T(8,128)(2,1)S(1)}, bf16[80,1792]{1,0:T(8,128)(2,1)S(1)}) custom-call(s32[1]{0:T(128)} %bitcast.3.refs_0_, bf16[160,768]{1,0:T(8,128)(2,1)S(1)} %shard_map.116.refs_1_.refs_9_, bf16[160,768]{1,0:T(8,128)(2,1)S(1)} %collective-permute-done.19.refs_2_.refs_10_, ...), custom_call_target="tpu_custom_call" | custom-call | tf_op jit(solution)/shard_map/pallas_call | solution.py:40
  102.3 1.4 collective-permute-done.25.refs_1_
  103.8 4.8 %collective-permute-done.27.refs_3_ = bf16[160,768]{1,0:T(8,128)(2,1)S(1)} collective-permute-done((bf16[160,768]{1,0:T(8,128)(2,1)S(1)}, bf16[160,768]{1,0:T(8,128)(2,1)S(1)}, u32[]{:S(2)}, u32[]{:S(2)}) %collective-permute-start.27) | collective-permute-done | bytes 245792 | tf_op jit(solution)/shard_map/ppermute | solution.py:366
  108.8 2.1 %collective-permute-start.30 = (bf16[160,768]{1,0:T(8,128)(2,1)S(1)}, bf16[160,768]{1,0:T(8,128)(2,1)S(1)}, u32[]{:S(2)}, u32[]{:S(2)}) collective-permute-start(bf16[160,768]{1,0:T(8,128)(2,1)S(1)} %shard_map.120.refs_2_.refs_1_.refs_13_), channel_id=1, source_target_pairs={{0,24},{8,16},{16,8},{24,0},{1,25},{9,17},{17,9},{25,1},{2,26},{10... | collective-permute-start | bytes 737288 | tf_op jit(solution)/shard_map/ppermute | solution.py:366
  111.5 4.4 %collective-permute-done.31.refs_3_.refs_1_.refs_28_ = bf16[80,3584]{1,0:T(8,128)(2,1)S(1)} collective-permute-done((bf16[80,3584]{1,0:T(8,128)(2,1)S(1)}, bf16[80,3584]{1,0:T(8,128)(2,1)S(1)}, u32[]{:S(2)}, u32[]{:S(2)}) %collective-permute-start.31) | collective-permute-done | bytes 573472 | tf_op jit(solution)/shard_map/ppermute | solution.py:363
  116.1 4.0 %shard_map.122 = (bf16[80,768]{1,0:T(8,128)(2,1)S(1)}, bf16[80,768]{1,0:T(8,128)(2,1)S(1)}, bf16[80,768]{1,0:T(8,128)(2,1)S(1)}, bf16[80,768]{1,0:T(8,128)(2,1)S(1)}) custom-call(s32[1]{0:T(128)} %bitcast.3.refs_0_, bf16[80,3584]{1,0:T(8,128)(2,1)S(1)} %collective-permute-done.31.refs_3_.refs_1_.refs_28_, bf16[1792,1024]{1,0:T(8,128)(2,1)S(1)} %bitcast.17, ...), custom_call_target="tpu_custom_call" | custom-call | tf_op jit(solution)/shard_map/pallas_call | solution.py:40
  120.5 2.4 %collective-permute-done.29.refs_3_.refs_15_ = bf16[160,768]{1,0:T(8,128)(2,1)S(1)} collective-permute-done((bf16[160,768]{1,0:T(8,128)(2,1)S(1)}, bf16[160,768]{1,0:T(8,128)(2,1)S(1)}, u32[]{:S(2)}, u32[]{:S(2)}) %collective-permute-start.29) | collective-permute-done | bytes 245792 | tf_op jit(solution)/shard_map/ppermute | solution.py:366
  123.7 1.4 collective-permute-start.37
  125.1 3.7 %shard_map.123 = (bf16[80,1792]{1,0:T(8,128)(2,1)S(1)}, bf16[80,1792]{1,0:T(8,128)(2,1)S(1)}) custom-call(s32[1]{0:T(128)} %bitcast.3.refs_0_, bf16[160,768]{1,0:T(8,128)(2,1)S(1)} %shard_map.120.refs_2_.refs_1_.refs_13_, bf16[160,768]{1,0:T(8,128)(2,1)S(1)} %collective-permute-done.28.refs_2_.refs_14_, ...), custom_call_target="tpu_custom_call" | custom-call | tf_op jit(solution)/shard_map/pallas_call | solution.py:40
  129.0 1.4 collective-permute-start.40
  130.3 2.0 %collective-permute-start.39 = (bf16[80,768]{1,0:T(8,128)(2,1)S(1)}, bf16[80,768]{1,0:T(8,128)(2,1)S(1)}, u32[]{:S(2)}, u32[]{:S(2)}) collective-permute-start(bf16[80,768]{1,0:T(8,128)(2,1)S(1)} %shard_map.124.refs_1_.refs_7_.refs_17_), channel_id=1, source_target_pairs={{0,16},{8,24},{16,0},{24,8},{1,17},{9,25},{17,1},{25,9},{2,18},{10... | collective-permute-start | bytes 368648 | tf_op jit(solution)/shard_map/ppermute | solution.py:366
  132.3 1.4 collective-permute-done.40.refs_4_.refs_20_
  133.7 2.6 %collective-permute-start.24 = (bf16[80,1792]{1,0:T(8,128)(2,1)S(1)}, bf16[80,1792]{1,0:T(8,128)(2,1)S(1)}, u32[]{:S(2)}, u32[]{:S(2)}) collective-permute-start(bf16[80,1792]{1,0:T(8,128)(2,1)S(1)} %get-tuple-element.64), channel_id=1, source_target_pairs={{0,2},{1,3},{2,0},{3,1},{4,6},{5,7},{6,4},{7,5},{8,10},{9,11},{10,... | collective-permute-start | bytes 860168 | tf_op jit(solution)/shard_map/ppermute | solution.py:363
  137.5 4.2 %collective-permute-start.33 = (bf16[80,1792]{1,0:T(8,128)(2,1)S(1)}, bf16[80,1792]{1,0:T(8,128)(2,1)S(1)}, u32[]{:S(2)}, u32[]{:S(2)}) collective-permute-start(bf16[80,1792]{1,0:T(8,128)(2,1)S(1)} %get-tuple-element.70), channel_id=1, source_target_pairs={{0,3},{1,2},{2,1},{3,0},{4,7},{5,6},{6,5},{7,4},{8,11},{9,10},{10,... | collective-permute-start | bytes 860168 | tf_op jit(solution)/shard_map/ppermute | solution.py:363
  141.7 3.3 %shard_map.125.refs_31_ = bf16[80,1792]{1,0:T(8,128)(2,1)S(1)} custom-call(s32[1]{0:T(128)} %bitcast.3.refs_0_, bf16[80,768]{1,0:T(8,128)(2,1)S(1)} %shard_map.124.refs_1_.refs_7_.refs_17_, bf16[80,768]{1,0:T(8,128)(2,1)S(1)} %collective-permute-done.38.refs_2_.refs_18_, bf16[80,768]{1,0:T(8,128)(2,1)S(1)} %collective-permute-done.39.refs_3_.refs_19_, ...), custom_call_target="tpu_custom_call" | custom-call | tf_op jit(solution)/shard_map/pallas_call | solution.py:40
  145.2 10.6 %shard_map.126 = (bf16[1024,1792]{1,0:T(8,128)(2,1)}, bf16[1024,1792]{1,0:T(8,128)(2,1)}, f32[8,128]{1,0:T(8,128)S(1)}) custom-call(s32[1]{0:T(128)} %bitcast.3.refs_0_, bf16[160,768]{1,0:T(8,128)(2,1)S(1)} %shard_map.108.refs_5_.refs_1_, bf16[160,768]{1,0:T(8,128)(2,1)S(1)} %collective-permute-done.10.refs_2_, ...), custom_call_target="tpu_custom_call" | custom-call | tf_op jit(solution)/shard_map/pallas_call | solution.py:40
  155.9 1.8 %shard_map.127.refs_6_ = bf16[512,1792]{1,0:T(8,128)(2,1)S(1)} custom-call(s32[1]{0:T(128)} %bitcast.refs_0_, s32[1,512]{1,0:T(1,128)S(1)} %copy-done.14, bf16[80,1792]{1,0:T(8,128)(2,1)S(1)} %get-tuple-element.57.refs_4_.refs_2_, bf16[80,1792]{1,0:T(8,128)(2,1)S(1)} %collective-permute-done.42.refs_3_, ...), custom_call_target="tpu_custom_call" | custom-call | tf_op jit(solution)/shard_map/pallas_call | solution.py:40
  157.7 4.9 %collective-permute-done.33.refs_3_ = bf16[80,1792]{1,0:T(8,128)(2,1)S(1)} collective-permute-done((bf16[80,1792]{1,0:T(8,128)(2,1)S(1)}, bf16[80,1792]{1,0:T(8,128)(2,1)S(1)}, u32[]{:S(2)}, u32[]{:S(2)}) %collective-permute-start.33) | collective-permute-done | bytes 286752 | tf_op jit(solution)/shard_map/ppermute | solution.py:363
  162.6 2.6 %collective-permute-done.41.refs_5_ = bf16[80,1792]{1,0:T(8,128)(2,1)S(1)} collective-permute-done((bf16[80,1792]{1,0:T(8,128)(2,1)S(1)}, bf16[80,1792]{1,0:T(8,128)(2,1)S(1)}, u32[]{:S(2)}, u32[]{:S(2)}) %collective-permute-start.41) | collective-permute-done | bytes 286752 | tf_op jit(solution)/shard_map/ppermute | solution.py:363
  165.2 2.7 %shard_map.128 = bf16[512,1792]{1,0:T(8,128)(2,1)} custom-call(s32[1]{0:T(128)} %bitcast.refs_0_, s32[1,512]{1,0:T(1,128)S(1)} %copy-done.14, bf16[80,1792]{1,0:T(8,128)(2,1)S(1)} %collective-permute-done.24.refs_2_, bf16[80,1792]{1,0:T(8,128)(2,1)S(1)} %collective-permute-done.33.refs_3_, bf16[80,1792]{1,0:T(8,128)(2,1)S(1)} %collective-permute-done.34.refs_4_, ...), custom_call_target="tpu_custom_call" | custom-call | tf_op jit(solution)/shard_map/pallas_call | solution.py:40
  (96 shorter events, 21.7 us)
Async XLA Ops:
  4.8 8.2 %collective-permute-start = (bf16[80,3584]{1,0:T(8,128)(2,1)}, bf16[80,3584]{1,0:T(8,128)(2,1)S(1)}, u32[]{:S(2)}, u32[]{:S(2)}) collective-permute-start(bf16[80,3584]{1,0:T(8,128)(2,1)} %get-tuple-element.45), channel_id=1, source_target_pairs={{0,1},{1,0},{2,3},{3,2},{4,5},{5,4},{6,7},{7,6},{8,9},{9,8},{10,11... | collective-permute-start | bytes 1720328 | tf_op jit(solution)/shard_map/ppermute | solution.py:363
  5.5 27.6 %collective-permute-start.2 = (bf16[80,3584]{1,0:T(8,128)(2,1)}, bf16[80,3584]{1,0:T(8,128)(2,1)S(1)}, u32[]{:S(2)}, u32[]{:S(2)}) collective-permute-start(bf16[80,3584]{1,0:T(8,128)(2,1)} %get-tuple-element.42.refs_5_), channel_id=1, source_target_pairs={{0,4},{1,5},{2,6},{3,7},{4,0},{5,1},{6,2},{7,3},{8,12},{9,13},{10,... | collective-permute-start | bytes 1720328 | tf_op jit(solution)/shard_map/ppermute | solution.py:363
  20.1 20.9 %copy-start.3 = (bf16[1,1792,1024]{2,1,0:T(8,128)(2,1)S(1)}, bf16[1,1792,1024]{2,1,0:T(8,128)(2,1)}, u32[]{:S(2)}) copy-start(bf16[1,1792,1024]{2,1,0:T(8,128)(2,1)} %param.13) | copy-start | bytes 11010052
  20.1 20.9 %copy-start.5 = (bf16[1,1024,1792]{2,1,0:T(8,128)(2,1)S(1)}, bf16[1,1024,1792]{2,1,0:T(8,128)(2,1)}, u32[]{:S(2)}) copy-start(bf16[1,1024,1792]{2,1,0:T(8,128)(2,1)} %param.14) | copy-start | bytes 11010052
  24.6 16.5 %copy-start.1 = (bf16[1,1792,1024]{2,1,0:T(8,128)(2,1)S(1)}, bf16[1,1792,1024]{2,1,0:T(8,128)(2,1)}, u32[]{:S(2)}) copy-start(bf16[1,1792,1024]{2,1,0:T(8,128)(2,1)} %param.12) | copy-start | bytes 11010052
  24.6 11.8 %collective-permute-start.4 = (bf16[160,768]{1,0:T(8,128)(2,1)S(1)}, bf16[160,768]{1,0:T(8,128)(2,1)S(1)}, u32[]{:S(2)}, u32[]{:S(2)}) collective-permute-start(bf16[160,768]{1,0:T(8,128)(2,1)S(1)} %get-tuple-element.50), channel_id=1, source_target_pairs={{0,8},{8,0},{16,24},{24,16},{1,9},{9,1},{17,25},{25,17},{2,10},{10... | collective-permute-start | bytes 737288 | tf_op jit(solution)/shard_map/ppermute | solution.py:366
  25.9 10.5 %collective-permute-start.5 = (bf16[160,768]{1,0:T(8,128)(2,1)S(1)}, bf16[160,768]{1,0:T(8,128)(2,1)S(1)}, u32[]{:S(2)}, u32[]{:S(2)}) collective-permute-start(bf16[160,768]{1,0:T(8,128)(2,1)S(1)} %get-tuple-element.51), channel_id=1, source_target_pairs={{0,16},{8,24},{16,0},{24,8},{1,17},{9,25},{17,1},{25,9},{2,18},{10... | collective-permute-start | bytes 737288 | tf_op jit(solution)/shard_map/ppermute | solution.py:366
  27.1 11.0 %collective-permute-start.6 = (bf16[160,768]{1,0:T(8,128)(2,1)S(1)}, bf16[160,768]{1,0:T(8,128)(2,1)S(1)}, u32[]{:S(2)}, u32[]{:S(2)}) collective-permute-start(bf16[160,768]{1,0:T(8,128)(2,1)S(1)} %get-tuple-element.52), channel_id=1, source_target_pairs={{0,24},{8,16},{16,8},{24,0},{1,25},{9,17},{17,9},{25,1},{2,26},{10... | collective-permute-start | bytes 737288 | tf_op jit(solution)/shard_map/ppermute | solution.py:366
  33.1 25.7 %collective-permute-start.3 = (bf16[80,3584]{1,0:T(8,128)(2,1)S(1)}, bf16[80,3584]{1,0:T(8,128)(2,1)S(1)}, u32[]{:S(2)}, u32[]{:S(2)}) collective-permute-start(bf16[80,3584]{1,0:T(8,128)(2,1)S(1)} %shard_map.107.refs_4_), channel_id=1, source_target_pairs={{0,2},{1,3},{2,0},{3,1},{4,6},{5,7},{6,4},{7,5},{8,10},{9,11},{10,... | collective-permute-start | bytes 1720328 | tf_op jit(solution)/shard_map/ppermute | solution.py:363
  33.7 27.9 %collective-permute-start.1 = (bf16[80,3584]{1,0:T(8,128)(2,1)S(1)}, bf16[80,3584]{1,0:T(8,128)(2,1)S(1)}, u32[]{:S(2)}, u32[]{:S(2)}) collective-permute-start(bf16[80,3584]{1,0:T(8,128)(2,1)S(1)} %shard_map.106.refs_1_), channel_id=1, source_target_pairs={{0,5},{1,4},{2,7},{3,6},{4,1},{5,0},{6,3},{7,2},{8,13},{9,12},{10,... | collective-permute-start | bytes 1720328 | tf_op jit(solution)/shard_map/ppermute | solution.py:363
  38.3 7.1 %collective-permute-start.12 = (bf16[160,768]{1,0:T(8,128)(2,1)S(1)}, bf16[160,768]{1,0:T(8,128)(2,1)S(1)}, u32[]{:S(2)}, u32[]{:S(2)}) collective-permute-start(bf16[160,768]{1,0:T(8,128)(2,1)S(1)} %shard_map.108.refs_5_.refs_1_), channel_id=1, source_target_pairs={{0,24},{8,16},{16,8},{24,0},{1,25},{9,17},{17,9},{25,1},{2,26},{10... | collective-permute-start | bytes 737288 | tf_op jit(solution)/shard_map/ppermute | solution.py:366
  39.5 12.9 %collective-permute-start.11 = (bf16[160,768]{1,0:T(8,128)(2,1)S(1)}, bf16[160,768]{1,0:T(8,128)(2,1)S(1)}, u32[]{:S(2)}, u32[]{:S(2)}) collective-permute-start(bf16[160,768]{1,0:T(8,128)(2,1)S(1)} %shard_map.108.refs_5_.refs_1_), channel_id=1, source_target_pairs={{0,16},{8,24},{16,0},{24,8},{1,17},{9,25},{17,1},{25,9},{2,18},{10... | collective-permute-start | bytes 737288 | tf_op jit(solution)/shard_map/ppermute | solution.py:366
  40.7 12.8 %collective-permute-start.10 = (bf16[160,768]{1,0:T(8,128)(2,1)S(1)}, bf16[160,768]{1,0:T(8,128)(2,1)S(1)}, u32[]{:S(2)}, u32[]{:S(2)}) collective-permute-start(bf16[160,768]{1,0:T(8,128)(2,1)S(1)} %shard_map.108.refs_5_.refs_1_), channel_id=1, source_target_pairs={{0,8},{8,0},{16,24},{24,16},{1,9},{9,1},{17,25},{25,17},{2,10},{10... | collective-permute-start | bytes 737288 | tf_op jit(solution)/shard_map/ppermute | solution.py:366
  45.4 13.1 %collective-permute-start.7 = (bf16[80,768]{1,0:T(8,128)(2,1)S(1)}, bf16[80,768]{1,0:T(8,128)(2,1)S(1)}, u32[]{:S(2)}, u32[]{:S(2)}) collective-permute-start(bf16[80,768]{1,0:T(8,128)(2,1)S(1)} %get-tuple-element.54), channel_id=1, source_target_pairs={{0,8},{8,0},{16,24},{24,16},{1,9},{9,1},{17,25},{25,17},{2,10},{10... | collective-permute-start | bytes 368648 | tf_op jit(solution)/shard_map/ppermute | solution.py:366
  52.4 6.1 %collective-permute-start.8 = (bf16[80,768]{1,0:T(8,128)(2,1)S(1)}, bf16[80,768]{1,0:T(8,128)(2,1)S(1)}, u32[]{:S(2)}, u32[]{:S(2)}) collective-permute-start(bf16[80,768]{1,0:T(8,128)(2,1)S(1)} %get-tuple-element.55), channel_id=1, source_target_pairs={{0,16},{8,24},{16,0},{24,8},{1,17},{9,25},{17,1},{25,9},{2,18},{10... | collective-permute-start | bytes 368648 | tf_op jit(solution)/shard_map/ppermute | solution.py:366
  53.6 5.1 %collective-permute-start.9 = (bf16[80,768]{1,0:T(8,128)(2,1)S(1)}, bf16[80,768]{1,0:T(8,128)(2,1)S(1)}, u32[]{:S(2)}, u32[]{:S(2)}) collective-permute-start(bf16[80,768]{1,0:T(8,128)(2,1)S(1)} %get-tuple-element.56), channel_id=1, source_target_pairs={{0,24},{8,16},{16,8},{24,0},{1,25},{9,17},{17,9},{25,1},{2,26},{10... | collective-permute-start | bytes 368648 | tf_op jit(solution)/shard_map/ppermute | solution.py:366
  58.8 27.1 %collective-permute-start.22 = (bf16[80,3584]{1,0:T(8,128)(2,1)S(1)}, bf16[80,3584]{1,0:T(8,128)(2,1)S(1)}, u32[]{:S(2)}, u32[]{:S(2)}) collective-permute-start(bf16[80,3584]{1,0:T(8,128)(2,1)S(1)} %shard_map.112.refs_1_), channel_id=1, source_target_pairs={{0,6},{1,7},{2,4},{3,5},{4,2},{5,3},{6,0},{7,1},{8,14},{9,15},{10,... | collective-permute-start | bytes 1720328 | tf_op jit(solution)/shard_map/ppermute | solution.py:363
  61.7 25.5 %collective-permute-start.23 = (bf16[80,3584]{1,0:T(8,128)(2,1)S(1)}, bf16[80,3584]{1,0:T(8,128)(2,1)S(1)}, u32[]{:S(2)}, u32[]{:S(2)}) collective-permute-start(bf16[80,3584]{1,0:T(8,128)(2,1)S(1)} %shard_map.113.refs_6_), channel_id=1, source_target_pairs={{0,3},{1,2},{2,1},{3,0},{4,7},{5,6},{6,5},{7,4},{8,11},{9,10},{10,... | collective-permute-start | bytes 1720328 | tf_op jit(solution)/shard_map/ppermute | solution.py:363
  63.0 6.9 %collective-permute-start.18 = (bf16[80,768]{1,0:T(8,128)(2,1)S(1)}, bf16[80,768]{1,0:T(8,128)(2,1)S(1)}, u32[]{:S(2)}, u32[]{:S(2)}) collective-permute-start(bf16[80,768]{1,0:T(8,128)(2,1)S(1)} %shard_map.111.refs_1_.refs_5_), channel_id=1, source_target_pairs={{0,24},{8,16},{16,8},{24,0},{1,25},{9,17},{17,9},{25,1},{2,26},{10... | collective-permute-start | bytes 368648 | tf_op jit(solution)/shard_map/ppermute | solution.py:366
  65.2 6.6 %collective-permute-start.17 = (bf16[80,768]{1,0:T(8,128)(2,1)S(1)}, bf16[80,768]{1,0:T(8,128)(2,1)S(1)}, u32[]{:S(2)}, u32[]{:S(2)}) collective-permute-start(bf16[80,768]{1,0:T(8,128)(2,1)S(1)} %shard_map.111.refs_1_.refs_5_), channel_id=1, source_target_pairs={{0,16},{8,24},{16,0},{24,8},{1,17},{9,25},{17,1},{25,9},{2,18},{10... | collective-permute-start | bytes 368648 | tf_op jit(solution)/shard_map/ppermute | solution.py:366
  65.4 7.6 %collective-permute-start.16 = (bf16[80,768]{1,0:T(8,128)(2,1)S(1)}, bf16[80,768]{1,0:T(8,128)(2,1)S(1)}, u32[]{:S(2)}, u32[]{:S(2)}) collective-permute-start(bf16[80,768]{1,0:T(8,128)(2,1)S(1)} %shard_map.111.refs_1_.refs_5_), channel_id=1, source_target_pairs={{0,8},{8,0},{16,24},{24,16},{1,9},{9,1},{17,25},{25,17},{2,10},{10... | collective-permute-start | bytes 368648 | tf_op jit(solution)/shard_map/ppermute | solution.py:366
  69.9 7.6 %collective-permute-start.13 = (bf16[160,768]{1,0:T(8,128)(2,1)S(1)}, bf16[160,768]{1,0:T(8,128)(2,1)S(1)}, u32[]{:S(2)}, u32[]{:S(2)}) collective-permute-start(bf16[160,768]{1,0:T(8,128)(2,1)S(1)} %get-tuple-element.59), channel_id=1, source_target_pairs={{0,8},{8,0},{16,24},{24,16},{1,9},{9,1},{17,25},{25,17},{2,10},{10... | collective-permute-start | bytes 737288 | tf_op jit(solution)/shard_map/ppermute | solution.py:366
  71.8 7.6 %collective-permute-start.14 = (bf16[160,768]{1,0:T(8,128)(2,1)S(1)}, bf16[160,768]{1,0:T(8,128)(2,1)S(1)}, u32[]{:S(2)}, u32[]{:S(2)}) collective-permute-start(bf16[160,768]{1,0:T(8,128)(2,1)S(1)} %get-tuple-element.60), channel_id=1, source_target_pairs={{0,16},{8,24},{16,0},{24,8},{1,17},{9,25},{17,1},{25,9},{2,18},{10... | collective-permute-start | bytes 737288 | tf_op jit(solution)/shard_map/ppermute | solution.py:366
  73.0 9.3 %collective-permute-start.15 = (bf16[160,768]{1,0:T(8,128)(2,1)S(1)}, bf16[160,768]{1,0:T(8,128)(2,1)S(1)}, u32[]{:S(2)}, u32[]{:S(2)}) collective-permute-start(bf16[160,768]{1,0:T(8,128)(2,1)S(1)} %get-tuple-element.61), channel_id=1, source_target_pairs={{0,24},{8,16},{16,8},{24,0},{1,25},{9,17},{17,9},{25,1},{2,26},{10... | collective-permute-start | bytes 737288 | tf_op jit(solution)/shard_map/ppermute | solution.py:366
  74.2 13.0 %copy-start.10 = (bf16[80,3584]{1,0:T(8,128)(2,1)S(1)}, bf16[80,3584]{1,0:T(8,128)(2,1)}, u32[]{:S(2)}) copy-start(bf16[80,3584]{1,0:T(8,128)(2,1)} %get-tuple-element.62.refs_0_) | copy-start | bytes 1720324
  82.5 13.8 %collective-permute-start.21 = (bf16[160,768]{1,0:T(8,128)(2,1)S(1)}, bf16[160,768]{1,0:T(8,128)(2,1)S(1)}, u32[]{:S(2)}, u32[]{:S(2)}) collective-permute-start(bf16[160,768]{1,0:T(8,128)(2,1)S(1)} %shard_map.116.refs_1_.refs_9_), channel_id=1, source_target_pairs={{0,24},{8,16},{16,8},{24,0},{1,25},{9,17},{17,9},{25,1},{2,26},{10... | collective-permute-start | bytes 737288 | tf_op jit(solution)/shard_map/ppermute | solution.py:366
  83.8 12.7 %collective-permute-start.20 = (bf16[160,768]{1,0:T(8,128)(2,1)S(1)}, bf16[160,768]{1,0:T(8,128)(2,1)S(1)}, u32[]{:S(2)}, u32[]{:S(2)}) collective-permute-start(bf16[160,768]{1,0:T(8,128)(2,1)S(1)} %shard_map.116.refs_1_.refs_9_), channel_id=1, source_target_pairs={{0,16},{8,24},{16,0},{24,8},{1,17},{9,25},{17,1},{25,9},{2,18},{10... | collective-permute-start | bytes 737288 | tf_op jit(solution)/shard_map/ppermute | solution.py:366
  87.2 28.7 %collective-permute-start.31 = (bf16[80,3584]{1,0:T(8,128)(2,1)S(1)}, bf16[80,3584]{1,0:T(8,128)(2,1)S(1)}, u32[]{:S(2)}, u32[]{:S(2)}) collective-permute-start(bf16[80,3584]{1,0:T(8,128)(2,1)S(1)} %shard_map.117.refs_6_), channel_id=1, source_target_pairs={{0,7},{1,6},{2,5},{3,4},{4,3},{5,2},{6,1},{7,0},{8,15},{9,14},{10,... | collective-permute-start | bytes 1720328 | tf_op jit(solution)/shard_map/ppermute | solution.py:363
  90.5 7.9 %collective-permute-start.19 = (bf16[160,768]{1,0:T(8,128)(2,1)S(1)}, bf16[160,768]{1,0:T(8,128)(2,1)S(1)}, u32[]{:S(2)}, u32[]{:S(2)}) collective-permute-start(bf16[160,768]{1,0:T(8,128)(2,1)S(1)} %shard_map.116.refs_1_.refs_9_), channel_id=1, source_target_pairs={{0,8},{8,0},{16,24},{24,16},{1,9},{9,1},{17,25},{25,17},{2,10},{10... | collective-permute-start | bytes 737288 | tf_op jit(solution)/shard_map/ppermute | solution.py:366
  95.0 8.7 %collective-permute-start.25 = (bf16[160,768]{1,0:T(8,128)(2,1)S(1)}, bf16[160,768]{1,0:T(8,128)(2,1)S(1)}, u32[]{:S(2)}, u32[]{:S(2)}) collective-permute-start(bf16[160,768]{1,0:T(8,128)(2,1)S(1)} %get-tuple-element.65), channel_id=1, source_target_pairs={{0,8},{8,0},{16,24},{24,16},{1,9},{9,1},{17,25},{25,17},{2,10},{10... | collective-permute-start | bytes 737288 | tf_op jit(solution)/shard_map/ppermute | solution.py:366
  96.3 7.5 %collective-permute-start.26 = (bf16[160,768]{1,0:T(8,128)(2,1)S(1)}, bf16[160,768]{1,0:T(8,128)(2,1)S(1)}, u32[]{:S(2)}, u32[]{:S(2)}) collective-permute-start(bf16[160,768]{1,0:T(8,128)(2,1)S(1)} %get-tuple-element.66), channel_id=1, source_target_pairs={{0,16},{8,24},{16,0},{24,8},{1,17},{9,25},{17,1},{25,9},{2,18},{10... | collective-permute-start | bytes 737288 | tf_op jit(solution)/shard_map/ppermute | solution.py:366
  96.4 12.2 %collective-permute-start.27 = (bf16[160,768]{1,0:T(8,128)(2,1)S(1)}, bf16[160,768]{1,0:T(8,128)(2,1)S(1)}, u32[]{:S(2)}, u32[]{:S(2)}) collective-permute-start(bf16[160,768]{1,0:T(8,128)(2,1)S(1)} %get-tuple-element.67), channel_id=1, source_target_pairs={{0,24},{8,16},{16,8},{24,0},{1,25},{9,17},{17,9},{25,1},{2,26},{10... | collective-permute-start | bytes 737288 | tf_op jit(solution)/shard_map/ppermute | solution.py:366
  102.2 9.3 %collective-permute-start.32 = (bf16[80,1792]{1,0:T(8,128)(2,1)S(1)}, bf16[80,1792]{1,0:T(8,128)(2,1)S(1)}, u32[]{:S(2)}, u32[]{:S(2)}) collective-permute-start(bf16[80,1792]{1,0:T(8,128)(2,1)S(1)} %get-tuple-element.68.refs_4_), channel_id=1, source_target_pairs={{0,1},{1,0},{2,3},{3,2},{4,5},{5,4},{6,7},{7,6},{8,9},{9,8},{10,11... | collective-permute-start | bytes 860168 | tf_op jit(solution)/shard_map/ppermute | solution.py:363
  108.8 11.4 %collective-permute-start.30 = (bf16[160,768]{1,0:T(8,128)(2,1)S(1)}, bf16[160,768]{1,0:T(8,128)(2,1)S(1)}, u32[]{:S(2)}, u32[]{:S(2)}) collective-permute-start(bf16[160,768]{1,0:T(8,128)(2,1)S(1)} %shard_map.120.refs_2_.refs_1_.refs_13_), channel_id=1, source_target_pairs={{0,24},{8,16},{16,8},{24,0},{1,25},{9,17},{17,9},{25,1},{2,26},{10... | collective-permute-start | bytes 737288 | tf_op jit(solution)/shard_map/ppermute | solution.py:366
  110.9 12.0 %collective-permute-start.29 = (bf16[160,768]{1,0:T(8,128)(2,1)S(1)}, bf16[160,768]{1,0:T(8,128)(2,1)S(1)}, u32[]{:S(2)}, u32[]{:S(2)}) collective-permute-start(bf16[160,768]{1,0:T(8,128)(2,1)S(1)} %shard_map.120.refs_2_.refs_1_.refs_13_), channel_id=1, source_target_pairs={{0,16},{8,24},{16,0},{24,8},{1,17},{9,25},{17,1},{25,9},{2,18},{10... | collective-permute-start | bytes 737288 | tf_op jit(solution)/shard_map/ppermute | solution.py:366
  111.2 12.6 %collective-permute-start.28 = (bf16[160,768]{1,0:T(8,128)(2,1)S(1)}, bf16[160,768]{1,0:T(8,128)(2,1)S(1)}, u32[]{:S(2)}, u32[]{:S(2)}) collective-permute-start(bf16[160,768]{1,0:T(8,128)(2,1)S(1)} %shard_map.120.refs_2_.refs_1_.refs_13_), channel_id=1, source_target_pairs={{0,8},{8,0},{16,24},{24,16},{1,9},{9,1},{17,25},{25,17},{2,10},{10... | collective-permute-start | bytes 737288 | tf_op jit(solution)/shard_map/ppermute | solution.py:366
  115.9 39.9 %collective-permute-start.43 = (bf16[160,1792]{1,0:T(8,128)(2,1)S(1)}, bf16[160,1792]{1,0:T(8,128)(2,1)S(1)}, u32[]{:S(2)}, u32[]{:S(2)}) collective-permute-start(bf16[160,1792]{1,0:T(8,128)(2,1)S(1)} %shard_map.121.refs_5_), channel_id=1, source_target_pairs={{0,4},{1,5},{2,6},{3,7},{4,0},{5,1},{6,2},{7,3},{8,12},{9,13},{10,... | collective-permute-start | bytes 1720328 | tf_op jit(solution)/shard_map/ppermute | solution.py:363
  116.0 29.1 %collective-permute-start.42 = (bf16[80,1792]{1,0:T(8,128)(2,1)S(1)}, bf16[80,1792]{1,0:T(8,128)(2,1)S(1)}, u32[]{:S(2)}, u32[]{:S(2)}) collective-permute-start(bf16[80,1792]{1,0:T(8,128)(2,1)S(1)} %get-tuple-element.75), channel_id=1, source_target_pairs={{0,1},{1,0},{2,3},{3,2},{4,5},{5,4},{6,7},{7,6},{8,9},{9,8},{10,11... | collective-permute-start | bytes 860168 | tf_op jit(solution)/shard_map/ppermute | solution.py:363
  120.2 8.7 %collective-permute-start.35 = (bf16[80,768]{1,0:T(8,128)(2,1)S(1)}, bf16[80,768]{1,0:T(8,128)(2,1)S(1)}, u32[]{:S(2)}, u32[]{:S(2)}) collective-permute-start(bf16[80,768]{1,0:T(8,128)(2,1)S(1)} %get-tuple-element.72), channel_id=1, source_target_pairs={{0,8},{8,0},{16,24},{24,16},{1,9},{9,1},{17,25},{25,17},{2,10},{10... | collective-permute-start | bytes 368648 | tf_op jit(solution)/shard_map/ppermute | solution.py:366
  122.9 6.0 %collective-permute-start.36 = (bf16[80,768]{1,0:T(8,128)(2,1)S(1)}, bf16[80,768]{1,0:T(8,128)(2,1)S(1)}, u32[]{:S(2)}, u32[]{:S(2)}) collective-permute-start(bf16[80,768]{1,0:T(8,128)(2,1)S(1)} %get-tuple-element.73), channel_id=1, source_target_pairs={{0,16},{8,24},{16,0},{24,8},{1,17},{9,25},{17,1},{25,9},{2,18},{10... | collective-permute-start | bytes 368648 | tf_op jit(solution)/shard_map/ppermute | solution.py:366
  123.7 5.1 %collective-permute-start.37 = (bf16[80,768]{1,0:T(8,128)(2,1)S(1)}, bf16[80,768]{1,0:T(8,128)(2,1)S(1)}, u32[]{:S(2)}, u32[]{:S(2)}) collective-permute-start(bf16[80,768]{1,0:T(8,128)(2,1)S(1)} %get-tuple-element.74), channel_id=1, source_target_pairs={{0,24},{8,16},{16,8},{24,0},{1,25},{9,17},{17,9},{25,1},{2,26},{10... | collective-permute-start | bytes 368648 | tf_op jit(solution)/shard_map/ppermute | solution.py:366
  129.0 4.7 %collective-permute-start.40 = (bf16[80,768]{1,0:T(8,128)(2,1)S(1)}, bf16[80,768]{1,0:T(8,128)(2,1)S(1)}, u32[]{:S(2)}, u32[]{:S(2)}) collective-permute-start(bf16[80,768]{1,0:T(8,128)(2,1)S(1)} %shard_map.124.refs_1_.refs_7_.refs_17_), channel_id=1, source_target_pairs={{0,24},{8,16},{16,8},{24,0},{1,25},{9,17},{17,9},{25,1},{2,26},{10... | collective-permute-start | bytes 368648 | tf_op jit(solution)/shard_map/ppermute | solution.py:366
  130.3 6.0 %collective-permute-start.39 = (bf16[80,768]{1,0:T(8,128)(2,1)S(1)}, bf16[80,768]{1,0:T(8,128)(2,1)S(1)}, u32[]{:S(2)}, u32[]{:S(2)}) collective-permute-start(bf16[80,768]{1,0:T(8,128)(2,1)S(1)} %shard_map.124.refs_1_.refs_7_.refs_17_), channel_id=1, source_target_pairs={{0,16},{8,24},{16,0},{24,8},{1,17},{9,25},{17,1},{25,9},{2,18},{10... | collective-permute-start | bytes 368648 | tf_op jit(solution)/shard_map/ppermute | solution.py:366
  132.3 5.2 %collective-permute-start.38 = (bf16[80,768]{1,0:T(8,128)(2,1)S(1)}, bf16[80,768]{1,0:T(8,128)(2,1)S(1)}, u32[]{:S(2)}, u32[]{:S(2)}) collective-permute-start(bf16[80,768]{1,0:T(8,128)(2,1)S(1)} %shard_map.124.refs_1_.refs_7_.refs_17_), channel_id=1, source_target_pairs={{0,8},{8,0},{16,24},{24,16},{1,9},{9,1},{17,25},{25,17},{2,10},{10... | collective-permute-start | bytes 368648 | tf_op jit(solution)/shard_map/ppermute | solution.py:366
  133.7 24.0 %collective-permute-start.24 = (bf16[80,1792]{1,0:T(8,128)(2,1)S(1)}, bf16[80,1792]{1,0:T(8,128)(2,1)S(1)}, u32[]{:S(2)}, u32[]{:S(2)}) collective-permute-start(bf16[80,1792]{1,0:T(8,128)(2,1)S(1)} %get-tuple-element.64), channel_id=1, source_target_pairs={{0,2},{1,3},{2,0},{3,1},{4,6},{5,7},{6,4},{7,5},{8,10},{9,11},{10,... | collective-permute-start | bytes 860168 | tf_op jit(solution)/shard_map/ppermute | solution.py:363
  136.3 26.3 %collective-permute-start.34 = (bf16[80,1792]{1,0:T(8,128)(2,1)S(1)}, bf16[80,1792]{1,0:T(8,128)(2,1)S(1)}, u32[]{:S(2)}, u32[]{:S(2)}) collective-permute-start(bf16[80,1792]{1,0:T(8,128)(2,1)S(1)} %get-tuple-element.71.refs_4_), channel_id=1, source_target_pairs={{0,6},{1,7},{2,4},{3,5},{4,2},{5,3},{6,0},{7,1},{8,14},{9,15},{10,... | collective-permute-start | bytes 860168 | tf_op jit(solution)/shard_map/ppermute | solution.py:363
  137.5 25.1 %collective-permute-start.33 = (bf16[80,1792]{1,0:T(8,128)(2,1)S(1)}, bf16[80,1792]{1,0:T(8,128)(2,1)S(1)}, u32[]{:S(2)}, u32[]{:S(2)}) collective-permute-start(bf16[80,1792]{1,0:T(8,128)(2,1)S(1)} %get-tuple-element.70), channel_id=1, source_target_pairs={{0,3},{1,2},{2,1},{3,0},{4,7},{5,6},{6,5},{7,4},{8,11},{9,10},{10,... | collective-permute-start | bytes 860168 | tf_op jit(solution)/shard_map/ppermute | solution.py:363
  145.1 20.1 %collective-permute-start.41 = (bf16[80,1792]{1,0:T(8,128)(2,1)S(1)}, bf16[80,1792]{1,0:T(8,128)(2,1)S(1)}, u32[]{:S(2)}, u32[]{:S(2)}) collective-permute-start(bf16[80,1792]{1,0:T(8,128)(2,1)S(1)} %shard_map.125.refs_31_), channel_id=1, source_target_pairs={{0,7},{1,6},{2,5},{3,4},{4,3},{5,2},{6,1},{7,0},{8,15},{9,14},{10,... | collective-permute-start | bytes 860168 | tf_op jit(solution)/shard_map/ppermute | solution.py:363
  (11 other events, 64.7 us)

commit v6 on v5

--- a/solution.py
+++ b/solution.py
@@ -86,11 +86,12 @@
         pltpu.make_async_copy(ids_ref, ids_v, sems.at[0]),
         pltpu.make_async_copy(codes_ref, codes_v, sems.at[1]),
     ]
-    large = []
-    for c0, c1 in cuts:
-        for ref, buf in ((x_ref, x_v), (g_ref, g_v)):
-            large.append(pltpu.make_async_copy(ref.at[:, c0:c1], buf.at[:, c0:c1], sems.at[2 + len(large)]))
-    for copy in small + large:
+    large = [[], []]
+    for which, (ref, buf) in enumerate(((x_ref, x_v), (g_ref, g_v))):
+        for r0, r1 in cuts:
+            at = sems.at[2 + which * len(cuts) + len(large[which])]
+            large[which].append(pltpu.make_async_copy(ref.at[r0:r1, :], buf.at[r0:r1, :], at))
+    for copy in small + large[0] + large[1]:
         copy.start()
     small[0].wait()
     ids = ids_v[...]
@@ -105,19 +106,18 @@
     target_ref[...] = target
     small[1].wait()
     pick, scaled = picks(cap, offs, me_ref[0], target, codes_v[...].astype(f32) / 256.0)
-    for j, (c0, c1) in enumerate(cuts):
-        for which, (left, buf, base) in enumerate(((pick, x_v, 0), (scaled, g_v, s))):
-            large[2 * j + which].wait()
-            for c in range(c0, c1, TILE):
-                rows = dot(left, buf[:, c : c + TILE]).astype(bf16)
-                for i, out in enumerate(outs):
-                    out[:, base + c : base + c + TILE] = rows[i * cap : (i + 1) * cap]
+    for left, buf, base, copies in ((pick, x_v, 0, large[0]), (scaled, g_v, s, large[1])):
+        for copy in copies:
+            copy.wait()
+        for c in range(0, s, TILE):
+            rows = dot(left, buf[:, c : c + TILE]).astype(bf16)
+            for i, out in enumerate(outs):
+                out[:, base + c : base + c + TILE] = rows[i * cap : (i + 1) * cap]
 
 
 def dispatch(n, cap, offs, me, ids, codes, x, g, deps):
     t, s = x.shape
-    half = s // (2 * TILE) * TILE
-    cuts = [(0, half), (half, s)]
+    cuts = [(r, r + t // 4) for r in range(0, t, t // 4)]
     out_shape = [jax.ShapeDtypeStruct((1, t), jnp.int32)] + [jax.ShapeDtypeStruct((cap, 2 * s), bf16) for _ in offs]
     far_memory = pl.BlockSpec(memory_space=pltpu.HBM)
     return call(
@@ -309,17 +309,19 @@
     backs = refs[:nb]
     prev = refs[nb] if chained else None
     out, pick_t, rows = refs[-3:]
-
-    @pl.when(pl.program_id(0) == 0)
+    part = out.shape[0]
+    i = pl.program_id(0)
+
+    @pl.when(i == 0)
     def _():
         target = tgt_ref[...]
         slots = lax.broadcasted_iota(jnp.int32, (cap, target.shape[1]), 0)
         hits = [jnp.where(slots + (me_ref[0] ^ k) * cap == target, 1.0, 0.0) for k in offs]
         pick_t[...] = jnp.concatenate(hits, axis=0).T.astype(bf16)
-
-    for i, blk in enumerate(backs):
-        rows[i * cap : (i + 1) * cap, :] = blk[...]
-    total = dot(pick_t[...], rows[...])
+        for j, blk in enumerate(backs):
+            rows[j * cap : (j + 1) * cap, :] = blk[...]
+
+    total = dot(pick_t[pl.ds(pl.multiple_of(i * part, part), part), :], rows[...])
     if chained:
         total = total + prev[...].astype(f32)
     out[...] = total.astype(bf16)
@@ -329,8 +331,8 @@
     t = target.shape[1]
     s = backs[0][0].shape[1]
     nb = len(offs)
-    wide = s // 2
-    col = pl.BlockSpec((t, wide), lambda c, i: (0, c))
+    part = t // 2
+    block = pl.BlockSpec((part, s), lambda c, i: (c, 0))
     extra = [] if prev is None else [prev]
     return call(
         functools.partial(combine_body, cap, offs, prev is not None),
@@ -338,12 +340,12 @@
         deps,
         jax.ShapeDtypeStruct((t, s), bf16),
         [whole((1, t))]
-        + [pl.BlockSpec((cap, wide), lambda c, i, part=part: (part, c)) for _, part in backs]
-        + [col] * len(extra),
-        col,
-        grid=(s // wide,),
+        + [pl.BlockSpec((cap, s), lambda c, i, at=at: (at, 0)) for _, at in backs]
+        + [block] * len(extra),
+        block,
+        grid=(2,),
         scalars=1,
-        scratch=[pltpu.VMEM((t, nb * cap), bf16), pltpu.VMEM((nb * cap, wide), bf16)],
+        scratch=[pltpu.VMEM((t, nb * cap), bf16), pltpu.VMEM((nb * cap, s), bf16)],
     )
 
 
@@ -414,15 +416,17 @@
     def gotten(offs):
         return [got[k] for k in offs]
 
-    offs = far[0] + near[0]
+    own, swapped = near[0][:1], near[0][1:]
+    offs = far[0] + swapped
     target, *sends = dispatch(n, cap, offs, me, ids, codes, tokens, grad_out, [])
     send.update(zip(offs, sends))
     mark[:] = [sends[0]]
     push(offs, None)
-    offs = far[1] + near[1] + far[2] + near[2] + far[3]
+    offs = own + far[1] + near[1] + far[2] + near[2] + far[3]
     _, *sends = dispatch(n, cap, offs, me, ids, codes, tokens, grad_out, mark)
     send.update(zip(offs, sends))
     mark[:] = [sends[0]]
+    push(own, None)
 
     fwd(0)
     push(far[1], [])
@@ -450,7 +454,6 @@
     bwd(4)
     give_back(far[3], None)
     give_back(near[1], None)
-    give_back(near[2], None)
     order = range(len(chunks))
     flat = [k for c in order for k in chunks[c]]
     new_down, new_moment, token = down(
@@ -465,7 +468,8 @@
         mark,
     )
     mark[:] = [token]
-    tail = near[1] + near[2] + far[2] + far[3]
+    give_back(near[2], None)
+    tail = far[1] + near[2] + far[3]
     early = [k for k in flat if k not in tail]
     part = combine(cap, early, me, target, [back[k] for k in early], None, mark)
     grad_tokens = combine(cap, tail, me, target, [back[k] for k in tail], part, [])

time: 170 us -> 169 us (level)
  waiting for transfers between devices: 47.9 us -> 44.9 us
  starting transfers between devices: 48 us -> 50.3 us
    ppermute x14, starting transfers between devices: 18.5 us -> 20.9 us  [swap_expert(): return lax.ppermute(v, 'expert', [(i, i ^ k) for i in range(n)])]
    ppermute x14, waiting for transfers between devices: 22.6 us -> 20.5 us  [swap_expert(): return lax.ppermute(v, 'expert', [(i, i ^ k) for i in range(n)])]
where the time goes in v6:
time: 169 us; the launch traced here: 166 us
  Pallas kernels  62.8 us (37%)
  starting transfers between devices  50.3 us (30%)
  waiting for transfers between devices  44.9 us (27%)
  local copies, waits for them, and re-layouts  7.21 us (4%)
    pallas_call x26, Pallas kernels, call(): pl.pallas_call(skipping(body, len(operands), len(deps)), out_shape=out_sh...  62.8 us
    ppermute x30, starting transfers between devices, swap_dp(): return lax.ppermute(v, 'dp', [(i, i ^ k) for i in range(ndp)])  29.4 us
    ppermute x30, waiting for transfers between devices, swap_dp(): return lax.ppermute(v, 'dp', [(i, i ^ k) for i in range(ndp)])  24.4 us
    ppermute x14, starting transfers between devices, swap_expert(): return lax.ppermute(v, 'expert', [(i, i ^ k) for i in range(n)])  20.9 us
    ppermute x14, waiting for transfers between devices, swap_expert(): return lax.ppermute(v, 'expert', [(i, i ^ k) for i in range(n)])  20.5 us
    unnamed x30, local copies, waits for them, and re-layouts  7.21 us
  transfers between devices with their start and end apart: 44, of which 21 were waited for; matrix products, arithmetic and copies ran while one was open for 0% of the time, Pallas kernels for 34%

profile of v6, /device:TPU:9, one launch (start us, length us, event | category | flops | bytes accessed | tf_op | source)
XLA Modules:
  0.0 166.2 jit_solution(9467099830920250284)
XLA Ops:
  0.6 3.6 %shard_map.103 = (s32[1,512]{1,0:T(1,128)}, bf16[80,3584]{1,0:T(8,128)(2,1)}, bf16[80,3584]{1,0:T(8,128)(2,1)}) custom-call(s32[1]{0:T(128)} %bitcast.refs_0_, s32[1,512]{1,0:T(1,128)} %bitcast.37, s32[1,512]{1,0:T(1,128)} %bitcast.39, bf16[512,1792]{1,0:T(8,128)(2,1)} %refs_3_.3, bf16[512,1792]{1,0:T(8,128)(2,1)} %refs_4_.3), custom_call_target="tpu_custom_call" | custom-call | tf_op jit(solution)/shard_map/pallas_call | solution.py:40
  5.0 2.3 %collective-permute-start = (bf16[80,3584]{1,0:T(8,128)(2,1)}, bf16[80,3584]{1,0:T(8,128)(2,1)S(1)}, u32[]{:S(2)}, u32[]{:S(2)}) collective-permute-start(bf16[80,3584]{1,0:T(8,128)(2,1)} %get-tuple-element.42.refs_5_), channel_id=1, source_target_pairs={{0,4},{1,5},{2,6},{3,7},{4,0},{5,1},{6,2},{7,3},{8,12},{9,13},{10,... | collective-permute-start | bytes 1720328 | tf_op jit(solution)/shard_map/ppermute | solution.py:365
  7.3 5.5 %shard_map.104 = (s32[1,512]{1,0:T(1,128)}, bf16[80,3584]{1,0:T(8,128)(2,1)}, bf16[80,3584]{1,0:T(8,128)(2,1)}, bf16[80,3584]{1,0:T(8,128)(2,1)}, bf16[80,3584]{...) custom-call(s32[1]{0:T(128)} %bitcast.refs_0_, s32[1,512]{1,0:T(1,128)} %bitcast.38, ...), custom_call_target="tpu_custom_call" | custom-call | tf_op jit(solution)/shard_map/pallas_call | solution.py:40
  12.9 2.0 %copy-done = bf16[1,1792,1024]{2,1,0:T(8,128)(2,1)S(1)} copy-done((bf16[1,1792,1024]{2,1,0:T(8,128)(2,1)S(1)}, bf16[1,1792,1024]{2,1,0:T(8,128)(2,1)}, u32[]{:S(2)}) %copy-start) | copy-done | bytes 3670040
  14.9 2.0 %copy-done.2 = bf16[1,1792,1024]{2,1,0:T(8,128)(2,1)S(1)} copy-done((bf16[1,1792,1024]{2,1,0:T(8,128)(2,1)S(1)}, bf16[1,1792,1024]{2,1,0:T(8,128)(2,1)}, u32[]{:S(2)}) %copy-start.2) | copy-done | bytes 3670040
  16.9 2.0 %copy-done.4 = bf16[1,1024,1792]{2,1,0:T(8,128)(2,1)S(1)} copy-done((bf16[1,1024,1792]{2,1,0:T(8,128)(2,1)S(1)}, bf16[1,1024,1792]{2,1,0:T(8,128)(2,1)}, u32[]{:S(2)}) %copy-start.4) | copy-done | bytes 3670040
  20.1 4.4 %shard_map.105 = (bf16[160,768]{1,0:T(8,128)(2,1)S(1)}, bf16[160,768]{1,0:T(8,128)(2,1)S(1)}, bf16[160,768]{1,0:T(8,128)(2,1)S(1)}, bf16[160,768]{1,0:T(8,128)(2,1)S(1)}) custom-call(s32[1]{0:T(128)} %bitcast.3.refs_0_, bf16[80,3584]{1,0:T(8,128)(2,1)S(1)} %copy-done.6, bf16[80,3584]{1,0:T(8,128)(2,1)S(1)} %collective-permute-done.1.refs_2_.refs_22_, ...), custom_call_target="tpu_custom_call" | custom-call | tf_op jit(solution)/shard_map/pallas_call | solution.py:40
  24.5 1.3 collective-permute-start.2
  27.2 5.3 %collective-permute-done.refs_2_.refs_1_.refs_23_ = bf16[80,3584]{1,0:T(8,128)(2,1)S(1)} collective-permute-done((bf16[80,3584]{1,0:T(8,128)(2,1)}, bf16[80,3584]{1,0:T(8,128)(2,1)S(1)}, u32[]{:S(2)}, u32[]{:S(2)}) %collective-permute-start) | collective-permute-done | bytes 573472 | tf_op jit(solution)/shard_map/ppermute | solution.py:365
  33.2 2.6 %collective-permute-start.14 = (bf16[80,3584]{1,0:T(8,128)(2,1)S(1)}, bf16[80,3584]{1,0:T(8,128)(2,1)S(1)}, u32[]{:S(2)}, u32[]{:S(2)}) collective-permute-start(bf16[80,3584]{1,0:T(8,128)(2,1)S(1)} %shard_map.106.refs_1_), channel_id=1, source_target_pairs={{0,5},{1,4},{2,7},{3,6},{4,1},{5,0},{6,3},{7,2},{8,13},{9,12},{10,... | collective-permute-start | bytes 1720328 | tf_op jit(solution)/shard_map/ppermute | solution.py:365
  35.9 2.2 %collective-permute-done.4.refs_3_ = bf16[160,768]{1,0:T(8,128)(2,1)S(1)} collective-permute-done((bf16[160,768]{1,0:T(8,128)(2,1)S(1)}, bf16[160,768]{1,0:T(8,128)(2,1)S(1)}, u32[]{:S(2)}, u32[]{:S(2)}) %collective-permute-start.4) | collective-permute-done | bytes 245792 | tf_op jit(solution)/shard_map/ppermute | solution.py:368
  41.0 4.0 %shard_map.109 = (bf16[80,768]{1,0:T(8,128)(2,1)S(1)}, bf16[80,768]{1,0:T(8,128)(2,1)S(1)}, bf16[80,768]{1,0:T(8,128)(2,1)S(1)}, bf16[80,768]{1,0:T(8,128)(2,1)S(1)}) custom-call(s32[1]{0:T(128)} %bitcast.3.refs_0_, bf16[80,3584]{1,0:T(8,128)(2,1)S(1)} %collective-permute-done.refs_2_.refs_1_.refs_23_, bf16[1792,1024]{1,0:T(8,128)(2,1)S(1)} %bitcast.11, ...), custom_call_target="tpu_custom_call" | custom-call | tf_op jit(solution)/shard_map/pallas_call | solution.py:40
  45.3 1.4 collective-permute-start.5
  46.7 5.7 %collective-permute-done.9.refs_3_ = bf16[160,768]{1,0:T(8,128)(2,1)S(1)} collective-permute-done((bf16[160,768]{1,0:T(8,128)(2,1)S(1)}, bf16[160,768]{1,0:T(8,128)(2,1)S(1)}, u32[]{:S(2)}, u32[]{:S(2)}) %collective-permute-start.9) | collective-permute-done | bytes 245792 | tf_op jit(solution)/shard_map/ppermute | solution.py:368
  54.7 3.7 %shard_map.110 = (bf16[80,1792]{1,0:T(8,128)(2,1)S(1)}, bf16[80,1792]{1,0:T(8,128)(2,1)S(1)}) custom-call(s32[1]{0:T(128)} %bitcast.3.refs_0_, bf16[160,768]{1,0:T(8,128)(2,1)S(1)} %shard_map.108.refs_5_.refs_1_, bf16[160,768]{1,0:T(8,128)(2,1)S(1)} %collective-permute-done.8.refs_2_, bf16[160,768]{1,0:T(8,128)(2,1)S(1)} %collective-permute-done.9.refs_3_, ...), custom_call_target="tpu_custom_call" | custom-call | tf_op jit(solution)/shard_map/pallas_call | solution.py:40
  58.8 2.4 %collective-permute-done.14.refs_2_.refs_1_.refs_24_ = bf16[80,3584]{1,0:T(8,128)(2,1)S(1)} collective-permute-done((bf16[80,3584]{1,0:T(8,128)(2,1)S(1)}, bf16[80,3584]{1,0:T(8,128)(2,1)S(1)}, u32[]{:S(2)}, u32[]{:S(2)}) %collective-permute-start.14) | collective-permute-done | bytes 573472 | tf_op jit(solution)/shard_map/ppermute | solution.py:365
  61.2 1.3 collective-permute-start.23
  62.5 2.2 %collective-permute-start.13 = (bf16[80,768]{1,0:T(8,128)(2,1)S(1)}, bf16[80,768]{1,0:T(8,128)(2,1)S(1)}, u32[]{:S(2)}, u32[]{:S(2)}) collective-permute-start(bf16[80,768]{1,0:T(8,128)(2,1)S(1)} %shard_map.111.refs_1_.refs_5_), channel_id=1, source_target_pairs={{0,24},{8,16},{16,8},{24,0},{1,25},{9,17},{17,9},{25,1},{2,26},{10... | collective-permute-start | bytes 368648 | tf_op jit(solution)/shard_map/ppermute | solution.py:368
  65.1 4.2 %shard_map.114 = (bf16[160,768]{1,0:T(8,128)(2,1)S(1)}, bf16[160,768]{1,0:T(8,128)(2,1)S(1)}, bf16[160,768]{1,0:T(8,128)(2,1)S(1)}, bf16[160,768]{1,0:T(8,128)(2,1)S(1)}) custom-call(s32[1]{0:T(128)} %bitcast.3.refs_0_, bf16[80,3584]{1,0:T(8,128)(2,1)S(1)} %collective-permute-done.14.refs_2_.refs_1_.refs_24_, ...), custom_call_target="tpu_custom_call" | custom-call | tf_op jit(solution)/shard_map/pallas_call | solution.py:40
  69.4 1.3 collective-permute-start.16
  73.7 3.3 %shard_map.115.refs_4_.refs_0_ = bf16[80,1792]{1,0:T(8,128)(2,1)S(1)} custom-call(s32[1]{0:T(128)} %bitcast.3.refs_0_, bf16[80,768]{1,0:T(8,128)(2,1)S(1)} %shard_map.111.refs_1_.refs_5_, bf16[80,768]{1,0:T(8,128)(2,1)S(1)} %collective-permute-done.11.refs_2_.refs_6_, bf16[80,768]{1,0:T(8,128)(2,1)S(1)} %collective-permute-done.12.refs_3_.refs_7_, ...), custom_call_target="tpu_custom_call" | custom-call | tf_op jit(solution)/shard_map/pallas_call | solution.py:40
  77.0 1.9 %collective-permute-done.17.refs_2_ = bf16[160,768]{1,0:T(8,128)(2,1)S(1)} collective-permute-done((bf16[160,768]{1,0:T(8,128)(2,1)S(1)}, bf16[160,768]{1,0:T(8,128)(2,1)S(1)}, u32[]{:S(2)}, u32[]{:S(2)}) %collective-permute-start.17) | collective-permute-done | bytes 245792 | tf_op jit(solution)/shard_map/ppermute | solution.py:368
  78.9 2.9 %collective-permute-done.18.refs_3_ = bf16[160,768]{1,0:T(8,128)(2,1)S(1)} collective-permute-done((bf16[160,768]{1,0:T(8,128)(2,1)S(1)}, bf16[160,768]{1,0:T(8,128)(2,1)S(1)}, u32[]{:S(2)}, u32[]{:S(2)}) %collective-permute-start.18) | collective-permute-done | bytes 245792 | tf_op jit(solution)/shard_map/ppermute | solution.py:368
  83.2 1.3 collective-permute-start.20
  85.3 1.3 collective-permute-done.23.refs_3_.refs_2_.refs_27_
  86.6 3.4 %collective-permute-start.28 = (bf16[80,3584]{1,0:T(8,128)(2,1)S(1)}, bf16[80,3584]{1,0:T(8,128)(2,1)S(1)}, u32[]{:S(2)}, u32[]{:S(2)}) collective-permute-start(bf16[80,3584]{1,0:T(8,128)(2,1)S(1)} %shard_map.117.refs_6_), channel_id=1, source_target_pairs={{0,7},{1,6},{2,5},{3,4},{4,3},{5,2},{6,1},{7,0},{8,15},{9,14},{10,... | collective-permute-start | bytes 1720328 | tf_op jit(solution)/shard_map/ppermute | solution.py:365
  90.3 4.2 %shard_map.118 = (bf16[160,768]{1,0:T(8,128)(2,1)S(1)}, bf16[160,768]{1,0:T(8,128)(2,1)S(1)}, bf16[160,768]{1,0:T(8,128)(2,1)S(1)}, bf16[160,768]{1,0:T(8,128)(2,1)S(1)}) custom-call(s32[1]{0:T(128)} %bitcast.3.refs_0_, bf16[80,3584]{1,0:T(8,128)(2,1)S(1)} %collective-permute-done.22.refs_2_.refs_1_.refs_26_, ...), custom_call_target="tpu_custom_call" | custom-call | tf_op jit(solution)/shard_map/pallas_call | solution.py:40
  94.5 1.3 collective-permute-start.25
  95.9 1.3 collective-permute-start.27
  97.7 3.7 %shard_map.119 = (bf16[80,1792]{1,0:T(8,128)(2,1)S(1)}, bf16[80,1792]{1,0:T(8,128)(2,1)S(1)}) custom-call(s32[1]{0:T(128)} %bitcast.3.refs_0_, bf16[160,768]{1,0:T(8,128)(2,1)S(1)} %shard_map.116.refs_1_.refs_9_, bf16[160,768]{1,0:T(8,128)(2,1)S(1)} %collective-permute-done.19.refs_2_.refs_10_, ...), custom_call_target="tpu_custom_call" | custom-call | tf_op jit(solution)/shard_map/pallas_call | solution.py:40
  103.3 4.8 %collective-permute-done.27.refs_3_ = bf16[160,768]{1,0:T(8,128)(2,1)S(1)} collective-permute-done((bf16[160,768]{1,0:T(8,128)(2,1)S(1)}, bf16[160,768]{1,0:T(8,128)(2,1)S(1)}, u32[]{:S(2)}, u32[]{:S(2)}) %collective-permute-start.27) | collective-permute-done | bytes 245792 | tf_op jit(solution)/shard_map/ppermute | solution.py:368
  108.3 2.1 %collective-permute-start.32 = (bf16[160,768]{1,0:T(8,128)(2,1)S(1)}, bf16[160,768]{1,0:T(8,128)(2,1)S(1)}, u32[]{:S(2)}, u32[]{:S(2)}) collective-permute-start(bf16[160,768]{1,0:T(8,128)(2,1)S(1)} %shard_map.120.refs_2_.refs_1_.refs_13_), channel_id=1, source_target_pairs={{0,24},{8,16},{16,8},{24,0},{1,25},{9,17},{17,9},{25,1},{2,26},{10... | collective-permute-start | bytes 737288 | tf_op jit(solution)/shard_map/ppermute | solution.py:368
  111.0 4.4 %collective-permute-done.28.refs_3_.refs_1_.refs_28_ = bf16[80,3584]{1,0:T(8,128)(2,1)S(1)} collective-permute-done((bf16[80,3584]{1,0:T(8,128)(2,1)S(1)}, bf16[80,3584]{1,0:T(8,128)(2,1)S(1)}, u32[]{:S(2)}, u32[]{:S(2)}) %collective-permute-start.28) | collective-permute-done | bytes 573472 | tf_op jit(solution)/shard_map/ppermute | solution.py:365
  115.6 4.0 %shard_map.122 = (bf16[80,768]{1,0:T(8,128)(2,1)S(1)}, bf16[80,768]{1,0:T(8,128)(2,1)S(1)}, bf16[80,768]{1,0:T(8,128)(2,1)S(1)}, bf16[80,768]{1,0:T(8,128)(2,1)S(1)}) custom-call(s32[1]{0:T(128)} %bitcast.3.refs_0_, bf16[80,3584]{1,0:T(8,128)(2,1)S(1)} %collective-permute-done.28.refs_3_.refs_1_.refs_28_, bf16[1792,1024]{1,0:T(8,128)(2,1)S(1)} %bitcast.17, ...), custom_call_target="tpu_custom_call" | custom-call | tf_op jit(solution)/shard_map/pallas_call | solution.py:40
  120.1 2.3 %collective-permute-done.31.refs_3_.refs_15_ = bf16[160,768]{1,0:T(8,128)(2,1)S(1)} collective-permute-done((bf16[160,768]{1,0:T(8,128)(2,1)S(1)}, bf16[160,768]{1,0:T(8,128)(2,1)S(1)}, u32[]{:S(2)}, u32[]{:S(2)}) %collective-permute-start.31) | collective-permute-done | bytes 245792 | tf_op jit(solution)/shard_map/ppermute | solution.py:368
  123.2 1.3 collective-permute-start.36
  124.5 3.7 %shard_map.123 = (bf16[80,1792]{1,0:T(8,128)(2,1)S(1)}, bf16[80,1792]{1,0:T(8,128)(2,1)S(1)}) custom-call(s32[1]{0:T(128)} %bitcast.3.refs_0_, bf16[160,768]{1,0:T(8,128)(2,1)S(1)} %shard_map.120.refs_2_.refs_1_.refs_13_, bf16[160,768]{1,0:T(8,128)(2,1)S(1)} %collective-permute-done.30.refs_2_.refs_14_, ...), custom_call_target="tpu_custom_call" | custom-call | tf_op jit(solution)/shard_map/pallas_call | solution.py:40
  128.4 1.3 collective-permute-start.39
  131.6 1.6 collective-permute-done.39.refs_4_.refs_20_
  133.2 1.7 %collective-permute-start.42 = (bf16[80,1792]{1,0:T(8,128)(2,1)S(1)}, bf16[80,1792]{1,0:T(8,128)(2,1)S(1)}, u32[]{:S(2)}, u32[]{:S(2)}) collective-permute-start(bf16[80,1792]{1,0:T(8,128)(2,1)S(1)} %get-tuple-element.75), channel_id=1, source_target_pairs={{0,2},{1,3},{2,0},{3,1},{4,6},{5,7},{6,4},{7,5},{8,10},{9,11},{10,... | collective-permute-start | bytes 860168 | tf_op jit(solution)/shard_map/ppermute | solution.py:365
  134.9 2.0 %collective-permute-start.43 = (bf16[80,1792]{1,0:T(8,128)(2,1)S(1)}, bf16[80,1792]{1,0:T(8,128)(2,1)S(1)}, u32[]{:S(2)}, u32[]{:S(2)}) collective-permute-start(bf16[80,1792]{1,0:T(8,128)(2,1)S(1)} %get-tuple-element.73.refs_4_), channel_id=1, source_target_pairs={{0,6},{1,7},{2,4},{3,5},{4,2},{5,3},{6,0},{7,1},{8,14},{9,15},{10,... | collective-permute-start | bytes 860168 | tf_op jit(solution)/shard_map/ppermute | solution.py:365
  136.9 5.4 %collective-permute-start.33 = (bf16[80,1792]{1,0:T(8,128)(2,1)S(1)}, bf16[80,1792]{1,0:T(8,128)(2,1)S(1)}, u32[]{:S(2)}, u32[]{:S(2)}) collective-permute-start(bf16[80,1792]{1,0:T(8,128)(2,1)S(1)} %get-tuple-element.69), channel_id=1, source_target_pairs={{0,3},{1,2},{2,1},{3,0},{4,7},{5,6},{6,5},{7,4},{8,11},{9,10},{10,... | collective-permute-start | bytes 860168 | tf_op jit(solution)/shard_map/ppermute | solution.py:365
  142.3 3.3 %shard_map.125.refs_31_ = bf16[80,1792]{1,0:T(8,128)(2,1)S(1)} custom-call(s32[1]{0:T(128)} %bitcast.3.refs_0_, bf16[80,768]{1,0:T(8,128)(2,1)S(1)} %shard_map.124.refs_1_.refs_7_.refs_17_, bf16[80,768]{1,0:T(8,128)(2,1)S(1)} %collective-permute-done.37.refs_2_.refs_18_, bf16[80,768]{1,0:T(8,128)(2,1)S(1)} %collective-permute-done.38.refs_3_.refs_19_, ...), custom_call_target="tpu_custom_call" | custom-call | tf_op jit(solution)/shard_map/pallas_call | solution.py:40
  145.7 10.7 %shard_map.126 = (bf16[1024,1792]{1,0:T(8,128)(2,1)}, bf16[1024,1792]{1,0:T(8,128)(2,1)}, f32[8,128]{1,0:T(8,128)S(1)}) custom-call(s32[1]{0:T(128)} %bitcast.3.refs_0_, bf16[160,768]{1,0:T(8,128)(2,1)S(1)} %shard_map.108.refs_5_.refs_1_, bf16[160,768]{1,0:T(8,128)(2,1)S(1)} %collective-permute-done.8.refs_2_, ...), custom_call_target="tpu_custom_call" | custom-call | tf_op jit(solution)/shard_map/pallas_call | solution.py:40
  156.5 1.6 shard_map.127.refs_5_
  158.0 3.8 %collective-permute-done.33.refs_3_ = bf16[80,1792]{1,0:T(8,128)(2,1)S(1)} collective-permute-done((bf16[80,1792]{1,0:T(8,128)(2,1)S(1)}, bf16[80,1792]{1,0:T(8,128)(2,1)S(1)}, u32[]{:S(2)}, u32[]{:S(2)}) %collective-permute-start.33) | collective-permute-done | bytes 286752 | tf_op jit(solution)/shard_map/ppermute | solution.py:365
  161.8 2.4 %collective-permute-done.40.refs_4_ = bf16[80,1792]{1,0:T(8,128)(2,1)S(1)} collective-permute-done((bf16[80,1792]{1,0:T(8,128)(2,1)S(1)}, bf16[80,1792]{1,0:T(8,128)(2,1)S(1)}, u32[]{:S(2)}, u32[]{:S(2)}) %collective-permute-start.40) | collective-permute-done | bytes 286752 | tf_op jit(solution)/shard_map/ppermute | solution.py:365
  164.3 1.9 %shard_map.128 = bf16[512,1792]{1,0:T(8,128)(2,1)} custom-call(s32[1]{0:T(128)} %bitcast.refs_0_, s32[1,512]{1,0:T(1,128)S(1)} %copy-done.14, bf16[160,1792]{1,0:T(8,128)(2,1)S(1)} %collective-permute-done.29.refs_4_.refs_2_, bf16[80,1792]{1,0:T(8,128)(2,1)S(1)} %collective-permute-done.33.refs_3_, bf16[80,1792]{1,0:T(8,128)(2,1)S(1)} %collective-permute-done.40.refs_4_, ...), custom_call_target="tpu_custom_call" | custom-call | tf_op jit(solution)/shard_map/pallas_call | solution.py:40
  (96 shorter events, 22.8 us)
Async XLA Ops:
  4.2 8.6 %collective-permute-start.1 = (bf16[80,3584]{1,0:T(8,128)(2,1)}, bf16[80,3584]{1,0:T(8,128)(2,1)S(1)}, u32[]{:S(2)}, u32[]{:S(2)}) collective-permute-start(bf16[80,3584]{1,0:T(8,128)(2,1)} %get-tuple-element.44), channel_id=1, source_target_pairs={{0,1},{1,0},{2,3},{3,2},{4,5},{5,4},{6,7},{7,6},{8,9},{9,8},{10,11... | collective-permute-start | bytes 1720328 | tf_op jit(solution)/shard_map/ppermute | solution.py:365
  5.0 27.6 %collective-permute-start = (bf16[80,3584]{1,0:T(8,128)(2,1)}, bf16[80,3584]{1,0:T(8,128)(2,1)S(1)}, u32[]{:S(2)}, u32[]{:S(2)}) collective-permute-start(bf16[80,3584]{1,0:T(8,128)(2,1)} %get-tuple-element.42.refs_5_), channel_id=1, source_target_pairs={{0,4},{1,5},{2,6},{3,7},{4,0},{5,1},{6,2},{7,3},{8,12},{9,13},{10,... | collective-permute-start | bytes 1720328 | tf_op jit(solution)/shard_map/ppermute | solution.py:365
  20.0 20.9 %copy-start.3 = (bf16[1,1792,1024]{2,1,0:T(8,128)(2,1)S(1)}, bf16[1,1792,1024]{2,1,0:T(8,128)(2,1)}, u32[]{:S(2)}) copy-start(bf16[1,1792,1024]{2,1,0:T(8,128)(2,1)} %param.13) | copy-start | bytes 11010052
  20.0 20.9 %copy-start.5 = (bf16[1,1024,1792]{2,1,0:T(8,128)(2,1)S(1)}, bf16[1,1024,1792]{2,1,0:T(8,128)(2,1)}, u32[]{:S(2)}) copy-start(bf16[1,1024,1792]{2,1,0:T(8,128)(2,1)} %param.14) | copy-start | bytes 11010052
  24.5 16.5 %copy-start.1 = (bf16[1,1792,1024]{2,1,0:T(8,128)(2,1)S(1)}, bf16[1,1792,1024]{2,1,0:T(8,128)(2,1)}, u32[]{:S(2)}) copy-start(bf16[1,1792,1024]{2,1,0:T(8,128)(2,1)} %param.12) | copy-start | bytes 11010052
  24.5 11.4 %collective-permute-start.2 = (bf16[160,768]{1,0:T(8,128)(2,1)S(1)}, bf16[160,768]{1,0:T(8,128)(2,1)S(1)}, u32[]{:S(2)}, u32[]{:S(2)}) collective-permute-start(bf16[160,768]{1,0:T(8,128)(2,1)S(1)} %get-tuple-element.46), channel_id=1, source_target_pairs={{0,8},{8,0},{16,24},{24,16},{1,9},{9,1},{17,25},{25,17},{2,10},{10... | collective-permute-start | bytes 737288 | tf_op jit(solution)/shard_map/ppermute | solution.py:368
  25.8 10.1 %collective-permute-start.3 = (bf16[160,768]{1,0:T(8,128)(2,1)S(1)}, bf16[160,768]{1,0:T(8,128)(2,1)S(1)}, u32[]{:S(2)}, u32[]{:S(2)}) collective-permute-start(bf16[160,768]{1,0:T(8,128)(2,1)S(1)} %get-tuple-element.47), channel_id=1, source_target_pairs={{0,16},{8,24},{16,0},{24,8},{1,17},{9,25},{17,1},{25,9},{2,18},{10... | collective-permute-start | bytes 737288 | tf_op jit(solution)/shard_map/ppermute | solution.py:368
  27.0 11.0 %collective-permute-start.4 = (bf16[160,768]{1,0:T(8,128)(2,1)S(1)}, bf16[160,768]{1,0:T(8,128)(2,1)S(1)}, u32[]{:S(2)}, u32[]{:S(2)}) collective-permute-start(bf16[160,768]{1,0:T(8,128)(2,1)S(1)} %get-tuple-element.48), channel_id=1, source_target_pairs={{0,24},{8,16},{16,8},{24,0},{1,25},{9,17},{17,9},{25,1},{2,26},{10... | collective-permute-start | bytes 737288 | tf_op jit(solution)/shard_map/ppermute | solution.py:368
  32.5 26.1 %collective-permute-start.15 = (bf16[80,3584]{1,0:T(8,128)(2,1)S(1)}, bf16[80,3584]{1,0:T(8,128)(2,1)S(1)}, u32[]{:S(2)}, u32[]{:S(2)}) collective-permute-start(bf16[80,3584]{1,0:T(8,128)(2,1)S(1)} %shard_map.107.refs_4_), channel_id=1, source_target_pairs={{0,2},{1,3},{2,0},{3,1},{4,6},{5,7},{6,4},{7,5},{8,10},{9,11},{10,... | collective-permute-start | bytes 1720328 | tf_op jit(solution)/shard_map/ppermute | solution.py:365
  33.2 27.9 %collective-permute-start.14 = (bf16[80,3584]{1,0:T(8,128)(2,1)S(1)}, bf16[80,3584]{1,0:T(8,128)(2,1)S(1)}, u32[]{:S(2)}, u32[]{:S(2)}) collective-permute-start(bf16[80,3584]{1,0:T(8,128)(2,1)S(1)} %shard_map.106.refs_1_), channel_id=1, source_target_pairs={{0,5},{1,4},{2,7},{3,6},{4,1},{5,0},{6,3},{7,2},{8,13},{9,12},{10,... | collective-permute-start | bytes 1720328 | tf_op jit(solution)/shard_map/ppermute | solution.py:365
  38.2 7.1 %collective-permute-start.10 = (bf16[160,768]{1,0:T(8,128)(2,1)S(1)}, bf16[160,768]{1,0:T(8,128)(2,1)S(1)}, u32[]{:S(2)}, u32[]{:S(2)}) collective-permute-start(bf16[160,768]{1,0:T(8,128)(2,1)S(1)} %shard_map.108.refs_5_.refs_1_), channel_id=1, source_target_pairs={{0,24},{8,16},{16,8},{24,0},{1,25},{9,17},{17,9},{25,1},{2,26},{10... | collective-permute-start | bytes 737288 | tf_op jit(solution)/shard_map/ppermute | solution.py:368
  39.5 12.9 %collective-permute-start.9 = (bf16[160,768]{1,0:T(8,128)(2,1)S(1)}, bf16[160,768]{1,0:T(8,128)(2,1)S(1)}, u32[]{:S(2)}, u32[]{:S(2)}) collective-permute-start(bf16[160,768]{1,0:T(8,128)(2,1)S(1)} %shard_map.108.refs_5_.refs_1_), channel_id=1, source_target_pairs={{0,16},{8,24},{16,0},{24,8},{1,17},{9,25},{17,1},{25,9},{2,18},{10... | collective-permute-start | bytes 737288 | tf_op jit(solution)/shard_map/ppermute | solution.py:368
  40.7 12.8 %collective-permute-start.8 = (bf16[160,768]{1,0:T(8,128)(2,1)S(1)}, bf16[160,768]{1,0:T(8,128)(2,1)S(1)}, u32[]{:S(2)}, u32[]{:S(2)}) collective-permute-start(bf16[160,768]{1,0:T(8,128)(2,1)S(1)} %shard_map.108.refs_5_.refs_1_), channel_id=1, source_target_pairs={{0,8},{8,0},{16,24},{24,16},{1,9},{9,1},{17,25},{25,17},{2,10},{10... | collective-permute-start | bytes 737288 | tf_op jit(solution)/shard_map/ppermute | solution.py:368
  45.3 13.1 %collective-permute-start.5 = (bf16[80,768]{1,0:T(8,128)(2,1)S(1)}, bf16[80,768]{1,0:T(8,128)(2,1)S(1)}, u32[]{:S(2)}, u32[]{:S(2)}) collective-permute-start(bf16[80,768]{1,0:T(8,128)(2,1)S(1)} %get-tuple-element.52), channel_id=1, source_target_pairs={{0,8},{8,0},{16,24},{24,16},{1,9},{9,1},{17,25},{25,17},{2,10},{10... | collective-permute-start | bytes 368648 | tf_op jit(solution)/shard_map/ppermute | solution.py:368
  52.3 6.1 %collective-permute-start.6 = (bf16[80,768]{1,0:T(8,128)(2,1)S(1)}, bf16[80,768]{1,0:T(8,128)(2,1)S(1)}, u32[]{:S(2)}, u32[]{:S(2)}) collective-permute-start(bf16[80,768]{1,0:T(8,128)(2,1)S(1)} %get-tuple-element.53), channel_id=1, source_target_pairs={{0,16},{8,24},{16,0},{24,8},{1,17},{9,25},{17,1},{25,9},{2,18},{10... | collective-permute-start | bytes 368648 | tf_op jit(solution)/shard_map/ppermute | solution.py:368
  53.5 5.1 %collective-permute-start.7 = (bf16[80,768]{1,0:T(8,128)(2,1)S(1)}, bf16[80,768]{1,0:T(8,128)(2,1)S(1)}, u32[]{:S(2)}, u32[]{:S(2)}) collective-permute-start(bf16[80,768]{1,0:T(8,128)(2,1)S(1)} %get-tuple-element.54), channel_id=1, source_target_pairs={{0,24},{8,16},{16,8},{24,0},{1,25},{9,17},{17,9},{25,1},{2,26},{10... | collective-permute-start | bytes 368648 | tf_op jit(solution)/shard_map/ppermute | solution.py:368
  58.7 26.6 %collective-permute-start.22 = (bf16[80,3584]{1,0:T(8,128)(2,1)S(1)}, bf16[80,3584]{1,0:T(8,128)(2,1)S(1)}, u32[]{:S(2)}, u32[]{:S(2)}) collective-permute-start(bf16[80,3584]{1,0:T(8,128)(2,1)S(1)} %shard_map.112.refs_1_), channel_id=1, source_target_pairs={{0,6},{1,7},{2,4},{3,5},{4,2},{5,3},{6,0},{7,1},{8,14},{9,15},{10,... | collective-permute-start | bytes 1720328 | tf_op jit(solution)/shard_map/ppermute | solution.py:365
  61.2 25.5 %collective-permute-start.23 = (bf16[80,3584]{1,0:T(8,128)(2,1)S(1)}, bf16[80,3584]{1,0:T(8,128)(2,1)S(1)}, u32[]{:S(2)}, u32[]{:S(2)}) collective-permute-start(bf16[80,3584]{1,0:T(8,128)(2,1)S(1)} %shard_map.113.refs_6_), channel_id=1, source_target_pairs={{0,3},{1,2},{2,1},{3,0},{4,7},{5,6},{6,5},{7,4},{8,11},{9,10},{10,... | collective-permute-start | bytes 1720328 | tf_op jit(solution)/shard_map/ppermute | solution.py:365
  62.5 6.9 %collective-permute-start.13 = (bf16[80,768]{1,0:T(8,128)(2,1)S(1)}, bf16[80,768]{1,0:T(8,128)(2,1)S(1)}, u32[]{:S(2)}, u32[]{:S(2)}) collective-permute-start(bf16[80,768]{1,0:T(8,128)(2,1)S(1)} %shard_map.111.refs_1_.refs_5_), channel_id=1, source_target_pairs={{0,24},{8,16},{16,8},{24,0},{1,25},{9,17},{17,9},{25,1},{2,26},{10... | collective-permute-start | bytes 368648 | tf_op jit(solution)/shard_map/ppermute | solution.py:368
  64.6 6.6 %collective-permute-start.12 = (bf16[80,768]{1,0:T(8,128)(2,1)S(1)}, bf16[80,768]{1,0:T(8,128)(2,1)S(1)}, u32[]{:S(2)}, u32[]{:S(2)}) collective-permute-start(bf16[80,768]{1,0:T(8,128)(2,1)S(1)} %shard_map.111.refs_1_.refs_5_), channel_id=1, source_target_pairs={{0,16},{8,24},{16,0},{24,8},{1,17},{9,25},{17,1},{25,9},{2,18},{10... | collective-permute-start | bytes 368648 | tf_op jit(solution)/shard_map/ppermute | solution.py:368
  64.9 7.6 %collective-permute-start.11 = (bf16[80,768]{1,0:T(8,128)(2,1)S(1)}, bf16[80,768]{1,0:T(8,128)(2,1)S(1)}, u32[]{:S(2)}, u32[]{:S(2)}) collective-permute-start(bf16[80,768]{1,0:T(8,128)(2,1)S(1)} %shard_map.111.refs_1_.refs_5_), channel_id=1, source_target_pairs={{0,8},{8,0},{16,24},{24,16},{1,9},{9,1},{17,25},{25,17},{2,10},{10... | collective-permute-start | bytes 368648 | tf_op jit(solution)/shard_map/ppermute | solution.py:368
  69.4 7.6 %collective-permute-start.16 = (bf16[160,768]{1,0:T(8,128)(2,1)S(1)}, bf16[160,768]{1,0:T(8,128)(2,1)S(1)}, u32[]{:S(2)}, u32[]{:S(2)}) collective-permute-start(bf16[160,768]{1,0:T(8,128)(2,1)S(1)} %get-tuple-element.59), channel_id=1, source_target_pairs={{0,8},{8,0},{16,24},{24,16},{1,9},{9,1},{17,25},{25,17},{2,10},{10... | collective-permute-start | bytes 737288 | tf_op jit(solution)/shard_map/ppermute | solution.py:368
  71.3 7.6 %collective-permute-start.17 = (bf16[160,768]{1,0:T(8,128)(2,1)S(1)}, bf16[160,768]{1,0:T(8,128)(2,1)S(1)}, u32[]{:S(2)}, u32[]{:S(2)}) collective-permute-start(bf16[160,768]{1,0:T(8,128)(2,1)S(1)} %get-tuple-element.60), channel_id=1, source_target_pairs={{0,16},{8,24},{16,0},{24,8},{1,17},{9,25},{17,1},{25,9},{2,18},{10... | collective-permute-start | bytes 737288 | tf_op jit(solution)/shard_map/ppermute | solution.py:368
  72.5 9.3 %collective-permute-start.18 = (bf16[160,768]{1,0:T(8,128)(2,1)S(1)}, bf16[160,768]{1,0:T(8,128)(2,1)S(1)}, u32[]{:S(2)}, u32[]{:S(2)}) collective-permute-start(bf16[160,768]{1,0:T(8,128)(2,1)S(1)} %get-tuple-element.61), channel_id=1, source_target_pairs={{0,24},{8,16},{16,8},{24,0},{1,25},{9,17},{17,9},{25,1},{2,26},{10... | collective-permute-start | bytes 737288 | tf_op jit(solution)/shard_map/ppermute | solution.py:368
  73.7 13.0 %copy-start.9 = (bf16[80,3584]{1,0:T(8,128)(2,1)S(1)}, bf16[80,3584]{1,0:T(8,128)(2,1)}, u32[]{:S(2)}) copy-start(bf16[80,3584]{1,0:T(8,128)(2,1)} %get-tuple-element.62.refs_0_) | copy-start | bytes 1720324
  82.0 13.8 %collective-permute-start.21 = (bf16[160,768]{1,0:T(8,128)(2,1)S(1)}, bf16[160,768]{1,0:T(8,128)(2,1)S(1)}, u32[]{:S(2)}, u32[]{:S(2)}) collective-permute-start(bf16[160,768]{1,0:T(8,128)(2,1)S(1)} %shard_map.116.refs_1_.refs_9_), channel_id=1, source_target_pairs={{0,24},{8,16},{16,8},{24,0},{1,25},{9,17},{17,9},{25,1},{2,26},{10... | collective-permute-start | bytes 737288 | tf_op jit(solution)/shard_map/ppermute | solution.py:368
  83.2 12.7 %collective-permute-start.20 = (bf16[160,768]{1,0:T(8,128)(2,1)S(1)}, bf16[160,768]{1,0:T(8,128)(2,1)S(1)}, u32[]{:S(2)}, u32[]{:S(2)}) collective-permute-start(bf16[160,768]{1,0:T(8,128)(2,1)S(1)} %shard_map.116.refs_1_.refs_9_), channel_id=1, source_target_pairs={{0,16},{8,24},{16,0},{24,8},{1,17},{9,25},{17,1},{25,9},{2,18},{10... | collective-permute-start | bytes 737288 | tf_op jit(solution)/shard_map/ppermute | solution.py:368
  86.6 28.7 %collective-permute-start.28 = (bf16[80,3584]{1,0:T(8,128)(2,1)S(1)}, bf16[80,3584]{1,0:T(8,128)(2,1)S(1)}, u32[]{:S(2)}, u32[]{:S(2)}) collective-permute-start(bf16[80,3584]{1,0:T(8,128)(2,1)S(1)} %shard_map.117.refs_6_), channel_id=1, source_target_pairs={{0,7},{1,6},{2,5},{3,4},{4,3},{5,2},{6,1},{7,0},{8,15},{9,14},{10,... | collective-permute-start | bytes 1720328 | tf_op jit(solution)/shard_map/ppermute | solution.py:365
  90.0 7.7 %collective-permute-start.19 = (bf16[160,768]{1,0:T(8,128)(2,1)S(1)}, bf16[160,768]{1,0:T(8,128)(2,1)S(1)}, u32[]{:S(2)}, u32[]{:S(2)}) collective-permute-start(bf16[160,768]{1,0:T(8,128)(2,1)S(1)} %shard_map.116.refs_1_.refs_9_), channel_id=1, source_target_pairs={{0,8},{8,0},{16,24},{24,16},{1,9},{9,1},{17,25},{25,17},{2,10},{10... | collective-permute-start | bytes 737288 | tf_op jit(solution)/shard_map/ppermute | solution.py:368
  94.5 8.5 %collective-permute-start.25 = (bf16[160,768]{1,0:T(8,128)(2,1)S(1)}, bf16[160,768]{1,0:T(8,128)(2,1)S(1)}, u32[]{:S(2)}, u32[]{:S(2)}) collective-permute-start(bf16[160,768]{1,0:T(8,128)(2,1)S(1)} %get-tuple-element.65), channel_id=1, source_target_pairs={{0,8},{8,0},{16,24},{24,16},{1,9},{9,1},{17,25},{25,17},{2,10},{10... | collective-permute-start | bytes 737288 | tf_op jit(solution)/shard_map/ppermute | solution.py:368
  95.8 7.5 %collective-permute-start.26 = (bf16[160,768]{1,0:T(8,128)(2,1)S(1)}, bf16[160,768]{1,0:T(8,128)(2,1)S(1)}, u32[]{:S(2)}, u32[]{:S(2)}) collective-permute-start(bf16[160,768]{1,0:T(8,128)(2,1)S(1)} %get-tuple-element.66), channel_id=1, source_target_pairs={{0,16},{8,24},{16,0},{24,8},{1,17},{9,25},{17,1},{25,9},{2,18},{10... | collective-permute-start | bytes 737288 | tf_op jit(solution)/shard_map/ppermute | solution.py:368
  95.9 12.2 %collective-permute-start.27 = (bf16[160,768]{1,0:T(8,128)(2,1)S(1)}, bf16[160,768]{1,0:T(8,128)(2,1)S(1)}, u32[]{:S(2)}, u32[]{:S(2)}) collective-permute-start(bf16[160,768]{1,0:T(8,128)(2,1)S(1)} %get-tuple-element.67), channel_id=1, source_target_pairs={{0,24},{8,16},{16,8},{24,0},{1,25},{9,17},{17,9},{25,1},{2,26},{10... | collective-permute-start | bytes 737288 | tf_op jit(solution)/shard_map/ppermute | solution.py:368
  101.4 9.6 %collective-permute-start.24 = (bf16[80,1792]{1,0:T(8,128)(2,1)S(1)}, bf16[80,1792]{1,0:T(8,128)(2,1)S(1)}, u32[]{:S(2)}, u32[]{:S(2)}) collective-permute-start(bf16[80,1792]{1,0:T(8,128)(2,1)S(1)} %get-tuple-element.64.refs_4_), channel_id=1, source_target_pairs={{0,1},{1,0},{2,3},{3,2},{4,5},{5,4},{6,7},{7,6},{8,9},{9,8},{10,11... | collective-permute-start | bytes 860168 | tf_op jit(solution)/shard_map/ppermute | solution.py:365
  108.3 11.4 %collective-permute-start.32 = (bf16[160,768]{1,0:T(8,128)(2,1)S(1)}, bf16[160,768]{1,0:T(8,128)(2,1)S(1)}, u32[]{:S(2)}, u32[]{:S(2)}) collective-permute-start(bf16[160,768]{1,0:T(8,128)(2,1)S(1)} %shard_map.120.refs_2_.refs_1_.refs_13_), channel_id=1, source_target_pairs={{0,24},{8,16},{16,8},{24,0},{1,25},{9,17},{17,9},{25,1},{2,26},{10... | collective-permute-start | bytes 737288 | tf_op jit(solution)/shard_map/ppermute | solution.py:368
  110.4 12.0 %collective-permute-start.31 = (bf16[160,768]{1,0:T(8,128)(2,1)S(1)}, bf16[160,768]{1,0:T(8,128)(2,1)S(1)}, u32[]{:S(2)}, u32[]{:S(2)}) collective-permute-start(bf16[160,768]{1,0:T(8,128)(2,1)S(1)} %shard_map.120.refs_2_.refs_1_.refs_13_), channel_id=1, source_target_pairs={{0,16},{8,24},{16,0},{24,8},{1,17},{9,25},{17,1},{25,9},{2,18},{10... | collective-permute-start | bytes 737288 | tf_op jit(solution)/shard_map/ppermute | solution.py:368
  110.4 12.8 %collective-permute-start.30 = (bf16[160,768]{1,0:T(8,128)(2,1)S(1)}, bf16[160,768]{1,0:T(8,128)(2,1)S(1)}, u32[]{:S(2)}, u32[]{:S(2)}) collective-permute-start(bf16[160,768]{1,0:T(8,128)(2,1)S(1)} %shard_map.120.refs_2_.refs_1_.refs_13_), channel_id=1, source_target_pairs={{0,8},{8,0},{16,24},{24,16},{1,9},{9,1},{17,25},{25,17},{2,10},{10... | collective-permute-start | bytes 737288 | tf_op jit(solution)/shard_map/ppermute | solution.py:368
  115.4 41.0 %collective-permute-start.29 = (bf16[160,1792]{1,0:T(8,128)(2,1)S(1)}, bf16[160,1792]{1,0:T(8,128)(2,1)S(1)}, u32[]{:S(2)}, u32[]{:S(2)}) collective-permute-start(bf16[160,1792]{1,0:T(8,128)(2,1)S(1)} %shard_map.121.refs_5_), channel_id=1, source_target_pairs={{0,4},{1,5},{2,6},{3,7},{4,0},{5,1},{6,2},{7,3},{8,12},{9,13},{10,... | collective-permute-start | bytes 1720328 | tf_op jit(solution)/shard_map/ppermute | solution.py:365
  115.5 30.1 %collective-permute-start.41 = (bf16[80,1792]{1,0:T(8,128)(2,1)S(1)}, bf16[80,1792]{1,0:T(8,128)(2,1)S(1)}, u32[]{:S(2)}, u32[]{:S(2)}) collective-permute-start(bf16[80,1792]{1,0:T(8,128)(2,1)S(1)} %get-tuple-element.74), channel_id=1, source_target_pairs={{0,1},{1,0},{2,3},{3,2},{4,5},{5,4},{6,7},{7,6},{8,9},{9,8},{10,11... | collective-permute-start | bytes 860168 | tf_op jit(solution)/shard_map/ppermute | solution.py:365
  119.6 8.5 %collective-permute-start.34 = (bf16[80,768]{1,0:T(8,128)(2,1)S(1)}, bf16[80,768]{1,0:T(8,128)(2,1)S(1)}, u32[]{:S(2)}, u32[]{:S(2)}) collective-permute-start(bf16[80,768]{1,0:T(8,128)(2,1)S(1)} %get-tuple-element.70), channel_id=1, source_target_pairs={{0,8},{8,0},{16,24},{24,16},{1,9},{9,1},{17,25},{25,17},{2,10},{10... | collective-permute-start | bytes 368648 | tf_op jit(solution)/shard_map/ppermute | solution.py:368
  122.4 5.8 %collective-permute-start.35 = (bf16[80,768]{1,0:T(8,128)(2,1)S(1)}, bf16[80,768]{1,0:T(8,128)(2,1)S(1)}, u32[]{:S(2)}, u32[]{:S(2)}) collective-permute-start(bf16[80,768]{1,0:T(8,128)(2,1)S(1)} %get-tuple-element.71), channel_id=1, source_target_pairs={{0,16},{8,24},{16,0},{24,8},{1,17},{9,25},{17,1},{25,9},{2,18},{10... | collective-permute-start | bytes 368648 | tf_op jit(solution)/shard_map/ppermute | solution.py:368
  123.2 5.1 %collective-permute-start.36 = (bf16[80,768]{1,0:T(8,128)(2,1)S(1)}, bf16[80,768]{1,0:T(8,128)(2,1)S(1)}, u32[]{:S(2)}, u32[]{:S(2)}) collective-permute-start(bf16[80,768]{1,0:T(8,128)(2,1)S(1)} %get-tuple-element.72), channel_id=1, source_target_pairs={{0,24},{8,16},{16,8},{24,0},{1,25},{9,17},{17,9},{25,1},{2,26},{10... | collective-permute-start | bytes 368648 | tf_op jit(solution)/shard_map/ppermute | solution.py:368
  128.4 4.8 %collective-permute-start.39 = (bf16[80,768]{1,0:T(8,128)(2,1)S(1)}, bf16[80,768]{1,0:T(8,128)(2,1)S(1)}, u32[]{:S(2)}, u32[]{:S(2)}) collective-permute-start(bf16[80,768]{1,0:T(8,128)(2,1)S(1)} %shard_map.124.refs_1_.refs_7_.refs_17_), channel_id=1, source_target_pairs={{0,24},{8,16},{16,8},{24,0},{1,25},{9,17},{17,9},{25,1},{2,26},{10... | collective-permute-start | bytes 368648 | tf_op jit(solution)/shard_map/ppermute | solution.py:368
  129.7 5.2 %collective-permute-start.38 = (bf16[80,768]{1,0:T(8,128)(2,1)S(1)}, bf16[80,768]{1,0:T(8,128)(2,1)S(1)}, u32[]{:S(2)}, u32[]{:S(2)}) collective-permute-start(bf16[80,768]{1,0:T(8,128)(2,1)S(1)} %shard_map.124.refs_1_.refs_7_.refs_17_), channel_id=1, source_target_pairs={{0,16},{8,24},{16,0},{24,8},{1,17},{9,25},{17,1},{25,9},{2,18},{10... | collective-permute-start | bytes 368648 | tf_op jit(solution)/shard_map/ppermute | solution.py:368
  130.6 6.3 %collective-permute-start.37 = (bf16[80,768]{1,0:T(8,128)(2,1)S(1)}, bf16[80,768]{1,0:T(8,128)(2,1)S(1)}, u32[]{:S(2)}, u32[]{:S(2)}) collective-permute-start(bf16[80,768]{1,0:T(8,128)(2,1)S(1)} %shard_map.124.refs_1_.refs_7_.refs_17_), channel_id=1, source_target_pairs={{0,8},{8,0},{16,24},{24,16},{1,9},{9,1},{17,25},{25,17},{2,10},{10... | collective-permute-start | bytes 368648 | tf_op jit(solution)/shard_map/ppermute | solution.py:368
  133.2 23.2 %collective-permute-start.42 = (bf16[80,1792]{1,0:T(8,128)(2,1)S(1)}, bf16[80,1792]{1,0:T(8,128)(2,1)S(1)}, u32[]{:S(2)}, u32[]{:S(2)}) collective-permute-start(bf16[80,1792]{1,0:T(8,128)(2,1)S(1)} %get-tuple-element.75), channel_id=1, source_target_pairs={{0,2},{1,3},{2,0},{3,1},{4,6},{5,7},{6,4},{7,5},{8,10},{9,11},{10,... | collective-permute-start | bytes 860168 | tf_op jit(solution)/shard_map/ppermute | solution.py:365
  134.9 21.5 %collective-permute-start.43 = (bf16[80,1792]{1,0:T(8,128)(2,1)S(1)}, bf16[80,1792]{1,0:T(8,128)(2,1)S(1)}, u32[]{:S(2)}, u32[]{:S(2)}) collective-permute-start(bf16[80,1792]{1,0:T(8,128)(2,1)S(1)} %get-tuple-element.73.refs_4_), channel_id=1, source_target_pairs={{0,6},{1,7},{2,4},{3,5},{4,2},{5,3},{6,0},{7,1},{8,14},{9,15},{10,... | collective-permute-start | bytes 860168 | tf_op jit(solution)/shard_map/ppermute | solution.py:365
  136.9 24.9 %collective-permute-start.33 = (bf16[80,1792]{1,0:T(8,128)(2,1)S(1)}, bf16[80,1792]{1,0:T(8,128)(2,1)S(1)}, u32[]{:S(2)}, u32[]{:S(2)}) collective-permute-start(bf16[80,1792]{1,0:T(8,128)(2,1)S(1)} %get-tuple-element.69), channel_id=1, source_target_pairs={{0,3},{1,2},{2,1},{3,0},{4,7},{5,6},{6,5},{7,4},{8,11},{9,10},{10,... | collective-permute-start | bytes 860168 | tf_op jit(solution)/shard_map/ppermute | solution.py:365
  145.6 18.6 %collective-permute-start.40 = (bf16[80,1792]{1,0:T(8,128)(2,1)S(1)}, bf16[80,1792]{1,0:T(8,128)(2,1)S(1)}, u32[]{:S(2)}, u32[]{:S(2)}) collective-permute-start(bf16[80,1792]{1,0:T(8,128)(2,1)S(1)} %shard_map.125.refs_31_), channel_id=1, source_target_pairs={{0,7},{1,6},{2,5},{3,4},{4,3},{5,2},{6,1},{7,0},{8,15},{9,14},{10,... | collective-permute-start | bytes 860168 | tf_op jit(solution)/shard_map/ppermute | solution.py:365
  (11 other events, 65.7 us)

commit v7 on v6

--- a/solution.py
+++ b/solution.py
@@ -304,48 +304,72 @@
     )
 
 
-def combine_body(cap, offs, chained, me_ref, tgt_ref, *refs):
+def transposed_picks(cap, offs, me, target):
+    slots = lax.broadcasted_iota(jnp.int32, (cap, target.shape[1]), 0)
+    hits = [jnp.where(slots + (me ^ k) * cap == target, 1.0, 0.0) for k in offs]
+    return jnp.concatenate(hits, axis=0).T.astype(bf16)
+
+
+def combine_body(cap, offs, later, me_ref, tgt_ref, *refs):
     nb = len(offs)
-    backs = refs[:nb]
-    prev = refs[nb] if chained else None
-    out, pick_t, rows = refs[-3:]
+    backs, (out, later_picks, picks, rows) = refs[:nb], refs[nb:]
     part = out.shape[0]
     i = pl.program_id(0)
 
     @pl.when(i == 0)
     def _():
-        target = tgt_ref[...]
-        slots = lax.broadcasted_iota(jnp.int32, (cap, target.shape[1]), 0)
-        hits = [jnp.where(slots + (me_ref[0] ^ k) * cap == target, 1.0, 0.0) for k in offs]
-        pick_t[...] = jnp.concatenate(hits, axis=0).T.astype(bf16)
+        picks[...] = transposed_picks(cap, offs, me_ref[0], tgt_ref[...])
+        later_picks[...] = transposed_picks(cap, later, me_ref[0], tgt_ref[...])
         for j, blk in enumerate(backs):
             rows[j * cap : (j + 1) * cap, :] = blk[...]
 
-    total = dot(pick_t[pl.ds(pl.multiple_of(i * part, part), part), :], rows[...])
-    if chained:
-        total = total + prev[...].astype(f32)
-    out[...] = total.astype(bf16)
-
-
-def combine(cap, offs, me, target, backs, prev, deps):
+    out[...] = dot(picks[pl.ds(pl.multiple_of(i * part, part), part), :], rows[...]).astype(bf16)
+
+
+def combine(cap, offs, later, me, target, backs, deps):
     t = target.shape[1]
     s = backs[0][0].shape[1]
     nb = len(offs)
     part = t // 2
-    block = pl.BlockSpec((part, s), lambda c, i: (c, 0))
-    extra = [] if prev is None else [prev]
-    return call(
-        functools.partial(combine_body, cap, offs, prev is not None),
-        [me, target, *[v for v, _ in backs], *extra],
+    return call(
+        functools.partial(combine_body, cap, offs, later),
+        [me, target, *[v for v, _ in backs]],
         deps,
-        jax.ShapeDtypeStruct((t, s), bf16),
-        [whole((1, t))]
-        + [pl.BlockSpec((cap, s), lambda c, i, at=at: (at, 0)) for _, at in backs]
-        + [block] * len(extra),
-        block,
+        [jax.ShapeDtypeStruct((t, s), bf16), jax.ShapeDtypeStruct((t, len(later) * cap), bf16)],
+        [whole((1, t))] + [pl.BlockSpec((cap, s), lambda c, i, at=at: (at, 0)) for _, at in backs],
+        [pl.BlockSpec((part, s), lambda c, i: (c, 0)), whole((t, len(later) * cap))],
         grid=(2,),
         scalars=1,
         scratch=[pltpu.VMEM((t, nb * cap), bf16), pltpu.VMEM((nb * cap, s), bf16)],
+    )
+
+
+def finish_body(cap, nb, picks, prev, *refs):
+    backs, (out, rows) = refs[:nb], refs[nb:]
+
+    @pl.when(pl.program_id(0) == 0)
+    def _():
+        for j, blk in enumerate(backs):
+            rows[j * cap : (j + 1) * cap, :] = blk[...]
+
+    out[...] = (dot(picks[...], rows[...]) + prev[...].astype(f32)).astype(bf16)
+
+
+def finish(cap, picks, prev, backs):
+    t, s = prev.shape
+    nb = len(backs)
+    part = t // 2
+    block = pl.BlockSpec((part, s), lambda c: (c, 0))
+    return call(
+        functools.partial(finish_body, cap, nb),
+        [picks, prev, *[v for v, _ in backs]],
+        [],
+        jax.ShapeDtypeStruct((t, s), bf16),
+        [pl.BlockSpec((part, nb * cap), lambda c: (c, 0)), block]
+        + [pl.BlockSpec((cap, s), lambda c, at=at: (at, 0)) for _, at in backs],
+        block,
+        grid=(2,),
+        scratch=[pltpu.VMEM((nb * cap, s), bf16)],
     )
 
 
@@ -471,8 +495,8 @@
     give_back(near[2], None)
     tail = far[1] + near[2] + far[3]
     early = [k for k in flat if k not in tail]
-    part = combine(cap, early, me, target, [back[k] for k in early], None, mark)
-    grad_tokens = combine(cap, tail, me, target, [back[k] for k in tail], part, [])
+    part, picks = combine(cap, early, tail, me, target, [back[k] for k in early], mark)
+    grad_tokens = finish(cap, picks, part, [back[k] for k in tail])
     return (grad_tokens, new_down[None], new_moment[None])
 
 

time: 169 us -> 169 us (level)
  transfers between devices with their start and end apart: 44 -> 44, of which waited for: 21 -> 21; matrix products, arithmetic and copies ran while one was open for 0% -> 0% of each run, Pallas kernels for 34% -> 35%
where the time goes in v7:
time: 169 us; the launch traced here: 166 us
  Pallas kernels  62.7 us (37%)
  starting transfers between devices  50.3 us (30%)
  waiting for transfers between devices  44.9 us (27%)
  local copies, waits for them, and re-layouts  7.21 us (4%)
    pallas_call x26, Pallas kernels, call(): pl.pallas_call(skipping(body, len(operands), len(deps)), out_shape=out_sh...  62.7 us
    ppermute x30, starting transfers between devices, swap_dp(): return lax.ppermute(v, 'dp', [(i, i ^ k) for i in range(ndp)])  29.4 us
    ppermute x30, waiting for transfers between devices, swap_dp(): return lax.ppermute(v, 'dp', [(i, i ^ k) for i in range(ndp)])  24.5 us
    ppermute x14, starting transfers between devices, swap_expert(): return lax.ppermute(v, 'expert', [(i, i ^ k) for i in range(n)])  20.9 us
    ppermute x14, waiting for transfers between devices, swap_expert(): return lax.ppermute(v, 'expert', [(i, i ^ k) for i in range(n)])  20.4 us
    unnamed x30, local copies, waits for them, and re-layouts  7.21 us
  transfers between devices with their start and end apart: 44, of which 21 were waited for; matrix products, arithmetic and copies ran while one was open for 0% of the time, Pallas kernels for 35%

profile of v7, /device:TPU:9, one launch (start us, length us, event | category | flops | bytes accessed | tf_op | source)
XLA Modules:
  0.0 166.1 jit_solution(4758323838846834642)
XLA Ops:
  0.6 3.6 %shard_map.103 = (s32[1,512]{1,0:T(1,128)}, bf16[80,3584]{1,0:T(8,128)(2,1)}, bf16[80,3584]{1,0:T(8,128)(2,1)}) custom-call(s32[1]{0:T(128)} %bitcast.refs_0_, s32[1,512]{1,0:T(1,128)} %bitcast.37, s32[1,512]{1,0:T(1,128)} %bitcast.39, bf16[512,1792]{1,0:T(8,128)(2,1)} %refs_3_.3, bf16[512,1792]{1,0:T(8,128)(2,1)} %refs_4_.3), custom_call_target="tpu_custom_call" | custom-call | tf_op jit(solution)/shard_map/pallas_call | solution.py:40
  5.0 2.3 %collective-permute-start.4 = (bf16[80,3584]{1,0:T(8,128)(2,1)}, bf16[80,3584]{1,0:T(8,128)(2,1)S(1)}, u32[]{:S(2)}, u32[]{:S(2)}) collective-permute-start(bf16[80,3584]{1,0:T(8,128)(2,1)} %get-tuple-element.44.refs_5_), channel_id=1, source_target_pairs={{0,4},{1,5},{2,6},{3,7},{4,0},{5,1},{6,2},{7,3},{8,12},{9,13},{10,... | collective-permute-start | bytes 1720328 | tf_op jit(solution)/shard_map/ppermute | solution.py:389
  7.3 5.5 %shard_map.104 = (s32[1,512]{1,0:T(1,128)}, bf16[80,3584]{1,0:T(8,128)(2,1)}, bf16[80,3584]{1,0:T(8,128)(2,1)}, bf16[80,3584]{1,0:T(8,128)(2,1)}, bf16[80,3584]{...) custom-call(s32[1]{0:T(128)} %bitcast.refs_0_, s32[1,512]{1,0:T(1,128)} %bitcast.38, ...), custom_call_target="tpu_custom_call" | custom-call | tf_op jit(solution)/shard_map/pallas_call | solution.py:40
  12.9 2.0 %copy-done = bf16[1,1792,1024]{2,1,0:T(8,128)(2,1)S(1)} copy-done((bf16[1,1792,1024]{2,1,0:T(8,128)(2,1)S(1)}, bf16[1,1792,1024]{2,1,0:T(8,128)(2,1)}, u32[]{:S(2)}) %copy-start) | copy-done | bytes 3670040
  14.9 2.0 %copy-done.2 = bf16[1,1792,1024]{2,1,0:T(8,128)(2,1)S(1)} copy-done((bf16[1,1792,1024]{2,1,0:T(8,128)(2,1)S(1)}, bf16[1,1792,1024]{2,1,0:T(8,128)(2,1)}, u32[]{:S(2)}) %copy-start.2) | copy-done | bytes 3670040
  16.9 2.0 %copy-done.4 = bf16[1,1024,1792]{2,1,0:T(8,128)(2,1)S(1)} copy-done((bf16[1,1024,1792]{2,1,0:T(8,128)(2,1)S(1)}, bf16[1,1024,1792]{2,1,0:T(8,128)(2,1)}, u32[]{:S(2)}) %copy-start.4) | copy-done | bytes 3670040
  20.0 4.4 %shard_map.105 = (bf16[160,768]{1,0:T(8,128)(2,1)S(1)}, bf16[160,768]{1,0:T(8,128)(2,1)S(1)}, bf16[160,768]{1,0:T(8,128)(2,1)S(1)}, bf16[160,768]{1,0:T(8,128)(2,1)S(1)}) custom-call(s32[1]{0:T(128)} %bitcast.3.refs_0_, bf16[80,3584]{1,0:T(8,128)(2,1)S(1)} %copy-done.6, bf16[80,3584]{1,0:T(8,128)(2,1)S(1)} %collective-permute-done.refs_2_.refs_22_, ...), custom_call_target="tpu_custom_call" | custom-call | tf_op jit(solution)/shard_map/pallas_call | solution.py:40
  24.5 1.3 collective-permute-start.1
  27.2 5.3 %collective-permute-done.4.refs_2_.refs_1_.refs_23_ = bf16[80,3584]{1,0:T(8,128)(2,1)S(1)} collective-permute-done((bf16[80,3584]{1,0:T(8,128)(2,1)}, bf16[80,3584]{1,0:T(8,128)(2,1)S(1)}, u32[]{:S(2)}, u32[]{:S(2)}) %collective-permute-start.4) | collective-permute-done | bytes 573472 | tf_op jit(solution)/shard_map/ppermute | solution.py:389
  33.2 2.6 %collective-permute-start.15 = (bf16[80,3584]{1,0:T(8,128)(2,1)S(1)}, bf16[80,3584]{1,0:T(8,128)(2,1)S(1)}, u32[]{:S(2)}, u32[]{:S(2)}) collective-permute-start(bf16[80,3584]{1,0:T(8,128)(2,1)S(1)} %shard_map.106.refs_1_), channel_id=1, source_target_pairs={{0,5},{1,4},{2,7},{3,6},{4,1},{5,0},{6,3},{7,2},{8,13},{9,12},{10,... | collective-permute-start | bytes 1720328 | tf_op jit(solution)/shard_map/ppermute | solution.py:389
  35.9 2.2 %collective-permute-done.3.refs_3_ = bf16[160,768]{1,0:T(8,128)(2,1)S(1)} collective-permute-done((bf16[160,768]{1,0:T(8,128)(2,1)S(1)}, bf16[160,768]{1,0:T(8,128)(2,1)S(1)}, u32[]{:S(2)}, u32[]{:S(2)}) %collective-permute-start.3) | collective-permute-done | bytes 245792 | tf_op jit(solution)/shard_map/ppermute | solution.py:392
  41.0 4.0 %shard_map.109 = (bf16[80,768]{1,0:T(8,128)(2,1)S(1)}, bf16[80,768]{1,0:T(8,128)(2,1)S(1)}, bf16[80,768]{1,0:T(8,128)(2,1)S(1)}, bf16[80,768]{1,0:T(8,128)(2,1)S(1)}) custom-call(s32[1]{0:T(128)} %bitcast.3.refs_0_, bf16[80,3584]{1,0:T(8,128)(2,1)S(1)} %collective-permute-done.4.refs_2_.refs_1_.refs_23_, bf16[1792,1024]{1,0:T(8,128)(2,1)S(1)} %bitcast.11, ...), custom_call_target="tpu_custom_call" | custom-call | tf_op jit(solution)/shard_map/pallas_call | solution.py:40
  45.3 1.3 collective-permute-start.9
  46.7 5.7 %collective-permute-done.6.refs_3_ = bf16[160,768]{1,0:T(8,128)(2,1)S(1)} collective-permute-done((bf16[160,768]{1,0:T(8,128)(2,1)S(1)}, bf16[160,768]{1,0:T(8,128)(2,1)S(1)}, u32[]{:S(2)}, u32[]{:S(2)}) %collective-permute-start.6) | collective-permute-done | bytes 245792 | tf_op jit(solution)/shard_map/ppermute | solution.py:392
  54.7 3.7 %shard_map.110 = (bf16[80,1792]{1,0:T(8,128)(2,1)S(1)}, bf16[80,1792]{1,0:T(8,128)(2,1)S(1)}) custom-call(s32[1]{0:T(128)} %bitcast.3.refs_0_, bf16[160,768]{1,0:T(8,128)(2,1)S(1)} %shard_map.108.refs_5_.refs_1_, bf16[160,768]{1,0:T(8,128)(2,1)S(1)} %collective-permute-done.5.refs_2_, bf16[160,768]{1,0:T(8,128)(2,1)S(1)} %collective-permute-done.6.refs_3_, ...), custom_call_target="tpu_custom_call" | custom-call | tf_op jit(solution)/shard_map/pallas_call | solution.py:40
  58.8 2.4 %collective-permute-done.15.refs_2_.refs_1_.refs_24_ = bf16[80,3584]{1,0:T(8,128)(2,1)S(1)} collective-permute-done((bf16[80,3584]{1,0:T(8,128)(2,1)S(1)}, bf16[80,3584]{1,0:T(8,128)(2,1)S(1)}, u32[]{:S(2)}, u32[]{:S(2)}) %collective-permute-start.15) | collective-permute-done | bytes 573472 | tf_op jit(solution)/shard_map/ppermute | solution.py:389
  61.2 1.3 collective-permute-start.24
  62.5 2.2 %collective-permute-start.14 = (bf16[80,768]{1,0:T(8,128)(2,1)S(1)}, bf16[80,768]{1,0:T(8,128)(2,1)S(1)}, u32[]{:S(2)}, u32[]{:S(2)}) collective-permute-start(bf16[80,768]{1,0:T(8,128)(2,1)S(1)} %shard_map.111.refs_1_.refs_5_), channel_id=1, source_target_pairs={{0,24},{8,16},{16,8},{24,0},{1,25},{9,17},{17,9},{25,1},{2,26},{10... | collective-permute-start | bytes 368648 | tf_op jit(solution)/shard_map/ppermute | solution.py:392
  65.1 4.2 %shard_map.114 = (bf16[160,768]{1,0:T(8,128)(2,1)S(1)}, bf16[160,768]{1,0:T(8,128)(2,1)S(1)}, bf16[160,768]{1,0:T(8,128)(2,1)S(1)}, bf16[160,768]{1,0:T(8,128)(2,1)S(1)}) custom-call(s32[1]{0:T(128)} %bitcast.3.refs_0_, bf16[80,3584]{1,0:T(8,128)(2,1)S(1)} %collective-permute-done.15.refs_2_.refs_1_.refs_24_, ...), custom_call_target="tpu_custom_call" | custom-call | tf_op jit(solution)/shard_map/pallas_call | solution.py:40
  69.4 1.3 collective-permute-start.17
  73.7 3.3 %shard_map.115.refs_4_.refs_0_ = bf16[80,1792]{1,0:T(8,128)(2,1)S(1)} custom-call(s32[1]{0:T(128)} %bitcast.3.refs_0_, bf16[80,768]{1,0:T(8,128)(2,1)S(1)} %shard_map.111.refs_1_.refs_5_, bf16[80,768]{1,0:T(8,128)(2,1)S(1)} %collective-permute-done.12.refs_2_.refs_6_, bf16[80,768]{1,0:T(8,128)(2,1)S(1)} %collective-permute-done.13.refs_3_.refs_7_, ...), custom_call_target="tpu_custom_call" | custom-call | tf_op jit(solution)/shard_map/pallas_call | solution.py:40
  77.0 1.9 %collective-permute-done.18.refs_2_ = bf16[160,768]{1,0:T(8,128)(2,1)S(1)} collective-permute-done((bf16[160,768]{1,0:T(8,128)(2,1)S(1)}, bf16[160,768]{1,0:T(8,128)(2,1)S(1)}, u32[]{:S(2)}, u32[]{:S(2)}) %collective-permute-start.18) | collective-permute-done | bytes 245792 | tf_op jit(solution)/shard_map/ppermute | solution.py:392
  78.9 2.9 %collective-permute-done.19.refs_3_ = bf16[160,768]{1,0:T(8,128)(2,1)S(1)} collective-permute-done((bf16[160,768]{1,0:T(8,128)(2,1)S(1)}, bf16[160,768]{1,0:T(8,128)(2,1)S(1)}, u32[]{:S(2)}, u32[]{:S(2)}) %collective-permute-start.19) | collective-permute-done | bytes 245792 | tf_op jit(solution)/shard_map/ppermute | solution.py:392
  83.2 1.3 collective-permute-start.21
  85.3 1.3 collective-permute-done.24.refs_3_.refs_2_.refs_27_
  86.6 3.4 %collective-permute-start.29 = (bf16[80,3584]{1,0:T(8,128)(2,1)S(1)}, bf16[80,3584]{1,0:T(8,128)(2,1)S(1)}, u32[]{:S(2)}, u32[]{:S(2)}) collective-permute-start(bf16[80,3584]{1,0:T(8,128)(2,1)S(1)} %shard_map.117.refs_6_), channel_id=1, source_target_pairs={{0,7},{1,6},{2,5},{3,4},{4,3},{5,2},{6,1},{7,0},{8,15},{9,14},{10,... | collective-permute-start | bytes 1720328 | tf_op jit(solution)/shard_map/ppermute | solution.py:389
  90.3 4.2 %shard_map.118 = (bf16[160,768]{1,0:T(8,128)(2,1)S(1)}, bf16[160,768]{1,0:T(8,128)(2,1)S(1)}, bf16[160,768]{1,0:T(8,128)(2,1)S(1)}, bf16[160,768]{1,0:T(8,128)(2,1)S(1)}) custom-call(s32[1]{0:T(128)} %bitcast.3.refs_0_, bf16[80,3584]{1,0:T(8,128)(2,1)S(1)} %collective-permute-done.23.refs_2_.refs_1_.refs_26_, ...), custom_call_target="tpu_custom_call" | custom-call | tf_op jit(solution)/shard_map/pallas_call | solution.py:40
  94.5 1.3 collective-permute-start.26
  95.9 1.3 collective-permute-start.28
  97.7 3.7 %shard_map.119 = (bf16[80,1792]{1,0:T(8,128)(2,1)S(1)}, bf16[80,1792]{1,0:T(8,128)(2,1)S(1)}) custom-call(s32[1]{0:T(128)} %bitcast.3.refs_0_, bf16[160,768]{1,0:T(8,128)(2,1)S(1)} %shard_map.116.refs_1_.refs_9_, bf16[160,768]{1,0:T(8,128)(2,1)S(1)} %collective-permute-done.20.refs_2_.refs_10_, ...), custom_call_target="tpu_custom_call" | custom-call | tf_op jit(solution)/shard_map/pallas_call | solution.py:40
  103.3 4.8 %collective-permute-done.28.refs_3_ = bf16[160,768]{1,0:T(8,128)(2,1)S(1)} collective-permute-done((bf16[160,768]{1,0:T(8,128)(2,1)S(1)}, bf16[160,768]{1,0:T(8,128)(2,1)S(1)}, u32[]{:S(2)}, u32[]{:S(2)}) %collective-permute-start.28) | collective-permute-done | bytes 245792 | tf_op jit(solution)/shard_map/ppermute | solution.py:392
  108.3 2.1 %collective-permute-start.34 = (bf16[160,768]{1,0:T(8,128)(2,1)S(1)}, bf16[160,768]{1,0:T(8,128)(2,1)S(1)}, u32[]{:S(2)}, u32[]{:S(2)}) collective-permute-start(bf16[160,768]{1,0:T(8,128)(2,1)S(1)} %shard_map.120.refs_2_.refs_1_.refs_13_), channel_id=1, source_target_pairs={{0,24},{8,16},{16,8},{24,0},{1,25},{9,17},{17,9},{25,1},{2,26},{10... | collective-permute-start | bytes 737288 | tf_op jit(solution)/shard_map/ppermute | solution.py:392
  111.0 4.4 %collective-permute-done.29.refs_3_.refs_1_.refs_28_ = bf16[80,3584]{1,0:T(8,128)(2,1)S(1)} collective-permute-done((bf16[80,3584]{1,0:T(8,128)(2,1)S(1)}, bf16[80,3584]{1,0:T(8,128)(2,1)S(1)}, u32[]{:S(2)}, u32[]{:S(2)}) %collective-permute-start.29) | collective-permute-done | bytes 573472 | tf_op jit(solution)/shard_map/ppermute | solution.py:389
  115.6 4.0 %shard_map.122 = (bf16[80,768]{1,0:T(8,128)(2,1)S(1)}, bf16[80,768]{1,0:T(8,128)(2,1)S(1)}, bf16[80,768]{1,0:T(8,128)(2,1)S(1)}, bf16[80,768]{1,0:T(8,128)(2,1)S(1)}) custom-call(s32[1]{0:T(128)} %bitcast.3.refs_0_, bf16[80,3584]{1,0:T(8,128)(2,1)S(1)} %collective-permute-done.29.refs_3_.refs_1_.refs_28_, bf16[1792,1024]{1,0:T(8,128)(2,1)S(1)} %bitcast.17, ...), custom_call_target="tpu_custom_call" | custom-call | tf_op jit(solution)/shard_map/pallas_call | solution.py:40
  120.1 2.3 %collective-permute-done.33.refs_3_.refs_15_ = bf16[160,768]{1,0:T(8,128)(2,1)S(1)} collective-permute-done((bf16[160,768]{1,0:T(8,128)(2,1)S(1)}, bf16[160,768]{1,0:T(8,128)(2,1)S(1)}, u32[]{:S(2)}, u32[]{:S(2)}) %collective-permute-start.33) | collective-permute-done | bytes 245792 | tf_op jit(solution)/shard_map/ppermute | solution.py:392
  123.2 1.3 collective-permute-start.38
  124.5 3.7 %shard_map.123 = (bf16[80,1792]{1,0:T(8,128)(2,1)S(1)}, bf16[80,1792]{1,0:T(8,128)(2,1)S(1)}) custom-call(s32[1]{0:T(128)} %bitcast.3.refs_0_, bf16[160,768]{1,0:T(8,128)(2,1)S(1)} %shard_map.120.refs_2_.refs_1_.refs_13_, bf16[160,768]{1,0:T(8,128)(2,1)S(1)} %collective-permute-done.32.refs_2_.refs_14_, ...), custom_call_target="tpu_custom_call" | custom-call | tf_op jit(solution)/shard_map/pallas_call | solution.py:40
  128.4 1.3 collective-permute-start.41
  131.6 1.6 collective-permute-done.41.refs_4_.refs_20_
  133.2 1.7 %collective-permute-start.31 = (bf16[80,1792]{1,0:T(8,128)(2,1)S(1)}, bf16[80,1792]{1,0:T(8,128)(2,1)S(1)}, u32[]{:S(2)}, u32[]{:S(2)}) collective-permute-start(bf16[80,1792]{1,0:T(8,128)(2,1)S(1)} %get-tuple-element.71), channel_id=1, source_target_pairs={{0,2},{1,3},{2,0},{3,1},{4,6},{5,7},{6,4},{7,5},{8,10},{9,11},{10,... | collective-permute-start | bytes 860168 | tf_op jit(solution)/shard_map/ppermute | solution.py:389
  134.9 1.9 %collective-permute-start.35 = (bf16[80,1792]{1,0:T(8,128)(2,1)S(1)}, bf16[80,1792]{1,0:T(8,128)(2,1)S(1)}, u32[]{:S(2)}, u32[]{:S(2)}) collective-permute-start(bf16[80,1792]{1,0:T(8,128)(2,1)S(1)} %get-tuple-element.73.refs_4_), channel_id=1, source_target_pairs={{0,6},{1,7},{2,4},{3,5},{4,2},{5,3},{6,0},{7,1},{8,14},{9,15},{10,... | collective-permute-start | bytes 860168 | tf_op jit(solution)/shard_map/ppermute | solution.py:389
  136.9 5.4 %collective-permute-start.42 = (bf16[80,1792]{1,0:T(8,128)(2,1)S(1)}, bf16[80,1792]{1,0:T(8,128)(2,1)S(1)}, u32[]{:S(2)}, u32[]{:S(2)}) collective-permute-start(bf16[80,1792]{1,0:T(8,128)(2,1)S(1)} %get-tuple-element.80), channel_id=1, source_target_pairs={{0,3},{1,2},{2,1},{3,0},{4,7},{5,6},{6,5},{7,4},{8,11},{9,10},{10,... | collective-permute-start | bytes 860168 | tf_op jit(solution)/shard_map/ppermute | solution.py:389
  142.3 3.3 %shard_map.125.refs_31_ = bf16[80,1792]{1,0:T(8,128)(2,1)S(1)} custom-call(s32[1]{0:T(128)} %bitcast.3.refs_0_, bf16[80,768]{1,0:T(8,128)(2,1)S(1)} %shard_map.124.refs_1_.refs_7_.refs_17_, bf16[80,768]{1,0:T(8,128)(2,1)S(1)} %collective-permute-done.39.refs_2_.refs_18_, bf16[80,768]{1,0:T(8,128)(2,1)S(1)} %collective-permute-done.40.refs_3_.refs_19_, ...), custom_call_target="tpu_custom_call" | custom-call | tf_op jit(solution)/shard_map/pallas_call | solution.py:40
  145.7 10.7 %shard_map.126 = (bf16[1024,1792]{1,0:T(8,128)(2,1)}, bf16[1024,1792]{1,0:T(8,128)(2,1)}, f32[8,128]{1,0:T(8,128)S(1)}) custom-call(s32[1]{0:T(128)} %bitcast.3.refs_0_, bf16[160,768]{1,0:T(8,128)(2,1)S(1)} %shard_map.108.refs_5_.refs_1_, bf16[160,768]{1,0:T(8,128)(2,1)S(1)} %collective-permute-done.5.refs_2_, ...), custom_call_target="tpu_custom_call" | custom-call | tf_op jit(solution)/shard_map/pallas_call | solution.py:40
  156.4 1.6 shard_map.127
  158.1 3.7 %collective-permute-done.42.refs_3_ = bf16[80,1792]{1,0:T(8,128)(2,1)S(1)} collective-permute-done((bf16[80,1792]{1,0:T(8,128)(2,1)S(1)}, bf16[80,1792]{1,0:T(8,128)(2,1)S(1)}, u32[]{:S(2)}, u32[]{:S(2)}) %collective-permute-start.42) | collective-permute-done | bytes 286752 | tf_op jit(solution)/shard_map/ppermute | solution.py:389
  161.8 2.4 %collective-permute-done.43.refs_4_ = bf16[80,1792]{1,0:T(8,128)(2,1)S(1)} collective-permute-done((bf16[80,1792]{1,0:T(8,128)(2,1)S(1)}, bf16[80,1792]{1,0:T(8,128)(2,1)S(1)}, u32[]{:S(2)}, u32[]{:S(2)}) %collective-permute-start.43) | collective-permute-done | bytes 286752 | tf_op jit(solution)/shard_map/ppermute | solution.py:389
  164.3 1.8 %shard_map.128 = bf16[512,1792]{1,0:T(8,128)(2,1)} custom-call(bf16[512,240]{1,0:T(8,128)(2,1)S(1)} %get-tuple-element.78.refs_0_, bf16[512,1792]{1,0:T(8,128)(2,1)S(1)} %get-tuple-element.79.refs_1_, bf16[160,1792]{1,0:T(8,128)(2,1)S(1)} %collective-permute-done.30.refs_4_.refs_2_, bf16[80,1792]{1,0:T(8,128)(2,1)S(1)} %collective-permute-done.42.refs_3_, ...), custom_call_target="tpu_custom_call" | custom-call | tf_op jit(solution)/shard_map/pallas_call | solution.py:40
  (96 shorter events, 22.7 us)
Async XLA Ops:
  4.2 8.6 %collective-permute-start = (bf16[80,3584]{1,0:T(8,128)(2,1)}, bf16[80,3584]{1,0:T(8,128)(2,1)S(1)}, u32[]{:S(2)}, u32[]{:S(2)}) collective-permute-start(bf16[80,3584]{1,0:T(8,128)(2,1)} %get-tuple-element.46), channel_id=1, source_target_pairs={{0,1},{1,0},{2,3},{3,2},{4,5},{5,4},{6,7},{7,6},{8,9},{9,8},{10,11... | collective-permute-start | bytes 1720328 | tf_op jit(solution)/shard_map/ppermute | solution.py:389
  5.0 27.6 %collective-permute-start.4 = (bf16[80,3584]{1,0:T(8,128)(2,1)}, bf16[80,3584]{1,0:T(8,128)(2,1)S(1)}, u32[]{:S(2)}, u32[]{:S(2)}) collective-permute-start(bf16[80,3584]{1,0:T(8,128)(2,1)} %get-tuple-element.44.refs_5_), channel_id=1, source_target_pairs={{0,4},{1,5},{2,6},{3,7},{4,0},{5,1},{6,2},{7,3},{8,12},{9,13},{10,... | collective-permute-start | bytes 1720328 | tf_op jit(solution)/shard_map/ppermute | solution.py:389
  20.0 20.9 %copy-start.3 = (bf16[1,1792,1024]{2,1,0:T(8,128)(2,1)S(1)}, bf16[1,1792,1024]{2,1,0:T(8,128)(2,1)}, u32[]{:S(2)}) copy-start(bf16[1,1792,1024]{2,1,0:T(8,128)(2,1)} %param.13) | copy-start | bytes 11010052
  20.0 20.9 %copy-start.5 = (bf16[1,1024,1792]{2,1,0:T(8,128)(2,1)S(1)}, bf16[1,1024,1792]{2,1,0:T(8,128)(2,1)}, u32[]{:S(2)}) copy-start(bf16[1,1024,1792]{2,1,0:T(8,128)(2,1)} %param.14) | copy-start | bytes 11010052
  24.5 16.5 %copy-start.1 = (bf16[1,1792,1024]{2,1,0:T(8,128)(2,1)S(1)}, bf16[1,1792,1024]{2,1,0:T(8,128)(2,1)}, u32[]{:S(2)}) copy-start(bf16[1,1792,1024]{2,1,0:T(8,128)(2,1)} %param.12) | copy-start | bytes 11010052
  24.5 11.4 %collective-permute-start.1 = (bf16[160,768]{1,0:T(8,128)(2,1)S(1)}, bf16[160,768]{1,0:T(8,128)(2,1)S(1)}, u32[]{:S(2)}, u32[]{:S(2)}) collective-permute-start(bf16[160,768]{1,0:T(8,128)(2,1)S(1)} %get-tuple-element.48), channel_id=1, source_target_pairs={{0,8},{8,0},{16,24},{24,16},{1,9},{9,1},{17,25},{25,17},{2,10},{10... | collective-permute-start | bytes 737288 | tf_op jit(solution)/shard_map/ppermute | solution.py:392
  25.8 10.1 %collective-permute-start.2 = (bf16[160,768]{1,0:T(8,128)(2,1)S(1)}, bf16[160,768]{1,0:T(8,128)(2,1)S(1)}, u32[]{:S(2)}, u32[]{:S(2)}) collective-permute-start(bf16[160,768]{1,0:T(8,128)(2,1)S(1)} %get-tuple-element.49), channel_id=1, source_target_pairs={{0,16},{8,24},{16,0},{24,8},{1,17},{9,25},{17,1},{25,9},{2,18},{10... | collective-permute-start | bytes 737288 | tf_op jit(solution)/shard_map/ppermute | solution.py:392
  27.0 11.0 %collective-permute-start.3 = (bf16[160,768]{1,0:T(8,128)(2,1)S(1)}, bf16[160,768]{1,0:T(8,128)(2,1)S(1)}, u32[]{:S(2)}, u32[]{:S(2)}) collective-permute-start(bf16[160,768]{1,0:T(8,128)(2,1)S(1)} %get-tuple-element.50), channel_id=1, source_target_pairs={{0,24},{8,16},{16,8},{24,0},{1,25},{9,17},{17,9},{25,1},{2,26},{10... | collective-permute-start | bytes 737288 | tf_op jit(solution)/shard_map/ppermute | solution.py:392
  32.5 26.1 %collective-permute-start.16 = (bf16[80,3584]{1,0:T(8,128)(2,1)S(1)}, bf16[80,3584]{1,0:T(8,128)(2,1)S(1)}, u32[]{:S(2)}, u32[]{:S(2)}) collective-permute-start(bf16[80,3584]{1,0:T(8,128)(2,1)S(1)} %shard_map.107.refs_4_), channel_id=1, source_target_pairs={{0,2},{1,3},{2,0},{3,1},{4,6},{5,7},{6,4},{7,5},{8,10},{9,11},{10,... | collective-permute-start | bytes 1720328 | tf_op jit(solution)/shard_map/ppermute | solution.py:389
  33.2 27.9 %collective-permute-start.15 = (bf16[80,3584]{1,0:T(8,128)(2,1)S(1)}, bf16[80,3584]{1,0:T(8,128)(2,1)S(1)}, u32[]{:S(2)}, u32[]{:S(2)}) collective-permute-start(bf16[80,3584]{1,0:T(8,128)(2,1)S(1)} %shard_map.106.refs_1_), channel_id=1, source_target_pairs={{0,5},{1,4},{2,7},{3,6},{4,1},{5,0},{6,3},{7,2},{8,13},{9,12},{10,... | collective-permute-start | bytes 1720328 | tf_op jit(solution)/shard_map/ppermute | solution.py:389
  38.2 7.1 %collective-permute-start.7 = (bf16[160,768]{1,0:T(8,128)(2,1)S(1)}, bf16[160,768]{1,0:T(8,128)(2,1)S(1)}, u32[]{:S(2)}, u32[]{:S(2)}) collective-permute-start(bf16[160,768]{1,0:T(8,128)(2,1)S(1)} %shard_map.108.refs_5_.refs_1_), channel_id=1, source_target_pairs={{0,24},{8,16},{16,8},{24,0},{1,25},{9,17},{17,9},{25,1},{2,26},{10... | collective-permute-start | bytes 737288 | tf_op jit(solution)/shard_map/ppermute | solution.py:392
  39.5 12.9 %collective-permute-start.6 = (bf16[160,768]{1,0:T(8,128)(2,1)S(1)}, bf16[160,768]{1,0:T(8,128)(2,1)S(1)}, u32[]{:S(2)}, u32[]{:S(2)}) collective-permute-start(bf16[160,768]{1,0:T(8,128)(2,1)S(1)} %shard_map.108.refs_5_.refs_1_), channel_id=1, source_target_pairs={{0,16},{8,24},{16,0},{24,8},{1,17},{9,25},{17,1},{25,9},{2,18},{10... | collective-permute-start | bytes 737288 | tf_op jit(solution)/shard_map/ppermute | solution.py:392
  40.6 12.8 %collective-permute-start.5 = (bf16[160,768]{1,0:T(8,128)(2,1)S(1)}, bf16[160,768]{1,0:T(8,128)(2,1)S(1)}, u32[]{:S(2)}, u32[]{:S(2)}) collective-permute-start(bf16[160,768]{1,0:T(8,128)(2,1)S(1)} %shard_map.108.refs_5_.refs_1_), channel_id=1, source_target_pairs={{0,8},{8,0},{16,24},{24,16},{1,9},{9,1},{17,25},{25,17},{2,10},{10... | collective-permute-start | bytes 737288 | tf_op jit(solution)/shard_map/ppermute | solution.py:392
  45.3 13.1 %collective-permute-start.9 = (bf16[80,768]{1,0:T(8,128)(2,1)S(1)}, bf16[80,768]{1,0:T(8,128)(2,1)S(1)}, u32[]{:S(2)}, u32[]{:S(2)}) collective-permute-start(bf16[80,768]{1,0:T(8,128)(2,1)S(1)} %get-tuple-element.56), channel_id=1, source_target_pairs={{0,8},{8,0},{16,24},{24,16},{1,9},{9,1},{17,25},{25,17},{2,10},{10... | collective-permute-start | bytes 368648 | tf_op jit(solution)/shard_map/ppermute | solution.py:392
  52.4 6.0 %collective-permute-start.10 = (bf16[80,768]{1,0:T(8,128)(2,1)S(1)}, bf16[80,768]{1,0:T(8,128)(2,1)S(1)}, u32[]{:S(2)}, u32[]{:S(2)}) collective-permute-start(bf16[80,768]{1,0:T(8,128)(2,1)S(1)} %get-tuple-element.57), channel_id=1, source_target_pairs={{0,16},{8,24},{16,0},{24,8},{1,17},{9,25},{17,1},{25,9},{2,18},{10... | collective-permute-start | bytes 368648 | tf_op jit(solution)/shard_map/ppermute | solution.py:392
  53.5 5.1 %collective-permute-start.11 = (bf16[80,768]{1,0:T(8,128)(2,1)S(1)}, bf16[80,768]{1,0:T(8,128)(2,1)S(1)}, u32[]{:S(2)}, u32[]{:S(2)}) collective-permute-start(bf16[80,768]{1,0:T(8,128)(2,1)S(1)} %get-tuple-element.58), channel_id=1, source_target_pairs={{0,24},{8,16},{16,8},{24,0},{1,25},{9,17},{17,9},{25,1},{2,26},{10... | collective-permute-start | bytes 368648 | tf_op jit(solution)/shard_map/ppermute | solution.py:392
  58.7 26.6 %collective-permute-start.23 = (bf16[80,3584]{1,0:T(8,128)(2,1)S(1)}, bf16[80,3584]{1,0:T(8,128)(2,1)S(1)}, u32[]{:S(2)}, u32[]{:S(2)}) collective-permute-start(bf16[80,3584]{1,0:T(8,128)(2,1)S(1)} %shard_map.112.refs_1_), channel_id=1, source_target_pairs={{0,6},{1,7},{2,4},{3,5},{4,2},{5,3},{6,0},{7,1},{8,14},{9,15},{10,... | collective-permute-start | bytes 1720328 | tf_op jit(solution)/shard_map/ppermute | solution.py:389
  61.2 25.5 %collective-permute-start.24 = (bf16[80,3584]{1,0:T(8,128)(2,1)S(1)}, bf16[80,3584]{1,0:T(8,128)(2,1)S(1)}, u32[]{:S(2)}, u32[]{:S(2)}) collective-permute-start(bf16[80,3584]{1,0:T(8,128)(2,1)S(1)} %shard_map.113.refs_6_), channel_id=1, source_target_pairs={{0,3},{1,2},{2,1},{3,0},{4,7},{5,6},{6,5},{7,4},{8,11},{9,10},{10,... | collective-permute-start | bytes 1720328 | tf_op jit(solution)/shard_map/ppermute | solution.py:389
  62.5 6.9 %collective-permute-start.14 = (bf16[80,768]{1,0:T(8,128)(2,1)S(1)}, bf16[80,768]{1,0:T(8,128)(2,1)S(1)}, u32[]{:S(2)}, u32[]{:S(2)}) collective-permute-start(bf16[80,768]{1,0:T(8,128)(2,1)S(1)} %shard_map.111.refs_1_.refs_5_), channel_id=1, source_target_pairs={{0,24},{8,16},{16,8},{24,0},{1,25},{9,17},{17,9},{25,1},{2,26},{10... | collective-permute-start | bytes 368648 | tf_op jit(solution)/shard_map/ppermute | solution.py:392
  64.6 6.6 %collective-permute-start.13 = (bf16[80,768]{1,0:T(8,128)(2,1)S(1)}, bf16[80,768]{1,0:T(8,128)(2,1)S(1)}, u32[]{:S(2)}, u32[]{:S(2)}) collective-permute-start(bf16[80,768]{1,0:T(8,128)(2,1)S(1)} %shard_map.111.refs_1_.refs_5_), channel_id=1, source_target_pairs={{0,16},{8,24},{16,0},{24,8},{1,17},{9,25},{17,1},{25,9},{2,18},{10... | collective-permute-start | bytes 368648 | tf_op jit(solution)/shard_map/ppermute | solution.py:392
  64.9 7.6 %collective-permute-start.12 = (bf16[80,768]{1,0:T(8,128)(2,1)S(1)}, bf16[80,768]{1,0:T(8,128)(2,1)S(1)}, u32[]{:S(2)}, u32[]{:S(2)}) collective-permute-start(bf16[80,768]{1,0:T(8,128)(2,1)S(1)} %shard_map.111.refs_1_.refs_5_), channel_id=1, source_target_pairs={{0,8},{8,0},{16,24},{24,16},{1,9},{9,1},{17,25},{25,17},{2,10},{10... | collective-permute-start | bytes 368648 | tf_op jit(solution)/shard_map/ppermute | solution.py:392
  69.4 7.6 %collective-permute-start.17 = (bf16[160,768]{1,0:T(8,128)(2,1)S(1)}, bf16[160,768]{1,0:T(8,128)(2,1)S(1)}, u32[]{:S(2)}, u32[]{:S(2)}) collective-permute-start(bf16[160,768]{1,0:T(8,128)(2,1)S(1)} %get-tuple-element.62), channel_id=1, source_target_pairs={{0,8},{8,0},{16,24},{24,16},{1,9},{9,1},{17,25},{25,17},{2,10},{10... | collective-permute-start | bytes 737288 | tf_op jit(solution)/shard_map/ppermute | solution.py:392
  71.3 7.6 %collective-permute-start.18 = (bf16[160,768]{1,0:T(8,128)(2,1)S(1)}, bf16[160,768]{1,0:T(8,128)(2,1)S(1)}, u32[]{:S(2)}, u32[]{:S(2)}) collective-permute-start(bf16[160,768]{1,0:T(8,128)(2,1)S(1)} %get-tuple-element.63), channel_id=1, source_target_pairs={{0,16},{8,24},{16,0},{24,8},{1,17},{9,25},{17,1},{25,9},{2,18},{10... | collective-permute-start | bytes 737288 | tf_op jit(solution)/shard_map/ppermute | solution.py:392
  72.5 9.3 %collective-permute-start.19 = (bf16[160,768]{1,0:T(8,128)(2,1)S(1)}, bf16[160,768]{1,0:T(8,128)(2,1)S(1)}, u32[]{:S(2)}, u32[]{:S(2)}) collective-permute-start(bf16[160,768]{1,0:T(8,128)(2,1)S(1)} %get-tuple-element.64), channel_id=1, source_target_pairs={{0,24},{8,16},{16,8},{24,0},{1,25},{9,17},{17,9},{25,1},{2,26},{10... | collective-permute-start | bytes 737288 | tf_op jit(solution)/shard_map/ppermute | solution.py:392
  73.7 13.0 %copy-start.9 = (bf16[80,3584]{1,0:T(8,128)(2,1)S(1)}, bf16[80,3584]{1,0:T(8,128)(2,1)}, u32[]{:S(2)}) copy-start(bf16[80,3584]{1,0:T(8,128)(2,1)} %get-tuple-element.65.refs_0_) | copy-start | bytes 1720324
  82.0 13.8 %collective-permute-start.22 = (bf16[160,768]{1,0:T(8,128)(2,1)S(1)}, bf16[160,768]{1,0:T(8,128)(2,1)S(1)}, u32[]{:S(2)}, u32[]{:S(2)}) collective-permute-start(bf16[160,768]{1,0:T(8,128)(2,1)S(1)} %shard_map.116.refs_1_.refs_9_), channel_id=1, source_target_pairs={{0,24},{8,16},{16,8},{24,0},{1,25},{9,17},{17,9},{25,1},{2,26},{10... | collective-permute-start | bytes 737288 | tf_op jit(solution)/shard_map/ppermute | solution.py:392
  83.2 12.7 %collective-permute-start.21 = (bf16[160,768]{1,0:T(8,128)(2,1)S(1)}, bf16[160,768]{1,0:T(8,128)(2,1)S(1)}, u32[]{:S(2)}, u32[]{:S(2)}) collective-permute-start(bf16[160,768]{1,0:T(8,128)(2,1)S(1)} %shard_map.116.refs_1_.refs_9_), channel_id=1, source_target_pairs={{0,16},{8,24},{16,0},{24,8},{1,17},{9,25},{17,1},{25,9},{2,18},{10... | collective-permute-start | bytes 737288 | tf_op jit(solution)/shard_map/ppermute | solution.py:392
  86.6 28.7 %collective-permute-start.29 = (bf16[80,3584]{1,0:T(8,128)(2,1)S(1)}, bf16[80,3584]{1,0:T(8,128)(2,1)S(1)}, u32[]{:S(2)}, u32[]{:S(2)}) collective-permute-start(bf16[80,3584]{1,0:T(8,128)(2,1)S(1)} %shard_map.117.refs_6_), channel_id=1, source_target_pairs={{0,7},{1,6},{2,5},{3,4},{4,3},{5,2},{6,1},{7,0},{8,15},{9,14},{10,... | collective-permute-start | bytes 1720328 | tf_op jit(solution)/shard_map/ppermute | solution.py:389
  90.0 7.7 %collective-permute-start.20 = (bf16[160,768]{1,0:T(8,128)(2,1)S(1)}, bf16[160,768]{1,0:T(8,128)(2,1)S(1)}, u32[]{:S(2)}, u32[]{:S(2)}) collective-permute-start(bf16[160,768]{1,0:T(8,128)(2,1)S(1)} %shard_map.116.refs_1_.refs_9_), channel_id=1, source_target_pairs={{0,8},{8,0},{16,24},{24,16},{1,9},{9,1},{17,25},{25,17},{2,10},{10... | collective-permute-start | bytes 737288 | tf_op jit(solution)/shard_map/ppermute | solution.py:392
  94.5 8.5 %collective-permute-start.26 = (bf16[160,768]{1,0:T(8,128)(2,1)S(1)}, bf16[160,768]{1,0:T(8,128)(2,1)S(1)}, u32[]{:S(2)}, u32[]{:S(2)}) collective-permute-start(bf16[160,768]{1,0:T(8,128)(2,1)S(1)} %get-tuple-element.68), channel_id=1, source_target_pairs={{0,8},{8,0},{16,24},{24,16},{1,9},{9,1},{17,25},{25,17},{2,10},{10... | collective-permute-start | bytes 737288 | tf_op jit(solution)/shard_map/ppermute | solution.py:392
  95.8 7.5 %collective-permute-start.27 = (bf16[160,768]{1,0:T(8,128)(2,1)S(1)}, bf16[160,768]{1,0:T(8,128)(2,1)S(1)}, u32[]{:S(2)}, u32[]{:S(2)}) collective-permute-start(bf16[160,768]{1,0:T(8,128)(2,1)S(1)} %get-tuple-element.69), channel_id=1, source_target_pairs={{0,16},{8,24},{16,0},{24,8},{1,17},{9,25},{17,1},{25,9},{2,18},{10... | collective-permute-start | bytes 737288 | tf_op jit(solution)/shard_map/ppermute | solution.py:392
  95.9 12.2 %collective-permute-start.28 = (bf16[160,768]{1,0:T(8,128)(2,1)S(1)}, bf16[160,768]{1,0:T(8,128)(2,1)S(1)}, u32[]{:S(2)}, u32[]{:S(2)}) collective-permute-start(bf16[160,768]{1,0:T(8,128)(2,1)S(1)} %get-tuple-element.70), channel_id=1, source_target_pairs={{0,24},{8,16},{16,8},{24,0},{1,25},{9,17},{17,9},{25,1},{2,26},{10... | collective-permute-start | bytes 737288 | tf_op jit(solution)/shard_map/ppermute | solution.py:392
  101.4 9.6 %collective-permute-start.25 = (bf16[80,1792]{1,0:T(8,128)(2,1)S(1)}, bf16[80,1792]{1,0:T(8,128)(2,1)S(1)}, u32[]{:S(2)}, u32[]{:S(2)}) collective-permute-start(bf16[80,1792]{1,0:T(8,128)(2,1)S(1)} %get-tuple-element.67.refs_4_), channel_id=1, source_target_pairs={{0,1},{1,0},{2,3},{3,2},{4,5},{5,4},{6,7},{7,6},{8,9},{9,8},{10,11... | collective-permute-start | bytes 860168 | tf_op jit(solution)/shard_map/ppermute | solution.py:389
  108.3 11.4 %collective-permute-start.34 = (bf16[160,768]{1,0:T(8,128)(2,1)S(1)}, bf16[160,768]{1,0:T(8,128)(2,1)S(1)}, u32[]{:S(2)}, u32[]{:S(2)}) collective-permute-start(bf16[160,768]{1,0:T(8,128)(2,1)S(1)} %shard_map.120.refs_2_.refs_1_.refs_13_), channel_id=1, source_target_pairs={{0,24},{8,16},{16,8},{24,0},{1,25},{9,17},{17,9},{25,1},{2,26},{10... | collective-permute-start | bytes 737288 | tf_op jit(solution)/shard_map/ppermute | solution.py:392
  110.4 12.0 %collective-permute-start.33 = (bf16[160,768]{1,0:T(8,128)(2,1)S(1)}, bf16[160,768]{1,0:T(8,128)(2,1)S(1)}, u32[]{:S(2)}, u32[]{:S(2)}) collective-permute-start(bf16[160,768]{1,0:T(8,128)(2,1)S(1)} %shard_map.120.refs_2_.refs_1_.refs_13_), channel_id=1, source_target_pairs={{0,16},{8,24},{16,0},{24,8},{1,17},{9,25},{17,1},{25,9},{2,18},{10... | collective-permute-start | bytes 737288 | tf_op jit(solution)/shard_map/ppermute | solution.py:392
  110.4 12.8 %collective-permute-start.32 = (bf16[160,768]{1,0:T(8,128)(2,1)S(1)}, bf16[160,768]{1,0:T(8,128)(2,1)S(1)}, u32[]{:S(2)}, u32[]{:S(2)}) collective-permute-start(bf16[160,768]{1,0:T(8,128)(2,1)S(1)} %shard_map.120.refs_2_.refs_1_.refs_13_), channel_id=1, source_target_pairs={{0,8},{8,0},{16,24},{24,16},{1,9},{9,1},{17,25},{25,17},{2,10},{10... | collective-permute-start | bytes 737288 | tf_op jit(solution)/shard_map/ppermute | solution.py:392
  115.4 41.0 %collective-permute-start.30 = (bf16[160,1792]{1,0:T(8,128)(2,1)S(1)}, bf16[160,1792]{1,0:T(8,128)(2,1)S(1)}, u32[]{:S(2)}, u32[]{:S(2)}) collective-permute-start(bf16[160,1792]{1,0:T(8,128)(2,1)S(1)} %shard_map.121.refs_5_), channel_id=1, source_target_pairs={{0,4},{1,5},{2,6},{3,7},{4,0},{5,1},{6,2},{7,3},{8,12},{9,13},{10,... | collective-permute-start | bytes 1720328 | tf_op jit(solution)/shard_map/ppermute | solution.py:389
  115.5 30.1 %collective-permute-start.8 = (bf16[80,1792]{1,0:T(8,128)(2,1)S(1)}, bf16[80,1792]{1,0:T(8,128)(2,1)S(1)}, u32[]{:S(2)}, u32[]{:S(2)}) collective-permute-start(bf16[80,1792]{1,0:T(8,128)(2,1)S(1)} %get-tuple-element.55), channel_id=1, source_target_pairs={{0,1},{1,0},{2,3},{3,2},{4,5},{5,4},{6,7},{7,6},{8,9},{9,8},{10,11... | collective-permute-start | bytes 860168 | tf_op jit(solution)/shard_map/ppermute | solution.py:389
  119.6 8.5 %collective-permute-start.36 = (bf16[80,768]{1,0:T(8,128)(2,1)S(1)}, bf16[80,768]{1,0:T(8,128)(2,1)S(1)}, u32[]{:S(2)}, u32[]{:S(2)}) collective-permute-start(bf16[80,768]{1,0:T(8,128)(2,1)S(1)} %get-tuple-element.74), channel_id=1, source_target_pairs={{0,8},{8,0},{16,24},{24,16},{1,9},{9,1},{17,25},{25,17},{2,10},{10... | collective-permute-start | bytes 368648 | tf_op jit(solution)/shard_map/ppermute | solution.py:392
  122.4 5.8 %collective-permute-start.37 = (bf16[80,768]{1,0:T(8,128)(2,1)S(1)}, bf16[80,768]{1,0:T(8,128)(2,1)S(1)}, u32[]{:S(2)}, u32[]{:S(2)}) collective-permute-start(bf16[80,768]{1,0:T(8,128)(2,1)S(1)} %get-tuple-element.75), channel_id=1, source_target_pairs={{0,16},{8,24},{16,0},{24,8},{1,17},{9,25},{17,1},{25,9},{2,18},{10... | collective-permute-start | bytes 368648 | tf_op jit(solution)/shard_map/ppermute | solution.py:392
  123.2 5.1 %collective-permute-start.38 = (bf16[80,768]{1,0:T(8,128)(2,1)S(1)}, bf16[80,768]{1,0:T(8,128)(2,1)S(1)}, u32[]{:S(2)}, u32[]{:S(2)}) collective-permute-start(bf16[80,768]{1,0:T(8,128)(2,1)S(1)} %get-tuple-element.76), channel_id=1, source_target_pairs={{0,24},{8,16},{16,8},{24,0},{1,25},{9,17},{17,9},{25,1},{2,26},{10... | collective-permute-start | bytes 368648 | tf_op jit(solution)/shard_map/ppermute | solution.py:392
  128.4 4.8 %collective-permute-start.41 = (bf16[80,768]{1,0:T(8,128)(2,1)S(1)}, bf16[80,768]{1,0:T(8,128)(2,1)S(1)}, u32[]{:S(2)}, u32[]{:S(2)}) collective-permute-start(bf16[80,768]{1,0:T(8,128)(2,1)S(1)} %shard_map.124.refs_1_.refs_7_.refs_17_), channel_id=1, source_target_pairs={{0,24},{8,16},{16,8},{24,0},{1,25},{9,17},{17,9},{25,1},{2,26},{10... | collective-permute-start | bytes 368648 | tf_op jit(solution)/shard_map/ppermute | solution.py:392
  129.7 5.2 %collective-permute-start.40 = (bf16[80,768]{1,0:T(8,128)(2,1)S(1)}, bf16[80,768]{1,0:T(8,128)(2,1)S(1)}, u32[]{:S(2)}, u32[]{:S(2)}) collective-permute-start(bf16[80,768]{1,0:T(8,128)(2,1)S(1)} %shard_map.124.refs_1_.refs_7_.refs_17_), channel_id=1, source_target_pairs={{0,16},{8,24},{16,0},{24,8},{1,17},{9,25},{17,1},{25,9},{2,18},{10... | collective-permute-start | bytes 368648 | tf_op jit(solution)/shard_map/ppermute | solution.py:392
  130.5 6.3 %collective-permute-start.39 = (bf16[80,768]{1,0:T(8,128)(2,1)S(1)}, bf16[80,768]{1,0:T(8,128)(2,1)S(1)}, u32[]{:S(2)}, u32[]{:S(2)}) collective-permute-start(bf16[80,768]{1,0:T(8,128)(2,1)S(1)} %shard_map.124.refs_1_.refs_7_.refs_17_), channel_id=1, source_target_pairs={{0,8},{8,0},{16,24},{24,16},{1,9},{9,1},{17,25},{25,17},{2,10},{10... | collective-permute-start | bytes 368648 | tf_op jit(solution)/shard_map/ppermute | solution.py:392
  133.2 23.2 %collective-permute-start.31 = (bf16[80,1792]{1,0:T(8,128)(2,1)S(1)}, bf16[80,1792]{1,0:T(8,128)(2,1)S(1)}, u32[]{:S(2)}, u32[]{:S(2)}) collective-permute-start(bf16[80,1792]{1,0:T(8,128)(2,1)S(1)} %get-tuple-element.71), channel_id=1, source_target_pairs={{0,2},{1,3},{2,0},{3,1},{4,6},{5,7},{6,4},{7,5},{8,10},{9,11},{10,... | collective-permute-start | bytes 860168 | tf_op jit(solution)/shard_map/ppermute | solution.py:389
  134.9 21.5 %collective-permute-start.35 = (bf16[80,1792]{1,0:T(8,128)(2,1)S(1)}, bf16[80,1792]{1,0:T(8,128)(2,1)S(1)}, u32[]{:S(2)}, u32[]{:S(2)}) collective-permute-start(bf16[80,1792]{1,0:T(8,128)(2,1)S(1)} %get-tuple-element.73.refs_4_), channel_id=1, source_target_pairs={{0,6},{1,7},{2,4},{3,5},{4,2},{5,3},{6,0},{7,1},{8,14},{9,15},{10,... | collective-permute-start | bytes 860168 | tf_op jit(solution)/shard_map/ppermute | solution.py:389
  136.9 24.9 %collective-permute-start.42 = (bf16[80,1792]{1,0:T(8,128)(2,1)S(1)}, bf16[80,1792]{1,0:T(8,128)(2,1)S(1)}, u32[]{:S(2)}, u32[]{:S(2)}) collective-permute-start(bf16[80,1792]{1,0:T(8,128)(2,1)S(1)} %get-tuple-element.80), channel_id=1, source_target_pairs={{0,3},{1,2},{2,1},{3,0},{4,7},{5,6},{6,5},{7,4},{8,11},{9,10},{10,... | collective-permute-start | bytes 860168 | tf_op jit(solution)/shard_map/ppermute | solution.py:389
  145.6 18.6 %collective-permute-start.43 = (bf16[80,1792]{1,0:T(8,128)(2,1)S(1)}, bf16[80,1792]{1,0:T(8,128)(2,1)S(1)}, u32[]{:S(2)}, u32[]{:S(2)}) collective-permute-start(bf16[80,1792]{1,0:T(8,128)(2,1)S(1)} %shard_map.125.refs_31_), channel_id=1, source_target_pairs={{0,7},{1,6},{2,5},{3,4},{4,3},{5,2},{6,1},{7,0},{8,15},{9,14},{10,... | collective-permute-start | bytes 860168 | tf_op jit(solution)/shard_map/ppermute | solution.py:389
  (11 other events, 65.7 us)
